TPU v7x, 32 devices: a whole 2x2x4 slice. The times are simulated.
32 devices in a mesh: dp: 8 (over y, x, core), head: 4 (over z).
Axes of the slice: x: 2, y: 2, z: 4, core: 2. Of those that a mesh axis runs over, the one named last changes fastest.
Arguments:
- stream_in: float32 [16384, 1024], P('dp', 'head'), may hold values from -60 to 60
- qkv_weight: bfloat16 [2, 3, 1024, 1024], P(None, None, 'dp', 'head'), may hold values from -0.1875 to 0.1875
- out_weight: bfloat16 [2, 1024, 1024], P(None, 'head', 'dp'), may hold values from -0.1875 to 0.1875
- up_weight: bfloat16 [2, 1024, 4096], P(None, 'dp', 'head'), may hold values from -2 to 2
- down_weight: bfloat16 [2, 4096, 1024], P(None, 'head', 'dp'), may hold values from -0.09375 to 0.09375
- norm_gains: float32 [2, 3, 1024], P(None, None, 'head'), may hold values from 0.5 to 1.5
- norm_shifts: float32 [2, 3, 1024], P(None, None, 'head'), may hold values from -1.8 to 1.8
- hidden_gains: float32 [2, 4096], P(None, 'head'), may hold values from 0.5 to 1.5
- hidden_shifts: float32 [2, 4096], P(None, 'head'), may hold values from -1.8 to 1.8
- buckets: int32 [8], P('dp'), may hold values from 0 to 1, as said below
- valid_mask: int32 [16384], P('dp'), may hold values from 0 to 1, as said below
- cotangent: float32 [16384, 1024], P('dp', 'head'), may hold values from -6 to 6
Outputs:
- stream_out: float32 [16384, 1024], P('dp', 'head')
- stream_grad: float32 [16384, 1024], P('dp', 'head')
- qkv_grad: float32 [2, 3, 1024, 1024], P(None, None, 'dp', 'head')
- out_grad: float32 [2, 1024, 1024], P(None, 'head', 'dp')
- up_grad: float32 [2, 1024, 4096], P(None, 'dp', 'head')
- down_grad: float32 [2, 4096, 1024], P(None, 'head', 'dp')
- gains_grad: float32 [2, 3, 1024], P(None, None, 'head')
- shifts_grad: float32 [2, 3, 1024], P(None, None, 'head')
- hidden_gains_grad: float32 [2, 4096], P(None, 'head')
- hidden_shifts_grad: float32 [2, 4096], P(None, 'head')
- usage_rms: float32 [2, 3], replicated
Inputs may be any that keep to these rules, and one draw needn't show every extreme that they name: `buckets`: 0: the slab holds 4 sequences of 512 tokens; 1: the slab holds one sequence of 2048 tokens. `valid_mask`: the real tokens of each sequence are a prefix of it, a quarter of its length or more.
All inputs are finite; a program needn't handle non-finite values.
Results may differ from a plain program's by a relative error of at most 0.038.
Values may be sent and summed in bfloat16 or wider, within the bound.
A program may use at most 320 MiB of HBM per device.

v0:
```python
from functools import partial
import math

import jax
import jax.numpy as jnp
from jax import lax
from jax.sharding import PartitionSpec as P

D = 1024
DH = 64
FF = 4096
LONG = 2048
SHORT = 512


norm_eps = 1e-05
masked_score = -1000000000.0


def full_norm(values, scale_row, shift_row):
    row_mean = jnp.mean(values, axis=1)
    centred = values - row_mean[:, None]
    row_scale = lax.rsqrt(jnp.mean(centred * centred, axis=1) + norm_eps)
    return (centred * row_scale[:, None] * scale_row + shift_row, row_mean, row_scale)


def widen(low_stream, scale_row, shift_row):
    gathered, scale_all, shift_all = (
        lax.all_gather(low_stream, "head", axis=1, tiled=True),
        lax.all_gather(scale_row.astype(jnp.bfloat16), "head", axis=0, tiled=True).astype(
            scale_row.dtype
        ),
        lax.all_gather(shift_row.astype(jnp.bfloat16), "head", axis=0, tiled=True).astype(
            shift_row.dtype
        ),
    )
    return full_norm(gathered.astype(jnp.float32), scale_all, shift_all)


def narrow(partial_sum):
    return lax.psum_scatter(
        partial_sum.astype(jnp.bfloat16), "head", scatter_dimension=1, tiled=True
    ).astype(jnp.float32)


def spread_grad(grad_low):
    return lax.all_gather(grad_low, "head", axis=1, tiled=True)


def collect(grad_term):
    return lax.psum_scatter(
        grad_term.astype(jnp.bfloat16), "head", scatter_dimension=1, tiled=True
    ).astype(jnp.float32)


def split_norm(values, scale_row, shift_row, full_width):
    row_mean = lax.psum(jnp.sum(values, axis=1), "head") / full_width
    centred = values - row_mean[:, None]
    variance = lax.psum(jnp.sum(centred * centred, axis=1), "head") / full_width
    row_scale = lax.rsqrt(variance + norm_eps)
    normal_hat = (values - row_mean[:, None]) * row_scale[:, None]
    return (normal_hat * scale_row + shift_row, row_mean, row_scale)


def split_back(grad_out, normal_hat, row_scale, scale_row, full_width):
    grad_hat = grad_out * scale_row
    first_sum, cross_sum = lax.psum(
        (jnp.sum(grad_hat, axis=1), jnp.sum(grad_hat * normal_hat, axis=1)), "head"
    )
    grad_in = row_scale[:, None] * (
        grad_hat - first_sum[:, None] / full_width - normal_hat * cross_sum[:, None] / full_width
    )
    return (grad_in, jnp.sum(grad_out * normal_hat, axis=0), jnp.sum(grad_out, axis=0))


def block_scores(query_rows, key_block, keep_row):
    factor = 1.0 / math.sqrt(query_rows.shape[-1])
    scores = (
        jnp.einsum("qhd,khd->hqk", query_rows, key_block, preferred_element_type=jnp.float32)
        * factor
    )
    return jnp.where(keep_row[None, None, :] == 1, scores, masked_score)


def block_attend(query_rows, key_block, value_block, keep_row):
    scores = block_scores(query_rows, key_block, keep_row)
    row_top = jnp.max(scores, axis=2, keepdims=True)
    raised = jnp.exp(scores - row_top)
    totals = jnp.sum(raised, axis=2, keepdims=True)
    probs = (raised / totals).astype(jnp.bfloat16)
    result = jnp.einsum("hqk,khd->qhd", probs, value_block, preferred_element_type=jnp.float32)
    return (result, (row_top + jnp.log(totals))[:, :, 0])


def block_grads(query_rows, key_block, value_block, keep_row, log_sum, grad_rows):
    factor = 1.0 / math.sqrt(query_rows.shape[-1])
    scores = block_scores(query_rows, key_block, keep_row)
    probs = jnp.exp(scores - log_sum[:, :, None])
    grad_probs = jnp.einsum(
        "qhd,khd->hqk", grad_rows, value_block, preferred_element_type=jnp.float32
    )
    row_delta = jnp.sum(grad_probs * probs, axis=2, keepdims=True)
    grad_scores = (probs * (grad_probs - row_delta)).astype(jnp.bfloat16)
    grad_q = (
        jnp.einsum("hqk,khd->qhd", grad_scores, key_block, preferred_element_type=jnp.float32)
        * factor
    )
    grad_k = (
        jnp.einsum("hqk,qhd->khd", grad_scores, query_rows, preferred_element_type=jnp.float32)
        * factor
    )
    grad_v = jnp.einsum(
        "hqk,qhd->khd", probs.astype(jnp.bfloat16), grad_rows, preferred_element_type=jnp.float32
    )
    return (grad_q, grad_k, grad_v)


def slab_attend(query_slab, key_slab, value_slab, keep_slab, bucket_id):
    blocks = query_slab.shape[0] // SHORT
    inner = (blocks, SHORT) + query_slab.shape[1:]
    query_parts = query_slab.reshape(inner)

    def local_blocks(unused):
        return lax.map(
            lambda packet: block_attend(*packet),
            (
                query_parts,
                key_slab.reshape(inner),
                value_slab.reshape(inner),
                keep_slab.reshape(blocks, SHORT),
            ),
        )

    def whole_slab(unused):
        return lax.map(
            lambda query_block: block_attend(query_block, key_slab, value_slab, keep_slab),
            query_parts,
        )

    result, log_sums = lax.cond(bucket_id == 1, whole_slab, local_blocks, 0)
    return (result.reshape(query_slab.shape), log_sums)


def slab_back(query_slab, key_slab, value_slab, keep_slab, bucket_id, log_sums, grad_slab):
    blocks = query_slab.shape[0] // SHORT
    inner = (blocks, SHORT) + query_slab.shape[1:]
    query_parts = query_slab.reshape(inner)
    grad_parts = grad_slab.reshape(inner)

    def local_blocks(unused):
        grad_q, grad_k, grad_v = lax.map(
            lambda packet: block_grads(*packet),
            (
                query_parts,
                key_slab.reshape(inner),
                value_slab.reshape(inner),
                keep_slab.reshape(blocks, SHORT),
                log_sums,
                grad_parts,
            ),
        )
        return (
            grad_q.reshape(query_slab.shape),
            grad_k.reshape(query_slab.shape),
            grad_v.reshape(query_slab.shape),
        )

    def whole_slab(unused):
        blank = jnp.zeros(query_slab.shape, jnp.float32)

        def advance(running, packet):
            grad_q, grad_k, grad_v = block_grads(
                packet[0], key_slab, value_slab, keep_slab, packet[1], packet[2]
            )
            return ((running[0] + grad_k, running[1] + grad_v), grad_q)

        (grad_k, grad_v), grad_q = lax.scan(
            advance, (blank, blank), (query_parts, log_sums, grad_parts)
        )
        return (grad_q.reshape(query_slab.shape), grad_k, grad_v)

    return lax.cond(bucket_id == 1, whole_slab, local_blocks, 0)


def attend(queries, key_rows, values, valid_mask, buckets):
    slab_count = buckets.shape[0]
    shaped = (slab_count, LONG) + queries.shape[1:]
    result, log_sums = lax.map(
        lambda packet: slab_attend(*packet),
        (
            queries.reshape(shaped),
            key_rows.reshape(shaped),
            values.reshape(shaped),
            valid_mask.reshape(slab_count, LONG),
            buckets,
        ),
    )
    return (result.reshape(queries.shape), log_sums)


def attend_back(queries, key_rows, values, valid_mask, buckets, log_sums, grad_rows):
    slab_count = buckets.shape[0]
    shaped = (slab_count, LONG) + queries.shape[1:]
    grad_q, grad_k, grad_v = lax.map(
        lambda packet: slab_back(*packet),
        (
            queries.reshape(shaped),
            key_rows.reshape(shaped),
            values.reshape(shaped),
            valid_mask.reshape(slab_count, LONG),
            buckets,
            log_sums,
            grad_rows.reshape(shaped),
        ),
    )
    return (
        grad_q.reshape(queries.shape),
        grad_k.reshape(queries.shape),
        grad_v.reshape(queries.shape),
    )


def fetch(qkv_weight, out_weight, up_weight, down_weight, layer_index):
    return (
        lax.all_gather(qkv_weight[layer_index], "dp", axis=1, tiled=True),
        lax.all_gather(out_weight[layer_index], "dp", axis=1, tiled=True),
        lax.all_gather(up_weight[layer_index], "dp", axis=0, tiled=True),
        lax.all_gather(down_weight[layer_index], "dp", axis=1, tiled=True),
    )


def attention_input_grad(grad_qkv, wq_full):
    return lax.psum_scatter(
        jnp.einsum("cte,cde->td", grad_qkv, wq_full, preferred_element_type=jnp.float32).astype(
            jnp.bfloat16
        ),
        "head",
        scatter_dimension=1,
        tiled=True,
    ).astype(jnp.float32)


def local(
    stream_in,
    qkv_weight,
    out_weight,
    up_weight,
    down_weight,
    norm_gains,
    norm_shifts,
    hidden_gains,
    hidden_shifts,
    buckets,
    valid_mask,
    cotangent,
):
    layer_count = qkv_weight.shape[0]
    row_weight = valid_mask.astype(jnp.float32)
    stream = stream_in
    kept_layers = []
    usage_rows = []
    for layer_index in range(layer_count):
        weights = fetch(qkv_weight, out_weight, up_weight, down_weight, layer_index)
        wq_full, wo_full, up_full, down_full = weights
        low_stream = stream.astype(jnp.bfloat16)
        normed_in, mean_a, scale_a = widen(
            low_stream, norm_gains[layer_index, 0], norm_shifts[layer_index, 0]
        )
        normed_in = normed_in.astype(jnp.bfloat16)
        qkv_rows = jnp.einsum(
            "td,cde->cte", normed_in, wq_full, preferred_element_type=jnp.float32
        ).astype(jnp.bfloat16)
        tokens = qkv_rows.shape[1]
        local_width = qkv_rows.shape[2]
        head_shape = (tokens, local_width // DH, DH)
        queries = qkv_rows[0].reshape(head_shape)
        key_rows = qkv_rows[1].reshape(head_shape)
        values = qkv_rows[2].reshape(head_shape)
        attended, log_sums = attend(queries, key_rows, values, valid_mask, buckets)
        attended = attended.reshape(tokens, local_width)
        normed_mid, mean_o, scale_o = split_norm(
            attended, norm_gains[layer_index, 1], norm_shifts[layer_index, 1], D
        )
        normed_mid = normed_mid.astype(jnp.bfloat16)
        branch = narrow(jnp.dot(normed_mid, wo_full, preferred_element_type=jnp.float32))
        middle = stream + branch
        low_middle = middle.astype(jnp.bfloat16)
        normed_ffn, mean_f, scale_f = widen(
            low_middle, norm_gains[layer_index, 2], norm_shifts[layer_index, 2]
        )
        normed_ffn = normed_ffn.astype(jnp.bfloat16)
        hidden = jnp.dot(normed_ffn, up_full, preferred_element_type=jnp.float32)
        active = jax.nn.gelu(hidden, approximate=False)
        normed_out, mean_g, scale_g = split_norm(
            active, hidden_gains[layer_index], hidden_shifts[layer_index], FF
        )
        normed_out = normed_out.astype(jnp.bfloat16)
        feed = narrow(jnp.dot(normed_out, down_full, preferred_element_type=jnp.float32))
        stream = middle + feed
        usage_rows.append(
            jnp.stack(
                [
                    jnp.sum(row_weight[:, None] * branch * branch),
                    jnp.sum(row_weight[:, None] * feed * feed),
                    jnp.sum(row_weight[:, None] * stream * stream),
                ]
            )
        )
        saved = {
            "low_stream": low_stream,
            "mean_a": mean_a,
            "scale_a": scale_a,
            "normed_in": normed_in,
            "queries": queries,
            "key_rows": key_rows,
            "values": values,
            "log_sums": log_sums,
            "attended": attended,
            "mean_o": mean_o,
            "scale_o": scale_o,
            "normed_mid": normed_mid,
            "low_middle": low_middle,
            "mean_f": mean_f,
            "scale_f": scale_f,
            "normed_ffn": normed_ffn,
            "hidden": hidden,
            "mean_g": mean_g,
            "scale_g": scale_g,
            "normed_out": normed_out,
        }
        kept_layers.append(saved)
    grad = cotangent
    qkv_parts = [None] * layer_count
    out_parts = [None] * layer_count
    up_parts = [None] * layer_count
    down_parts = [None] * layer_count
    gain_parts = [None] * layer_count
    shift_parts = [None] * layer_count
    hidden_gain_parts = [None] * layer_count
    hidden_shift_parts = [None] * layer_count
    for layer_index in reversed(range(layer_count)):
        saved = kept_layers[layer_index]
        wq_full, wo_full, up_full, down_full = (
            lax.all_gather(qkv_weight[layer_index], "dp", axis=1, tiled=True),
            lax.all_gather(out_weight[layer_index], "dp", axis=1, tiled=True),
            lax.all_gather(up_weight[layer_index], "dp", axis=0, tiled=True),
            lax.all_gather(down_weight[layer_index], "dp", axis=1, tiled=True),
        )
        grad_full = spread_grad(grad.astype(jnp.bfloat16))
        down_term = jnp.einsum(
            "tf,td->fd", saved["normed_out"], grad_full, preferred_element_type=jnp.float32
        )
        grad_normed = jnp.einsum(
            "td,fd->tf", grad_full, down_full, preferred_element_type=jnp.float32
        )
        hidden = saved["hidden"]
        active, gelu_back = jax.vjp(partial(jax.nn.gelu, approximate=False), hidden)
        hat_g = (active - saved["mean_g"][:, None]) * saved["scale_g"][:, None]
        grad_active, hidden_gain_parts[layer_index], hidden_shift_parts[layer_index] = split_back(
            grad_normed, hat_g, saved["scale_g"], hidden_gains[layer_index], FF
        )
        grad_hidden = gelu_back(grad_active)[0].astype(jnp.bfloat16)
        up_term = jnp.einsum(
            "td,tf->df", saved["normed_ffn"], grad_hidden, preferred_element_type=jnp.float32
        )
        grad_ffn = collect(
            jnp.einsum("tf,df->td", grad_hidden, up_full, preferred_element_type=jnp.float32)
        )
        hat_f = (saved["low_middle"].astype(jnp.float32) - saved["mean_f"][:, None]) * saved[
            "scale_f"
        ][:, None]
        grad_middle, gain_two, shift_two = split_back(
            grad_ffn, hat_f, saved["scale_f"], norm_gains[layer_index, 2], D
        )
        grad = grad + grad_middle
        grad_full = spread_grad(grad.astype(jnp.bfloat16))
        out_term = jnp.einsum(
            "te,td->ed", saved["normed_mid"], grad_full, preferred_element_type=jnp.float32
        )
        grad_mid = jnp.einsum("td,ed->te", grad_full, wo_full, preferred_element_type=jnp.float32)
        hat_o = (saved["attended"] - saved["mean_o"][:, None]) * saved["scale_o"][:, None]
        grad_attended, gain_one, shift_one = split_back(
            grad_mid, hat_o, saved["scale_o"], norm_gains[layer_index, 1], D
        )
        queries = saved["queries"]
        tokens = queries.shape[0]
        local_width = queries.shape[1] * queries.shape[2]
        grad_low = grad_attended.astype(jnp.bfloat16).reshape(queries.shape)
        grad_q, grad_k, grad_v = attend_back(
            queries,
            saved["key_rows"],
            saved["values"],
            valid_mask,
            buckets,
            saved["log_sums"],
            grad_low,
        )
        grad_qkv = (
            jnp.stack([grad_q, grad_k, grad_v]).reshape(3, tokens, local_width).astype(jnp.bfloat16)
        )
        qkv_term = jnp.einsum(
            "td,cte->cde", saved["normed_in"], grad_qkv, preferred_element_type=jnp.float32
        )
        grad_in = attention_input_grad(grad_qkv, wq_full)
        hat_a = (saved["low_stream"].astype(jnp.float32) - saved["mean_a"][:, None]) * saved[
            "scale_a"
        ][:, None]
        grad_stream, gain_zero, shift_zero = split_back(
            grad_in, hat_a, saved["scale_a"], norm_gains[layer_index, 0], D
        )
        grad = grad + grad_stream
        gain_parts[layer_index] = jnp.stack([gain_zero, gain_one, gain_two])
        shift_parts[layer_index] = jnp.stack([shift_zero, shift_one, shift_two])
        (
            qkv_parts[layer_index],
            out_parts[layer_index],
            up_parts[layer_index],
            down_parts[layer_index],
        ) = (
            lax.psum_scatter(
                qkv_term.astype(jnp.bfloat16), "dp", scatter_dimension=1, tiled=True
            ).astype(jnp.float32),
            lax.psum_scatter(
                out_term.astype(jnp.bfloat16), "dp", scatter_dimension=1, tiled=True
            ).astype(jnp.float32),
            lax.psum_scatter(
                up_term.astype(jnp.bfloat16), "dp", scatter_dimension=0, tiled=True
            ).astype(jnp.float32),
            lax.psum_scatter(
                down_term.astype(jnp.bfloat16), "dp", scatter_dimension=1, tiled=True
            ).astype(jnp.float32),
        )
    gains_grad, shifts_grad, hidden_gains_grad, hidden_shifts_grad = lax.psum(
        (
            jnp.stack(gain_parts),
            jnp.stack(shift_parts),
            jnp.stack(hidden_gain_parts),
            jnp.stack(hidden_shift_parts),
        ),
        "dp",
    )
    usage_sums, denominator = lax.psum(
        (jnp.stack(usage_rows), jnp.sum(row_weight) * stream.shape[1]), ("dp", "head")
    )
    usage_rms = jnp.sqrt(usage_sums / denominator)
    return (
        stream,
        grad,
        jnp.stack(qkv_parts),
        jnp.stack(out_parts),
        jnp.stack(up_parts),
        jnp.stack(down_parts),
        gains_grad,
        shifts_grad,
        hidden_gains_grad,
        hidden_shifts_grad,
        usage_rms,
    )


def solution(mesh):
    return jax.shard_map(
        local,
        mesh=mesh,
        in_specs=(
            P("dp", "head"),
            P(None, None, "dp", "head"),
            P(None, "head", "dp"),
            P(None, "dp", "head"),
            P(None, "head", "dp"),
            P(None, None, "head"),
            P(None, None, "head"),
            P(None, "head"),
            P(None, "head"),
            P("dp"),
            P("dp"),
            P("dp", "head"),
        ),
        out_specs=(
            P("dp", "head"),
            P("dp", "head"),
            P(None, None, "dp", "head"),
            P(None, "head", "dp"),
            P(None, "dp", "head"),
            P(None, "head", "dp"),
            P(None, None, "head"),
            P(None, None, "head"),
            P(None, "head"),
            P(None, "head"),
            P(),
        ),
        check_vma=False,
    )
```

profile of v0, /device:TPU:0, one launch (start us, length us, event | category | flops | bytes accessed | tf_op | source)
XLA Modules:
  0.0 2555.1 jit_solution(16665801480515377343)
XLA Ops:
  12.9 12.7 all-gather
  46.7 46.8 %all-gather.31.cloned.1.call-done = bf16[2048,1024]{1,0:T(8,128)(2,1)} async-done(((bf16[2048,256]{1,0:T(8,128)(2,1)}), bf16[2048,1024]{1,0:T(8,128)(2,1)}) %all-gather.31.cloned.1.call-update) | async-done | bytes 4194320 | tf_op jit(solution)/shard_map/all_gather | solution.py:29
  98.4 21.7 all-gather.47.cloned.1.call-done
  129.5 26.8 %conditional.4 = (f32[4,512,4,64]{1,3,2,0:T(8,128)}, f32[4,4,512]{2,1,0:T(4,128)}) conditional(s32[]{:T(128)} %bitcast.46, (bf16[2048,4,64]{0,2,1:T(8,128)(2,1)}, bf16[2048,4,64]{0,2,1:T(8,128)(2,1)}, s32[2048]{0:T(1024)S(1)}, bf16[4,512,4,64]{1,0,3,2:T(4,128)(2,1)}) %tuple.424, (s32[2048]{0:T(1024)S(1)}, bf16[4,512,4,64]{1,0,3,2:T(4,128)(2,1)}, ...), branch_computations={%region_2.7_spmd, %region_7.12_spmd} | conditional | flops 1124073472 | bytes 55394496 | solution.py:140
  133.8 22.2 while.92
  162.9 11.8 psum.210
  193.8 107.9 %reduce-scatter.29.cloned.1.call-done = bf16[2048,256]{1,0:T(8,128)(2,1)} async-done(((bf16[2048,1024]{1,0:T(8,128)(2,1)}), bf16[2048,256]{1,0:T(8,128)(2,1)}) %reduce-scatter.29.cloned.1.call-update) | async-done | bytes 1048592 | tf_op jit(solution)/shard_map/reduce_scatter | solution.py:41
  325.6 59.8 %all-gather.33.cloned.1.call-done = bf16[2048,1024]{1,0:T(8,128)(2,1)} async-done(((bf16[2048,256]{1,0:T(8,128)(2,1)}), bf16[2048,1024]{1,0:T(8,128)(2,1)}) %all-gather.33.cloned.1.call-update) | async-done | bytes 4194320 | tf_op jit(solution)/shard_map/all_gather | solution.py:29
  390.3 23.7 all-gather.49.cloned.1.call-done
  414.0 27.7 %fusion.309 = (f32[2048]{0:T(1024)S(1)}, f32[2048,1024]{0,1:T(8,128)}, f32[2048,1024]{0,1:T(8,128)}, f32[2048,1024]{0,1:T(8,128)}) fusion(bf16[1,1024,1024]{2,1,0:T(8,128)(2,1)} %all-gather.49.cloned.1.call-done, bf16[2048,1024]{1,0:T(8,128)(2,1)} %all-gather.33.cloned.1.call-done, f32[1024]{0:T(1024)S(1)} %bitcast.682, f32[1024]{0:T(1024)S(1)} %bitcast.684, ...), kind=kOutput, calls=%fused_computation.482 | convolution fusion | flops 4443863040 | bytes 31490048 | tf_op jit(solution)/shard_map/dot_general | solution.py:292
  441.7 11.8 psum.212
  481.7 75.5 %reduce-scatter.31.cloned.1.call-done = bf16[2048,256]{1,0:T(8,128)(2,1)} async-done(((bf16[2048,1024]{1,0:T(8,128)(2,1)}), bf16[2048,256]{1,0:T(8,128)(2,1)}) %reduce-scatter.31.cloned.1.call-update) | async-done | bytes 1048592 | tf_op jit(solution)/shard_map/reduce_scatter | solution.py:41
  590.5 51.2 %all-gather.35.cloned.1.call-done = bf16[2048,1024]{1,0:T(8,128)(2,1)} async-done(((bf16[2048,256]{1,0:T(8,128)(2,1)}), bf16[2048,1024]{1,0:T(8,128)(2,1)}) %all-gather.35.cloned.1.call-update) | async-done | bytes 4194320 | tf_op jit(solution)/shard_map/all_gather | solution.py:29
  646.6 21.7 all-gather.53.cloned.1.call-done
  678.5 30.8 %conditional.5 = (f32[4,512,4,64]{1,3,2,0:T(8,128)}, f32[4,4,512]{2,1,0:T(4,128)}) conditional(s32[]{:T(128)} %bitcast.46, (bf16[2048,4,64]{0,2,1:T(8,128)(2,1)S(1)}, bf16[2048,4,64]{0,2,1:T(8,128)(2,1)S(1)}, s32[2048]{0:T(1024)S(1)}, bf16[4,512,4,64]{1,0,3,2:T(4,128)(2,1)}) %tuple.426, (s32[2048]{0:T(1024)S(1)}, ...), branch_computations={%region_26.31_spmd, %region_31.36_spmd} | conditional | flops 1124073472 | bytes 55394496 | solution.py:140
  683.0 26.3 %while.93 = (s32[]{:T(128)}, f32[4,512,4,64]{1,3,2,0:T(8,128)}, f32[4,4,512]{2,1,0:T(4,128)}, bf16[4,512,4,64]{1,3,2,0:T(8,128)(2,1)}, s32[4,512]{1,0:T(4,128)S(...) while((s32[]{:T(128)}, f32[4,512,4,64]{1,3,2,0:T(8,128)}, ...), condition=%wide.region_30.30_spmd, body=%wide.region_27.29_spmd.sunk | while | flops 281016832 | bytes 13965413 | solution.py:124
  715.9 11.8 psum.214
  752.0 97.7 %reduce-scatter.33.cloned.1.call-done = bf16[2048,256]{1,0:T(8,128)(2,1)} async-done(((bf16[2048,1024]{1,0:T(8,128)(2,1)}), bf16[2048,256]{1,0:T(8,128)(2,1)}) %reduce-scatter.33.cloned.1.call-update) | async-done | bytes 1048592 | tf_op jit(solution)/shard_map/reduce_scatter | solution.py:41
  880.5 82.1 %all-gather.39.cloned.1.call-done = bf16[2048,1024]{1,0:T(8,128)(2,1)} async-done(((bf16[2048,256]{1,0:T(8,128)(2,1)}), bf16[2048,1024]{1,0:T(8,128)(2,1)}) %all-gather.39.cloned.1.call-update) | async-done | bytes 4194320 | tf_op jit(solution)/shard_map/all_gather | solution.py:47
  983.0 60.0 %all-gather.37.cloned.1.call-done = bf16[2048,1024]{1,0:T(8,128)(2,1)} async-done(((bf16[2048,256]{1,0:T(8,128)(2,1)}), bf16[2048,1024]{1,0:T(8,128)(2,1)}) %all-gather.37.cloned.1.call-update) | async-done | bytes 4194320 | tf_op jit(solution)/shard_map/all_gather | solution.py:29
  1047.9 23.7 all-gather.55.cloned.1.call-done
  1071.6 27.6 %fusion.306 = (f32[2048]{0:T(1024)S(1)}, f32[2048,1024]{0,1:T(8,128)}, f32[2048,1024]{0,1:T(8,128)}, f32[2048,1024]{0,1:T(8,128)}) fusion(bf16[1,1024,1024]{2,1,0:T(8,128)(2,1)} %all-gather.55.cloned.1.call-done, bf16[2048,1024]{1,0:T(8,128)(2,1)} %all-gather.37.cloned.1.call-done, f32[1024]{0:T(1024)S(1)} %bitcast.690, f32[1024]{0:T(1024)S(1)} %bitcast.692, ...), kind=kOutput, calls=%fused_computation.480 | convolution fusion | flops 4443863040 | bytes 31490048 | tf_op jit(solution)/shard_map/dot_general | solution.py:292
  1099.3 11.8 psum.216
  1131.9 17.9 all-reduce.9
  1149.8 15.5 add_convert_fusion.1
  1173.7 74.1 %reduce-scatter.37.cloned.1.call-done = bf16[2048,256]{1,0:T(8,128)(2,1)} async-done(((bf16[2048,1024]{1,0:T(8,128)(2,1)}), bf16[2048,256]{1,0:T(8,128)(2,1)}) %reduce-scatter.37.cloned.1.call-update) | async-done | bytes 1048592 | tf_op jit(solution)/shard_map/reduce_scatter | solution.py:51
  1250.9 18.0 all-reduce.8
  1274.4 79.1 %all-gather.41.cloned.1.call-done = bf16[2048,1024]{1,0:T(8,128)(2,1)} async-done(((bf16[2048,256]{1,0:T(8,128)(2,1)}), bf16[2048,1024]{1,0:T(8,128)(2,1)}) %all-gather.41.cloned.1.call-update) | async-done | bytes 4194320 | tf_op jit(solution)/shard_map/all_gather | solution.py:47
  1359.9 15.9 all-reduce.7
  1384.2 72.4 %conditional.6 = (bf16[4,512,4,64]{1,3,2,0:T(8,128)(2,1)}, bf16[1,2048,256]{2,1,0:T(8,128)(2,1)}, bf16[1,2048,256]{2,1,0:T(8,128)(2,1)S(1)}) conditional(s32[]{:T(128)} %bitcast.46, (bf16[2048,4,64]{0,2,1:T(8,128)(2,1)S(1)}, bf16[2048,4,64]{0,2,1:T(8,128)(2,1)S(1)}, s32[2048]{0:T(1024)S(1)}, bf16[4,512,4,64]{1,0,3,2:T(4,128)(2,1)}, ...), branch_computations={%region_61.65_spmd, %region_65.69_spmd} | conditional | flops 2751070208 | bytes 187244864 | solution.py:182
  1390.8 48.8 %while.96 = (s32[]{:T(128)}, bf16[4,512,4,64]{1,3,2,0:T(8,128)(2,1)}, bf16[4,512,4,64]{1,3,2,0:T(8,128)(2,1)}, bf16[4,512,4,64]{1,3,2,0:T(8,128)(2,1)}, bf16[4,5...) while((s32[]{:T(128)}, ...), condition=%wide.region_64.64_spmd, body=%wide.region_62.63_spmd.sunk | while | flops 687077888 | bytes 64292160 | solution.py:151
  1471.1 179.2 %reduce-scatter.39.cloned.1.call-done = bf16[2048,256]{1,0:T(8,128)(2,1)} async-done(((bf16[2048,1024]{1,0:T(8,128)(2,1)}), bf16[2048,256]{1,0:T(8,128)(2,1)}) %reduce-scatter.39.cloned.1.call-update) | async-done | bytes 1048592 | tf_op jit(solution)/shard_map/reduce_scatter | solution.py:233
  1653.4 18.0 all-reduce.6
  1675.8 79.1 %all-gather.43.cloned.1.call-done = bf16[2048,1024]{1,0:T(8,128)(2,1)} async-done(((bf16[2048,256]{1,0:T(8,128)(2,1)}), bf16[2048,1024]{1,0:T(8,128)(2,1)}) %all-gather.43.cloned.1.call-update) | async-done | bytes 4194320 | tf_op jit(solution)/shard_map/all_gather | solution.py:47
  1783.2 16.4 all-reduce.5
  1799.6 13.8 add_convert_fusion
  1821.6 75.1 %reduce-scatter.41.cloned.1.call-done = bf16[2048,256]{1,0:T(8,128)(2,1)} async-done(((bf16[2048,1024]{1,0:T(8,128)(2,1)}), bf16[2048,256]{1,0:T(8,128)(2,1)}) %reduce-scatter.41.cloned.1.call-update) | async-done | bytes 1048592 | tf_op jit(solution)/shard_map/reduce_scatter | solution.py:51
  1899.8 18.0 all-reduce.4
  2006.9 16.7 all-reduce.3
  2037.1 60.9 %conditional.7 = (bf16[4,512,4,64]{1,3,2,0:T(8,128)(2,1)}, bf16[1,2048,256]{2,1,0:T(8,128)(2,1)}, bf16[1,2048,256]{2,1,0:T(8,128)(2,1)S(1)}) conditional(s32[]{:T(128)} %bitcast.46, (bf16[2048,4,64]{0,2,1:T(8,128)(2,1)}, bf16[2048,4,64]{0,2,1:T(8,128)(2,1)}, s32[2048]{0:T(1024)S(1)}, bf16[4,512,4,64]{1,0,3,2:T(4,128)(2,1)}, ...), branch_computations={%region_87.91_spmd, %region_91.95_spmd} | conditional | flops 2751070208 | bytes 187244864 | solution.py:182
  2042.7 38.4 %while.97 = (s32[]{:T(128)}, bf16[4,512,4,64]{1,3,2,0:T(8,128)(2,1)}, bf16[4,512,4,64]{1,3,2,0:T(8,128)(2,1)}, bf16[4,512,4,64]{1,3,2,0:T(8,128)(2,1)}, bf16[4,5...) while((s32[]{:T(128)}, ...), condition=%wide.region_90.90_spmd, body=%wide.region_88.89_spmd.sunk | while | flops 687077888 | bytes 60097828 | solution.py:151
  2140.2 152.7 %all-reduce = (f32[2,3]{1,0:T(2,128)S(1)}, f32[]{:T(128)}) all-reduce(f32[2,3]{1,0:T(2,128)S(1)} %pad_maximum_fusion.4, f32[]{:T(128)S(6)} %mul.776), channel_id=1, replica_groups=mesh['dp'=8,'head'=4] {'dp','head'}, use_global_device_ids=true, to_apply=%region_134.135 | all-reduce | flops 7 | bytes 56 | tf_op jit(solution)/shard_map/psum | solution.py:442
  2298.7 39.8 %reduce-scatter.45.cloned.1.call-done = bf16[128,1024]{1,0:T(8,128)(2,1)} async-done(((bf16[1024,1024]{1,0:T(8,128)(2,1)}), bf16[128,1024]{1,0:T(8,128)(2,1)}) %reduce-scatter.45.cloned.1.call-update) | async-done | bytes 262160 | tf_op jit(solution)/shard_map/reduce_scatter | solution.py:426
  2340.6 35.1 %reduce-scatter.53.cloned.1.call-done = bf16[128,256]{1,0:T(8,128)(2,1)} async-done(((bf16[1024,256]{1,0:T(8,128)(2,1)}), bf16[128,256]{1,0:T(8,128)(2,1)}) %reduce-scatter.53.cloned.1.call-update) | async-done | bytes 65552
  2377.4 40.4 %reduce-scatter.49.cloned.1.call-done = bf16[128,768]{1,0:T(8,128)(2,1)} async-done(((bf16[1024,768]{1,0:T(8,128)(2,1)}), bf16[128,768]{1,0:T(8,128)(2,1)}) %reduce-scatter.49.cloned.1.call-update) | async-done | bytes 196624
  2420.3 76.6 %reduce-scatter.43.cloned.1.call-done = bf16[2048,256]{1,0:T(8,128)(2,1)} async-done(((bf16[2048,1024]{1,0:T(8,128)(2,1)}), bf16[2048,256]{1,0:T(8,128)(2,1)}) %reduce-scatter.43.cloned.1.call-update) | async-done | bytes 1048592 | tf_op jit(solution)/shard_map/reduce_scatter | solution.py:233
  2499.4 24.6 all-reduce.1
  2525.2 18.2 all-reduce.2
  (728 shorter events, 709.0 us)
Async XLA Ops:
  7.2 86.3 %all-gather.31.cloned.1.call-start = ((), (), s32[]{:S(2)}) async-start(), calls=%async_computation.16 | async-start | bytes 5242880 | tf_op jit(solution)/shard_map/all_gather | solution.py:29
  10.0 110.0 %all-gather.47.cloned.1.call-start = ((), (), s32[]{:S(2)}) async-start(), calls=%async_computation.34 | async-start | bytes 1769472 | tf_op jit(solution)/shard_map/all_gather | solution.py:225
  11.6 290.0 %reduce-scatter.29.cloned.1.call-start = ((), (), s32[]{:S(2)}) async-start(), calls=%async_computation.17 | async-start | bytes 5242880 | tf_op jit(solution)/shard_map/reduce_scatter | solution.py:41
  193.8 191.7 %all-gather.33.cloned.1.call-start = ((), (), s32[]{:S(2)}) async-start(), calls=%async_computation.18 | async-start | bytes 5242880 | tf_op jit(solution)/shard_map/all_gather | solution.py:29
  304.2 109.9 %all-gather.49.cloned.1.call-start = ((), (), s32[]{:S(2)}) async-start(), calls=%async_computation.35 | async-start | bytes 2359296 | tf_op jit(solution)/shard_map/all_gather | solution.py:227
  305.1 167.1 %all-gather.51.cloned.1.call-start = ((), (), s32[]{:S(2)}) async-start(), calls=%async_computation.36 | async-start | bytes 2359296 | tf_op jit(solution)/shard_map/all_gather | solution.py:228
  306.0 251.2 %reduce-scatter.31.cloned.1.call-start = ((), (), s32[]{:S(2)}) async-start(), calls=%async_computation.19 | async-start | bytes 5242880 | tf_op jit(solution)/shard_map/reduce_scatter | solution.py:41
  481.6 160.1 %all-gather.35.cloned.1.call-start = ((), (), s32[]{:S(2)}) async-start(), calls=%async_computation.20 | async-start | bytes 5242880 | tf_op jit(solution)/shard_map/all_gather | solution.py:29
  560.4 107.8 %all-gather.53.cloned.1.call-start = ((), (), s32[]{:S(2)}) async-start(), calls=%async_computation.37 | async-start | bytes 1769472 | tf_op jit(solution)/shard_map/all_gather | solution.py:225
  561.3 288.4 %reduce-scatter.33.cloned.1.call-start = ((), (), s32[]{:S(2)}) async-start(), calls=%async_computation.21 | async-start | bytes 5242880 | tf_op jit(solution)/shard_map/reduce_scatter | solution.py:41
  727.7 648.0 %copy-start.46 = (f32[2048]{0:T(1024)}, f32[2048]{0:T(1024)S(1)}, u32[]{:S(2)}) copy-start(f32[2048]{0:T(1024)S(1)} %broadcast_multiply_fusion.11) | copy-start | bytes 24580
  738.3 637.5 %copy-start.51 = (f32[2048]{0:T(1024)}, f32[2048]{0:T(1024)S(1)}, u32[]{:S(2)}) copy-start(f32[2048]{0:T(1024)S(1)} %add_rsqrt_fusion.2) | copy-start | bytes 24580
  748.4 132.1 %all-gather.57.cloned.1.call-start = ((), (), s32[]{:S(2)}) async-start(), calls=%async_computation.39 | async-start | bytes 2359296 | tf_op jit(solution)/shard_map/all_gather | solution.py:228
  749.2 213.4 %all-gather.39.cloned.1.call-start = ((), (), s32[]{:S(2)}) async-start(), calls=%async_computation.24 | async-start | bytes 5242880 | tf_op jit(solution)/shard_map/all_gather | solution.py:47
  752.0 291.1 %all-gather.37.cloned.1.call-start = ((), (), s32[]{:S(2)}) async-start(), calls=%async_computation.22 | async-start | bytes 5242880 | tf_op jit(solution)/shard_map/all_gather | solution.py:29
  852.8 218.8 %all-gather.55.cloned.1.call-start = ((), (), s32[]{:S(2)}) async-start(), calls=%async_computation.38 | async-start | bytes 2359296 | tf_op jit(solution)/shard_map/all_gather | solution.py:227
  853.4 394.4 %reduce-scatter.37.cloned.1.call-start = ((), (), s32[]{:S(2)}) async-start(), calls=%async_computation.25 | async-start | bytes 5242880 | tf_op jit(solution)/shard_map/reduce_scatter | solution.py:51
  863.6 208.0 %copy-start.117 = (f32[1,1,1024]{2,0,1:T(1,128)}, f32[1,1,1024]{2,0,1:T(1,128)S(1)}, u32[]{:S(2)}) copy-start(f32[1,1,1024]{2,0,1:T(1,128)S(1)} %convert_element_type.369) | copy-start | bytes 12292
  871.2 200.4 %copy-start.119 = (f32[4,1,256]{2,1,0:T(1,128)}, f32[4,1,256]{2,1,0:T(1,128)S(1)}, u32[]{:S(2)}) copy-start(f32[4,1,256]{2,1,0:T(1,128)S(1)} %convert_element_type.373) | copy-start | bytes 12292
  1046.5 222.4 %copy-start.62 = (f32[2048]{0:T(1024)}, f32[2048]{0:T(1024)S(1)}, u32[]{:S(2)}) copy-start(f32[2048]{0:T(1024)S(1)} %broadcast_multiply_fusion.10) | copy-start | bytes 24580
  1047.9 221.0 %copy-start.72 = (f32[2048]{0:T(1024)}, f32[2048]{0:T(1024)S(1)}, u32[]{:S(2)}) copy-start(f32[2048]{0:T(1024)S(1)} %add_rsqrt_fusion.1) | copy-start | bytes 24580
  1173.6 179.9 %all-gather.41.cloned.1.call-start = ((), (), s32[]{:S(2)}) async-start(), calls=%async_computation.26 | async-start | bytes 5242880 | tf_op jit(solution)/shard_map/all_gather | solution.py:47
  1274.4 376.0 %reduce-scatter.39.cloned.1.call-start = ((), (), s32[]{:S(2)}) async-start(), calls=%async_computation.27 | async-start | bytes 5242880 | tf_op jit(solution)/shard_map/reduce_scatter | solution.py:233
  1471.0 179.3 %copy-start.13 = (bf16[2048,256]{1,0:T(8,128)(2,1)S(1)}, bf16[2048,256]{1,0:T(8,128)(2,1)}, u32[]{:S(2)}) copy-start(bf16[2048,256]{1,0:T(8,128)(2,1)} %get-tuple-element.1144) | copy-start | bytes 3145732
  1471.0 179.3 %copy-start.61 = (f32[2048]{0:T(1024)S(1)}, f32[2048]{0:T(1024)}, u32[]{:S(2)}) copy-start(f32[2048]{0:T(1024)} %copy-done.60) | copy-start | bytes 24580
  1471.0 179.3 %copy-start.71 = (f32[2048]{0:T(1024)S(1)}, f32[2048]{0:T(1024)}, u32[]{:S(2)}) copy-start(f32[2048]{0:T(1024)} %copy-done.70) | copy-start | bytes 24580
  1471.0 179.3 %copy-start.90 = (f32[1,1,256]{2,0,1:T(1,128)S(1)}, f32[1,1,256]{2,0,1:T(1,128)}, u32[]{:S(2)}) copy-start(f32[1,1,256]{2,0,1:T(1,128)} %get-tuple-element.1194) | copy-start | bytes 3076
  1471.0 200.4 %copy-start.17 = (f32[2048,256]{1,0:T(8,128)S(1)}, f32[2048,256]{1,0:T(8,128)}, u32[]{:S(2)}) copy-start(f32[2048,256]{1,0:T(8,128)} %get-tuple-element.1140) | copy-start | bytes 6291460
  1471.1 283.7 %all-gather.43.cloned.1.call-start = ((), (), s32[]{:S(2)}) async-start(), calls=%async_computation.28 | async-start | bytes 5242880 | tf_op jit(solution)/shard_map/all_gather | solution.py:47
  1675.7 221.0 %reduce-scatter.41.cloned.1.call-start = ((), (), s32[]{:S(2)}) async-start(), calls=%async_computation.29 | async-start | bytes 5242880 | tf_op jit(solution)/shard_map/reduce_scatter | solution.py:51
  1821.6 179.6 %all-gather.45.cloned.1.call-start = ((), (), s32[]{:S(2)}) async-start(), calls=%async_computation.30 | async-start | bytes 5242880 | tf_op jit(solution)/shard_map/all_gather | solution.py:47
  1922.0 208.2 %reduce-scatter.35.cloned.1.call-start = ((), (), s32[]{:S(2)}) async-start(), calls=%async_computation.23 | async-start | bytes 5242880 | tf_op jit(solution)/shard_map/reduce_scatter | solution.py:41
  1931.7 207.4 %reduce-scatter.59.cloned.1.call-start = ((), (), s32[]{:S(2)}) async-start(), calls=%async_computation.45 | async-start | bytes 2359296
  1945.4 348.7 %reduce-scatter.55.cloned.1.call-start = ((), (), s32[]{:S(2)}) async-start(), calls=%async_computation.43 | async-start | bytes 589824
  1950.5 344.5 %reduce-scatter.51.cloned.1.call-start = ((), (), s32[]{:S(2)}) async-start(), calls=%async_computation.41 | async-start | bytes 1769472
  1963.5 332.9 %reduce-scatter.57.cloned.1.call-start = ((), (), s32[]{:S(2)}) async-start(), calls=%async_computation.44 | async-start | bytes 2359296
  1974.2 324.5 %reduce-scatter.47.cloned.1.call-start = ((), (), s32[]{:S(2)}) async-start(), calls=%async_computation.33 | async-start | bytes 2359296 | tf_op jit(solution)/shard_map/reduce_scatter | solution.py:426
  1984.7 353.8 %reduce-scatter.45.cloned.1.call-start = ((), (), s32[]{:S(2)}) async-start(), calls=%async_computation.32 | async-start | bytes 2359296 | tf_op jit(solution)/shard_map/reduce_scatter | solution.py:426
  1994.9 380.9 %reduce-scatter.53.cloned.1.call-start = ((), (), s32[]{:S(2)}) async-start(), calls=%async_computation.42 | async-start | bytes 589824
  2105.6 312.3 %reduce-scatter.49.cloned.1.call-start = ((), (), s32[]{:S(2)}) async-start(), calls=%async_computation.40 | async-start | bytes 1769472
  2120.8 376.1 %reduce-scatter.43.cloned.1.call-start = ((), (), s32[]{:S(2)}) async-start(), calls=%async_computation.31 | async-start | bytes 5242880 | tf_op jit(solution)/shard_map/reduce_scatter | solution.py:233
  2130.2 166.1 %copy-start.78 = (f32[1024]{0:T(1024)S(1)}, f32[1024]{0:T(1024)}, u32[]{:S(2)}) copy-start(f32[1024]{0:T(1024)} %get-tuple-element.942) | copy-start | bytes 12292
  2130.2 166.1 %copy-start.79 = (f32[1024]{0:T(1024)S(1)}, f32[1024]{0:T(1024)}, u32[]{:S(2)}) copy-start(f32[1024]{0:T(1024)} %get-tuple-element.940) | copy-start | bytes 12292
  2130.2 166.1 %copy-start.124 = (f32[1024]{0:T(1024)S(1)}, f32[1024]{0:T(1024)}, u32[]{:S(2)}) copy-start(f32[1024]{0:T(1024)} %get-tuple-element.1209) | copy-start | bytes 12292
  2130.2 166.1 %copy-start.125 = (f32[1024]{0:T(1024)S(1)}, f32[1024]{0:T(1024)}, u32[]{:S(2)}) copy-start(f32[1024]{0:T(1024)} %get-tuple-element.1211) | copy-start | bytes 12292
  2296.1 200.8 %copy-start.3 = (f32[2048,256]{1,0:T(8,128)S(1)}, f32[2048,256]{1,0:T(8,128)}, u32[]{:S(2)}) copy-start(f32[2048,256]{1,0:T(8,128)} %param.36) | copy-start | bytes 6291460
  2296.1 200.8 %copy-start.86 = (f32[1,1,256]{2,0,1:T(1,128)S(1)}, f32[1,1,256]{2,0,1:T(1,128)}, u32[]{:S(2)}) copy-start(f32[1,1,256]{2,0,1:T(1,128)} %copy-done.85) | copy-start | bytes 3076
  2338.5 160.8 %copy-start.99 = (f32[256]{0:T(256)S(1)}, f32[256]{0:T(256)}, u32[]{:S(2)}) copy-start(f32[256]{0:T(256)} %get-tuple-element.969) | copy-start | bytes 3076
  (152 other events, 4822.5 us)
Sparse Core Ops, SparseCore 0:
  10.2 83.2 all-gather.30
  96.0 24.0 all-gather.46
  193.8 107.8 reduce-scatter.28
  304.3 81.1 all-gather.32
  387.9 26.0 all-gather.48
  416.5 28.1 all-gather.50
  481.7 75.4 reduce-scatter.30
  560.5 81.1 all-gather.34
  644.2 24.0 all-gather.52
  748.6 101.1 reduce-scatter.32
  851.8 28.6 all-gather.56
  882.0 80.5 all-gather.38
  964.2 78.7 all-gather.36
  1045.5 26.0 all-gather.54
  1173.7 73.9 reduce-scatter.36
  1274.5 78.9 all-gather.40
  1471.2 179.1 reduce-scatter.38
  1675.8 78.9 all-gather.42
  1821.7 74.9 reduce-scatter.40
  1922.1 78.9 all-gather.44
  2003.4 75.4 reduce-scatter.34
  2082.6 41.7 reduce-scatter.58
  2128.0 34.1 reduce-scatter.54
  2165.7 38.4 reduce-scatter.50
  2207.8 41.1 reduce-scatter.56
  2252.2 41.6 reduce-scatter.46
  2297.4 41.0 reduce-scatter.44
  2341.6 34.1 reduce-scatter.52
  2379.4 38.4 reduce-scatter.48
  2420.1 76.7 reduce-scatter.42
where the time goes:
time: 2570 us; the launch traced here: 2560 us
  waiting for transfers between devices  1370 us (53%)
  blocking collectives  494 us (19%)
  matrix products  310 us (12%)
  other arithmetic  174 us (7%)
  local copies, waits for them, and re-layouts  173 us (7%)
    reduce_scatter x4, waiting for transfers between devices, narrow(): lax.psum_scatter(partial_sum.astype(jnp.bfloat16), 'head', scatter_dimens...  281 us
    reduce_scatter x2, waiting for transfers between devices, attention_input_grad(): lax.psum_scatter(jnp.einsum('cte,cde->td', grad_qkv, wq_full, preferred_e...  256 us
    all_gather x4, waiting for transfers between devices, spread_grad(): return lax.all_gather(grad_low, 'head', axis=1, tiled=True)  246 us
    all_gather x4, waiting for transfers between devices, widen(): lax.all_gather(low_stream, 'head', axis=1, tiled=True)  218 us
    psum x1, blocking collectives, local(): lax.psum((jnp.stack(usage_rows), jnp.sum(row_weight) * stream.shape[1]),...  153 us
    reduce_scatter x2, waiting for transfers between devices, collect(): lax.psum_scatter(grad_term.astype(jnp.bfloat16), 'head', scatter_dimensio...  149 us
    psum x8, blocking collectives, split_back(): lax.psum((jnp.sum(grad_hat, axis=1), jnp.sum(grad_hat * normal_hat, axis=...  139 us
    unnamed x36, waiting for transfers between devices  77.1 us
  transfers between devices with their start and end apart: 30, of which 23 were waited for; matrix products, arithmetic and copies ran while one was open for 11% of the time, Pallas kernels for 0%

commit v1 on v0

v1 whole, which is shorter than its diff:
```python
import math

import jax
import jax.numpy as jnp
from jax import lax
from jax.experimental import pallas as pl
from jax.experimental.pallas import tpu as pltpu
from jax.sharding import PartitionSpec as P

D = 1024
FF = 4096
LONG = 2048
SHORT = 512
DH = 64
LANES = 128
BLOCKS = D // LANES
GROUPS = 4
WIDE = FF // GROUPS
EPS = 1e-05
MASKED = -1000000000.0
ROWS = 128
VMEM_BYTES = 60 * 1024 * 1024

f32 = jnp.float32
bf16 = jnp.bfloat16


def dot(a, b):
    return jnp.dot(a, b, preferred_element_type=f32)


def dot_nt(a, b):
    return lax.dot_general(a, b, (((1,), (1,)), ((), ())), preferred_element_type=f32)


def flip(a):
    return jnp.transpose(a.astype(f32), (1, 0)).astype(a.dtype)


def wide_pair(ref, one, two):
    return jnp.concatenate([ref[one], ref[two]], axis=1)


def row_loop(total, step, body):
    def advance(i, carry):
        body(pl.ds(pl.multiple_of(i * step, step), step))
        return carry

    lax.fori_loop(0, total // step, advance, 0)


def row_stats(blocks, width):
    mean = sum_lanes(blocks) / width
    square = sum_lanes([(b - mean) * (b - mean) for b in blocks]) / width
    return mean, lax.rsqrt(square + EPS)


def sum_lanes(blocks):
    total = blocks[0]
    for b in blocks[1:]:
        total = total + b
    return jnp.sum(total, axis=1, keepdims=True)


def params(**kw):
    return pltpu.CompilerParams(vmem_limit_bytes=VMEM_BYTES, **kw)


def cost(flops, size, trans=0):
    return pl.CostEstimate(flops=int(flops), bytes_accessed=int(size), transcendentals=int(trans))


def whole(shape):
    zeros = (0,) * len(shape)
    return pl.BlockSpec(shape, lambda *_: zeros)


def norm_back(dy, hat, rstd, gains, width):
    dx = [a * g for a, g in zip(dy, gains)]
    first = sum_lanes(dx) / width
    cross = sum_lanes([a * h for a, h in zip(dx, hat)]) / width
    return [rstd * (a - first - h * cross) for a, h in zip(dx, hat)]


def qkv_kernel(sc, x, gain, shift, *refs):
    weights, outs, xs = refs[:8], refs[8:16], refs[16]
    step = pl.program_id(0)
    tokens = x.shape[1]

    @pl.when(step == 0)
    def _():
        def body(r):
            blocks = [x[b, r, :].astype(f32) for b in range(BLOCKS)]
            mean, rstd = row_stats(blocks, D)
            for b in range(BLOCKS):
                xs[b, r, :] = ((blocks[b] - mean) * rstd * gain[b] + shift[b]).astype(bf16)

        row_loop(tokens, ROWS, body)

    for c in range(3):
        total = None
        for q in range(4):
            left = wide_pair(xs, sc[2 * q], sc[2 * q + 1])
            right = jnp.concatenate([weights[2 * q][0, c], weights[2 * q + 1][0, c]], axis=0)
            term = dot(left, right)
            total = term if total is None else total + term
        total = total.astype(bf16)
        for k in range(GROUPS):

            @pl.when(step == k)
            def _(k=k, c=c, total=total):
                outs[2 * k][c] = total[:, :LANES]
                outs[2 * k + 1][c] = total[:, LANES:]


def qkv_call(sc, x, gain, shift, pieces):
    tokens = x.shape[1]
    out = jax.ShapeDtypeStruct((3, tokens, LANES), bf16)
    return pl.pallas_call(
        qkv_kernel,
        out_shape=[out] * 8,
        grid_spec=pltpu.PrefetchScalarGridSpec(
            num_scalar_prefetch=1,
            grid=(GROUPS,),
            in_specs=[whole(x.shape), whole(gain.shape), whole(shift.shape)]
            + [
                pl.BlockSpec((1, 3, LANES, 256), lambda k, sc: ((sc[8] + k) % GROUPS, 0, 0, 0))
            ]
            * 8,
            out_specs=[whole(out.shape)] * 8,
            scratch_shapes=[pltpu.VMEM((BLOCKS, tokens, LANES), bf16)],
        ),
        compiler_params=params(),
        cost_estimate=cost(2 * tokens * D * 3 * D, 10 * 2**20),
        name="qkv",
    )(sc, x, gain, shift, *pieces)


def head_lanes(value, head):
    lane = lax.broadcasted_iota(jnp.int32, value.shape, 1)
    keep = (lane < DH) if head == 0 else (lane >= DH)
    return jnp.where(keep, value, jnp.zeros_like(value))


def attn_kernel(need, aux, one, *refs):
    n = (len(refs) - 6) // 2
    qkv, outs = refs[:n], refs[n : 2 * n]
    lse, kx, vt, qs, top, acc = refs[2 * n :]
    tokens = aux.shape[1]
    for r in range(n):
        kx[r] = jnp.concatenate([qkv[r][1], aux[r]], axis=1)
        turned = flip(qkv[r][2])
        ones = jnp.ones((16, tokens), bf16)
        vt[r, 0] = jnp.concatenate([turned[:DH], ones], axis=0)
        vt[r, 1] = jnp.concatenate([turned[DH:], ones], axis=0)
        qs[r] = (qkv[r][0].astype(f32) * (1.0 / math.sqrt(DH))).astype(bf16)

    def each_query(i, carry):
        query = qs[i]
        extended = [jnp.concatenate([head_lanes(query, h), one[...]], axis=1) for h in range(2)]
        top[...] = jnp.full_like(top, -3e38)
        acc[...] = jnp.zeros_like(acc)

        def each_key(j, inner):
            @pl.when(need[i * n + j] == 1)
            def _():
                for h in range(2):
                    scores = dot_nt(kx[j], extended[h])
                    before = top[h : h + 1]
                    now = jnp.maximum(before, jnp.max(scores, axis=0, keepdims=True))
                    raised = jnp.exp(scores - now).astype(bf16)
                    top[h : h + 1] = now
                    acc[h] = acc[h] * jnp.exp(before - now) + dot(vt[j, h], raised)

            return inner

        lax.fori_loop(0, n, each_key, 0)
        sums = [acc[h][DH : DH + 1] for h in range(2)]
        both = jnp.concatenate([acc[h][:DH] / sums[h] for h in range(2)], axis=0)
        qs[i] = jnp.transpose(both, (1, 0)).astype(bf16)
        for h in range(2):
            lse[i, h : h + 1] = top[h : h + 1] + jnp.log(sums[h])
        return carry

    lax.fori_loop(0, n, each_query, 0)
    for r in range(n):
        outs[r][...] = qs[r]


def attn_call(need, aux, one, parts):
    n = len(parts)
    tokens = aux.shape[1]
    out = jax.ShapeDtypeStruct((tokens, LANES), bf16)
    sums = jax.ShapeDtypeStruct((n, 8, tokens), f32)
    total = n * tokens
    res = pl.pallas_call(
        attn_kernel,
        out_shape=[out] * n + [sums],
        grid_spec=pltpu.PrefetchScalarGridSpec(
            num_scalar_prefetch=1,
            grid=(),
            in_specs=[pl.BlockSpec(memory_space=pltpu.VMEM)] * (2 + n),
            out_specs=[pl.BlockSpec(memory_space=pltpu.VMEM)] * (n + 1),
            scratch_shapes=[
                pltpu.VMEM((n, tokens, 2 * LANES), bf16),
                pltpu.VMEM((n, 2, DH + 16, tokens), bf16),
                pltpu.VMEM((n, tokens, LANES), bf16),
                pltpu.VMEM((8, tokens), f32),
                pltpu.VMEM((2, DH + 16, tokens), f32),
            ],
        ),
        compiler_params=params(),
        cost_estimate=cost(2 * total * total * 512, 4 * 2**20, 2 * total * total),
        name="attention",
    )(need, aux, one, *parts)
    return res[:n], res[n]


def proj_kernel(sc, valid, stream, gain, shift, *refs):
    att, weights = refs[:8], refs[8:16]
    mid, use, xs = refs[16:]
    tokens = stream.shape[1]

    def body(r):
        blocks = [a[r, :].astype(f32) for a in att]
        mean, rstd = row_stats(blocks, D)
        for i in range(BLOCKS):
            t = sc[8 + i]
            xs[t, r, :] = ((blocks[i] - mean) * rstd * gain[t] + shift[t]).astype(bf16)

    row_loop(tokens, ROWS, body)
    use[...] = jnp.zeros_like(use)
    keep = valid[...]
    for q in range(4):
        total = None
        for j in range(GROUPS):
            right = jnp.concatenate([weights[2 * q][j], weights[2 * q + 1][j]], axis=1)
            term = dot(wide_pair(xs, 2 * j, 2 * j + 1), right)
            total = term if total is None else total + term
        for half in range(2):
            part = total[:, half * LANES : (half + 1) * LANES]
            t = sc[2 * q + half]
            mid[t] = stream[t] + part
            use[0:1] += jnp.sum(keep * part * part, axis=0, keepdims=True)


def proj_call(sc, valid, stream, gain, shift, att, pieces):
    tokens = stream.shape[1]
    return pl.pallas_call(
        proj_kernel,
        out_shape=[
            jax.ShapeDtypeStruct(stream.shape, f32),
            jax.ShapeDtypeStruct((8, LANES), f32),
        ],
        grid_spec=pltpu.PrefetchScalarGridSpec(
            num_scalar_prefetch=1,
            grid=(),
            in_specs=[pl.BlockSpec(memory_space=pltpu.VMEM)] * 20,
            out_specs=[pl.BlockSpec(memory_space=pltpu.VMEM)] * 2,
            scratch_shapes=[pltpu.VMEM((BLOCKS, tokens, LANES), bf16)],
        ),
        compiler_params=params(),
        cost_estimate=cost(2 * tokens * D * D, 7 * 2**20),
        name="projection",
    )(sc, valid, stream, gain, shift, *att, *pieces)


def gelu_parts(h):
    half = 0.5 * (1.0 + lax.erf(h * (1.0 / math.sqrt(2.0))))
    return half


def up_kernel(sc, mid, gain, shift, hgain, hshift, *refs):
    weights = refs[:8]
    hidden, normed, low, mean_out, rstd_out, xs, act, buf = refs[8:]
    step = pl.program_id(0)
    tokens = mid.shape[1]

    @pl.when(step == 0)
    def _():
        def body(r):
            raw = [mid[b, r, :].astype(bf16) for b in range(BLOCKS)]
            blocks = [v.astype(f32) for v in raw]
            mean, rstd = row_stats(blocks, D)
            for b in range(BLOCKS):
                low[b, r, :] = raw[b]
                xs[b, r, :] = ((blocks[b] - mean) * rstd * gain[b] + shift[b]).astype(bf16)

        row_loop(tokens, ROWS, body)

    total = None
    for q in range(4):
        left = wide_pair(xs, sc[2 * q], sc[2 * q + 1])
        right = jnp.concatenate([weights[2 * q][0], weights[2 * q + 1][0]], axis=0)
        term = dot(left, right)
        total = term if total is None else total + term
    buf[...] = total

    def shape_rows(r):
        h = buf[r, :]
        hidden[0, r, :] = h.astype(bf16)
        act[step, r, :] = h * gelu_parts(h)

    row_loop(tokens, 64, shape_rows)

    @pl.when(step == GROUPS - 1)
    def _():
        def body(r):
            blocks = [act[z, r, :] for z in range(GROUPS)]
            mean, rstd = row_stats(blocks, FF)
            for z in range(GROUPS):
                normed[z, r, :] = ((blocks[z] - mean) * rstd * hgain[z] + hshift[z]).astype(bf16)
            mean_out[r, :] = jnp.broadcast_to(mean, (32, LANES))
            rstd_out[r, :] = jnp.broadcast_to(rstd, (32, LANES))

        row_loop(tokens, 32, body)


def up_call(sc, mid, gain, shift, hgain, hshift, pieces):
    tokens = mid.shape[1]
    return pl.pallas_call(
        up_kernel,
        out_shape=[
            jax.ShapeDtypeStruct((GROUPS, tokens, WIDE), bf16),
            jax.ShapeDtypeStruct((GROUPS, tokens, WIDE), bf16),
            jax.ShapeDtypeStruct(mid.shape, bf16),
            jax.ShapeDtypeStruct((tokens, LANES), f32),
            jax.ShapeDtypeStruct((tokens, LANES), f32),
        ],
        grid_spec=pltpu.PrefetchScalarGridSpec(
            num_scalar_prefetch=1,
            grid=(GROUPS,),
            in_specs=[whole(v.shape) for v in (mid, gain, shift, hgain, hshift)]
            + [pl.BlockSpec((1, LANES, WIDE), lambda k, sc: (k, 0, 0))] * 8,
            out_specs=[
                pl.BlockSpec((1, tokens, WIDE), lambda k, sc: (k, 0, 0)),
                whole((GROUPS, tokens, WIDE)),
                whole(mid.shape),
                whole((tokens, LANES)),
                whole((tokens, LANES)),
            ],
            scratch_shapes=[
                pltpu.VMEM((BLOCKS, tokens, LANES), bf16),
                pltpu.VMEM((GROUPS, tokens, WIDE), f32),
                pltpu.VMEM((tokens, WIDE), f32),
            ],
        ),
        compiler_params=params(),
        cost_estimate=cost(2 * tokens * D * FF, 20 * 2**20, tokens * FF),
        name="up",
    )(sc, mid, gain, shift, hgain, hshift, *pieces)


def down_kernel(sc, valid, mid, normed, *refs):
    weights = refs[:8]
    stream, low, use = refs[8:]
    step = pl.program_id(0)
    for q in range(4):
        right = jnp.concatenate([weights[2 * q][0], weights[2 * q + 1][0]], axis=1)
        total = dot(normed[0], right)
        for half in range(2):
            part = total[:, half * LANES : (half + 1) * LANES]
            t = sc[2 * q + half]

            @pl.when(step == 0)
            def _(t=t, part=part):
                stream[t] = part

            @pl.when(step > 0)
            def _(t=t, part=part):
                stream[t] += part

    @pl.when(step == GROUPS - 1)
    def _():
        use[...] = jnp.zeros_like(use)
        keep = valid[...]
        for b in range(BLOCKS):
            feed = stream[b]
            out = mid[b] + feed
            stream[b] = out
            low[b] = out.astype(bf16)
            use[0:1] += jnp.sum(keep * feed * feed, axis=0, keepdims=True)
            use[1:2] += jnp.sum(keep * out * out, axis=0, keepdims=True)


def down_call(sc, valid, mid, normed, pieces):
    tokens = mid.shape[1]
    return pl.pallas_call(
        down_kernel,
        out_shape=[
            jax.ShapeDtypeStruct(mid.shape, f32),
            jax.ShapeDtypeStruct(mid.shape, bf16),
            jax.ShapeDtypeStruct((8, LANES), f32),
        ],
        grid_spec=pltpu.PrefetchScalarGridSpec(
            num_scalar_prefetch=1,
            grid=(GROUPS,),
            in_specs=[
                whole(valid.shape),
                whole(mid.shape),
                pl.BlockSpec((1, tokens, WIDE), lambda k, sc: (k, 0, 0)),
            ]
            + [pl.BlockSpec((1, WIDE, LANES), lambda k, sc: (k, 0, 0))] * 8,
            out_specs=[whole(mid.shape), whole(mid.shape), whole((8, LANES))],
        ),
        compiler_params=params(),
        cost_estimate=cost(2 * tokens * D * FF, 18 * 2**20),
        name="down",
    )(sc, valid, mid, normed, *pieces)


def ffn_back_kernel(sc, grad, hidden, mean_in, rstd_in, low, gain, shift, hgain, *refs):
    downs, ups = refs[:8], refs[8:16]
    (dhid, grad_turned, normed_turned, grad_out, hgain_grad, hshift_grad, gain_grad, shift_grad) = (
        refs[16:24]
    )
    gs, dxs, hats, slopes, buf, first, cross, acc = refs[24:]
    step = pl.program_id(0)
    tokens = grad.shape[1]

    @pl.when(step == 0)
    def _():
        first[...] = jnp.zeros_like(first)
        cross[...] = jnp.zeros_like(cross)
        for b in range(BLOCKS):
            gs[b] = grad[b].astype(bf16)
            grad_turned[b] = flip(gs[b])

    @pl.when(step < GROUPS)
    def _():
        total = None
        for q in range(4):
            left = wide_pair(gs, sc[2 * q], sc[2 * q + 1])
            right = jnp.concatenate([downs[2 * q][0], downs[2 * q + 1][0]], axis=1)
            term = dot_nt(left, right)
            total = term if total is None else total + term
        buf[...] = total
        hgain_grad[step] = jnp.zeros((1, WIDE), f32)
        hshift_grad[step] = jnp.zeros((1, WIDE), f32)

        def body(r):
            h = hidden[0, r, :].astype(f32)
            half = gelu_parts(h)
            slope = half + h * (jnp.exp(-0.5 * h * h) * (1.0 / math.sqrt(2.0 * math.pi)))
            hat = (h * half - mean_in[r, 0:1]) * rstd_in[r, 0:1]
            dy = buf[r, :]
            dx = dy * hgain[step]
            both = dy * hat
            hgain_grad[step] += jnp.sum(both, axis=0, keepdims=True)
            hshift_grad[step] += jnp.sum(dy, axis=0, keepdims=True)
            first[r, :] += jnp.sum(dx, axis=1, keepdims=True) * (1.0 / FF)
            cross[r, :] += jnp.sum(dx * hat, axis=1, keepdims=True) * (1.0 / FF)
            dxs[step, r, :] = dx
            hats[step, r, :] = hat
            slopes[step, r, :] = slope.astype(bf16)

        row_loop(tokens, 32, body)

    @pl.when(step >= GROUPS)
    def _():
        z = step - GROUPS

        def body(r):
            inner = dxs[z, r, :] - first[r, 0:1] - hats[z, r, :] * cross[r, 0:1]
            dact = rstd_in[r, 0:1] * inner
            dhid[0, r, :] = (slopes[z, r, :].astype(f32) * dact).astype(bf16)

        row_loop(tokens, 64, body)
        for q in range(4):
            right = jnp.concatenate([ups[2 * q][0], ups[2 * q + 1][0]], axis=0)
            total = dot_nt(dhid[0], right)
            for part in range(2):
                t = sc[2 * q + part]
                value = total[:, part * LANES : (part + 1) * LANES]

                @pl.when(z == 0)
                def _(t=t, value=value):
                    acc[t] = value

                @pl.when(z > 0)
                def _(t=t, value=value):
                    acc[t] += value

    @pl.when(step == 2 * GROUPS - 1)
    def _():
        gain_grad[...] = jnp.zeros_like(gain_grad)
        shift_grad[...] = jnp.zeros_like(shift_grad)

        def body(r):
            blocks = [low[b, r, :].astype(f32) for b in range(BLOCKS)]
            mean, rstd = row_stats(blocks, D)
            hat = [(v - mean) * rstd for v in blocks]
            dy = [acc[b, r, :] for b in range(BLOCKS)]
            dv = norm_back(dy, hat, rstd, [gain[b] for b in range(BLOCKS)], D)
            for b in range(BLOCKS):
                gain_grad[b] += jnp.sum(dy[b] * hat[b], axis=0, keepdims=True)
                shift_grad[b] += jnp.sum(dy[b], axis=0, keepdims=True)
                grad_out[b, r, :] = grad[b, r, :] + dv[b]
                gs[b, r, :] = (hat[b] * gain[b] + shift[b]).astype(bf16)

        row_loop(tokens, ROWS, body)
        for b in range(BLOCKS):
            normed_turned[b] = flip(gs[b])


def ffn_back_call(sc, grad, hidden, mean, rstd, low, gain, shift, hgain, downs, ups):
    tokens = grad.shape[1]
    turned = (BLOCKS, LANES, tokens)
    first_half = lambda k, sc: (jnp.minimum(k, GROUPS - 1), 0, 0)
    second_half = lambda k, sc: (jnp.maximum(k - GROUPS, 0), 0, 0)
    big = (GROUPS, tokens, WIDE)
    return pl.pallas_call(
        ffn_back_kernel,
        out_shape=[
            jax.ShapeDtypeStruct(big, bf16),
            jax.ShapeDtypeStruct(turned, bf16),
            jax.ShapeDtypeStruct(turned, bf16),
            jax.ShapeDtypeStruct(grad.shape, f32),
            jax.ShapeDtypeStruct((GROUPS, 1, WIDE), f32),
            jax.ShapeDtypeStruct((GROUPS, 1, WIDE), f32),
            jax.ShapeDtypeStruct((BLOCKS, 1, LANES), f32),
            jax.ShapeDtypeStruct((BLOCKS, 1, LANES), f32),
        ],
        grid_spec=pltpu.PrefetchScalarGridSpec(
            num_scalar_prefetch=1,
            grid=(2 * GROUPS,),
            in_specs=[
                whole(grad.shape),
                pl.BlockSpec((1, tokens, WIDE), first_half),
            ]
            + [whole(v.shape) for v in (mean, rstd, low, gain, shift, hgain)]
            + [pl.BlockSpec((1, WIDE, LANES), first_half)] * 8
            + [pl.BlockSpec((1, LANES, WIDE), second_half)] * 8,
            out_specs=[
                pl.BlockSpec((1, tokens, WIDE), second_half),
                whole(turned),
                whole(turned),
                whole(grad.shape),
                whole((GROUPS, 1, WIDE)),
                whole((GROUPS, 1, WIDE)),
                whole((BLOCKS, 1, LANES)),
                whole((BLOCKS, 1, LANES)),
            ],
            scratch_shapes=[
                pltpu.VMEM((BLOCKS, tokens, LANES), bf16),
                pltpu.VMEM(big, f32),
                pltpu.VMEM(big, f32),
                pltpu.VMEM(big, bf16),
                pltpu.VMEM((tokens, WIDE), f32),
                pltpu.VMEM((tokens, LANES), f32),
                pltpu.VMEM((tokens, LANES), f32),
                pltpu.VMEM((BLOCKS, tokens, LANES), f32),
            ],
        ),
        compiler_params=params(),
        cost_estimate=cost(4 * tokens * D * FF, 32 * 2**20, 2 * tokens * FF),
        name="ffn_back",
    )(sc, grad, hidden, mean, rstd, low, gain, shift, hgain, *downs, *ups)


def proj_back_kernel(sc, grad, gain, shift, *refs):
    att, weights, outs = refs[:8], refs[8:16], refs[16:24]
    grad_turned, normed, gain_grad, shift_grad, gs, dm = refs[24:]
    tokens = grad.shape[1]
    for b in range(BLOCKS):
        gs[b] = grad[b].astype(bf16)
        grad_turned[b] = flip(gs[b])
    for j in range(GROUPS):
        total = None
        for q in range(4):
            left = wide_pair(gs, sc[2 * q], sc[2 * q + 1])
            right = jnp.concatenate([weights[2 * q][j], weights[2 * q + 1][j]], axis=1)
            term = dot_nt(left, right)
            total = term if total is None else total + term
        dm[2 * j] = total[:, :LANES]
        dm[2 * j + 1] = total[:, LANES:]
    gain_grad[...] = jnp.zeros_like(gain_grad)
    shift_grad[...] = jnp.zeros_like(shift_grad)

    def body(r):
        at = [sc[8 + i] for i in range(BLOCKS)]
        blocks = [a[r, :].astype(f32) for a in att]
        mean, rstd = row_stats(blocks, D)
        hat = [(v - mean) * rstd for v in blocks]
        dy = [dm[t, r, :] for t in at]
        dv = norm_back(dy, hat, rstd, [gain[t] for t in at], D)
        for i in range(BLOCKS):
            t = at[i]
            gain_grad[t] += jnp.sum(dy[i] * hat[i], axis=0, keepdims=True)
            shift_grad[t] += jnp.sum(dy[i], axis=0, keepdims=True)
            outs[i][r, :] = dv[i].astype(bf16)
            normed[t, r, :] = (hat[i] * gain[t] + shift[t]).astype(bf16)

    row_loop(tokens, ROWS, body)


def proj_back_call(sc, grad, gain, shift, att, pieces):
    tokens = grad.shape[1]
    return pl.pallas_call(
        proj_back_kernel,
        out_shape=[jax.ShapeDtypeStruct((tokens, LANES), bf16)] * 8
        + [
            jax.ShapeDtypeStruct((BLOCKS, LANES, tokens), bf16),
            jax.ShapeDtypeStruct((BLOCKS, tokens, LANES), bf16),
            jax.ShapeDtypeStruct((BLOCKS, 1, LANES), f32),
            jax.ShapeDtypeStruct((BLOCKS, 1, LANES), f32),
        ],
        grid_spec=pltpu.PrefetchScalarGridSpec(
            num_scalar_prefetch=1,
            grid=(),
            in_specs=[pl.BlockSpec(memory_space=pltpu.VMEM)] * 19,
            out_specs=[pl.BlockSpec(memory_space=pltpu.VMEM)] * 12,
            scratch_shapes=[
                pltpu.VMEM((BLOCKS, tokens, LANES), bf16),
                pltpu.VMEM((BLOCKS, tokens, LANES), f32),
            ],
        ),
        compiler_params=params(),
        cost_estimate=cost(2 * tokens * D * D, 9 * 2**20),
        name="projection_back",
    )(sc, grad, gain, shift, *att, *pieces)


def attn_back_kernel(need, aux, one, *refs):
    n = (len(refs) - 11) // 4
    qkv, att, datt, lse = refs[:n], refs[n : 2 * n], refs[2 * n : 3 * n], refs[3 * n]
    outs = refs[3 * n + 1 : 4 * n + 1]
    kx, kt, qs, vs, ds, delta, dq, dkey, dval, dkv = refs[4 * n + 1 :]
    for r in range(n):
        kx[r] = jnp.concatenate([qkv[r][1], aux[r]], axis=1)
        kt[r] = flip(qkv[r][1])
        qs[r] = (qkv[r][0].astype(f32) * (1.0 / math.sqrt(DH))).astype(bf16)
        vs[r] = qkv[r][2]
        ds[r] = datt[r][...]
        both = jnp.transpose(att[r][...].astype(f32) * datt[r][...].astype(f32), (1, 0))
        delta[r, 0:1] = jnp.sum(both[:DH], axis=0, keepdims=True)
        delta[r, 1:2] = jnp.sum(both[DH:], axis=0, keepdims=True)
    dq[...] = jnp.zeros_like(dq)

    def each_key(j, carry):
        dkey[...] = jnp.zeros_like(dkey)
        dval[...] = jnp.zeros_like(dval)

        def each_query(i, inner):
            @pl.when(need[i * n + j] == 1)
            def _():
                for h in range(2):
                    query = head_lanes(qs[i], h)
                    out = head_lanes(ds[i], h)
                    scores = dot_nt(kx[j], jnp.concatenate([query, one[...]], axis=1))
                    probs = jnp.exp(scores - lse[i, h : h + 1])
                    dprobs = dot_nt(vs[j], out)
                    dscores = (probs * (dprobs - delta[i, h : h + 1])).astype(bf16)
                    dval[...] += dot(probs.astype(bf16), out)
                    dkey[...] += dot(dscores, query)
                    rows = slice(h * DH, (h + 1) * DH)
                    dq[i, rows] += dot(kt[j, rows], dscores)

            return inner

        lax.fori_loop(0, n, each_query, 0)
        dkv[j, 0] = dkey[...].astype(bf16)
        dkv[j, 1] = dval[...].astype(bf16)
        return carry

    lax.fori_loop(0, n, each_key, 0)
    for r in range(n):
        outs[r][0] = (jnp.transpose(dq[r], (1, 0)) * (1.0 / math.sqrt(DH))).astype(bf16)
        outs[r][1] = dkv[r, 0]
        outs[r][2] = dkv[r, 1]


def attn_back_call(need, aux, one, parts, att, datt, lse):
    n = len(parts)
    tokens = aux.shape[1]
    total = n * tokens
    block = (n, tokens, LANES)
    return pl.pallas_call(
        attn_back_kernel,
        out_shape=[jax.ShapeDtypeStruct((3, tokens, LANES), bf16)] * n,
        grid_spec=pltpu.PrefetchScalarGridSpec(
            num_scalar_prefetch=1,
            grid=(),
            in_specs=[pl.BlockSpec(memory_space=pltpu.VMEM)] * (3 + 3 * n),
            out_specs=[pl.BlockSpec(memory_space=pltpu.VMEM)] * n,
            scratch_shapes=[
                pltpu.VMEM((n, tokens, 2 * LANES), bf16),
                pltpu.VMEM((n, LANES, tokens), bf16),
                pltpu.VMEM(block, bf16),
                pltpu.VMEM(block, bf16),
                pltpu.VMEM(block, bf16),
                pltpu.VMEM((n, 8, tokens), f32),
                pltpu.VMEM((n, LANES, tokens), f32),
                pltpu.VMEM((tokens, LANES), f32),
                pltpu.VMEM((tokens, LANES), f32),
                pltpu.VMEM((n, 2, tokens, LANES), bf16),
            ],
        ),
        compiler_params=params(),
        cost_estimate=cost(5 * total * total * 512, 8 * 2**20, 2 * total * total),
        name="attention_back",
    )(need, aux, one, *parts, *att, *datt, lse)


def qkv_back_kernel(sc, grad, low, gain, shift, *refs):
    dqkv, weights = refs[:8], refs[8:16]
    grad_out, normed_turned, gain_grad, shift_grad, acc, ns = refs[16:]
    tokens = grad.shape[1]
    for q in range(4):
        total = None
        for k in range(GROUPS):
            z = lax.rem(sc[16] + k, GROUPS)
            for c in range(3):
                left = jnp.concatenate([dqkv[2 * k][c], dqkv[2 * k + 1][c]], axis=1)
                right = jnp.concatenate(
                    [weights[2 * q][z, c], weights[2 * q + 1][z, c]], axis=0
                )
                term = dot_nt(left, right)
                total = term if total is None else total + term
        acc[sc[2 * q]] = total[:, :LANES]
        acc[sc[2 * q + 1]] = total[:, LANES:]
    gain_grad[...] = jnp.zeros_like(gain_grad)
    shift_grad[...] = jnp.zeros_like(shift_grad)

    def body(r):
        blocks = [low[b, r, :].astype(f32) for b in range(BLOCKS)]
        mean, rstd = row_stats(blocks, D)
        hat = [(v - mean) * rstd for v in blocks]
        dy = [acc[b, r, :] for b in range(BLOCKS)]
        dv = norm_back(dy, hat, rstd, [gain[b] for b in range(BLOCKS)], D)
        for b in range(BLOCKS):
            gain_grad[b] += jnp.sum(dy[b] * hat[b], axis=0, keepdims=True)
            shift_grad[b] += jnp.sum(dy[b], axis=0, keepdims=True)
            grad_out[b, r, :] = grad[b, r, :] + dv[b]
            ns[b, r, :] = (hat[b] * gain[b] + shift[b]).astype(bf16)

    row_loop(tokens, ROWS, body)
    for b in range(BLOCKS):
        normed_turned[b] = flip(ns[b])


def qkv_back_call(sc, grad, low, gain, shift, dqkv, pieces):
    tokens = grad.shape[1]
    return pl.pallas_call(
        qkv_back_kernel,
        out_shape=[
            jax.ShapeDtypeStruct(grad.shape, f32),
            jax.ShapeDtypeStruct((BLOCKS, LANES, tokens), bf16),
            jax.ShapeDtypeStruct((BLOCKS, 1, LANES), f32),
            jax.ShapeDtypeStruct((BLOCKS, 1, LANES), f32),
        ],
        grid_spec=pltpu.PrefetchScalarGridSpec(
            num_scalar_prefetch=1,
            grid=(),
            in_specs=[pl.BlockSpec(memory_space=pltpu.VMEM)] * 20,
            out_specs=[pl.BlockSpec(memory_space=pltpu.VMEM)] * 4,
            scratch_shapes=[
                pltpu.VMEM((BLOCKS, tokens, LANES), f32),
                pltpu.VMEM((BLOCKS, tokens, LANES), bf16),
            ],
        ),
        compiler_params=params(),
        cost_estimate=cost(6 * tokens * D * D, 18 * 2**20),
        name="qkv_back",
    )(sc, grad, low, gain, shift, *dqkv, *pieces)


def weight_grad_kernel(kind, added, sc, turned, *refs):
    count = {"wide": 1, "pair": 1, "qkv": 8}[kind]
    right_refs, rest = refs[:count], refs[count:]
    left = jnp.concatenate([turned[sc[m]] for m in range(4)], axis=0)
    extra = rest[0] if added else None
    outs = rest[1:] if added else rest

    def put(spot, value):
        for m in range(4):
            part = value[m * LANES : (m + 1) * LANES]
            if added:
                part = part + extra[(m,) + spot].astype(f32)
                outs[m // 2][(m % 2,) + spot] = part.astype(bf16)
            else:
                outs[0][(m,) + spot] = part.astype(bf16)

    if kind == "wide":
        put((0,), dot(left, right_refs[0][0]))
    elif kind == "pair":
        for z in range(GROUPS):
            put((z,), dot(left, wide_pair(right_refs[0], 2 * z, 2 * z + 1)))
    else:
        for k in range(GROUPS):
            z = lax.rem(sc[4] + k, GROUPS)
            for c in range(3):
                right = jnp.concatenate(
                    [right_refs[2 * k][c], right_refs[2 * k + 1][c]], axis=1
                )
                put((z, c), dot(left, right))


def weight_grad_call(kind, sc, turned, rights, extra=None):
    tokens = turned.shape[2]
    inner = {
        "wide": (GROUPS, LANES, WIDE),
        "pair": (GROUPS, LANES, 256),
        "qkv": (GROUPS, 3, LANES, 256),
    }[kind]
    added = extra is not None
    if kind == "wide":
        grid = (GROUPS,)
        right_specs = [pl.BlockSpec((1, tokens, WIDE), lambda k, sc: (k, 0, 0))]
        piece = lambda m: pl.BlockSpec((m, 1, LANES, WIDE), lambda k, sc: (0, k, 0, 0))
    else:
        grid = (1,)
        right_specs = [whole(v.shape) for v in rights]
        piece = lambda m: whole((m,) + inner)
    outs = [2, 2] if added else [4]
    width = math.prod(inner) // LANES
    return pl.pallas_call(
        lambda *refs: weight_grad_kernel(kind, added, *refs),
        out_shape=[jax.ShapeDtypeStruct((m,) + inner, bf16) for m in outs],
        grid_spec=pltpu.PrefetchScalarGridSpec(
            num_scalar_prefetch=1,
            grid=grid,
            in_specs=[whole(turned.shape)] + right_specs + ([piece(4)] if added else []),
            out_specs=[piece(m) for m in outs],
        ),
        compiler_params=params(),
        cost_estimate=cost(tokens * D * width, 2 * D * width),
        name="weight_grad_" + kind,
    )(sc, turned, *rights, *([extra] if added else []))


class Net:
    def __init__(self, n_dp, n_head):
        self.n_dp, self.n = n_dp, n_head
        self.own = lax.axis_index("dp")
        self.z = lax.axis_index("head")
        self.lo = self.own % n_head
        self.fast = n_dp == 8 and n_head == 4
        core_zero = [2, 4]
        self.one_way = [(i, i ^ core_zero[i % 2]) for i in range(n_dp)]
        self.other_way = [(i, i ^ core_zero[1 - i % 2]) for i in range(n_dp)]
        self.core = [(i, i ^ 1) for i in range(n_dp)]
        if self.fast:
            core = self.own % 2
            step = jnp.where(core == 0, 2, 4).astype(jnp.int32)
            mine = [jnp.int32(0), step, 6 - step, jnp.int32(6)]
            theirs = [jnp.int32(0), 6 - step, step, jnp.int32(6)]
            self.even = jnp.stack([jnp.bitwise_xor(self.own, v) for v in mine])
            self.odd = jnp.stack([jnp.bitwise_xor(self.own, v ^ 1) for v in theirs])
            self.rel = self.lo
            units = BLOCKS // n_head
            self.features = jnp.stack(
                [units * ((self.lo + i // units) % n_head) + i % units for i in range(BLOCKS)]
            )
        else:
            self.even = jnp.arange(4, dtype=jnp.int32)
            self.odd = jnp.arange(4, 8, dtype=jnp.int32)
            self.rel = jnp.int32(0)
            self.features = jnp.arange(BLOCKS, dtype=jnp.int32)
        self.even = self.even.astype(jnp.int32)
        self.odd = self.odd.astype(jnp.int32)
        self.table = jnp.concatenate([self.even, self.odd])
        self.scalars = jnp.concatenate(
            [self.table, self.features.astype(jnp.int32), self.rel.astype(jnp.int32)[None]]
        )

    def shift(self, value, k):
        n = self.n
        if k % n == 0:
            return value
        pairs = [(i, (i // n) * n + (i + k) % n) for i in range(self.n_dp)]
        return lax.ppermute(value, "dp", pairs)

    def gather(self, shard, kind):
        if self.fast:
            start = lax.all_gather(shard, "head")
            near = lax.ppermute(start, "dp", self.one_way)
            half = [start, near] + [lax.ppermute(v, "dp", self.other_way) for v in (start, near)]
            return half + [lax.ppermute(v, "dp", self.core) for v in half]
        tall, flat = {"qkv": (1, 2), "up": (0, 1), "out": (1, 0), "down": (1, 0)}[kind]
        full = lax.all_gather(shard, "head", axis=flat, tiled=True)
        full = lax.all_gather(full, "dp", axis=tall, tiled=True)
        if kind == "qkv":
            full = full.reshape(3, BLOCKS, LANES, GROUPS, 256).transpose(1, 3, 0, 2, 4)
        elif kind == "up":
            full = full.reshape(BLOCKS, LANES, GROUPS, WIDE).transpose(0, 2, 1, 3)
        else:
            full = full.reshape(GROUPS, -1, BLOCKS, LANES).transpose(2, 0, 1, 3)
        return [full[i] for i in range(BLOCKS)]

    def reduce(self, kind, turned, rights):
        shape = "qkv" if kind == "qkv" else ("pair" if kind == "out" else "wide")
        rel = self.rel.astype(jnp.int32)[None]
        odd_table = jnp.concatenate([self.odd, rel])
        even_table = jnp.concatenate([self.even, rel])
        (odd,) = weight_grad_call(shape, odd_table, turned, rights)
        if self.fast:
            other = lax.ppermute(odd, "dp", self.core)
            keep, send = weight_grad_call(shape, even_table, turned, rights, other)
            pair = lax.ppermute(send, "dp", self.other_way)
            mine = (keep[0].astype(f32) + pair[0].astype(f32)).astype(bf16)
            sent = (keep[1].astype(f32) + pair[1].astype(f32)).astype(bf16)
            last = lax.ppermute(sent, "dp", self.one_way)
            block = (mine.astype(f32) + last.astype(f32)).astype(bf16)
            block = lax.psum_scatter(block, "head", scatter_dimension=0, tiled=False)
            block = block.astype(f32)
            return block.T if kind in ("out", "down") else block
        (even,) = weight_grad_call(shape, even_table, turned, rights)
        full = jnp.concatenate([even, odd], axis=0)
        if kind == "qkv":
            full = full.transpose(2, 0, 3, 1, 4).reshape(3, D, D)
            tall, flat = 1, 2
        elif kind == "up":
            full = full.transpose(0, 2, 1, 3).reshape(D, FF)
            tall, flat = 0, 1
        else:
            full = full.transpose(1, 3, 0, 2).reshape(-1, D)
            tall, flat = 1, 0
        full = lax.psum_scatter(full, "dp", scatter_dimension=tall, tiled=True)
        return lax.psum_scatter(full, "head", scatter_dimension=flat, tiled=True).astype(f32)

    def to_heads(self, blocks):
        n, units = self.n, BLOCKS // self.n
        if not self.fast:
            stacked = jnp.stack(blocks)
            blocks = [
                lax.dynamic_index_in_dim(stacked, units * ((self.lo + k) % n) + u, 0, False)
                for k in range(n)
                for u in range(units)
            ]
        return [[self.shift(blocks[k * units + u], k) for k in range(n)] for u in range(units)]

    def to_tokens(self, units):
        n, count = self.n, BLOCKS // self.n
        blocks = [self.shift(units[u][k], -k) for k in range(n) for u in range(count)]
        if not self.fast:
            stacked = jnp.stack(blocks)
            order = [count * ((i // count - self.lo) % n) + i % count for i in range(BLOCKS)]
            blocks = [lax.dynamic_index_in_dim(stacked, v, 0, False) for v in order]
        return blocks

    def turn(self, k):
        n = self.n
        pairs = []
        for hi in range(self.n_dp // n):
            for lo in range(n):
                for z in range(n):
                    pairs.append(((hi * n + lo) * n + z, (hi * n + (z + k) % n) * n + lo))
        return pairs

    def rows_in(self, array):
        n = self.n
        tokens = array.shape[0] // n
        low = array.astype(bf16).reshape(n, tokens, array.shape[1])
        got = []
        for k in range(n):
            piece = lax.dynamic_index_in_dim(low, (self.z + k) % n, 0, False)
            got.append(lax.ppermute(piece, ("dp", "head"), self.turn(k)))
        stacked = jnp.stack(got)
        order = (self.lo - jnp.arange(n)) % n
        stacked = jnp.take(stacked, order, axis=0)
        units = BLOCKS // n
        stacked = stacked.reshape(n, tokens, units, LANES).transpose(0, 2, 1, 3)
        return stacked.reshape(BLOCKS, tokens, LANES)

    def rows_out(self, array):
        n = self.n
        units = BLOCKS // n
        tokens = array.shape[1]
        low = array.astype(bf16).reshape(n, units, tokens, LANES)
        got = []
        for k in range(n):
            piece = lax.dynamic_index_in_dim(low, (self.lo - k) % n, 0, False)
            back = [(b, a) for a, b in self.turn(k)]
            got.append(lax.ppermute(piece, ("dp", "head"), back))
        stacked = jnp.stack(got)
        order = (jnp.arange(n) - self.z) % n
        stacked = jnp.take(stacked, order, axis=0)
        return stacked.transpose(0, 2, 1, 3).reshape(n * tokens, units * LANES).astype(f32)


def local(
    n_dp,
    n_head,
    stream_in,
    qkv_weight,
    out_weight,
    up_weight,
    down_weight,
    norm_gains,
    norm_shifts,
    hidden_gains,
    hidden_shifts,
    buckets,
    valid_mask,
    cotangent,
):
    net = Net(n_dp, n_head)
    n = n_head
    layers = qkv_weight.shape[0]
    tokens = LONG // n
    units = BLOCKS // n

    gathered = []
    stream_low = net.rows_in(stream_in)
    for l in range(layers):
        gathered.append(
            {
                "qkv": net.gather(qkv_weight[l], "qkv"),
                "out": net.gather(out_weight[l], "out"),
                "up": net.gather(up_weight[l], "up"),
                "down": net.gather(down_weight[l], "down"),
            }
        )
    vectors = [
        v.reshape(layers, -1) for v in (norm_gains, norm_shifts, hidden_gains, hidden_shifts)
    ]
    packed = lax.all_gather(jnp.concatenate(vectors, axis=1), "head")
    third = 3 * (D // n)
    wide = FF // n

    def unpack(l):
        part = packed[:, l]
        norm = lambda v: v.reshape(n, 3, -1).transpose(1, 0, 2).reshape(3, BLOCKS, 1, LANES)
        hid = lambda v: v.reshape(GROUPS, 1, WIDE)
        return (
            norm(part[:, :third]),
            norm(part[:, third : 2 * third]),
            hid(part[:, 2 * third : 2 * third + wide]),
            hid(part[:, 2 * third + wide :]),
        )

    flags = jnp.concatenate([valid_mask, buckets])
    flags = lax.ppermute(flags, ("dp", "head"), net.turn(0))
    slab_mask = flags[:LONG].reshape(n, tokens)
    bucket = flags[LONG]
    rel_blocks = (net.lo - jnp.arange(n)) % n
    rel_mask = jnp.take(slab_mask, rel_blocks, axis=0)
    lane = jnp.arange(LANES)[None, None, :] == 0
    aux = jnp.where((rel_mask[:, :, None] == 0) & lane, MASKED, 0.0).astype(bf16)
    one = jnp.broadcast_to((jnp.arange(LANES)[None, :] == 0), (tokens, LANES)).astype(bf16)
    sequence = jnp.where(bucket == 1, 0, (rel_blocks * tokens) // SHORT)
    alive = jnp.sum(rel_mask, axis=1) > 0
    need = ((sequence[:, None] == sequence[None, :]) & alive[None, :]).astype(jnp.int32)
    need = need.reshape(n * n)
    valid = lax.dynamic_index_in_dim(slab_mask, net.lo, 0, False).astype(f32)[:, None]

    stream = stream_low.astype(f32)
    low = stream_low
    kept = []
    usage = []
    for l in range(layers):
        w = gathered[l]
        gains, shifts, hgain, hshift = unpack(l)
        blocks = qkv_call(net.scalars[jnp.array([0, 1, 2, 3, 4, 5, 6, 7, 16])], low, gains[0], shifts[0], w["qkv"])
        parts = net.to_heads(blocks)
        att, sums = [], []
        for u in range(units):
            out, lse = attn_call(need, aux, one, parts[u])
            att.append(out)
            sums.append(lse)
        rows = net.to_tokens(att)
        mid, use_branch = proj_call(
            net.scalars, valid, stream, gains[1], shifts[1], rows, w["out"]
        )
        hidden, normed, low_mid, mean, rstd = up_call(
            net.scalars, mid, gains[2], shifts[2], hgain, hshift, w["up"]
        )
        stream, next_low, use_rest = down_call(net.scalars, valid, mid, normed, w["down"])
        usage += [jnp.sum(use_branch[0]), jnp.sum(use_rest[0]), jnp.sum(use_rest[1])]
        kept.append((low, parts, att, sums, rows, hidden, normed, low_mid, mean, rstd))
        low = next_low

    stream_out = net.rows_out(stream)
    grad = net.rows_in(cotangent).astype(f32)
    weight_grads = [None] * layers
    vector_grads = [None] * layers
    for l in reversed(range(layers)):
        w = gathered[l]
        gains, shifts, hgain, hshift = unpack(l)
        low, parts, att, sums, rows, hidden, normed, low_mid, mean, rstd = kept[l]
        (dhid, grad_turned, ffn_turned, grad, hg, hs, g2, s2) = ffn_back_call(
            net.scalars, grad, hidden, mean, rstd, low_mid, gains[2], shifts[2], hgain,
            w["down"], w["up"],
        )
        down_grad = net.reduce("down", grad_turned, [normed])
        up_grad = net.reduce("up", ffn_turned, [dhid])
        res = proj_back_call(net.scalars, grad, gains[1], shifts[1], rows, w["out"])
        dmid, (turned, normed_mid, g1, s1) = res[:8], res[8:]
        datt = net.to_heads(dmid)
        dparts = [
            attn_back_call(need, aux, one, parts[u], att[u], datt[u], sums[u])
            for u in range(units)
        ]
        dqkv = net.to_tokens(dparts)
        out_grad = net.reduce("out", turned, [normed_mid])
        grad, in_turned, g0, s0 = qkv_back_call(
            net.scalars, grad, low, gains[0], shifts[0], dqkv, w["qkv"]
        )
        qkv_grad = net.reduce("qkv", in_turned, dqkv)
        weight_grads[l] = (qkv_grad, out_grad, up_grad, down_grad)
        vector_grads[l] = jnp.concatenate(
            [v.reshape(-1) for v in (g0, g1, g2, s0, s1, s2, hg, hs)]
        )
    stream_grad = net.rows_out(grad)
    tail = jnp.stack(usage + [jnp.sum(valid) * D])
    summed = lax.psum(jnp.concatenate(vector_grads + [tail]), ("dp", "head"))
    usage_rms = jnp.sqrt(summed[-1 - 3 * layers : -1] / summed[-1]).reshape(layers, 3)
    rest = summed[: -1 - 3 * layers].reshape(layers, -1)
    cut = lambda v: lax.dynamic_slice_in_dim(
        v, net.z * (v.shape[-1] // n), v.shape[-1] // n, v.ndim - 1
    )
    gains_grad = cut(rest[:, : 3 * D].reshape(layers, 3, D))
    shifts_grad = cut(rest[:, 3 * D : 6 * D].reshape(layers, 3, D))
    hidden_gains_grad = cut(rest[:, 6 * D : 6 * D + FF])
    hidden_shifts_grad = cut(rest[:, 6 * D + FF :])
    stacked = [jnp.stack([weight_grads[l][k] for l in range(layers)]) for k in range(4)]
    return (
        stream_out,
        stream_grad,
        stacked[0],
        stacked[1],
        stacked[2],
        stacked[3],
        gains_grad,
        shifts_grad,
        hidden_gains_grad,
        hidden_shifts_grad,
        usage_rms,
    )


def solution(mesh):
    n_dp, n_head = mesh.shape["dp"], mesh.shape["head"]

    def run(*args):
        return local(n_dp, n_head, *args)

    return jax.shard_map(
        run,
        mesh=mesh,
        in_specs=(
            P("dp", "head"),
            P(None, None, "dp", "head"),
            P(None, "head", "dp"),
            P(None, "dp", "head"),
            P(None, "head", "dp"),
            P(None, None, "head"),
            P(None, None, "head"),
            P(None, "head"),
            P(None, "head"),
            P("dp"),
            P("dp"),
            P("dp", "head"),
        ),
        out_specs=(
            P("dp", "head"),
            P("dp", "head"),
            P(None, None, "dp", "head"),
            P(None, "head", "dp"),
            P(None, "dp", "head"),
            P(None, "head", "dp"),
            P(None, None, "head"),
            P(None, None, "head"),
            P(None, "head"),
            P(None, "head"),
            P(),
        ),
        check_vma=False,
    )
```

time: 2570 us -> 1390 us (0.54)
  waiting for transfers between devices: 1370 us -> 344 us
  Pallas kernels: 0 us -> 471 us
  matrix products: 310 us -> 0 us
  blocking collectives: 494 us -> 191 us
  starting transfers between devices: 2.21 us -> 234 us
  local copies, waits for them, and re-layouts: 173 us -> 54.1 us
  other arithmetic: 174 us -> 61.8 us
    reduce_scatter x10 -> x8, waiting for transfers between devices: 726 us -> 104 us  [reduce(): block = lax.psum_scatter(block, 'head', scatter_dimension=0, tiled=False)]
    all_gather x14 -> x4, waiting for transfers between devices: 564 us -> 0.03 us  [gather(): start = lax.all_gather(shard, 'head')]
    pallas_call x0 -> x38, Pallas kernels: none -> 471 us  [the longest x16 104 us: weight_grad_call(): pl.pallas_call(lambda *refs: weight_grad_kernel(kind, added, *refs), out_...]
    psum x18 -> x0, blocking collectives: 398 us -> none  [the longest x1 153 us: local(): lax.psum((jnp.stack(usage_rows), jnp.sum(row_weight) * stream.shape[1]),...]
    dot_general x80 -> x0, matrix products: 310 us -> none  [the longest x2 55.3 us: local(): hidden = jnp.dot(normed_ffn, up_full, preferred_element_type=jnp.float32)]
    ppermute x0 -> x145, waiting for transfers between devices: none -> 238 us  [the longest x48 76.9 us: shift(): return lax.ppermute(value, 'dp', pairs)]
    ppermute x0 -> x145, starting transfers between devices: none -> 233 us  [the longest x8 119 us: rows_out(): got.append(lax.ppermute(piece, ('dp', 'head'), back))]
    all_gather x10 -> x5, blocking collectives: 96.5 us -> 191 us  [the longest x4 128 us: gather(): start = lax.all_gather(shard, 'head')]
  transfers between devices with their start and end apart: 30 -> 158, of which waited for: 23 -> 45; matrix products, arithmetic and copies ran while one was open for 11% -> 7% of each run, Pallas kernels for 0% -> 26%
where the time goes in v1:
time: 1390 us; the launch traced here: 1370 us
  Pallas kernels  471 us (34%)
  waiting for transfers between devices  344 us (25%)
  starting transfers between devices  234 us (17%)
  blocking collectives  191 us (14%)
  other arithmetic  61.8 us (4%)
  local copies, waits for them, and re-layouts  54.1 us (4%)
  between operations  18.1 us (1%)
    all_gather x4, blocking collectives, gather(): start = lax.all_gather(shard, 'head')  128 us
    ppermute x8, starting transfers between devices, rows_out(): got.append(lax.ppermute(piece, ('dp', 'head'), back))  119 us
    reduce_scatter x8, waiting for transfers between devices, reduce(): block = lax.psum_scatter(block, 'head', scatter_dimension=0, tiled=False)  104 us
    pallas_call x16, Pallas kernels, weight_grad_call(): pl.pallas_call(lambda *refs: weight_grad_kernel(kind, added, *refs), out_...  104 us
    pallas_call x2, Pallas kernels, ffn_back_call(): pl.pallas_call(ffn_back_kernel, out_shape=[jax.ShapeDtypeStruct(big, bf16...  88.3 us
    ppermute x48, waiting for transfers between devices, shift(): return lax.ppermute(value, 'dp', pairs)  76.9 us
    pallas_call x4, Pallas kernels, attn_back_call(): pl.pallas_call(attn_back_kernel, out_shape=[jax.ShapeDtypeStruct((3, toke...  67.9 us
    all_gather x1, blocking collectives, local(): packed = lax.all_gather(jnp.concatenate(vectors, axis=1), 'head')  63.8 us
  transfers between devices with their start and end apart: 158, of which 45 were waited for; matrix products, arithmetic and copies ran while one was open for 7% of the time, Pallas kernels for 26%

profile of v1, /device:TPU:0, one launch (start us, length us, event | category | flops | bytes accessed | tf_op | source)
XLA Modules:
  0.0 1374.2 jit_solution(16259219458614102035)
XLA Ops:
  24.8 71.6 %all_gather.33.refs_8_ = bf16[4,256,128]{2,1,0:T(8,128)(2,1)S(1)} all-gather(bf16[1,256,128]{2,1,0:T(8,128)(2,1)S(1)} %get-tuple-element.358), channel_id=1, replica_groups=mesh['dp'=8,'head'=4] {'head'}, dimensions={0}, use_global_device_ids=true | all-gather | bytes 327680 | tf_op jit(solution)/shard_map/all_gather | solution.py:876
  96.7 15.6 %all_gather.37.refs_8_ = bf16[4,256,128]{2,1,0:T(8,128)(2,1)S(1)} all-gather(bf16[1,256,128]{2,1,0:T(8,128)(2,1)S(1)} %get-tuple-element.357), channel_id=1, replica_groups=mesh['dp'=8,'head'=4] {'head'}, dimensions={0}, use_global_device_ids=true | all-gather | bytes 327680 | tf_op jit(solution)/shard_map/all_gather | solution.py:876
  119.1 63.8 %all-gather.1 = f32[4,2,3584]{2,1,0:T(2,128)S(1)} all-gather(f32[1,2,3584]{2,1,0:T(2,128)S(1)} %maximum_bitcast_fusion), channel_id=2, replica_groups=mesh['dp'=8,'head'=4] {'head'}, dimensions={0}, use_global_device_ids=true | all-gather | bytes 143360 | tf_op jit(solution)/shard_map/all_gather | solution.py:1018
  187.3 22.5 %all_gather.32.refs_0_.refs_8_ = bf16[4,3,128,256]{3,2,1,0:T(8,128)(2,1)S(1)} all-gather(bf16[1,3,128,256]{3,2,1,0:T(8,128)(2,1)S(1)} %get-tuple-element.356), channel_id=1, replica_groups=mesh['dp'=8,'head'=4] {'head'}, dimensions={0}, use_global_device_ids=true | all-gather | bytes 983040 | tf_op jit(solution)/shard_map/all_gather | solution.py:876
  226.4 17.9 %all_gather.36.refs_0_.refs_8_ = bf16[4,3,128,256]{3,2,1,0:T(8,128)(2,1)S(1)} all-gather(bf16[1,3,128,256]{3,2,1,0:T(8,128)(2,1)S(1)} %get-tuple-element.355), channel_id=1, replica_groups=mesh['dp'=8,'head'=4] {'head'}, dimensions={0}, use_global_device_ids=true | all-gather | bytes 983040 | tf_op jit(solution)/shard_map/all_gather | solution.py:876
  248.6 15.3 %collective-permute-done.6.refs_2_.refs_10_ = bf16[4,3,128,256]{3,2,1,0:T(8,128)(2,1)} collective-permute-done((bf16[4,3,128,256]{3,2,1,0:T(8,128)(2,1)S(1)}, bf16[4,3,128,256]{3,2,1,0:T(8,128)(2,1)}, u32[]{:S(2)}, u32[]{:S(2)}) %collective-permute-start.6) | collective-permute-done | bytes 786464 | tf_op jit(solution)/shard_map/ppermute | solution.py:878
  299.8 9.0 collective-permute-done.31.refs_1_.refs_9_
  308.8 8.2 collective-permute-done.32.refs_2_.refs_10_
  321.9 13.4 qkv.2
  340.0 13.8 %collective-permute-done.71.refs_1_.refs_9_ = bf16[4,128,1024]{2,1,0:T(8,128)(2,1)} collective-permute-done((bf16[4,128,1024]{2,1,0:T(8,128)(2,1)}, bf16[4,128,1024]{2,1,0:T(8,128)(2,1)}, u32[]{:S(2)}, u32[]{:S(2)}) %collective-permute-start.71) | collective-permute-done | bytes 1048608 | tf_op jit(solution)/shard_map/ppermute | solution.py:877
  358.0 8.3 collective-permute-done.15.refs_1_
  375.0 8.1 collective-permute-done.12.refs_1_
  385.3 13.8 %attention.5 = (bf16[512,128]{1,0:T(8,128)(2,1)}, bf16[512,128]{1,0:T(8,128)(2,1)}, bf16[512,128]{1,0:T(8,128)(2,1)}, bf16[512,128]{1,0:T(8,128)(2,1)}, f32[4,8,512]{2,1,0:T(8,128)}) custom-call(s32[16]{0:T(128)} %reshape.471.need, bf16[4,512,128]{2,1,0:T(8,128)(2,1)} %select_convert_fusion.aux, bf16[512,128]{1,0:T(8,128)(2,1)} %broadcast_in_dim.86.one, ...), custom_call_target="tpu_custom_call" | custom-call | flops 4294967296 | bytes 4194304 | tf_op jit(solution)/shard_map/attention/pallas_call | solution.py:196
  400.2 13.9 %attention.4 = (bf16[512,128]{1,0:T(8,128)(2,1)}, bf16[512,128]{1,0:T(8,128)(2,1)}, bf16[512,128]{1,0:T(8,128)(2,1)}, bf16[512,128]{1,0:T(8,128)(2,1)}, f32[4,8,512]{2,1,0:T(8,128)}) custom-call(s32[16]{0:T(128)} %reshape.471.need, bf16[4,512,128]{2,1,0:T(8,128)(2,1)} %select_convert_fusion.aux, bf16[512,128]{1,0:T(8,128)(2,1)} %broadcast_in_dim.86.one, ...), custom_call_target="tpu_custom_call" | custom-call | flops 4294967296 | bytes 4194304 | tf_op jit(solution)/shard_map/attention/pallas_call | solution.py:196
  441.9 18.6 %up.2 = (bf16[4,512,1024]{2,1,0:T(8,128)(2,1)}, bf16[4,512,1024]{2,1,0:T(8,128)(2,1)}, bf16[8,512,128]{2,1,0:T(8,128)(2,1)}, f32[512,128]{1,0:T(8,128)}, f32[512,128]{1,0:T(8,128)}) custom-call(s32[17]{0:T(128)} %copy-done, f32[8,512,128]{2,1,0:T(8,128)} %get-tuple-element.164.mid, f32[8,1,128]{2,1,0:T(1,128)} %squeeze.159.gain, ...), custom_call_target="tpu_custom_call" | custom-call | flops 4294967296 | bytes 20971520 | tf_op jit(solution)/shard_map/up/pallas_call | solution.py:321
  460.5 18.0 %down.2 = (f32[8,512,128]{2,1,0:T(8,128)}, bf16[8,512,128]{2,1,0:T(8,128)(2,1)}, f32[8,128]{1,0:T(8,128)}) custom-call(s32[17]{0:T(128)} %copy-done, f32[512,1]{1,0:T(8,128)} %copy.76.valid, f32[8,512,128]{2,1,0:T(8,128)} %get-tuple-element.164.mid, bf16[4,512,1024]{2,1,0:T(8,128)(2,1)} %get-tuple-element.165.normed.refs_2_, ...), custom_call_target="tpu_custom_call" | custom-call | flops 4294967296 | bytes 18874368 | tf_op jit(solution)/shard_map/down/pallas_call | solution.py:388
  478.5 13.4 qkv.3
  495.0 7.5 collective-permute-done.55.refs_1_
  513.1 13.8 %attention.7 = (bf16[512,128]{1,0:T(8,128)(2,1)}, bf16[512,128]{1,0:T(8,128)(2,1)}, bf16[512,128]{1,0:T(8,128)(2,1)}, bf16[512,128]{1,0:T(8,128)(2,1)}, f32[4,8,512]{2,1,0:T(8,128)}) custom-call(s32[16]{0:T(128)} %reshape.471.need, bf16[4,512,128]{2,1,0:T(8,128)(2,1)} %select_convert_fusion.aux, bf16[512,128]{1,0:T(8,128)(2,1)} %broadcast_in_dim.86.one, ...), custom_call_target="tpu_custom_call" | custom-call | flops 4294967296 | bytes 4194304 | tf_op jit(solution)/shard_map/attention/pallas_call | solution.py:196
  526.9 9.0 collective-permute-done.52.refs_1_
  542.1 14.0 %attention.6 = (bf16[512,128]{1,0:T(8,128)(2,1)}, bf16[512,128]{1,0:T(8,128)(2,1)}, bf16[512,128]{1,0:T(8,128)(2,1)}, bf16[512,128]{1,0:T(8,128)(2,1)}, f32[4,8,512]{2,1,0:T(8,128)}) custom-call(s32[16]{0:T(128)} %reshape.471.need, bf16[4,512,128]{2,1,0:T(8,128)(2,1)} %select_convert_fusion.aux, bf16[512,128]{1,0:T(8,128)(2,1)} %broadcast_in_dim.86.one, ...), custom_call_target="tpu_custom_call" | custom-call | flops 4294967296 | bytes 4194304 | tf_op jit(solution)/shard_map/attention/pallas_call | solution.py:196
  576.3 18.5 %up.3 = (bf16[4,512,1024]{2,1,0:T(8,128)(2,1)}, bf16[4,512,1024]{2,1,0:T(8,128)(2,1)}, bf16[8,512,128]{2,1,0:T(8,128)(2,1)}, f32[512,128]{1,0:T(8,128)}, f32[512,128]{1,0:T(8,128)}) custom-call(s32[17]{0:T(128)} %copy-done, f32[8,512,128]{2,1,0:T(8,128)} %get-tuple-element.184.mid, f32[8,1,128]{2,1,0:T(1,128)} %squeeze.166.gain, ...), custom_call_target="tpu_custom_call" | custom-call | flops 4294967296 | bytes 20971520 | tf_op jit(solution)/shard_map/up/pallas_call | solution.py:321
  594.8 44.1 %ffn_back.2 = (bf16[4,512,1024]{2,1,0:T(8,128)(2,1)}, bf16[8,128,512]{2,1,0:T(8,128)(2,1)}, bf16[8,128,512]{2,1,0:T(8,128)(2,1)}, f32[8,512,128]{2,1,0:T(8,128)}...) custom-call(s32[17]{0:T(128)} %copy-done, ...), custom_call_target="tpu_custom_call" | custom-call | flops 8589934592 | bytes 33554432 | tf_op jit(solution)/shard_map/ffn_back/pallas_call | solution.py:512
  638.9 8.2 projection_back.2
  656.0 17.0 %attention_back.5 = (bf16[3,512,128]{2,1,0:T(8,128)(2,1)}, bf16[3,512,128]{2,1,0:T(8,128)(2,1)}, bf16[3,512,128]{2,1,0:T(8,128)(2,1)}, bf16[3,512,128]{2,1,0:T(8,128)(2,1)}) custom-call(s32[16]{0:T(128)} %reshape.471.need, bf16[4,512,128]{2,1,0:T(8,128)(2,1)} %select_convert_fusion.aux, bf16[512,128]{1,0:T(8,128)(2,1)} %broadcast_in_dim.86.one, ...), custom_call_target="tpu_custom_call" | custom-call | flops 10737418240 | bytes 8388608 | tf_op jit(solution)/shard_map/attention_back/pallas_call | solution.py:678
  677.2 17.0 %attention_back.4 = (bf16[3,512,128]{2,1,0:T(8,128)(2,1)}, bf16[3,512,128]{2,1,0:T(8,128)(2,1)}, bf16[3,512,128]{2,1,0:T(8,128)(2,1)}, bf16[3,512,128]{2,1,0:T(8,128)(2,1)}) custom-call(s32[16]{0:T(128)} %reshape.471.need, bf16[4,512,128]{2,1,0:T(8,128)(2,1)} %select_convert_fusion.aux, bf16[512,128]{1,0:T(8,128)(2,1)} %broadcast_in_dim.86.one, ...), custom_call_target="tpu_custom_call" | custom-call | flops 10737418240 | bytes 8388608 | tf_op jit(solution)/shard_map/attention_back/pallas_call | solution.py:678
  697.4 9.1 collective-permute-done.101.refs_4_.refs_6_
  706.4 8.1 collective-permute-done.103.refs_6_.refs_8_
  715.4 12.6 qkv_back.2
  728.0 44.2 %ffn_back.3 = (bf16[4,512,1024]{2,1,0:T(8,128)(2,1)}, bf16[8,128,512]{2,1,0:T(8,128)(2,1)}, bf16[8,128,512]{2,1,0:T(8,128)(2,1)}, f32[8,512,128]{2,1,0:T(8,128)}...) custom-call(s32[17]{0:T(128)} %copy-done, ...), custom_call_target="tpu_custom_call" | custom-call | flops 8589934592 | bytes 33554432 | tf_op jit(solution)/shard_map/ffn_back/pallas_call | solution.py:512
  772.2 8.2 projection_back.3
  793.0 17.0 %attention_back.7 = (bf16[3,512,128]{2,1,0:T(8,128)(2,1)}, bf16[3,512,128]{2,1,0:T(8,128)(2,1)}, bf16[3,512,128]{2,1,0:T(8,128)(2,1)}, bf16[3,512,128]{2,1,0:T(8,128)(2,1)}) custom-call(s32[16]{0:T(128)} %reshape.471.need, bf16[4,512,128]{2,1,0:T(8,128)(2,1)} %select_convert_fusion.aux, bf16[512,128]{1,0:T(8,128)(2,1)} %broadcast_in_dim.86.one, ...), custom_call_target="tpu_custom_call" | custom-call | flops 10737418240 | bytes 8388608 | tf_op jit(solution)/shard_map/attention_back/pallas_call | solution.py:678
  812.8 16.9 %attention_back.6 = (bf16[3,512,128]{2,1,0:T(8,128)(2,1)}, bf16[3,512,128]{2,1,0:T(8,128)(2,1)}, bf16[3,512,128]{2,1,0:T(8,128)(2,1)}, bf16[3,512,128]{2,1,0:T(8,128)(2,1)}) custom-call(s32[16]{0:T(128)} %reshape.471.need, bf16[4,512,128]{2,1,0:T(8,128)(2,1)} %select_convert_fusion.aux, bf16[512,128]{1,0:T(8,128)(2,1)} %broadcast_in_dim.86.one, ...), custom_call_target="tpu_custom_call" | custom-call | flops 10737418240 | bytes 8388608 | tf_op jit(solution)/shard_map/attention_back/pallas_call | solution.py:678
  851.5 12.6 qkv_back.3
  908.4 17.9 %down.3 = (f32[8,512,128]{2,1,0:T(8,128)}, bf16[8,512,128]{2,1,0:T(8,128)(2,1)}, f32[8,128]{1,0:T(8,128)}) custom-call(s32[17]{0:T(128)} %copy-done, f32[512,1]{1,0:T(8,128)} %copy.76.valid, f32[8,512,128]{2,1,0:T(8,128)} %get-tuple-element.184.mid, bf16[4,512,1024]{2,1,0:T(8,128)(2,1)} %get-tuple-element.185.normed.refs_2_, ...), custom_call_target="tpu_custom_call" | custom-call | flops 4294967296 | bytes 18874368 | tf_op jit(solution)/shard_map/down/pallas_call | solution.py:388
  960.9 8.2 weight_grad_wide.15
  986.3 8.0 weight_grad_wide.13
  1009.6 25.4 %collective-permute-done.144 = bf16[4,128,1024]{2,1,0:T(8,128)(2,1)S(1)} collective-permute-done((bf16[4,128,1024]{2,1,0:T(8,128)(2,1)S(1)}, bf16[4,128,1024]{2,1,0:T(8,128)(2,1)S(1)}, u32[]{:S(2)}, u32[]{:S(2)}) %collective-permute-start.144) | collective-permute-done | bytes 1048608 | tf_op jit(solution)/shard_map/ppermute | solution.py:903
  1037.9 8.2 weight_grad_wide.11
  1050.2 25.2 %collective-permute-done.141 = bf16[4,128,1024]{2,1,0:T(8,128)(2,1)S(1)} collective-permute-done((bf16[4,128,1024]{2,1,0:T(8,128)(2,1)S(1)}, bf16[4,128,1024]{2,1,0:T(8,128)(2,1)S(1)}, u32[]{:S(2)}, u32[]{:S(2)}) %collective-permute-start.141) | collective-permute-done | bytes 1048608 | tf_op jit(solution)/shard_map/ppermute | solution.py:903
  1078.4 8.1 weight_grad_wide.9
  1091.2 41.2 %collective-permute-start.86 = (bf16[2,512,128]{2,1,0:T(8,128)(2,1)S(1)}, bf16[2,512,128]{2,1,0:T(8,128)(2,1)S(1)}, u32[]{:S(2)}, u32[]{:S(2)}) collective-permute-start(bf16[2,512,128]{2,1,0:T(8,128)(2,1)S(1)} %get-tuple-element.344), channel_id=1, source_target_pairs={{4,0},{8,1},{12,2},{0,3},{5,4},{9,5},{13,6},{1,7},{6,8},{10,9},{14... | collective-permute-start | bytes 786440 | tf_op jit(solution)/shard_map/ppermute | solution.py:975
  1132.3 37.3 %collective-permute-start.87 = (bf16[2,512,128]{2,1,0:T(8,128)(2,1)S(1)}, bf16[2,512,128]{2,1,0:T(8,128)(2,1)S(1)}, u32[]{:S(2)}, u32[]{:S(2)}) collective-permute-start(bf16[2,512,128]{2,1,0:T(8,128)(2,1)S(1)} %get-tuple-element.343), channel_id=1, source_target_pairs={{8,0},{12,1},{0,2},{4,3},{9,4},{13,5},{1,6},{5,7},{10,8},{14,9},{2... | collective-permute-start | bytes 786440 | tf_op jit(solution)/shard_map/ppermute | solution.py:975
  1169.6 27.0 %collective-permute-start.88 = (bf16[2,512,128]{2,1,0:T(8,128)(2,1)S(1)}, bf16[2,512,128]{2,1,0:T(8,128)(2,1)S(1)}, u32[]{:S(2)}, u32[]{:S(2)}) collective-permute-start(bf16[2,512,128]{2,1,0:T(8,128)(2,1)S(1)} %get-tuple-element.342), channel_id=1, source_target_pairs={{12,0},{0,1},{4,2},{8,3},{13,4},{1,5},{5,6},{9,7},{14,8},{2,9},{6,... | collective-permute-start | bytes 786440 | tf_op jit(solution)/shard_map/ppermute | solution.py:975
  1258.5 21.8 %reduce-scatter.23.cloned.1.call-done = bf16[1,128,1024]{2,1,0:T(8,128)(2,1)} async-done(((bf16[4,128,1024]{2,1,0:T(8,128)(2,1)}), bf16[1,128,1024]{2,1,0:T(8,128)(2,1)}) %reduce-scatter.23.cloned.1.call-update) | async-done | bytes 262160 | tf_op jit(solution)/shard_map/reduce_scatter | solution.py:905
  1280.3 28.2 %reduce-scatter.21.cloned.1.call-done = bf16[1,128,1024]{2,1,0:T(8,128)(2,1)} async-done(((bf16[4,128,1024]{2,1,0:T(8,128)(2,1)}), bf16[1,128,1024]{2,1,0:T(8,128)(2,1)}) %reduce-scatter.21.cloned.1.call-update) | async-done | bytes 262160 | tf_op jit(solution)/shard_map/reduce_scatter | solution.py:905
  1311.0 26.1 %reduce-scatter.19.cloned.1.call-done = bf16[1,128,1024]{2,1,0:T(8,128)(2,1)} async-done(((bf16[4,128,1024]{2,1,0:T(8,128)(2,1)}), bf16[1,128,1024]{2,1,0:T(8,128)(2,1)}) %reduce-scatter.19.cloned.1.call-update) | async-done | bytes 262160 | tf_op jit(solution)/shard_map/reduce_scatter | solution.py:905
  1337.1 28.2 %reduce-scatter.17.cloned.1.call-done = bf16[1,128,1024]{2,1,0:T(8,128)(2,1)} async-done(((bf16[4,128,1024]{2,1,0:T(8,128)(2,1)}), bf16[1,128,1024]{2,1,0:T(8,128)(2,1)}) %reduce-scatter.17.cloned.1.call-update) | async-done | bytes 262160 | tf_op jit(solution)/shard_map/reduce_scatter | solution.py:905
  (708 shorter events, 422.2 us)
Async XLA Ops:
  7.2 275.2 %all-gather.7.cloned.1.call-start = ((), (), s32[]{:S(2)}) async-start(), calls=%async_computation.8 | async-start | bytes 1310720 | tf_op jit(solution)/shard_map/all_gather | solution.py:876
  9.3 288.2 %all-gather.9.cloned.1.call-start = ((), (), s32[]{:S(2)}) async-start(), calls=%async_computation.9 | async-start | bytes 1310720 | tf_op jit(solution)/shard_map/all_gather | solution.py:876
  11.2 297.6 %all-gather.11.cloned.1.call-start = ((), (), s32[]{:S(2)}) async-start(), calls=%async_computation.10 | async-start | bytes 1310720 | tf_op jit(solution)/shard_map/all_gather | solution.py:876
  12.0 426.3 %all-gather.13.cloned.1.call-start = ((), (), s32[]{:S(2)}) async-start(), calls=%async_computation.11 | async-start | bytes 1310720 | tf_op jit(solution)/shard_map/all_gather | solution.py:876
  13.3 99.6 %collective-permute-start.1 = (bf16[512,256]{1,0:T(8,128)(2,1)}, bf16[512,256]{1,0:T(8,128)(2,1)S(1)}, u32[]{:S(2)}, u32[]{:S(2)}) collective-permute-start(bf16[512,256]{1,0:T(8,128)(2,1)} %get-tuple-element.347), channel_id=1, source_target_pairs={{0,0},{1,4},{2,8},{3,12},{4,1},{5,5},{6,9},{7,13},{8,2},{9,6},{10,... | collective-permute-start | bytes 786440 | tf_op jit(solution)/shard_map/ppermute | solution.py:958
  15.0 100.1 %collective-permute-start.2 = (bf16[512,256]{1,0:T(8,128)(2,1)}, bf16[512,256]{1,0:T(8,128)(2,1)S(1)}, u32[]{:S(2)}, u32[]{:S(2)}) collective-permute-start(bf16[512,256]{1,0:T(8,128)(2,1)} %get-tuple-element.350), channel_id=1, source_target_pairs={{0,4},{1,8},{2,12},{3,0},{4,5},{5,9},{6,13},{7,1},{8,6},{9,10},{10... | collective-permute-start | bytes 786440 | tf_op jit(solution)/shard_map/ppermute | solution.py:958
  18.5 97.9 %collective-permute-start.3 = (bf16[512,256]{1,0:T(8,128)(2,1)}, bf16[512,256]{1,0:T(8,128)(2,1)S(1)}, u32[]{:S(2)}, u32[]{:S(2)}) collective-permute-start(bf16[512,256]{1,0:T(8,128)(2,1)} %get-tuple-element.349), channel_id=1, source_target_pairs={{0,8},{1,12},{2,0},{3,4},{4,9},{5,13},{6,1},{7,5},{8,10},{9,14},{1... | collective-permute-start | bytes 786440 | tf_op jit(solution)/shard_map/ppermute | solution.py:958
  22.0 97.1 %collective-permute-start.4 = (bf16[512,256]{1,0:T(8,128)(2,1)}, bf16[512,256]{1,0:T(8,128)(2,1)}, u32[]{:S(2)}, u32[]{:S(2)}) collective-permute-start(bf16[512,256]{1,0:T(8,128)(2,1)} %get-tuple-element.348), channel_id=1, source_target_pairs={{0,12},{1,0},{2,4},{3,8},{4,13},{5,1},{6,5},{7,9},{8,14},{9,2},{10... | collective-permute-start | bytes 786440 | tf_op jit(solution)/shard_map/ppermute | solution.py:958
  24.0 88.2 %collective-permute-start = (s32[2049]{0:T(1024)S(1)}, s32[2049]{0:T(1024)S(1)}, u32[]{:S(2)}, u32[]{:S(2)}) collective-permute-start(s32[2049]{0:T(1024)S(1)} %pad_add_fusion), channel_id=1, source_target_pairs={{0,0},{1,4},{2,8},{3,12},{4,1},{5,5},{6,9},{7,13},{8,2},{9,6},{10,... | collective-permute-start | bytes 24596 | tf_op jit(solution)/shard_map/ppermute | solution.py:1034
  24.7 1201.0 %all-reduce.2.cloned.1.call-start = ((), (), s32[]{:S(2)}) async-start(), calls=%async_computation.20 | async-start | bytes 237568 | tf_op jit(solution)/shard_map/psum | solution.py:1107
  112.2 70.7 %collective-permute-start.89 = (bf16[512,256]{1,0:T(8,128)(2,1)S(1)}, bf16[512,256]{1,0:T(8,128)(2,1)S(1)}, u32[]{:S(2)}, u32[]{:S(2)}) collective-permute-start(bf16[512,256]{1,0:T(8,128)(2,1)S(1)} %get-tuple-element.337), channel_id=1, source_target_pairs={{0,0},{1,4},{2,8},{3,12},{4,1},{5,5},{6,9},{7,13},{8,2},{9,6},{10,... | collective-permute-start | bytes 786440 | tf_op jit(solution)/shard_map/ppermute | solution.py:958
  112.9 71.6 %collective-permute-start.90 = (bf16[512,256]{1,0:T(8,128)(2,1)S(1)}, bf16[512,256]{1,0:T(8,128)(2,1)S(1)}, u32[]{:S(2)}, u32[]{:S(2)}) collective-permute-start(bf16[512,256]{1,0:T(8,128)(2,1)S(1)} %get-tuple-element.340), channel_id=1, source_target_pairs={{0,4},{1,8},{2,12},{3,0},{4,5},{5,9},{6,13},{7,1},{8,6},{9,10},{10... | collective-permute-start | bytes 786440 | tf_op jit(solution)/shard_map/ppermute | solution.py:958
  115.1 70.2 %collective-permute-start.91 = (bf16[512,256]{1,0:T(8,128)(2,1)S(1)}, bf16[512,256]{1,0:T(8,128)(2,1)S(1)}, u32[]{:S(2)}, u32[]{:S(2)}) collective-permute-start(bf16[512,256]{1,0:T(8,128)(2,1)S(1)} %get-tuple-element.339), channel_id=1, source_target_pairs={{0,8},{1,12},{2,0},{3,4},{4,9},{5,13},{6,1},{7,5},{8,10},{9,14},{1... | collective-permute-start | bytes 786440 | tf_op jit(solution)/shard_map/ppermute | solution.py:958
  116.4 70.5 %collective-permute-start.92 = (bf16[512,256]{1,0:T(8,128)(2,1)S(1)}, bf16[512,256]{1,0:T(8,128)(2,1)S(1)}, u32[]{:S(2)}, u32[]{:S(2)}) collective-permute-start(bf16[512,256]{1,0:T(8,128)(2,1)S(1)} %get-tuple-element.338), channel_id=1, source_target_pairs={{0,12},{1,0},{2,4},{3,8},{4,13},{5,1},{6,5},{7,9},{8,14},{9,2},{10... | collective-permute-start | bytes 786440 | tf_op jit(solution)/shard_map/ppermute | solution.py:958
  119.1 68.1 %collective-permute-start.24 = (bf16[4,256,128]{2,1,0:T(8,128)(2,1)S(1)}, bf16[4,256,128]{2,1,0:T(8,128)(2,1)S(1)}, u32[]{:S(2)}, u32[]{:S(2)}) collective-permute-start(bf16[4,256,128]{2,1,0:T(8,128)(2,1)S(1)} %all_gather.33.refs_8_), channel_id=1, source_target_pairs={{0,8},{4,20},{8,0},{12,28},{16,24},{20,4},{24,16},{28,12},{1,9},{5... | collective-permute-start | bytes 786440 | tf_op jit(solution)/shard_map/ppermute | solution.py:877
  298.3 41.2 %collective-permute-start.39 = (bf16[4,1024,128]{2,1,0:T(8,128)(2,1)}, bf16[4,1024,128]{2,1,0:T(8,128)(2,1)}, u32[]{:S(2)}, u32[]{:S(2)}) collective-permute-start(bf16[4,1024,128]{2,1,0:T(8,128)(2,1)} %all-gather.9.cloned.1.call-done.refs_0_), channel_id=1, source_target_pairs={{0,16},{4,12},{8,24},{12,4},{16,0},{20,28},{24,8},{28,20},{1,17},{... | collective-permute-start | bytes 3145736 | tf_op jit(solution)/shard_map/ppermute | solution.py:878
  357.5 41.6 %collective-permute-start.13 = (bf16[3,512,128]{2,1,0:T(8,128)(2,1)}, bf16[3,512,128]{2,1,0:T(8,128)(2,1)S(1)}, u32[]{:S(2)}, u32[]{:S(2)}) collective-permute-start(bf16[3,512,128]{2,1,0:T(8,128)(2,1)} %get-tuple-element.150), channel_id=1, source_target_pairs={{0,8},{4,12},{8,0},{12,4},{16,24},{20,28},{24,16},{28,20},{1,9},{5... | collective-permute-start | bytes 1179656 | tf_op jit(solution)/shard_map/ppermute | solution.py:872
  367.1 58.1 %collective-permute-start.33 = (bf16[4,128,1024]{2,1,0:T(8,128)(2,1)}, bf16[4,128,1024]{2,1,0:T(8,128)(2,1)}, u32[]{:S(2)}, u32[]{:S(2)}) collective-permute-start(bf16[4,128,1024]{2,1,0:T(8,128)(2,1)} %collective-permute-done.31.refs_1_.refs_9_), channel_id=1, source_target_pairs={{0,16},{4,12},{8,24},{12,4},{16,0},{20,28},{24,8},{28,20},{1,17},{... | collective-permute-start | bytes 3145736 | tf_op jit(solution)/shard_map/ppermute | solution.py:878
  368.6 57.1 %collective-permute-start.35 = (bf16[4,128,1024]{2,1,0:T(8,128)(2,1)}, bf16[4,128,1024]{2,1,0:T(8,128)(2,1)}, u32[]{:S(2)}, u32[]{:S(2)}) collective-permute-start(bf16[4,128,1024]{2,1,0:T(8,128)(2,1)} %collective-permute-done.31.refs_1_.refs_9_), channel_id=1, source_target_pairs={{0,4},{4,0},{8,12},{12,8},{16,20},{20,16},{24,28},{28,24},{1,5},{5... | collective-permute-start | bytes 3145736 | tf_op jit(solution)/shard_map/ppermute | solution.py:879
  383.1 42.6 %collective-permute-start.40 = (bf16[4,1024,128]{2,1,0:T(8,128)(2,1)}, bf16[4,1024,128]{2,1,0:T(8,128)(2,1)}, u32[]{:S(2)}, u32[]{:S(2)}) collective-permute-start(bf16[4,1024,128]{2,1,0:T(8,128)(2,1)} %collective-permute-done.38.refs_1_), channel_id=1, source_target_pairs={{0,16},{4,12},{8,24},{12,4},{16,0},{20,28},{24,8},{28,20},{1,17},{... | collective-permute-start | bytes 3145736 | tf_op jit(solution)/shard_map/ppermute | solution.py:878
  438.1 53.8 %collective-permute-start.74 = (bf16[4,128,1024]{2,1,0:T(8,128)(2,1)}, bf16[4,128,1024]{2,1,0:T(8,128)(2,1)}, u32[]{:S(2)}, u32[]{:S(2)}) collective-permute-start(bf16[4,128,1024]{2,1,0:T(8,128)(2,1)} %all-gather.11.cloned.1.call-done.refs_0_.refs_8_), channel_id=1, source_target_pairs={{0,4},{4,0},{8,12},{12,8},{16,20},{20,16},{24,28},{28,24},{1,5},{5... | collective-permute-start | bytes 3145736 | tf_op jit(solution)/shard_map/ppermute | solution.py:879
  438.3 54.3 %collective-permute-start.78 = (bf16[4,1024,128]{2,1,0:T(8,128)(2,1)}, bf16[4,1024,128]{2,1,0:T(8,128)(2,1)S(1)}, u32[]{:S(2)}, u32[]{:S(2)}) collective-permute-start(bf16[4,1024,128]{2,1,0:T(8,128)(2,1)} %all-gather.13.cloned.1.call-done.refs_0_), channel_id=1, source_target_pairs={{0,8},{4,20},{8,0},{12,28},{16,24},{20,4},{24,16},{28,12},{1,9},{5... | collective-permute-start | bytes 3145736 | tf_op jit(solution)/shard_map/ppermute | solution.py:877
  439.9 53.1 %collective-permute-start.79 = (bf16[4,1024,128]{2,1,0:T(8,128)(2,1)}, bf16[4,1024,128]{2,1,0:T(8,128)(2,1)}, u32[]{:S(2)}, u32[]{:S(2)}) collective-permute-start(bf16[4,1024,128]{2,1,0:T(8,128)(2,1)} %all-gather.13.cloned.1.call-done.refs_0_), channel_id=1, source_target_pairs={{0,16},{4,12},{8,24},{12,4},{16,0},{20,28},{24,8},{28,20},{1,17},{... | collective-permute-start | bytes 3145736 | tf_op jit(solution)/shard_map/ppermute | solution.py:878
  440.6 53.4 %collective-permute-start.73 = (bf16[4,128,1024]{2,1,0:T(8,128)(2,1)}, bf16[4,128,1024]{2,1,0:T(8,128)(2,1)}, u32[]{:S(2)}, u32[]{:S(2)}) collective-permute-start(bf16[4,128,1024]{2,1,0:T(8,128)(2,1)} %collective-permute-done.71.refs_1_.refs_9_), channel_id=1, source_target_pairs={{0,16},{4,12},{8,24},{12,4},{16,0},{20,28},{24,8},{28,20},{1,17},{... | collective-permute-start | bytes 3145736 | tf_op jit(solution)/shard_map/ppermute | solution.py:878
  441.9 52.0 %collective-permute-start.75 = (bf16[4,128,1024]{2,1,0:T(8,128)(2,1)}, bf16[4,128,1024]{2,1,0:T(8,128)(2,1)}, u32[]{:S(2)}, u32[]{:S(2)}) collective-permute-start(bf16[4,128,1024]{2,1,0:T(8,128)(2,1)} %collective-permute-done.71.refs_1_.refs_9_), channel_id=1, source_target_pairs={{0,4},{4,0},{8,12},{12,8},{16,20},{20,16},{24,28},{28,24},{1,5},{5... | collective-permute-start | bytes 3145736 | tf_op jit(solution)/shard_map/ppermute | solution.py:879
  494.0 62.1 %collective-permute-start.76 = (bf16[4,128,1024]{2,1,0:T(8,128)(2,1)}, bf16[4,128,1024]{2,1,0:T(8,128)(2,1)}, u32[]{:S(2)}, u32[]{:S(2)}) collective-permute-start(bf16[4,128,1024]{2,1,0:T(8,128)(2,1)} %copy-done.103), channel_id=1, source_target_pairs={{0,4},{4,0},{8,12},{12,8},{16,20},{20,16},{24,28},{28,24},{1,5},{5... | collective-permute-start | bytes 3145736 | tf_op jit(solution)/shard_map/ppermute | solution.py:879
  494.0 62.2 %collective-permute-start.80 = (bf16[4,1024,128]{2,1,0:T(8,128)(2,1)S(1)}, bf16[4,1024,128]{2,1,0:T(8,128)(2,1)}, u32[]{:S(2)}, u32[]{:S(2)}) collective-permute-start(bf16[4,1024,128]{2,1,0:T(8,128)(2,1)S(1)} %collective-permute-done.78.refs_1_), channel_id=1, source_target_pairs={{0,16},{4,12},{8,24},{12,4},{16,0},{20,28},{24,8},{28,20},{1,17},{... | collective-permute-start | bytes 3145736 | tf_op jit(solution)/shard_map/ppermute | solution.py:878
  792.3 95.6 %collective-permute-start.124 = (bf16[4,4,3,128,256]{4,3,2,1,0:T(8,128)(2,1)}, bf16[4,4,3,128,256]{4,3,2,1,0:T(8,128)(2,1)}, u32[]{:S(2)}, u32[]{:S(2)}) collective-permute-start(bf16[4,4,3,128,256]{4,3,2,1,0:T(8,128)(2,1)} %weight_grad_qkv.6), channel_id=1, source_target_pairs={{0,4},{4,0},{8,12},{12,8},{16,20},{20,16},{24,28},{28,24},{1,5},{5... | collective-permute-start | bytes 9437192 | tf_op jit(solution)/shard_map/ppermute | solution.py:898
  843.5 117.4 %collective-permute-start.142 = (bf16[4,4,128,1024]{3,2,1,0:T(8,128)(2,1)}, bf16[4,4,128,1024]{3,2,1,0:T(8,128)(2,1)}, u32[]{:S(2)}, u32[]{:S(2)}) collective-permute-start(bf16[4,4,128,1024]{3,2,1,0:T(8,128)(2,1)} %weight_grad_wide.14), channel_id=1, source_target_pairs={{0,4},{4,0},{8,12},{12,8},{16,20},{20,16},{24,28},{28,24},{1,5},{5... | collective-permute-start | bytes 12582920 | tf_op jit(solution)/shard_map/ppermute | solution.py:898
  870.4 67.7 %collective-permute-start.121 = (bf16[4,4,3,128,256]{4,3,2,1,0:T(8,128)(2,1)}, bf16[4,4,3,128,256]{4,3,2,1,0:T(8,128)(2,1)S(1)}, u32[]{:S(2)}, u32[]{:S(2)}) collective-permute-start(bf16[4,4,3,128,256]{4,3,2,1,0:T(8,128)(2,1)} %weight_grad_qkv.4), channel_id=1, source_target_pairs={{0,4},{4,0},{8,12},{12,8},{16,20},{20,16},{24,28},{28,24},{1,5},{5... | collective-permute-start | bytes 9437192 | tf_op jit(solution)/shard_map/ppermute | solution.py:898
  887.8 98.5 %collective-permute-start.139 = (bf16[4,4,128,1024]{3,2,1,0:T(8,128)(2,1)}, bf16[4,4,128,1024]{3,2,1,0:T(8,128)(2,1)}, u32[]{:S(2)}, u32[]{:S(2)}) collective-permute-start(bf16[4,4,128,1024]{3,2,1,0:T(8,128)(2,1)} %weight_grad_wide.12), channel_id=1, source_target_pairs={{0,4},{4,0},{8,12},{12,8},{16,20},{20,16},{24,28},{28,24},{1,5},{5... | collective-permute-start | bytes 12582920 | tf_op jit(solution)/shard_map/ppermute | solution.py:898
  895.8 52.5 %collective-permute-start.125 = (bf16[2,4,3,128,256]{4,3,2,1,0:T(8,128)(2,1)}, bf16[2,4,3,128,256]{4,3,2,1,0:T(8,128)(2,1)}, u32[]{:S(2)}, u32[]{:S(2)}) collective-permute-start(bf16[2,4,3,128,256]{4,3,2,1,0:T(8,128)(2,1)} %get-tuple-element.240), channel_id=1, source_target_pairs={{0,16},{4,12},{8,24},{12,4},{16,0},{20,28},{24,8},{28,20},{1,17},{... | collective-permute-start | bytes 4718600 | tf_op jit(solution)/shard_map/ppermute | solution.py:900
  933.6 321.2 %reduce-scatter.15.cloned.1.call-start = ((), (), s32[]{:S(2)}) async-start(), calls=%async_computation.15 | async-start | bytes 327680 | tf_op jit(solution)/shard_map/reduce_scatter | solution.py:905
  935.6 319.2 %reduce-scatter.13.cloned.1.call-start = ((), (), s32[]{:S(2)}) async-start(), calls=%async_computation.14 | async-start | bytes 327680 | tf_op jit(solution)/shard_map/reduce_scatter | solution.py:905
  959.0 78.9 %collective-permute-start.136 = (bf16[4,4,128,1024]{3,2,1,0:T(8,128)(2,1)}, bf16[4,4,128,1024]{3,2,1,0:T(8,128)(2,1)}, u32[]{:S(2)}, u32[]{:S(2)}) collective-permute-start(bf16[4,4,128,1024]{3,2,1,0:T(8,128)(2,1)} %weight_grad_wide.10), channel_id=1, source_target_pairs={{0,4},{4,0},{8,12},{12,8},{16,20},{20,16},{24,28},{28,24},{1,5},{5... | collective-permute-start | bytes 12582920 | tf_op jit(solution)/shard_map/ppermute | solution.py:898
  960.9 295.7 %reduce-scatter.11.cloned.1.call-start = ((), (), s32[]{:S(2)}) async-start(), calls=%async_computation.13 | async-start | bytes 983040 | tf_op jit(solution)/shard_map/reduce_scatter | solution.py:905
  974.2 282.4 %reduce-scatter.9.cloned.1.call-start = ((), (), s32[]{:S(2)}) async-start(), calls=%async_computation.12 | async-start | bytes 983040 | tf_op jit(solution)/shard_map/reduce_scatter | solution.py:905
  986.3 92.1 %collective-permute-start.133 = (bf16[4,4,128,1024]{3,2,1,0:T(8,128)(2,1)}, bf16[4,4,128,1024]{3,2,1,0:T(8,128)(2,1)}, u32[]{:S(2)}, u32[]{:S(2)}) collective-permute-start(bf16[4,4,128,1024]{3,2,1,0:T(8,128)(2,1)} %weight_grad_wide.8), channel_id=1, source_target_pairs={{0,4},{4,0},{8,12},{12,8},{16,20},{20,16},{24,28},{28,24},{1,5},{5... | collective-permute-start | bytes 12582920 | tf_op jit(solution)/shard_map/ppermute | solution.py:898
  994.4 53.1 %collective-permute-start.140 = (bf16[2,4,128,1024]{3,2,1,0:T(8,128)(2,1)}, bf16[2,4,128,1024]{3,2,1,0:T(8,128)(2,1)}, u32[]{:S(2)}, u32[]{:S(2)}) collective-permute-start(bf16[2,4,128,1024]{3,2,1,0:T(8,128)(2,1)} %get-tuple-element.259), channel_id=1, source_target_pairs={{0,16},{4,12},{8,24},{12,4},{16,0},{20,28},{24,8},{28,20},{1,17},{... | collective-permute-start | bytes 6291464 | tf_op jit(solution)/shard_map/ppermute | solution.py:900
  1001.6 278.8 %reduce-scatter.23.cloned.1.call-start = ((), (), s32[]{:S(2)}) async-start(), calls=%async_computation.19 | async-start | bytes 1310720 | tf_op jit(solution)/shard_map/reduce_scatter | solution.py:905
  1037.9 270.7 %reduce-scatter.21.cloned.1.call-start = ((), (), s32[]{:S(2)}) async-start(), calls=%async_computation.18 | async-start | bytes 1310720 | tf_op jit(solution)/shard_map/reduce_scatter | solution.py:905
  1078.3 258.8 %reduce-scatter.19.cloned.1.call-start = ((), (), s32[]{:S(2)}) async-start(), calls=%async_computation.17 | async-start | bytes 1310720 | tf_op jit(solution)/shard_map/reduce_scatter | solution.py:905
  1086.5 121.3 %collective-permute-start.134 = (bf16[2,4,128,1024]{3,2,1,0:T(8,128)(2,1)}, bf16[2,4,128,1024]{3,2,1,0:T(8,128)(2,1)}, u32[]{:S(2)}, u32[]{:S(2)}) collective-permute-start(bf16[2,4,128,1024]{3,2,1,0:T(8,128)(2,1)} %get-tuple-element.252), channel_id=1, source_target_pairs={{0,16},{4,12},{8,24},{12,4},{16,0},{20,28},{24,8},{28,20},{1,17},{... | collective-permute-start | bytes 6291464 | tf_op jit(solution)/shard_map/ppermute | solution.py:900
  1089.1 80.5 %collective-permute-start.138 = (bf16[4,128,1024]{2,1,0:T(8,128)(2,1)S(1)}, bf16[4,128,1024]{2,1,0:T(8,128)(2,1)}, u32[]{:S(2)}, u32[]{:S(2)}) collective-permute-start(bf16[4,128,1024]{2,1,0:T(8,128)(2,1)S(1)} %fusion.9), channel_id=1, source_target_pairs={{0,8},{4,20},{8,0},{12,28},{16,24},{20,4},{24,16},{28,12},{1,9},{5... | collective-permute-start | bytes 3145736 | tf_op jit(solution)/shard_map/ppermute | solution.py:903
  1090.4 109.7 %collective-permute-start.85 = (bf16[2,512,128]{2,1,0:T(8,128)(2,1)S(1)}, bf16[2,512,128]{2,1,0:T(8,128)(2,1)S(1)}, u32[]{:S(2)}, u32[]{:S(2)}) collective-permute-start(bf16[2,512,128]{2,1,0:T(8,128)(2,1)S(1)} %get-tuple-element.341), channel_id=1, source_target_pairs={{0,0},{4,1},{8,2},{12,3},{1,4},{5,5},{9,6},{13,7},{2,8},{6,9},{10,... | collective-permute-start | bytes 786440 | tf_op jit(solution)/shard_map/ppermute | solution.py:975
  1091.2 108.9 %collective-permute-start.86 = (bf16[2,512,128]{2,1,0:T(8,128)(2,1)S(1)}, bf16[2,512,128]{2,1,0:T(8,128)(2,1)S(1)}, u32[]{:S(2)}, u32[]{:S(2)}) collective-permute-start(bf16[2,512,128]{2,1,0:T(8,128)(2,1)S(1)} %get-tuple-element.344), channel_id=1, source_target_pairs={{4,0},{8,1},{12,2},{0,3},{5,4},{9,5},{13,6},{1,7},{6,8},{10,9},{14... | collective-permute-start | bytes 786440 | tf_op jit(solution)/shard_map/ppermute | solution.py:975
  1132.3 67.7 %collective-permute-start.87 = (bf16[2,512,128]{2,1,0:T(8,128)(2,1)S(1)}, bf16[2,512,128]{2,1,0:T(8,128)(2,1)S(1)}, u32[]{:S(2)}, u32[]{:S(2)}) collective-permute-start(bf16[2,512,128]{2,1,0:T(8,128)(2,1)S(1)} %get-tuple-element.343), channel_id=1, source_target_pairs={{8,0},{12,1},{0,2},{4,3},{9,4},{13,5},{1,6},{5,7},{10,8},{14,9},{2... | collective-permute-start | bytes 786440 | tf_op jit(solution)/shard_map/ppermute | solution.py:975
  1199.8 165.6 %reduce-scatter.17.cloned.1.call-start = ((), (), s32[]{:S(2)}) async-start(), calls=%async_computation.16 | async-start | bytes 1310720 | tf_op jit(solution)/shard_map/reduce_scatter | solution.py:905
  (237 other events, 5353.0 us)
Sparse Core Ops, SparseCore 0:
  9.6 63.1 all-gather.6
  74.3 34.6 all-gather.8
  110.6 54.7 all-gather.10
  166.8 35.4 all-gather.12
  933.8 198.9 all-reduce.1
  1134.9 19.7 reduce-scatter.14
  1157.1 19.4 reduce-scatter.12
  1179.4 25.1 reduce-scatter.10
  1207.0 38.8 reduce-scatter.8
  1248.0 32.2 reduce-scatter.22
  1282.7 25.7 reduce-scatter.20
  1311.3 25.7 reduce-scatter.18
  1339.5 25.7 reduce-scatter.16

commit v2 on v0

v2 whole, which is shorter than its diff:
```python
import functools
import math

import jax
import jax.numpy as jnp
from jax import lax
from jax.experimental import pallas as pl
from jax.experimental.pallas import tpu as pltpu
from jax.sharding import PartitionSpec as P

D = 1024
FF = 4096
LONG = 2048
SHORT = 512
DH = 64
LANES = 128
BLOCKS = D // LANES
GROUPS = 4
WIDE = FF // GROUPS
HEADS = D // GROUPS
NARROW = 4 * HEADS
BROAD = 2 * WIDE
EPS = 1e-05
MASKED = -1000000000.0
ROWS = 64
VMEM_BYTES = 60 * 1024 * 1024
MESH = pl.DeviceIdType.MESH

f32 = jnp.float32
bf16 = jnp.bfloat16


def dot(a, b):
    return jnp.dot(a, b, preferred_element_type=f32)


def dot_nt(a, b):
    return lax.dot_general(a, b, (((1,), (1,)), ((), ())), preferred_element_type=f32)


def flip(a):
    return jnp.transpose(a.astype(f32), (1, 0)).astype(a.dtype)


def row_loop(total, step, body):
    def advance(i, carry):
        body(pl.ds(pl.multiple_of(i * step, step), step))
        return carry

    lax.fori_loop(0, total // step, advance, 0)


def sum_lanes(value):
    return jnp.sum(value, axis=1, keepdims=True)


def fold_lanes(value):
    total = value[:, :LANES]
    for i in range(1, value.shape[1] // LANES):
        total = total + value[:, i * LANES : (i + 1) * LANES]
    return total


def fold_rows(value):
    total = value[:8]
    for i in range(1, value.shape[0] // 8):
        total = total + value[i * 8 : (i + 1) * 8]
    return total


def row_stats(value):
    mean = sum_lanes(value) / D
    centred = value - mean
    rstd = lax.rsqrt(sum_lanes(centred * centred) / D + EPS)
    return centred * rstd, rstd


def norm_back(dy, hat, rstd, gain):
    dx = dy * gain
    first = sum_lanes(dx) / D
    cross = sum_lanes(dx * hat) / D
    return rstd * (dx - first - hat * cross)


class Vectors:
    def __init__(self, n, layer, ref):
        self.n, self.ref = n, ref
        self.few, self.many = BLOCKS // n, 4 * BLOCKS // n
        self.at = layer * (6 * self.few + 2 * self.many)

    def rows(self, z, first, count):
        return [self.ref[z, first + p : first + p + 1, :] for p in range(count)]

    def norm(self, kind, which):
        first = self.at + (3 * kind + which) * self.few
        parts = [v for z in range(self.n) for v in self.rows(z, first, self.few)]
        return jnp.concatenate(parts, axis=1)

    def hidden(self, kind, group):
        first = self.at + 6 * self.few + kind * self.many
        share = self.n // GROUPS
        parts = [v for i in range(share) for v in self.rows(group * share + i, first, self.many)]
        return jnp.concatenate(parts, axis=1)


def params(**kw):
    return pltpu.CompilerParams(vmem_limit_bytes=VMEM_BYTES, **kw)


def cost(flops, size, trans=0):
    return pl.CostEstimate(flops=int(flops), bytes_accessed=int(size), transcendentals=int(trans))


def whole(shape):
    zeros = (0,) * len(shape)
    return pl.BlockSpec(shape, lambda *_: zeros)


def shape(dims, kind):
    return jax.ShapeDtypeStruct(dims, kind)


VM = pl.BlockSpec(memory_space=pltpu.VMEM)
HB = pl.BlockSpec(memory_space=pl.ANY)
DMA = pltpu.SemaphoreType.DMA


def group_place(n):
    dp = lax.axis_index("dp")
    lo = lax.rem(dp, n)
    return dp - lo, lo


def group_send(n, k, source, target, send_sem, recv_sem):
    base, lo = group_place(n)
    return pltpu.make_async_remote_copy(
        src_ref=source,
        dst_ref=target,
        send_sem=send_sem,
        recv_sem=recv_sem,
        device_id={"dp": base + lax.rem(lo + k + n, n)},
        device_id_type=MESH,
    )


def order_of(n):
    return [k for k in (n // 2, *range(1, n // 2), *range(n // 2 + 1, n)) if k]


def head_columns(n, k):
    _, lo = group_place(n)
    unit = lax.rem(lo + k + n, n) * (BLOCKS // n)
    if n == GROUPS:
        return lax.rem(lo + k + n, n), 0
    return unit // 2, pl.multiple_of(lax.rem(unit, 2) * LANES, LANES)


class Place:
    def __init__(self):
        dp = lax.axis_index("dp")
        self.z = lax.axis_index("head")
        self.lo = lax.rem(dp, GROUPS)
        core = lax.rem(dp, 2)
        bit_x = lax.rem(dp // 2, 2)
        bit_y = lax.rem(dp // 4, 2)
        by_x = dp + 2 - 4 * bit_x
        by_y = dp + 4 - 8 * bit_y
        self.dp, self.core, self.bit_x = dp, core, bit_x
        self.by_x, self.by_y = by_x, by_y
        self.first = by_x * (1 - core) + by_y * core
        self.second = by_y * (1 - core) + by_x * core
        self.both = by_x + by_y - dp
        self.mate = dp + 1 - 2 * core

    def partner(self, way):
        return {"mate": self.mate, "first": self.first, "second": self.second}[way]

    def others(self):
        return [{"head": lax.rem(self.z + k, GROUPS)} for k in range(1, GROUPS)]


def unlike(a, b):
    return jnp.where(a == b, 0, 1)


class Hop:
    aliases = {}

    def __init__(self, array, way):
        self.arrays, self.way = [array], way
        self.outs = [jax.ShapeDtypeStruct(array.shape, array.dtype)]
        self.sems = [DMA((2,))]

    def peers(self, at):
        return [{"dp": at.partner(self.way)}], [], 1

    def copy(self, at, ins, outs, sems):
        return pltpu.make_async_remote_copy(
            src_ref=ins[0],
            dst_ref=outs[0],
            send_sem=sems[0].at[0],
            recv_sem=sems[0].at[1],
            device_id={"dp": at.partner(self.way)},
            device_id_type=MESH,
        )

    def start(self, *args):
        self.copy(*args).start()

    def middle(self, *args):
        pass

    def finish(self, *args):
        self.copy(*args).wait()


class Near:
    aliases = {}

    def __init__(self, array):
        self.arrays = [array]
        self.outs = [jax.ShapeDtypeStruct((GROUPS - 1,) + array.shape[1:], array.dtype)]
        self.sems = [DMA((2, GROUPS - 1))]

    def peers(self, at):
        return at.others(), [], GROUPS - 1

    def copies(self, at, ins, outs, sems):
        return [
            pltpu.make_async_remote_copy(
                src_ref=ins[0].at[k],
                dst_ref=outs[0].at[k - 1],
                send_sem=sems[0].at[0, k - 1],
                recv_sem=sems[0].at[1, k - 1],
                device_id={"head": lax.rem(at.z + k, GROUPS)},
                device_id_type=MESH,
            )
            for k in (2, 1, 3)
        ]

    def start(self, *args):
        for copy in self.copies(*args):
            copy.start()

    def middle(self, *args):
        pass

    def finish(self, *args):
        for copy in self.copies(*args):
            copy.wait()


class Turn:
    aliases = {}

    def __init__(self, array, back):
        self.arrays, self.back = [array], back
        if back:
            tokens, wide = array.shape[0], array.shape[1] // GROUPS
            out = (GROUPS, tokens, wide)
        else:
            tokens, wide = array.shape[1:]
            out = (tokens, GROUPS * wide)
        self.wide = wide
        self.outs = [jax.ShapeDtypeStruct(out, array.dtype)]
        self.sems = [DMA((2, GROUPS)), DMA]

    def many(self, at):
        return [(at.dp - at.lo + t, at.lo) for t in range(GROUPS)]

    def one(self, at):
        return [(at.dp - at.lo + at.z, g) for g in range(GROUPS)]

    def peers(self, at):
        from_ = self.many(at) if self.back else self.one(at)
        return [], from_, GROUPS - 1 + unlike(at.z, at.lo)

    def each(self, op, at, ins, outs, sems):
        targets = self.one(at) if self.back else self.many(at)
        for i, (dp, z) in enumerate(targets):
            if self.back:
                source = ins[0].at[:, pl.ds(i * self.wide, self.wide)]
                target, slot = outs[0].at[at.lo], at.lo
            else:
                source = ins[0].at[i]
                column = pl.multiple_of(at.z * self.wide, self.wide)
                target, slot = outs[0].at[:, pl.ds(column, self.wide)], at.z

            def remote(i=i, dp=dp, z=z, source=source, target=target, slot=slot):
                copy = pltpu.make_async_remote_copy(
                    src_ref=source,
                    dst_ref=target,
                    send_sem=sems[0].at[0, i],
                    recv_sem=sems[0].at[1, slot],
                    device_id={"dp": dp, "head": z},
                    device_id_type=MESH,
                )
                copy.start() if op == "start" else copy.wait_send()

            def inside(source=source, target=target):
                copy = pltpu.make_async_copy(source, target, sems[1])
                copy.start() if op == "start" else copy.wait()

            away = (dp != at.dp) | (z != at.z)
            pl.when(away)(remote)
            pl.when(jnp.logical_not(away))(inside)

    def start(self, *args):
        self.each("start", *args)

    def middle(self, *args):
        pass

    def finish(self, at, ins, outs, sems):
        self.each("wait", at, ins, outs, sems)
        sources = self.many(at) if self.back else self.one(at)
        for slot, (dp, z) in enumerate(sources):

            @pl.when((dp != at.dp) | (z != at.z))
            def _(slot=slot):
                if self.back:
                    spot = outs[0].at[slot]
                else:
                    spot = outs[0].at[:, pl.ds(slot * self.wide, self.wide)]
                pltpu.make_async_remote_copy(
                    src_ref=spot,
                    dst_ref=spot,
                    send_sem=sems[0].at[0, 0],
                    recv_sem=sems[0].at[1, slot],
                    device_id={"dp": at.mate},
                    device_id_type=MESH,
                ).wait_recv()


class Host:
    def __init__(self, n, parts):
        self.n, self.parts = n, parts
        self.at = Place() if parts else None

    def barrier(self, group=True):
        n = self.n
        sem = pltpu.get_barrier_semaphore()
        count = 0
        if group:
            base, lo = group_place(n)
            for k in range(1, n):
                pl.semaphore_signal(
                    sem, inc=1, device_id={"dp": base + lax.rem(lo + k, n)}, device_id_type=MESH
                )
            count = n - 1
        for job, *_ in self.parts:
            plain, pairs, more = job.peers(self.at)
            for device in plain:
                pl.semaphore_signal(sem, inc=1, device_id=device, device_id_type=MESH)
            for dp, z in pairs:

                @pl.when((dp != self.at.dp) | (z != self.at.z))
                def _(dp=dp, z=z):
                    pl.semaphore_signal(
                        sem, inc=1, device_id={"dp": dp, "head": z}, device_id_type=MESH
                    )

            count = count + more
        pl.semaphore_wait(sem, count)

    def start(self):
        for job, *refs in self.parts:
            job.start(self.at, *refs)

    def middle(self):
        for job, *refs in self.parts:
            job.middle(self.at, *refs)

    def finish(self):
        for job, *refs in self.parts:
            job.finish(self.at, *refs)


def plain_call(
    body, n, name, ident, inputs, in_specs, out_shape, out_specs, scratch, flops, jobs, grid=()
):
    return list(
        pl.pallas_call(
            lambda *refs: body(Host(n, []), *refs),
            out_shape=out_shape,
            grid=grid,
            in_specs=in_specs,
            out_specs=out_specs,
            scratch_shapes=scratch,
            compiler_params=params(),
            cost_estimate=cost(flops, 10 * 2**20),
            name=name,
        )(*inputs)
    )


def remote_call(
    body, n, name, ident, inputs, in_specs, out_shape, out_specs, scratch, flops, jobs, grid=()
):
    job_in = [v for job in jobs for v in job.arrays]
    job_out = [v for job in jobs for v in job.outs]
    job_sems = [v for job in jobs for v in job.sems]
    aliases = {}
    i, o = len(inputs), len(out_shape)
    for job in jobs:
        aliases.update({i + a: o + b for a, b in job.aliases.items()})
        i, o = i + len(job.arrays), o + len(job.outs)

    def kernel(*refs):
        refs = list(refs)

        def take(count):
            taken = refs[:count]
            del refs[:count]
            return taken

        own_in, extra_in = take(len(inputs)), take(len(job_in))
        own_out, extra_out = take(len(out_shape)), take(len(job_out))
        own_scratch, extra_sems = take(len(scratch)), take(len(job_sems))
        parts = []
        for job in jobs:
            sizes = (len(job.arrays), len(job.outs), len(job.sems))
            lists = (extra_in, extra_out, extra_sems)
            part = [job]
            for values, size in zip(lists, sizes):
                part.append(values[:size])
                del values[:size]
            parts.append(part)
        body(Host(n, parts), *own_in, *own_out, *own_scratch)

    res = pl.pallas_call(
        kernel,
        out_shape=list(out_shape) + job_out,
        grid=grid,
        in_specs=list(in_specs) + [HB] * len(job_in),
        out_specs=list(out_specs) + [HB] * len(job_out),
        scratch_shapes=list(scratch) + job_sems,
        input_output_aliases=aliases,
        compiler_params=params(collective_id=ident, has_side_effects=True),
        cost_estimate=cost(flops, 10 * 2**20),
        name=name,
    )(*inputs, *job_in)
    return list(res)


def qkv_kernel(layer, host, low, packed, weight, *refs):
    n = host.n
    vectors = Vectors(n, layer, packed)
    gain, shift = vectors.norm(0, 0), vectors.norm(1, 0)
    outs, (xs, wide, send, wsem, ssem, rsem, lsem) = refs[:-7], refs[-7:]
    tokens = low.shape[0]
    units = BLOCKS // n
    width = units * LANES
    steps = order_of(n) + [0]

    def fetch(i):
        group, offset = head_columns(n, steps[i])
        return [
            pltpu.make_async_copy(
                weight.at[:, group, :, pl.ds(c * HEADS + offset, width)],
                wide.at[i % 2, c],
                wsem.at[i % 2, c],
            )
            for c in range(3)
        ]

    for copy in fetch(0):
        copy.start()

    def body(r):
        hat, _ = row_stats(low[r, :].astype(f32))
        xs[r, :] = (hat * gain + shift).astype(bf16)

    row_loop(tokens, ROWS, body)
    host.barrier()
    host.start()
    copies = []
    for i, k in enumerate(steps):
        if i + 1 < n:
            for copy in fetch(i + 1):
                copy.start()
        for c, copy in enumerate(fetch(i)):
            copy.wait()
            value = dot(xs[...], wide[i % 2, c].reshape(D, width)).astype(bf16)
            send[k, c] = value[:, :LANES]
            for u in range(1, units):
                outs[u * n + k][c] = value[:, u * LANES : (u + 1) * LANES]
        if k:
            copy = group_send(n, k, send.at[k], outs[k], ssem.at[k], rsem.at[k])
        else:
            copy = pltpu.make_async_copy(send.at[0], outs[0], lsem)
        copy.start()
        copies.append(copy)
    host.middle()
    for copy in copies:
        copy.wait()
    host.finish()


def qkv_call(n, ident, jobs, layer, low, packed, weight):
    tokens = low.shape[0]
    units = BLOCKS // n
    block = (3, tokens, LANES)
    res = remote_call(
        functools.partial(qkv_kernel, layer), n, "qkv", ident,
        [low, packed, weight], [VM, VM, HB],
        [jax.ShapeDtypeStruct(block, bf16)] * (n * units), [HB] * n + [VM] * (n * (units - 1)),
        [
            pltpu.VMEM((tokens, D), bf16),
            pltpu.VMEM((2, 3, BLOCKS, LANES, units * LANES), bf16),
            pltpu.VMEM((n,) + block, bf16),
            DMA((2, 3)),
            DMA((n,)),
            DMA((n,)),
            DMA,
        ],
        60 * tokens * D * D, jobs,
    )
    return [res[u * n : (u + 1) * n] for u in range(units)], res[n * units :]


def head_lanes(value, head):
    lane = lax.broadcasted_iota(jnp.int32, value.shape, 1)
    keep = (lane < DH) if head == 0 else (lane >= DH)
    return jnp.where(keep, value, jnp.zeros_like(value))


def attn_kernel(n, need, aux, one, *refs):
    qkv, (outs, lse, kx, vt, qs, top, acc) = refs[:n], refs[n:]
    tokens = aux.shape[1]
    for r in range(n):
        kx[r] = jnp.concatenate([qkv[r][1], aux[r]], axis=1)
        turned = flip(qkv[r][2])
        ones = jnp.ones((16, tokens), bf16)
        vt[r, 0] = jnp.concatenate([turned[:DH], ones], axis=0)
        vt[r, 1] = jnp.concatenate([turned[DH:], ones], axis=0)
        qs[r] = (qkv[r][0].astype(f32) * (1.0 / math.sqrt(DH))).astype(bf16)

    def each_query(i, carry):
        query = qs[i]
        extended = [jnp.concatenate([head_lanes(query, h), one[...]], axis=1) for h in range(2)]
        top[...] = jnp.full_like(top, -3e38)
        acc[...] = jnp.zeros_like(acc)

        def each_key(j, inner):
            @pl.when(need[i * n + j] == 1)
            def _():
                for h in range(2):
                    scores = dot_nt(kx[j], extended[h])
                    before = top[h : h + 1]
                    now = jnp.maximum(before, jnp.max(scores, axis=0, keepdims=True))
                    raised = jnp.exp(scores - now).astype(bf16)
                    top[h : h + 1] = now
                    acc[h] = acc[h] * jnp.exp(before - now) + dot(vt[j, h], raised)

            return inner

        lax.fori_loop(0, n, each_key, 0)
        sums = [acc[h][DH : DH + 1] for h in range(2)]
        both = jnp.concatenate([acc[h][:DH] / sums[h] for h in range(2)], axis=0)
        outs[i] = jnp.transpose(both, (1, 0)).astype(bf16)
        for h in range(2):
            lse[i, h : h + 1] = top[h : h + 1] + jnp.log(sums[h])
        return carry

    lax.fori_loop(0, n, each_query, 0)


def unit_call(kernel, n, need, aux, one, arrays, out_shape, scratch, work, name):
    total = n * aux.shape[1]
    return pl.pallas_call(
        lambda *refs: kernel(n, *refs),
        out_shape=out_shape,
        grid_spec=pltpu.PrefetchScalarGridSpec(
            num_scalar_prefetch=1,
            grid=(),
            in_specs=[VM] * (2 + len(arrays)),
            out_specs=[VM] * len(out_shape),
            scratch_shapes=scratch,
        ),
        compiler_params=params(),
        cost_estimate=cost(work * total * total * 512, 8 * 2**20),
        name=name,
    )(need, aux, one, *arrays)


def attn_call(n, need, aux, one, parts):
    tokens = aux.shape[1]
    return unit_call(
        attn_kernel, n, need, aux, one, parts,
        [
            jax.ShapeDtypeStruct((n, tokens, LANES), bf16),
            jax.ShapeDtypeStruct((n, 8, tokens), f32),
        ],
        [
            pltpu.VMEM((n, tokens, 2 * LANES), bf16),
            pltpu.VMEM((n, 2, DH + 16, tokens), bf16),
            pltpu.VMEM((n, tokens, LANES), bf16),
            pltpu.VMEM((8, tokens), f32),
            pltpu.VMEM((2, DH + 16, tokens), f32),
        ],
        12, "attention",
    )


def proj_kernel(layer, host, valid, stream, packed, weight, *refs):
    n = host.n
    vectors = Vectors(n, layer, packed)
    gain, shift = vectors.norm(0, 1), vectors.norm(1, 1)
    tokens = stream.shape[0]
    units = BLOCKS // n
    att, (mid, rows, use, xs, rx, ssem, rsem, lsem) = refs[:units], refs[units:]
    host.barrier()
    copies = [
        group_send(n, -k, att[u].at[k], rx.at[k, u], ssem.at[u, k], rsem.at[u, k])
        for k in order_of(n)
        for u in range(units)
    ]
    copies += [pltpu.make_async_copy(att[u].at[0], rx.at[0, u], lsem.at[u]) for u in range(units)]
    for copy in copies:
        copy.start()
    host.start()
    for copy in copies:
        copy.wait()
    _, lo = group_place(n)
    for k in range(n):
        first = lax.rem(lo + k, n) * (units * LANES)
        for u in range(units):
            at = pl.multiple_of(first + u * LANES, LANES)
            rows[:, pl.ds(at, LANES)] = rx[k, u]

    def body(r):
        hat, _ = row_stats(rows[r, :].astype(f32))
        xs[r, :] = (hat * gain + shift).astype(bf16)

    row_loop(tokens, ROWS, body)
    branch = None
    for g in range(GROUPS):
        term = dot_nt(xs[:, g * HEADS : (g + 1) * HEADS], weight[:, g].reshape(D, HEADS))
        branch = term if branch is None else branch + term
    mid[...] = branch
    use[...] = jnp.zeros_like(use)

    def finish(r):
        part = mid[r, :]
        use[...] += fold_rows(valid[r, :] * part * part)
        mid[r, :] = stream[r, :] + part

    row_loop(tokens, ROWS, finish)
    host.middle()
    host.finish()


def proj_call(n, ident, jobs, layer, valid, stream, packed, weight, att):
    tokens = stream.shape[0]
    units = BLOCKS // n
    flat = whole(stream.shape)
    return remote_call(
        functools.partial(proj_kernel, layer), n, "projection", ident,
        [valid, stream, packed, weight, *att],
        [whole(v.shape) for v in (valid, stream, packed)]
        + [pl.BlockSpec((BLOCKS, GROUPS, LANES, HEADS), lambda i: (0, 0, 0, 3))]
        + [whole(v.shape) for v in att],
        [
            jax.ShapeDtypeStruct(stream.shape, f32),
            jax.ShapeDtypeStruct(stream.shape, bf16),
            jax.ShapeDtypeStruct((8, D), f32),
        ],
        [flat, flat, whole((8, D))],
        [
            pltpu.VMEM((tokens, D), bf16),
            pltpu.VMEM((n, units, tokens, LANES), bf16),
            DMA((units, n)),
            DMA((units, n)),
            DMA((units,)),
        ],
        30 * tokens * D * D, jobs, grid=(1,),
    )


def ffn_kernel(
    layer, host, valid, mid, packed, weight,
    slope, hat, normed, low_mid, rstd_out, stream, low, use,
    xs, act, mean, buf, acc,
):
    step = pl.program_id(0)
    tokens = mid.shape[0]
    vectors = Vectors(host.n, layer, packed)

    @pl.when(step == 0)
    def _():
        gain, shift = vectors.norm(0, 2), vectors.norm(1, 2)
        use[...] = jnp.zeros_like(use)

        def body(r):
            raw = mid[r, :].astype(bf16)
            value, _ = row_stats(raw.astype(f32))
            low_mid[r, :] = raw
            xs[r, :] = (value * gain + shift).astype(bf16)

        row_loop(tokens, ROWS, body)
        if host.parts:
            host.barrier(False)
            host.start()

    @pl.when(step < GROUPS)
    def _():
        buf[...] = dot(xs[...], weight[...].reshape(D, WIDE))

        def body(r):
            h = buf[r, :]
            half = 0.5 * (1.0 + lax.erf(h * (1.0 / math.sqrt(2.0))))
            bell = jnp.exp(-0.5 * h * h) * (1.0 / math.sqrt(2.0 * math.pi))
            act[step, r, :] = h * half
            slope[0, r, :] = (half + h * bell).astype(bf16)

        row_loop(tokens, 32, body)

    @pl.when(step == GROUPS)
    def _():
        acc[...] = jnp.zeros_like(acc)

        def body(r):
            blocks = [act[g, r, :] for g in range(GROUPS)]
            total = sum_lanes(sum(fold_lanes(b) for b in blocks)) / FF
            square = sum(fold_lanes((b - total) * (b - total)) for b in blocks)
            rstd = lax.rsqrt(sum_lanes(square) / FF + EPS)
            mean[r, :] = jnp.broadcast_to(total, (32, LANES))
            rstd_out[r, :] = jnp.broadcast_to(rstd, (32, LANES))

        row_loop(tokens, 32, body)

    @pl.when(step >= GROUPS)
    def _():
        g = step - GROUPS
        hgain, hshift = vectors.hidden(0, g), vectors.hidden(1, g)

        def body(r):
            value = (act[g, r, :] - mean[r, 0:1]) * rstd_out[r, 0:1]
            hat[0, r, :] = value.astype(bf16)
            normed[0, r, :] = (value * hgain + hshift).astype(bf16)

        row_loop(tokens, 32, body)
        acc[...] += dot_nt(normed[0], weight[...].reshape(D, WIDE))

    @pl.when(step == 2 * GROUPS - 1)
    def _():
        def body(r):
            feed = acc[r, :]
            out = mid[r, :] + feed
            keep = valid[r, :]
            stream[r, :] = out
            low[r, :] = out.astype(bf16)
            use[0] += fold_rows(keep * feed * feed)
            use[1] += fold_rows(keep * out * out)

        row_loop(tokens, ROWS, body)
        host.middle()
        host.finish()


def first_half(s):
    return jnp.minimum(s, GROUPS - 1)


def second_half(s):
    return jnp.maximum(s - GROUPS, 0)


def half_specs(tokens):
    early = pl.BlockSpec((1, tokens, WIDE), lambda s: (first_half(s), 0, 0))
    late = pl.BlockSpec((1, tokens, WIDE), lambda s: (second_half(s), 0, 0))
    return early, late


def ffn_call(n, ident, jobs, layer, valid, mid, packed, weight):
    tokens = mid.shape[0]
    big = (GROUPS, tokens, WIDE)
    early, late = half_specs(tokens)
    flat = (tokens, D)
    call = remote_call if jobs else plain_call
    return call(
        functools.partial(ffn_kernel, layer), n, "ffn", ident,
        [valid, mid, packed, weight],
        [whole(v.shape) for v in (valid, mid, packed)]
        + [
            pl.BlockSpec(
                (BLOCKS, 1, LANES, WIDE), lambda s: (0, lax.rem(s, GROUPS), 0, s // GROUPS)
            )
        ],
        [jax.ShapeDtypeStruct(big, bf16)] * 3
        + [
            jax.ShapeDtypeStruct(flat, bf16),
            jax.ShapeDtypeStruct((tokens, LANES), f32),
            jax.ShapeDtypeStruct(flat, f32),
            jax.ShapeDtypeStruct(flat, bf16),
            jax.ShapeDtypeStruct((2, 8, D), f32),
        ],
        [early, late, late]
        + [whole(flat), whole((tokens, LANES)), whole(flat), whole(flat), whole((2, 8, D))],
        [
            pltpu.VMEM(flat, bf16),
            pltpu.VMEM(big, f32),
            pltpu.VMEM((tokens, LANES), f32),
            pltpu.VMEM((tokens, WIDE), f32),
            pltpu.VMEM(flat, f32),
        ],
        16 * tokens * D * FF, jobs, grid=(2 * GROUPS,),
    )


def ffn_back_kernel(
    layer, host, grad, hat, slope, rstd_in, low_mid, packed, weight,
    dhid, grad_turned, normed_turned, grad_out, hgrads, grads,
    gs, dxs, buf, first, cross, acc,
):
    step = pl.program_id(0)
    tokens = grad.shape[0]
    vectors = Vectors(host.n, layer, packed)

    @pl.when(step == 0)
    def _():
        first[...] = jnp.zeros_like(first)
        cross[...] = jnp.zeros_like(cross)
        hgrads[...] = jnp.zeros_like(hgrads)
        grads[...] = jnp.zeros_like(grads)
        gs[...] = grad[...].astype(bf16)
        for b in range(BLOCKS):
            grad_turned[b] = flip(gs[:, b * LANES : (b + 1) * LANES])
        if host.parts:
            host.barrier(False)
            host.start()

    @pl.when(step < GROUPS)
    def _():
        buf[...] = dot(gs[...], weight[...].reshape(D, WIDE))
        hgain = vectors.hidden(0, step)

        def body(r):
            value = hat[0, r, :].astype(f32)
            dy = buf[r, :]
            dx = dy * hgain
            hgrads[0, step] += fold_rows(dy * value)
            hgrads[1, step] += fold_rows(dy)
            first[r, :] += fold_lanes(dx)
            cross[r, :] += fold_lanes(dx * value)
            dxs[step, r, :] = dx

        row_loop(tokens, 32, body)

    @pl.when(step == GROUPS)
    def _():
        acc[...] = jnp.zeros_like(acc)

        def body(r):
            first[r, :] = jnp.broadcast_to(sum_lanes(first[r, :]) / FF, (ROWS, LANES))
            cross[r, :] = jnp.broadcast_to(sum_lanes(cross[r, :]) / FF, (ROWS, LANES))

        row_loop(tokens, ROWS, body)

    @pl.when(step >= GROUPS)
    def _():
        g = step - GROUPS

        def body(r):
            inner = dxs[g, r, :] - first[r, 0:1] - hat[0, r, :].astype(f32) * cross[r, 0:1]
            dhid[0, r, :] = (slope[0, r, :].astype(f32) * (rstd_in[r, 0:1] * inner)).astype(bf16)

        row_loop(tokens, 32, body)
        acc[...] += dot_nt(dhid[0], weight[...].reshape(D, WIDE))

    @pl.when(step == 2 * GROUPS - 1)
    def _():
        gain, shift = vectors.norm(0, 2), vectors.norm(1, 2)

        def body(r):
            value, rstd = row_stats(low_mid[r, :].astype(f32))
            dy = acc[r, :]
            grads[0] += fold_rows(dy * value)
            grads[1] += fold_rows(dy)
            grad_out[r, :] = grad[r, :] + norm_back(dy, value, rstd, gain)
            gs[r, :] = (value * gain + shift).astype(bf16)

        row_loop(tokens, ROWS, body)
        for b in range(BLOCKS):
            normed_turned[b] = flip(gs[:, b * LANES : (b + 1) * LANES])
        host.middle()
        host.finish()


def ffn_back_call(n, ident, jobs, layer, grad, hat, slope, rstd, low_mid, packed, weight):
    tokens = grad.shape[0]
    turned = (BLOCKS, LANES, tokens)
    big = (GROUPS, tokens, WIDE)
    _, late = half_specs(tokens)
    flat = (tokens, D)
    call = remote_call if jobs else plain_call
    return call(
        functools.partial(ffn_back_kernel, layer), n, "ffn_back", ident,
        [grad, hat, slope, rstd, low_mid, packed, weight],
        [
            whole(flat),
            pl.BlockSpec((1, tokens, WIDE), lambda s: (lax.rem(s, GROUPS), 0, 0)),
            late,
        ]
        + [whole(v.shape) for v in (rstd, low_mid, packed)]
        + [
            pl.BlockSpec(
                (BLOCKS, 1, LANES, WIDE), lambda s: (0, lax.rem(s, GROUPS), 0, 1 - s // GROUPS)
            )
        ],
        [
            jax.ShapeDtypeStruct(big, bf16),
            jax.ShapeDtypeStruct(turned, bf16),
            jax.ShapeDtypeStruct(turned, bf16),
            jax.ShapeDtypeStruct(flat, f32),
            jax.ShapeDtypeStruct((2, GROUPS, 8, WIDE), f32),
            jax.ShapeDtypeStruct((2, 8, D), f32),
        ],
        [late, whole(turned), whole(turned), whole(flat)]
        + [whole((2, GROUPS, 8, WIDE)), whole((2, 8, D))],
        [
            pltpu.VMEM(flat, bf16),
            pltpu.VMEM(big, f32),
            pltpu.VMEM((tokens, WIDE), f32),
            pltpu.VMEM((tokens, LANES), f32),
            pltpu.VMEM((tokens, LANES), f32),
            pltpu.VMEM(flat, f32),
        ],
        16 * tokens * D * FF, jobs, grid=(2 * GROUPS,),
    )


def proj_back_kernel(
    layer, host, grad, packed, weight, rows, *refs
):
    n = host.n
    vectors = Vectors(n, layer, packed)
    gain, shift = vectors.norm(0, 1), vectors.norm(1, 1)
    tokens = grad.shape[0]
    units = BLOCKS // n
    outs, refs = refs[:units], refs[units:]
    grad_turned, normed, grads, gs, dm, send, ssem, rsem, lsem = refs
    host.barrier()
    host.start()
    gs[...] = grad[...].astype(bf16)
    for g in range(GROUPS):
        dm[:, g * HEADS : (g + 1) * HEADS] = dot(gs[...], weight[:, g].reshape(D, HEADS))
    grads[...] = jnp.zeros_like(grads)

    def body(r):
        value, rstd = row_stats(rows[r, :].astype(f32))
        dy = dm[r, :]
        grads[0] += fold_rows(dy * value)
        grads[1] += fold_rows(dy)
        dv = norm_back(dy, value, rstd, gain).astype(bf16)
        for b in range(BLOCKS):
            send[b, r, :] = dv[:, b * LANES : (b + 1) * LANES]
        normed[r, :] = (value * gain + shift).astype(bf16)

    row_loop(tokens, ROWS, body)
    _, lo = group_place(n)
    copies = []
    for k in order_of(n) + [0]:
        for u in range(units):
            source = send.at[lax.rem(lo + k, n) * units + u]
            if k:
                copy = group_send(n, k, source, outs[u].at[k], ssem.at[u, k], rsem.at[u, k])
            else:
                copy = pltpu.make_async_copy(source, outs[u].at[0], lsem.at[u])
            copy.start()
            copies.append(copy)
    for b in range(BLOCKS):
        grad_turned[b] = flip(gs[:, b * LANES : (b + 1) * LANES])
    host.middle()
    for copy in copies:
        copy.wait()
    host.finish()


def proj_back_call(n, ident, jobs, layer, grad, packed, weight, rows):
    tokens = grad.shape[0]
    units = BLOCKS // n
    turned = (BLOCKS, LANES, tokens)
    flat = (tokens, D)
    return remote_call(
        functools.partial(proj_back_kernel, layer), n, "projection_back", ident,
        [grad, packed, weight, rows],
        [whole(v.shape) for v in (grad, packed)]
        + [pl.BlockSpec((BLOCKS, GROUPS, LANES, HEADS), lambda i: (0, 0, 0, 3)), whole(flat)],
        [
            *[jax.ShapeDtypeStruct((n, tokens, LANES), bf16)] * units,
            jax.ShapeDtypeStruct(turned, bf16),
            jax.ShapeDtypeStruct(flat, bf16),
            jax.ShapeDtypeStruct((2, 8, D), f32),
        ],
        [HB] * units + [whole(turned), whole(flat), whole((2, 8, D))],
        [
            pltpu.VMEM(flat, bf16),
            pltpu.VMEM(flat, f32),
            pltpu.VMEM((BLOCKS, tokens, LANES), bf16),
            DMA((units, n)),
            DMA((units, n)),
            DMA((units,)),
        ],
        30 * tokens * D * D, jobs, grid=(1,),
    )


def attn_back_kernel(n, need, aux, one, *refs):
    qkv, (att, datt, lse) = refs[:n], refs[n : n + 3]
    outs, refs = refs[n + 3 : 2 * n + 3], refs[2 * n + 3 :]
    kx, kt, qs, vs, delta, dq, dkey, dval, dkv = refs
    for r in range(n):
        kx[r] = jnp.concatenate([qkv[r][1], aux[r]], axis=1)
        kt[r] = flip(qkv[r][1])
        vs[r] = qkv[r][2]
        qs[r] = (qkv[r][0].astype(f32) * (1.0 / math.sqrt(DH))).astype(bf16)
        both = jnp.transpose(att[r].astype(f32) * datt[r].astype(f32), (1, 0))
        delta[r, 0:1] = jnp.sum(both[:DH], axis=0, keepdims=True)
        delta[r, 1:2] = jnp.sum(both[DH:], axis=0, keepdims=True)
    dq[...] = jnp.zeros_like(dq)

    def each_key(j, carry):
        dkey[...] = jnp.zeros_like(dkey)
        dval[...] = jnp.zeros_like(dval)

        def each_query(i, inner):
            @pl.when(need[i * n + j] == 1)
            def _():
                for h in range(2):
                    query = head_lanes(qs[i], h)
                    out = head_lanes(datt[i], h)
                    scores = dot_nt(kx[j], jnp.concatenate([query, one[...]], axis=1))
                    probs = jnp.exp(scores - lse[i, h : h + 1])
                    dprobs = dot_nt(vs[j], out)
                    dscores = (probs * (dprobs - delta[i, h : h + 1])).astype(bf16)
                    dval[...] += dot(probs.astype(bf16), out)
                    dkey[...] += dot(dscores, query)
                    rows = slice(h * DH, (h + 1) * DH)
                    dq[i, rows] += dot(kt[j, rows], dscores)

            return inner

        lax.fori_loop(0, n, each_query, 0)
        dkv[j, 0] = dkey[...].astype(bf16)
        dkv[j, 1] = dval[...].astype(bf16)
        return carry

    lax.fori_loop(0, n, each_key, 0)
    for r in range(n):
        outs[r][0] = (jnp.transpose(dq[r], (1, 0)) * (1.0 / math.sqrt(DH))).astype(bf16)
        outs[r][1] = dkv[r, 0]
        outs[r][2] = dkv[r, 1]


def attn_back_call(n, need, aux, one, parts, att, datt, lse):
    tokens = aux.shape[1]
    return unit_call(
        attn_back_kernel, n, need, aux, one, [*parts, att, datt, lse],
        [jax.ShapeDtypeStruct((3, tokens, LANES), bf16)] * n,
        [
            pltpu.VMEM((n, tokens, 2 * LANES), bf16),
            pltpu.VMEM((n, LANES, tokens), bf16),
            pltpu.VMEM((n, tokens, LANES), bf16),
            pltpu.VMEM((n, tokens, LANES), bf16),
            pltpu.VMEM((n, 8, tokens), f32),
            pltpu.VMEM((n, LANES, tokens), f32),
            pltpu.VMEM((tokens, LANES), f32),
            pltpu.VMEM((tokens, LANES), f32),
            pltpu.VMEM((n, 2, tokens, LANES), bf16),
        ],
        14, "attention_back",
    )


def qkv_back_kernel(
    layer, host, grad, low, packed, wq, wk, wv, *refs
):
    n = host.n
    vectors = Vectors(n, layer, packed)
    gain, shift = vectors.norm(0, 0), vectors.norm(1, 0)
    tokens = grad.shape[0]
    units = BLOCKS // n
    early_count = n * (units - 1)
    ready, refs = refs[:early_count], refs[early_count:]
    dparts, refs = refs[:n], refs[n:]
    dlast, refs = refs[:n], refs[n:]
    grad_out, normed_turned, grads, grad_low, acc, ns, ssem, rsem, lsem = refs
    blocks = [ready[u * n : (u + 1) * n] for u in range(units - 1)] + [dlast]
    host.barrier()
    steps = [0] + order_of(n)[::-1]
    copies = {}
    for k in order_of(n):
        copies[k] = group_send(n, -k, dparts[k], dlast[k], ssem.at[k], rsem.at[k])
        copies[k].start()
    copies[0] = pltpu.make_async_copy(dparts[0], dlast[0], lsem)
    copies[0].start()
    host.start()
    grads[...] = jnp.zeros_like(grads)

    def early(r):
        value, _ = row_stats(low[r, :].astype(f32))
        ns[r, :] = (value * gain + shift).astype(bf16)

    row_loop(tokens, ROWS, early)
    for b in range(BLOCKS):
        normed_turned[b] = flip(ns[:, b * LANES : (b + 1) * LANES])
    for i, k in enumerate(steps):
        copies[k].wait()
        group, offset = head_columns(n, k)
        total = None
        for c, weight in enumerate((wq, wk, wv)):
            left = jnp.concatenate([blocks[u][k][c] for u in range(units)], axis=1)
            right = weight[:, group, :, pl.ds(offset, units * LANES)].reshape(D, units * LANES)
            term = dot_nt(left, right)
            total = term if total is None else total + term
        if i == 0:
            acc[...] = total
        else:
            acc[...] += total

    def body(r):
        value, rstd = row_stats(low[r, :].astype(f32))
        dy = acc[r, :]
        grads[0] += fold_rows(dy * value)
        grads[1] += fold_rows(dy)
        total = grad[r, :] + norm_back(dy, value, rstd, gain)
        grad_out[r, :] = total
        grad_low[r, :] = total.astype(bf16)

    row_loop(tokens, ROWS, body)
    host.middle()
    host.finish()


def qkv_back_call(n, ident, jobs, layer, grad, low, packed, weight, ready, dparts):
    tokens = grad.shape[0]
    turned = (BLOCKS, LANES, tokens)
    flat = (tokens, D)
    columns = lambda c: pl.BlockSpec((BLOCKS, GROUPS, LANES, HEADS), lambda i: (0, 0, 0, c))
    block = (3, tokens, LANES)
    res = remote_call(
        functools.partial(qkv_back_kernel, layer), n, "qkv_back", ident,
        [grad, low, packed, weight, weight, weight, *ready, *dparts],
        [whole(v.shape) for v in (grad, low, packed)]
        + [columns(0), columns(1), columns(2)]
        + [whole(block)] * (len(ready) + n),
        [jax.ShapeDtypeStruct(block, bf16)] * n
        + [
            jax.ShapeDtypeStruct(flat, f32),
            jax.ShapeDtypeStruct(turned, bf16),
            jax.ShapeDtypeStruct((2, 8, D), f32),
            jax.ShapeDtypeStruct(flat, bf16),
        ],
        [whole(block)] * n + [whole(flat), whole(turned), whole((2, 8, D)), whole(flat)],
        [
            pltpu.VMEM(flat, f32),
            pltpu.VMEM(flat, bf16),
            DMA((n,)),
            DMA((n,)),
            DMA,
        ],
        50 * tokens * D * D, jobs, grid=(1,),
    )
    return [res[:n], *res[n:]]


def pick_rows(sc, turned, count):
    return jnp.concatenate([turned[sc[m]] for m in range(count)], axis=0)


def put_rows(value, extra, outs, spot):
    rows = value.shape[0] // LANES
    for m in range(rows):
        part = value[m * LANES : (m + 1) * LANES]
        if extra is not None:
            part = part + extra[(m,) + spot].astype(f32)
            outs[m // 2][(m % 2,) + spot] = part.astype(bf16)
        else:
            outs[0][(m,) + spot] = part.astype(bf16)


def ffn_grad_kernel(count, added, sc, up_turned, down_turned, dhid, normed, *refs):
    extra, outs = (refs[0], refs[1:]) if added else (None, refs)

    @pl.when(pl.program_id(0) == 0)
    def _():
        put_rows(dot(pick_rows(sc, up_turned, count), dhid[0]), extra, outs, (0,))

    @pl.when(pl.program_id(0) == 1)
    def _():
        put_rows(dot(pick_rows(sc, down_turned, count), normed[0]), extra, outs, (0,))


def ffn_grad_call(count, sc, up_turned, down_turned, dhid, normed, extra=None):
    tokens = up_turned.shape[2]
    added = extra is not None
    at = lambda g, sc: lax.rem(g + sc[count], GROUPS)
    left = pl.BlockSpec(
        (1, tokens, WIDE), lambda j, g, sc: (at(jnp.where(j == 0, g, GROUPS - 1), sc), 0, 0)
    )
    right = pl.BlockSpec((1, tokens, WIDE), lambda j, g, sc: (at(jnp.where(j == 1, g, 0), sc), 0, 0))
    piece = lambda m: pl.BlockSpec((m, 1, LANES, WIDE), lambda j, g, sc: (0, g, 0, j))
    outs = [2, 2] if added else [count]
    return pl.pallas_call(
        lambda *refs: ffn_grad_kernel(count, added, *refs),
        out_shape=[jax.ShapeDtypeStruct((m, GROUPS, LANES, 2 * WIDE), bf16) for m in outs],
        grid_spec=pltpu.PrefetchScalarGridSpec(
            num_scalar_prefetch=1,
            grid=(2, GROUPS),
            in_specs=[whole(up_turned.shape), whole(down_turned.shape), left, right]
            + ([piece(count)] if added else []),
            out_specs=[piece(m) for m in outs],
        ),
        compiler_params=params(),
        cost_estimate=cost(16 * tokens * count * LANES * FF, 24 * 2**20),
        name="ffn_grad",
    )(sc, up_turned, down_turned, dhid, normed, *([extra] if added else []))


def head_grad_kernel(n, count, added, sc, in_turned, out_turned, normed, *refs):
    units = BLOCKS // n
    dqkv, refs = refs[: n * units], refs[n * units :]
    extra, outs = (refs[0], refs[1:]) if added else (None, refs)
    left = pick_rows(sc, in_turned, count)
    for k in range(n):
        for c in range(3):
            right = jnp.concatenate([dqkv[u * n + k][c] for u in range(units)], axis=1)
            value = dot(left, right)
            if n == GROUPS:
                slot = lax.rem(lax.rem(sc[count + 1] + k, n) + GROUPS - sc[count], GROUPS)
                put_rows(value, extra, outs, (slot, slice(None), slice(c * HEADS, (c + 1) * HEADS)))
            else:
                unit = lax.rem(sc[count + 1] + k, n) * units
                at = pl.multiple_of(c * HEADS + lax.rem(unit, 2) * LANES, LANES)
                put_rows(value, extra, outs, (unit // 2, slice(None), pl.ds(at, LANES)))
    left = pick_rows(sc, out_turned, count)
    for g in range(GROUPS):
        slot = lax.rem(g + GROUPS - sc[count], GROUPS)
        value = dot(left, normed[:, g * HEADS : (g + 1) * HEADS])
        put_rows(value, extra, outs, (slot, slice(None), slice(3 * HEADS, 4 * HEADS)))


def head_grad_call(n, count, sc, in_turned, out_turned, dqkv, normed, extra=None):
    tokens = in_turned.shape[2]
    added = extra is not None
    outs = [2, 2] if added else [count]
    inner = (GROUPS, LANES, 4 * HEADS)
    return pl.pallas_call(
        lambda *refs: head_grad_kernel(n, count, added, *refs),
        out_shape=[jax.ShapeDtypeStruct((m,) + inner, bf16) for m in outs],
        grid_spec=pltpu.PrefetchScalarGridSpec(
            num_scalar_prefetch=1,
            grid=(1,),
            in_specs=[whole(v.shape) for v in (in_turned, out_turned, normed, *dqkv)]
            + ([whole((count,) + inner)] if added else []),
            out_specs=[whole((m,) + inner) for m in outs],
        ),
        compiler_params=params(),
        cost_estimate=cost(16 * tokens * count * LANES * 4 * D, 16 * 2**20),
        name="head_grad",
    )(sc, in_turned, out_turned, normed, *dqkv, *([extra] if added else []))


def pack_kernel(qkv, out, up, down, *refs):
    layers = qkv.shape[0]
    for l in range(layers):
        narrow, broad = refs[2 * l : 2 * l + 2]
        for c in range(3):
            narrow[:, c * HEADS : (c + 1) * HEADS] = qkv[l, c]
        narrow[:, 3 * HEADS :] = flip(out[l])
        broad[:, :WIDE] = up[l]
        broad[:, WIDE:] = flip(down[l])


def pack_call(qkv, out, up, down):
    layers = qkv.shape[0]
    flat = pl.pallas_call(
        pack_kernel,
        out_shape=[
            jax.ShapeDtypeStruct((LANES, NARROW), bf16),
            jax.ShapeDtypeStruct((LANES, BROAD), bf16),
        ]
        * layers,
        in_specs=[VM] * 4,
        out_specs=[VM] * (2 * layers),
        compiler_params=params(),
        cost_estimate=cost(0, 4 * 2**20),
        name="pack",
    )(qkv, out, up, down)
    return flat[::2], flat[1::2]


def greet(sem, place, z, others, count):
    n = GROUPS
    for k in range(1, n):
        pl.semaphore_signal(
            sem, inc=1, device_id={"head": lax.rem(z + k, n)}, device_id_type=MESH
        )
    for other in (place.by_x, place.by_y, place.mate):
        pl.semaphore_signal(sem, inc=1, device_id={"dp": other}, device_id_type=MESH)
    for to_dp, to_z in others:

        @pl.when((to_dp != place.dp) | (to_z != z))
        def _(to_dp=to_dp, to_z=to_z):
            pl.semaphore_signal(
                sem, inc=1, device_id={"dp": to_dp, "head": to_z}, device_id_type=MESH
            )

    pl.semaphore_wait(sem, n + 2 + count)


class Weights:
    def __init__(self, at, chunks, shards, gathered, hsem, ssem, rsem, lsem):
        self.at, self.chunks, self.pairs = at, chunks, list(zip(shards, gathered))
        self.hsem, self.ssem, self.rsem = hsem, ssem, rsem
        self.owns = [
            pltpu.make_async_copy(shard, out.at[at.dp, at.z], lsem.at[i])
            for i, (shard, out) in enumerate(self.pairs)
        ]

    def near(self, c):
        kind, columns = self.chunks[c][0], pl.ds(*self.chunks[c][1:])
        shard, out = self.pairs[kind]
        at = self.at
        return [
            pltpu.make_async_remote_copy(
                src_ref=shard.at[:, columns],
                dst_ref=out.at[at.dp, at.z, :, columns],
                send_sem=self.hsem.at[0, k - 1, c],
                recv_sem=self.hsem.at[1, k - 1, c],
                device_id={"head": lax.rem(at.z + k, GROUPS)},
                device_id_type=MESH,
            )
            for k in (2, 1, 3)
        ]

    def far(self, slot, row, target, c):
        kind, columns = self.chunks[c][0], pl.ds(*self.chunks[c][1:])
        out = self.pairs[kind][1]
        return pltpu.make_async_remote_copy(
            src_ref=out.at[row, :, :, columns],
            dst_ref=out.at[row, :, :, columns],
            send_sem=self.ssem.at[slot, c],
            recv_sem=self.rsem.at[slot, c],
            device_id={"dp": target},
            device_id_type=MESH,
        )

    def hops(self, stage, c):
        at = self.at
        if stage == 0:
            return self.near(c)
        if stage == 1:
            return [self.far(0, at.dp, at.first, c)]
        if stage == 2:
            return [self.far(1, at.dp, at.second, c), self.far(2, at.first, at.second, c)]
        rows = (at.dp, at.first, at.second, at.both)
        return [self.far(3 + i, row, at.mate, c) for i, row in enumerate(rows)]

    def run(self, aside):
        parts = len(self.chunks)
        for c in range(min(2, parts)):
            for copy in self.near(c):
                copy.start()
        for t in range(parts + 3):
            for stage in (1, 2, 3):
                c = t + 1 - stage
                if 0 <= c < parts:
                    if stage == 1 and c == 0:
                        for copy in self.owns:
                            copy.wait()
                    for copy in self.hops(stage - 1, c):
                        copy.wait()
                    for copy in self.hops(stage, c):
                        copy.start()
            if t + 2 < parts:
                for copy in self.near(t + 2):
                    copy.start()
            aside(t)
            c = t - 3
            if 0 <= c < parts:
                for copy in self.hops(3, c):
                    copy.wait()


def weight_chunks(shards):
    step = 512
    return [(i, c, step) for i, v in enumerate(shards) for c in range(0, v.shape[1], step)]


def weight_sems(shards):
    parts = len(weight_chunks(shards))
    return [DMA((2, 3, parts)), DMA((7, parts)), DMA((7, parts)), DMA((len(shards),))]


def gather_call(shards):
    count = len(shards)

    def kernel(*refs):
        at = Place()
        weights = Weights(at, weight_chunks(shards), refs[:count], refs[count : 2 * count], *refs[2 * count :])
        for copy in weights.owns:
            copy.start()
        greet(pltpu.get_barrier_semaphore(), at, at.z, [], 0)
        weights.run(lambda t: None)

    return pl.pallas_call(
        kernel,
        out_shape=[jax.ShapeDtypeStruct((BLOCKS, GROUPS) + v.shape, bf16) for v in shards],
        in_specs=[HB] * count,
        out_specs=[HB] * count,
        scratch_shapes=weight_sems(shards),
        compiler_params=params(collective_id=7, has_side_effects=True),
        cost_estimate=cost(0, 150 * 2**20),
        name="gather",
    )(*shards)


def start_kernel(
    chunks, shards, rows, vector, flags, gathered, low, side, vectors, flags_out,
    hsem, ssem, rsem, wsem, xsem, tsem, vsem, fsem, lsem,
):
    at = Place()
    weights = Weights(at, chunks, shards, gathered, hsem, ssem, rsem, wsem)
    dp, core, bit_x, by_x = at.dp, at.core, at.bit_x, at.by_x
    z = at.z
    n = GROUPS
    lo = lax.rem(dp, n)
    wide = rows.shape[2]
    sem = pltpu.get_barrier_semaphore()

    def targets():
        return [(xs, c2, dp - core + c2, 2 * xs + core) for xs in range(2) for c2 in range(2)]

    def sources():
        return [(dp - core + lax.rem(z, 2), g) for g in range(n)]

    turn_dp, turn_z = dp - lo + z, lo
    for copy in weights.owns:
        copy.start()
    own_vector = pltpu.make_async_copy(vector, vectors.at[z], lsem.at[2])
    own_vector.start()
    turned = [(turn_dp, turn_z)]
    greet(sem, at, z, sources() + turned, n - 1 + unlike(lax.rem(z, 2), core) + unlike(z, lo))
    small = [
        pltpu.make_async_remote_copy(
            src_ref=vector,
            dst_ref=vectors.at[z],
            send_sem=vsem.at[0, k - 1],
            recv_sem=vsem.at[1, k - 1],
            device_id={"head": lax.rem(z + k, n)},
            device_id_type=MESH,
        )
        for k in range(1, n)
    ]

    def flag_copy(op):
        def remote():
            copy = pltpu.make_async_remote_copy(
                src_ref=flags,
                dst_ref=flags_out,
                send_sem=fsem.at[0],
                recv_sem=fsem.at[1],
                device_id={"dp": turn_dp, "head": turn_z},
                device_id_type=MESH,
            )
            copy.start() if op == "start" else copy.wait()

        def inside():
            copy = pltpu.make_async_copy(flags, flags_out, lsem.at[3])
            copy.start() if op == "start" else copy.wait()

        pl.when((turn_dp != dp) | (turn_z != z))(remote)
        pl.when((turn_dp == dp) & (turn_z == z))(inside)

    flag_copy("start")
    for copy in small:
        copy.start()

    cross = pltpu.make_async_remote_copy(
        src_ref=rows.at[pl.ds(2 - 2 * bit_x, 2)],
        dst_ref=side,
        send_sem=xsem.at[0],
        recv_sem=xsem.at[1],
        device_id={"dp": by_x},
        device_id_type=MESH,
    )
    place = low.at[:, pl.ds(pl.multiple_of(z * wide, wide), wide)]

    def spread(op):
        for i, (xs, c2, to_dp, to_z) in enumerate(targets()):

            def here(source, i=i, to_dp=to_dp, to_z=to_z):
                def remote():
                    copy = pltpu.make_async_remote_copy(
                        src_ref=source,
                        dst_ref=place,
                        send_sem=tsem.at[0, i],
                        recv_sem=tsem.at[1, z],
                        device_id={"dp": to_dp, "head": to_z},
                        device_id_type=MESH,
                    )
                    if op == "start":
                        copy.start()
                    else:
                        copy.wait_send()

                pl.when((to_dp != dp) | (to_z != z))(remote)

                def inside():
                    copy = pltpu.make_async_copy(source, place, lsem.at[1])
                    if op == "start":
                        copy.start()
                    else:
                        copy.wait()

                pl.when((to_dp == dp) & (to_z == z))(inside)

            pl.when(bit_x == xs)(lambda xs=xs, c2=c2, here=here: here(rows.at[2 * xs + c2]))
            pl.when(bit_x != xs)(lambda c2=c2, here=here: here(side.at[c2]))

    cross.start()

    def aside(t):
        if t == 1:
            cross.wait()
            spread("start")

    weights.run(aside)
    own_vector.wait()
    flag_copy("wait")
    for copy in small:
        copy.wait()
    spread("wait")
    for from_dp, g in sources():

        @pl.when((from_dp != dp) | (g != z))
        def _(g=g):
            spot = low.at[:, pl.ds(g * wide, wide)]
            pltpu.make_async_remote_copy(
                src_ref=spot,
                dst_ref=spot,
                send_sem=tsem.at[0, 0],
                recv_sem=tsem.at[1, g],
                device_id={"dp": by_x},
                device_id_type=MESH,
            ).wait_recv()


def start_call(shards, rows, vector, flags):
    count = len(shards)
    chunks = weight_chunks(shards)
    tokens, wide = rows.shape[1:]

    def kernel(*refs):
        taken, refs = refs[:count], refs[count:]
        start_kernel(chunks, taken, *refs[:3], refs[3 : 3 + count], *refs[3 + count :])

    res = pl.pallas_call(
        kernel,
        out_shape=[jax.ShapeDtypeStruct((BLOCKS, GROUPS) + v.shape, bf16) for v in shards]
        + [
            jax.ShapeDtypeStruct((tokens, GROUPS * wide), bf16),
            jax.ShapeDtypeStruct((2, tokens, wide), bf16),
            jax.ShapeDtypeStruct((GROUPS,) + vector.shape, f32),
            jax.ShapeDtypeStruct(flags.shape, jnp.int32),
        ],
        in_specs=[HB] * (count + 3),
        out_specs=[HB] * (count + 4),
        scratch_shapes=[
            *weight_sems(shards),
            DMA((2,)),
            DMA((2, GROUPS)),
            DMA((2, 3)),
            DMA((2,)),
            DMA((4,)),
        ],
        compiler_params=params(collective_id=5, has_side_effects=True),
        cost_estimate=cost(0, 300 * 2**20),
        name="start",
    )(*shards, rows, vector, flags)
    return [res[:count], *res[count:]]


def vector_rows(layers):
    return -(-(28 * layers + 3 * layers + 1) // 8) * 8


def end_kernel(
    layers, rows, grads, fmine, fsent, valid, tops, vecs, uses,
    rows_out, qkv_out, out_out, up_out, down_out, vectors_out,
    mine, got, pair, last, near, pieces, fm, flast, fnear, vec, vgot, vsum,
    gsem, hsem, psem, qsem, nsem, zsem, tsem, xsem, vsem, lsem, fsem, esem,
):
    at = Place()
    dp, core, bit_x = at.dp, at.core, at.bit_x
    z = at.z
    n = GROUPS
    parts = 4
    width = grads.shape[3] // parts
    step = fmine.shape[2] // parts
    wide = rows.shape[1] // n
    sem = pltpu.get_barrier_semaphore()

    def columns(c):
        return pl.ds(c * width, width)

    def broad(c):
        return pl.ds(c * step, step)

    def loads(c):
        return [
            pltpu.make_async_copy(
                grads.at[pl.ds(0, 4), :, :, columns(c)], mine.at[:, :, :, columns(c)], gsem.at[0, c]
            ),
            pltpu.make_async_copy(
                fmine.at[:, :, broad(c)], fm.at[:, :, broad(c)], gsem.at[1, c]
            ),
        ]

    for c in range(parts):
        for copy in loads(c):
            copy.start()

    vec[...] = jnp.zeros_like(vec)
    for l in range(layers):
        base = 28 * l
        norms, hidden = vecs[4 * l : 4 * l + 3], vecs[4 * l + 3]
        for kind in range(2):
            for i in range(3):
                total = jnp.sum(norms[i][kind], axis=0, keepdims=True)
                for b in range(BLOCKS):
                    row = base + (3 * kind + i) * 2 + b % 2
                    vec[b // 2, row : row + 1, :] = total[:, b * LANES : (b + 1) * LANES]
            for g in range(n):
                total = jnp.sum(hidden[kind, g], axis=0, keepdims=True)
                for b in range(BLOCKS):
                    row = base + 12 + 8 * kind + b
                    vec[g, row : row + 1, :] = total[:, b * LANES : (b + 1) * LANES]
        branch, rest = uses[2 * l : 2 * l + 2]
        for i, value in enumerate((branch[...], rest[0], rest[1])):
            row = 28 * layers + 3 * l + i
            total = fold_lanes(jnp.sum(value, axis=0, keepdims=True))
            for g in range(n):
                vec[g, row : row + 1, :] = total
    row = 31 * layers
    count = jnp.sum(valid[...], axis=0, keepdims=True) * (D / LANES)
    for g in range(n):
        vec[g, row : row + 1, :] = jnp.broadcast_to(count, (1, LANES))

    to_dp = dp - core + lax.rem(z, 2)
    sources = [(dp - core + c2, 2 * xs + core) for xs in range(2) for c2 in range(2)]
    greet(sem, at, z, sources, n - 1 + unlike(lax.rem(z, 2), core))

    def hop(stage, c):
        if stage == 0:
            return pltpu.make_async_remote_copy(
                src_ref=grads.at[pl.ds(4, 4), :, :, columns(c)],
                dst_ref=got.at[:, :, :, columns(c)],
                send_sem=hsem.at[0, c],
                recv_sem=hsem.at[1, c],
                device_id={"dp": at.mate},
                device_id_type=MESH,
            )
        if stage == 1:
            return pltpu.make_async_remote_copy(
                src_ref=mine.at[pl.ds(2, 2), :, :, columns(c)],
                dst_ref=pair.at[:, :, :, columns(c)],
                send_sem=psem.at[0, c],
                recv_sem=psem.at[1, c],
                device_id={"dp": at.second},
                device_id_type=MESH,
            )
        return pltpu.make_async_remote_copy(
            src_ref=mine.at[1, :, :, columns(c)],
            dst_ref=last.at[:, :, columns(c)],
            send_sem=qsem.at[0, c],
            recv_sem=qsem.at[1, c],
            device_id={"dp": at.first},
            device_id_type=MESH,
        )

    def ffn_hop(c):
        return pltpu.make_async_remote_copy(
            src_ref=fsent.at[:, :, broad(c)],
            dst_ref=flast.at[:, :, broad(c)],
            send_sem=fsem.at[0, c],
            recv_sem=fsem.at[1, c],
            device_id={"dp": at.first},
            device_id_type=MESH,
        )

    def around(source, target, cols, sems, c):
        return [
            pltpu.make_async_remote_copy(
                src_ref=source(k, cols),
                dst_ref=target.at[k - 1, :, cols],
                send_sem=sems.at[0, k - 1, c],
                recv_sem=sems.at[1, k - 1, c],
                device_id={"head": lax.rem(z + k, n)},
                device_id_type=MESH,
            )
            for k in (2, 1, 3)
        ]

    def head_around(c):
        return around(lambda k, cols: mine.at[0, k, :, cols], near, columns(c), nsem, c)

    def ffn_around(c):
        return around(lambda k, cols: fm.at[k, :, cols], fnear, broad(c), esem, c)

    def add(count, other, c):
        def body(i, carry):
            m, g = i // GROUPS, lax.rem(i, GROUPS)
            value = mine[m, g, :, columns(c)].astype(f32) + other(m, g).astype(f32)
            mine[m, g, :, columns(c)] = value.astype(bf16)
            return carry

        lax.fori_loop(0, count * GROUPS, body, 0)

    def row_copies(op):
        for j in range(n):
            source = rows.at[:, pl.ds(j * wide, wide)]
            target = pieces.at[z // 2, core]

            def remote(j=j, source=source, target=target):
                copy = pltpu.make_async_remote_copy(
                    src_ref=source,
                    dst_ref=target,
                    send_sem=tsem.at[0, j],
                    recv_sem=tsem.at[1, 2 * (z // 2) + core],
                    device_id={"dp": to_dp, "head": j},
                    device_id_type=MESH,
                )
                copy.start() if op == "start" else copy.wait_send()

            def inside(source=source, target=target):
                copy = pltpu.make_async_copy(source, target, lsem.at[0])
                copy.start() if op == "start" else copy.wait()

            pl.when((to_dp != dp) | (j != z))(remote)
            pl.when((to_dp == dp) & (j == z))(inside)

    def row_arrivals():
        for xs in range(2):
            for c2 in range(2):

                @pl.when((dp - core + c2 != dp) | (2 * xs + core != z))
                def _(xs=xs, c2=c2):
                    spot = pieces.at[xs, c2]
                    pltpu.make_async_remote_copy(
                        src_ref=spot,
                        dst_ref=spot,
                        send_sem=tsem.at[0, 0],
                        recv_sem=tsem.at[1, 2 * xs + c2],
                        device_id={"dp": at.by_x},
                        device_id_type=MESH,
                    ).wait_recv()

    cross = pltpu.make_async_remote_copy(
        src_ref=pieces.at[1 - bit_x],
        dst_ref=rows_out.at[pl.ds(2 * bit_x, 2)],
        send_sem=xsem.at[0],
        recv_sem=xsem.at[1],
        device_id={"dp": at.by_x},
        device_id_type=MESH,
    )
    stay = pltpu.make_async_copy(pieces.at[bit_x], rows_out.at[pl.ds(2 * bit_x, 2)], lsem.at[1])

    def vector_near(k):
        return pltpu.make_async_remote_copy(
            src_ref=vec.at[lax.rem(z + k, n)],
            dst_ref=vgot.at[k - 1],
            send_sem=vsem.at[0, k - 1],
            recv_sem=vsem.at[1, k - 1],
            device_id={"head": lax.rem(z + k, n)},
            device_id_type=MESH,
        )

    def vector_far(i, target):
        return pltpu.make_async_remote_copy(
            src_ref=vsum.at[i],
            dst_ref=vgot.at[3 + i],
            send_sem=vsem.at[0, 3 + i],
            recv_sem=vsem.at[1, 3 + i],
            device_id={"dp": target},
            device_id_type=MESH,
        )

    def put_head(l, c, value):
        if c < 3:
            qkv_out[l, c] = value
        else:
            out_out[l] = jnp.transpose(value, (1, 0))

    def total_of(own, others):
        value = own.astype(f32)
        for other in others:
            value = value + other.astype(f32)
        return value

    row_copies("start")
    for c in range(parts):
        ffn_hop(c).start()
        hop(0, c).start()
    for k in range(1, n):
        vector_near(k).start()
    partners = (at.mate, at.first, at.second)
    for t in range(parts + 4):
        c = t
        if c < parts:
            for copy in loads(c):
                copy.wait()
            hop(0, c).wait()
            add(4, lambda m, g, c=c: got[m, g, :, columns(c)], c)
            hop(1, c).start()
            ffn_hop(c).wait()

            def body(g, carry, c=c):
                value = fm[g, :, broad(c)].astype(f32) + flast[g, :, broad(c)].astype(f32)
                fm[g, :, broad(c)] = value.astype(bf16)
                return carry

            lax.fori_loop(0, GROUPS, body, 0)
            for copy in ffn_around(c):
                copy.start()
        c = t - 1
        if 0 <= c < parts:
            hop(1, c).wait()
            add(2, lambda m, g, c=c: pair[m, g, :, columns(c)], c)
            hop(2, c).start()
        c = t - 2
        if 0 <= c < parts:
            hop(2, c).wait()
            add(1, lambda m, g, c=c: last[g, :, columns(c)], c)
            for copy in head_around(c):
                copy.start()
        if t == 1:
            for k in range(1, n):
                vector_near(k).wait()
            vsum[0] = vec[z] + vgot[0] + vgot[1] + vgot[2]
            vector_far(0, partners[0]).start()
        if 2 <= t < 5:
            i = t - 2
            vector_far(i, partners[i]).wait()
            vsum[i + 1] = vsum[i] + vgot[3 + i]
            if i < 2:
                vector_far(i + 1, partners[i + 1]).start()
        if t == 2:
            row_copies("wait")
            row_arrivals()
            cross.start()
            stay.start()
        if t == 4:
            for l in range(1, layers):
                heads, hnear, ups, unear, downs, dnear = tops[6 * l - 6 : 6 * l]
                for c in range(parts):
                    cols = slice(c * width, (c + 1) * width)
                    put_head(l, c, total_of(heads[0, :, cols], [hnear[k, :, cols] for k in range(3)]))
                up_out[l] = total_of(ups[0], [unear[k] for k in range(3)])
                down_out[l] = jnp.transpose(total_of(downs[0], [dnear[k] for k in range(3)]), (1, 0))
        c = t - 4
        if 0 <= c < parts:
            for copy in ffn_around(c):
                copy.wait()
            value = total_of(fm[0, :, broad(c)], [fnear[k, :, broad(c)] for k in range(3)])
            if c < parts // 2:
                up_out[0, :, broad(c)] = value
            else:
                down_out[0, pl.ds(c * step - WIDE, step), :] = jnp.transpose(value, (1, 0))
    for c in range(parts):
        for copy in head_around(c):
            copy.wait()
        others = [near[k, :, columns(c)] for k in range(3)]
        put_head(0, c, total_of(mine[0, 0, :, columns(c)], others))
    vectors_out[...] = vsum[3]
    cross.wait()
    stay.wait()


def end_call(rows, grads, fmine, fsent, valid, tops, vecs, uses):
    parts = 4
    layers = len(vecs) // 4
    tokens = rows.shape[0]
    wide = rows.shape[1] // GROUPS
    block = grads.shape[1:]
    broad = fmine.shape
    vector = (vector_rows(layers), LANES)
    inputs = [rows, grads, fmine, fsent, valid, *tops, *vecs, *uses]

    def spec(i, v):
        if i % 2 == 0:
            return pl.BlockSpec((1,) + v.shape[1:], lambda g: (0, 0, 0))
        return whole(v.shape)

    def kernel(*refs):
        fixed, refs = refs[:5], refs[5:]
        lists = []
        for values in (tops, vecs, uses):
            lists.append(refs[: len(values)])
            refs = refs[len(values) :]
        end_kernel(layers, *fixed, *lists, *refs)

    outs = [
        jax.ShapeDtypeStruct((layers, 3, LANES, HEADS), f32),
        jax.ShapeDtypeStruct((layers, HEADS, LANES), f32),
        jax.ShapeDtypeStruct((layers, LANES, WIDE), f32),
        jax.ShapeDtypeStruct((layers, WIDE, LANES), f32),
        jax.ShapeDtypeStruct(vector, f32),
    ]
    return pl.pallas_call(
        kernel,
        out_shape=[jax.ShapeDtypeStruct((GROUPS, tokens, wide), bf16)] + outs,
        grid=(1,),
        in_specs=[HB] * 4
        + [whole(valid.shape)]
        + [spec(i, v) for i, v in enumerate(tops)]
        + [whole(v.shape) for v in (*vecs, *uses)],
        out_specs=[HB] + [whole(v.shape) for v in outs],
        scratch_shapes=[
            pltpu.VMEM((4,) + block, bf16),
            pltpu.VMEM((4,) + block, bf16),
            pltpu.VMEM((2,) + block, bf16),
            pltpu.VMEM(block, bf16),
            pltpu.VMEM((3,) + block[1:], bf16),
            pltpu.VMEM((2, 2, tokens, wide), bf16),
            pltpu.VMEM(broad, bf16),
            pltpu.VMEM(broad, bf16),
            pltpu.VMEM((3,) + broad[1:], bf16),
            pltpu.VMEM((GROUPS,) + vector, f32),
            pltpu.VMEM((6,) + vector, f32),
            pltpu.VMEM((4,) + vector, f32),
            DMA((2, parts)),
            DMA((2, parts)),
            DMA((2, parts)),
            DMA((2, parts)),
            DMA((2, 3, parts)),
            DMA((2, 3, parts)),
            DMA((2, 4)),
            DMA((2,)),
            DMA((2, 6)),
            DMA((2,)),
            DMA((2, parts)),
            DMA((2, 3, parts)),
        ],
        compiler_params=params(collective_id=6, has_side_effects=True),
        cost_estimate=cost(0, 300 * 2**20),
        name="end",
    )(*inputs)


def after(value, *tokens):
    return lax.optimization_barrier((value, tokens))[0]


class Order:
    def __init__(self):
        self.token = None
        self.wanted = []

    def __call__(self, call, *args, first=0):
        args = list(args)
        if self.token is not None:
            args[first] = after(args[first], self.token, *self.wanted)
            self.wanted = []
        out = call(*args)
        self.token = out
        while isinstance(self.token, (list, tuple)):
            self.token = self.token[0]
        return out

    def hold(self, value):
        return after(value, self.token)

    def want(self, value):
        self.wanted.append(value)
        return value


class Net:
    def __init__(self, n_dp, n_head):
        self.n_dp, self.n = n_dp, n_head
        self.own = lax.axis_index("dp").astype(jnp.int32)
        self.z = lax.axis_index("head").astype(jnp.int32)
        self.lo = self.own % n_head
        self.fast = n_dp == BLOCKS and n_head == GROUPS
        core_zero = [2, 4]
        self.one_way = [(i, i ^ core_zero[i % 2]) for i in range(n_dp)]
        self.other_way = [(i, i ^ core_zero[1 - i % 2]) for i in range(n_dp)]
        self.core = [(i, i ^ 1) for i in range(n_dp)]
        ends = [jnp.int32(0), self.lo]
        self.all_rows = jnp.stack([jnp.int32(i) for i in range(BLOCKS)] + ends)
        if self.fast:
            step = jnp.where(self.own % 2 == 0, 2, 4).astype(jnp.int32)
            mine = [jnp.int32(0), step, 6 - step, jnp.int32(6)]
            theirs = [jnp.int32(0), 6 - step, step, jnp.int32(6)]
            ends = [self.z, self.lo]
            self.even = jnp.stack([self.own ^ v for v in mine] + ends)
            self.odd = jnp.stack([self.own ^ v ^ 1 for v in theirs] + ends)
            self.pieces = jnp.concatenate([self.even[:4], self.odd])

    def shift(self, value, k):
        n = self.n
        if k % n == 0:
            return value
        pairs = [(i, (i // n) * n + (i + k) % n) for i in range(self.n_dp)]
        return lax.ppermute(value, "dp", pairs)

    def spin(self, value, k):
        n = self.n
        return lax.ppermute(value, "head", [(i, (i + k) % n) for i in range(n)])

    def gather(self, shard):
        return lax.all_gather(shard, ("dp", "head")).reshape(BLOCKS, GROUPS, LANES, -1)

    def gather_any(self, qkv, out, up, down):
        qkv = lax.all_gather(qkv, "head", axis=2, tiled=True)
        qkv = lax.all_gather(qkv, "dp", axis=1, tiled=True).transpose(1, 0, 2).reshape(D, 3 * D)
        up = lax.all_gather(up, "head", axis=1, tiled=True)
        up = lax.all_gather(up, "dp", axis=0, tiled=True)
        out, down = [
            lax.all_gather(lax.all_gather(v, "head", axis=0, tiled=True), "dp", axis=1, tiled=True)
            for v in (out, down)
        ]

        def blocks(*parts):
            cut = [v.reshape(BLOCKS, LANES, GROUPS, -1) for v in parts]
            return jnp.concatenate(cut, axis=3).transpose(0, 2, 1, 3)

        heads = [qkv[:, c * D : (c + 1) * D] for c in range(3)]
        return blocks(*heads, out.T), blocks(up, down.T)

    def scatter(self, full, widths):
        columns = full.shape[3]
        if self.fast:
            full = full.reshape(BLOCKS * GROUPS, LANES, columns)
        else:
            full = full.transpose(0, 2, 1, 3).reshape(D, GROUPS, columns)
            parts, at = [], 0
            for w in widths:
                part = full[:, :, at : at + w].reshape(D, self.n, GROUPS * w // self.n)
                parts.append(part)
                at += w
            full = jnp.concatenate(parts, axis=2)
            full = full.reshape(self.n_dp, D // self.n_dp, self.n, -1).transpose(0, 2, 1, 3)
            full = full.reshape(self.n_dp * self.n, D // self.n_dp, -1)
        mine = lax.psum_scatter(full, ("dp", "head"), scatter_dimension=0, tiled=False)
        return mine.astype(f32)


    def add_pair(self, keep, pair):
        add = lambda i: (keep[i].astype(f32) + pair[i].astype(f32)).astype(bf16)
        return add(0), add(1)

    def add_last(self, mine, last):
        return (mine.astype(f32) + last.astype(f32)).astype(bf16)

    def turn(self, k):
        n = self.n
        pairs = []
        for hi in range(self.n_dp // n):
            for lo in range(n):
                for z in range(n):
                    pairs.append(((hi * n + lo) * n + z, (hi * n + (z + k) % n) * n + lo))
        return pairs

    def rows_in(self, array):
        n = self.n
        tokens = array.shape[0] // n
        low = array.astype(bf16).reshape(n, tokens, array.shape[1])
        got = []
        for k in range(n):
            piece = lax.dynamic_index_in_dim(low, (self.z + k) % n, 0, False)
            got.append(lax.ppermute(piece, ("dp", "head"), self.turn(k)))
        return got

    def rows_in_end(self, got):
        stacked = jnp.take(jnp.stack(got), (self.lo - jnp.arange(self.n)) % self.n, axis=0)
        return stacked.transpose(1, 0, 2).reshape(got[0].shape[0], D)

    def rows_out(self, array):
        n = self.n
        width = D // n
        low = array.astype(bf16)
        got = []
        for k in range(n):
            piece = lax.dynamic_slice_in_dim(low, ((self.lo - k) % n) * width, width, 1)
            got.append(lax.ppermute(piece, ("dp", "head"), [(b, a) for a, b in self.turn(k)]))
        return got

    def rows_out_end(self, got):
        stacked = jnp.take(jnp.stack(got), (jnp.arange(self.n) - self.z) % self.n, axis=0)
        return stacked.reshape(-1, got[0].shape[1]).astype(f32)


def local(
    n_dp,
    n_head,
    stream_in,
    qkv_weight,
    out_weight,
    up_weight,
    down_weight,
    norm_gains,
    norm_shifts,
    hidden_gains,
    hidden_shifts,
    buckets,
    valid_mask,
    cotangent,
):
    net = Net(n_dp, n_head)
    n = n_head
    layers = qkv_weight.shape[0]
    tokens = LONG // n
    order = Order()

    flags = jnp.concatenate([valid_mask, buckets])
    vectors = [
        v.reshape(layers, -1) for v in (norm_gains, norm_shifts, hidden_gains, hidden_shifts)
    ]
    packed = jnp.concatenate(vectors, axis=1)
    narrow, broad = [None] * layers, [None] * layers
    if net.fast:
        small, large = pack_call(qkv_weight, out_weight, up_weight, down_weight)
        rows = stream_in.astype(bf16).reshape(n, tokens, D // n)
        flags = jnp.pad(flags, (0, -flags.shape[0] % 1024)).reshape(-1, LANES)
        vector = packed.reshape(-1, LANES)
        started = order(start_call, small[:1], rows, vector, flags, first=1)
        (narrow[0],), stream, _, packed, flags = started
        flags = flags.reshape(-1)
        broad[0] = net.gather(order.hold(large[0]))
    else:
        for l in range(layers):
            narrow[l], broad[l] = net.gather_any(
                qkv_weight[l], out_weight[l], up_weight[l], down_weight[l]
            )
        stream = net.rows_in_end(net.rows_in(stream_in))
        flags = lax.ppermute(flags, ("dp", "head"), net.turn(0))
        packed = lax.all_gather(packed.reshape(-1, LANES), "head")
    slab_mask = flags[:LONG].reshape(n, tokens)
    bucket = flags[LONG]
    rel_blocks = (net.lo - jnp.arange(n)) % n
    rel_mask = jnp.take(slab_mask, rel_blocks, axis=0)
    lane = jnp.arange(LANES)[None, None, :] == 0
    aux = jnp.where((rel_mask[:, :, None] == 0) & lane, MASKED, 0.0).astype(bf16)
    one = jnp.broadcast_to((jnp.arange(LANES)[None, :] == 0), (tokens, LANES)).astype(bf16)
    sequence = jnp.where(bucket == 1, 0, (rel_blocks * tokens) // SHORT)
    alive = jnp.sum(rel_mask, axis=1) > 0
    need = ((sequence[:, None] == sequence[None, :]) & alive[None, :]).astype(jnp.int32)
    need = need.reshape(n * n)
    valid = lax.dynamic_index_in_dim(slab_mask, net.lo, 0, False).astype(f32)[:, None]

    low = stream
    stream = stream.astype(f32)
    halves = lambda v, axis: jnp.split(v, 2, axis=axis)
    cot = cotangent.astype(bf16).reshape(n, tokens, D // n)
    kept = []
    usage = []
    idents = iter(range(10, 64))
    for l in range(layers):
        ahead = net.fast and l + 1 < layers
        parts, _ = order(qkv_call, n, next(idents), [], l, low, packed, narrow[l], first=4)
        parts = [parts[0]] + [[net.shift(v, k) for k, v in enumerate(p)] for p in parts[1:]]
        att, lse = [], []
        for p in parts:
            outs = order(attn_call, n, need, aux, one, p, first=2)
            att.append(outs[0])
            lse.append(outs[1])
        if ahead:
            broad[l + 1] = net.gather(order.hold(large[l + 1]))
        rows_job = []
        if net.fast and l + 1 == layers:
            rows_job = [Turn(half, False) for half in halves(cot, 1)]
        mid, rows, use_branch, *late = order(
            proj_call, n, next(idents), rows_job[1:], l, valid, stream, packed, narrow[l], att,
            first=5,
        )
        if ahead:
            (narrow[l + 1],) = order(gather_call, [order.hold(small[l + 1])], first=0)
        slope, hat, normed, low_mid, rstd, stream, next_low, use_rest, *early = order(
            ffn_call, n, next(idents), rows_job[:1], l, valid, mid, packed, broad[l], first=5
        )
        if rows_job:
            grad = jnp.concatenate(early + late, axis=0).astype(f32)
        usage += [use_branch, use_rest]
        kept.append((low, parts, att, lse, rows, slope, hat, normed, low_mid, rstd))
        low = next_low

    if not net.fast:
        grad = net.rows_in_end(net.rows_in(cotangent)).astype(f32)
    if not net.fast:
        grad = net.rows_in_end(net.rows_in(cotangent)).astype(f32)
    units = BLOCKS // n
    ffn_grads, head_grads = [None] * layers, [None] * layers
    vectors, tops = [None] * layers, []

    for l in reversed(range(layers)):
        low, parts, att, lse, rows, slope, hat, normed, low_mid, rstd = kept[l]
        more = net.fast and l + 1 < layers
        last = net.fast and l + 1 == layers
        jobs = []
        if last:
            jobs = [Turn(half, True) for half in halves(stream.astype(bf16), 0)]
        if more:
            ffn_mine, sent = net.add_pair(order.hold(ffn_keep), ffn_pair)
            jobs = [Hop(head_odd, "mate"), Hop(sent, "first")]
        dhid, grad_turned, ffn_turned, grad, hgrads, grads2, *extra = order(
            ffn_back_call, n, next(idents), jobs[:1] if last else jobs, l, grad, hat, slope, rstd,
            low_mid, packed, broad[l], first=4,
        )
        ffn_args = (ffn_turned, grad_turned, dhid, normed)
        if net.fast:
            moved = extra
            if more:
                ups = net.add_last(ffn_mine[..., :WIDE], extra[1][..., :WIDE])
                downs = net.add_last(ffn_mine[..., WIDE:], extra[1][..., WIDE:])
                head_keep, send = order(
                    head_grad_call, n, 4, net.even, *head_args, extra[0], first=3
                )
                head_pair = lax.ppermute(order.hold(send), "dp", net.other_way)
            (odd,) = order(ffn_grad_call, 4, net.odd, *ffn_args, first=2)
            jobs = [Hop(odd, "mate")] + ([Near(ups)] if more else jobs[1:])
        else:
            (full,) = order(ffn_grad_call, BLOCKS, net.all_rows, *ffn_args, first=2)
            ffn_grads[l] = net.scatter(full, (WIDE, WIDE))
        res = order(
            proj_back_call, n, next(idents), jobs, l, grad, packed, narrow[l], rows, first=4
        )
        datt, (out_turned, normed_mid, grads1, *extra) = res[:units], res[units:]
        if net.fast:
            if last:
                stream_out = jnp.concatenate([moved[0], extra[1]], axis=1)
                stream_out = stream_out.reshape(LONG, D // n).astype(f32)
            if more:
                unear = extra[1]
                head_mine, sent = net.add_pair(order.hold(head_keep), head_pair)
                head_last = lax.ppermute(sent, "dp", net.one_way)
                order.want(sent)
            ffn_keep, send = order(ffn_grad_call, 4, net.even, *ffn_args, extra[0], first=2)
            ffn_pair = lax.ppermute(order.hold(send), "dp", net.other_way)
        dparts, ready = [], []
        for u in range(units):
            ready += [net.shift(v, -k) for k, v in enumerate(dparts)]
            dparts = order(
                attn_back_call, n, need, aux, one, parts[u], att[u], datt[u], lse[u], first=2
            )
            if more and u == 0:
                head_sum = order.want(net.add_last(order.hold(head_mine), head_last))
        jobs = [Near(downs), Near(head_sum)] if more else []
        dlast, grad, in_turned, grads0, grad_low, *extra = order(
            qkv_back_call, n, next(idents), jobs, l, grad, low, packed, narrow[l], ready, dparts,
            first=4,
        )
        head_args = (in_turned, out_turned, ready + dlast, normed_mid)
        vectors[l] = [grads0, grads1, grads2, hgrads]
        if net.fast:
            if more:
                tops = [head_sum, extra[1], ups, unear, downs, extra[0]] + tops
            if l:
                (head_odd,) = order(head_grad_call, n, 4, net.odd, *head_args, first=3)
            else:
                (full,) = order(head_grad_call, n, BLOCKS, net.pieces, *head_args, first=3)
        else:
            (full,) = order(head_grad_call, n, BLOCKS, net.all_rows, *head_args, first=3)
            head_grads[l] = net.scatter(full, (HEADS,) * 4)
    vectors = [v for part in vectors for v in part]
    if net.fast:
        ffn_mine, sent = net.add_pair(order.hold(ffn_keep), ffn_pair)
        moved, qkv_grad, out_grad, up_grad, down_grad, summed = order(
            end_call, grad_low, full, ffn_mine, sent, valid, tops, vectors, usage
        )
        stream_grad = moved.reshape(LONG, D // n).astype(f32)
        stacked = [qkv_grad, out_grad, up_grad, down_grad]
        norms = summed[: 28 * layers].reshape(layers, 28, LANES)
        hids = norms[:, 12:].reshape(layers, 2, FF // n)
        norms = norms[:, :12].reshape(layers, 2, 3, D // n)
        totals = jnp.sum(summed[28 * layers : 31 * layers + 1], axis=1)
        usage_rms = jnp.sqrt(totals[:-1] / totals[-1]).reshape(layers, 3)
    else:
        stream_out = net.rows_out_end(net.rows_out(stream))
        stream_grad = net.rows_out_end(net.rows_out(grad))
        norms = [jnp.sum(jnp.stack(vectors[4 * l : 4 * l + 3], 1), axis=2) for l in range(layers)]
        norms = lax.psum(jnp.stack(norms), ("dp", "head"))
        hids = [jnp.sum(vectors[4 * l + 3], axis=2).reshape(2, FF) for l in range(layers)]
        hids = lax.psum(jnp.stack(hids), ("dp", "head"))
        share = lambda v: lax.dynamic_slice_in_dim(
            v, net.z * (v.shape[-1] // n), v.shape[-1] // n, v.ndim - 1
        )
        norms, hids = share(norms), share(hids)
        totals = []
        for l in range(layers):
            branch, rest = usage[2 * l : 2 * l + 2]
            totals += [jnp.sum(branch), jnp.sum(rest[0]), jnp.sum(rest[1])]
        totals = lax.psum(jnp.stack(totals + [jnp.sum(valid) * D]), ("dp", "head"))
        usage_rms = jnp.sqrt(totals[:-1] / totals[-1]).reshape(layers, 3)
        weight_grads = []
        for l in range(layers):
            heads = head_grads[l]
            width = heads.shape[1] // 4
            qkv = heads[:, : 3 * width].reshape(-1, 3, width).transpose(1, 0, 2)
            half = ffn_grads[l].shape[1] // 2
            weight_grads.append(
                (qkv, heads[:, 3 * width :].T, ffn_grads[l][:, :half], ffn_grads[l][:, half:].T)
            )
        stacked = [jnp.stack([weight_grads[l][k] for l in range(layers)]) for k in range(4)]
    gains_grad, shifts_grad = norms[:, 0], norms[:, 1]
    hidden_gains_grad, hidden_shifts_grad = hids[:, 0], hids[:, 1]
    return (
        stream_out,
        stream_grad,
        stacked[0],
        stacked[1],
        stacked[2],
        stacked[3],
        gains_grad,
        shifts_grad,
        hidden_gains_grad,
        hidden_shifts_grad,
        usage_rms,
    )


def solution(mesh):
    n_dp, n_head = mesh.shape["dp"], mesh.shape["head"]

    def run(*args):
        return local(n_dp, n_head, *args)

    return jax.shard_map(
        run,
        mesh=mesh,
        in_specs=(
            P("dp", "head"),
            P(None, None, "dp", "head"),
            P(None, "head", "dp"),
            P(None, "dp", "head"),
            P(None, "head", "dp"),
            P(None, None, "head"),
            P(None, None, "head"),
            P(None, "head"),
            P(None, "head"),
            P("dp"),
            P("dp"),
            P("dp", "head"),
        ),
        out_specs=(
            P("dp", "head"),
            P("dp", "head"),
            P(None, None, "dp", "head"),
            P(None, "head", "dp"),
            P(None, "dp", "head"),
            P(None, "head", "dp"),
            P(None, None, "head"),
            P(None, None, "head"),
            P(None, "head"),
            P(None, "head"),
            P(),
        ),
        check_vma=False,
    )
```

time: 2570 us -> 1060 us (0.41)
  waiting for transfers between devices: 1370 us -> 27.6 us
  Pallas kernels: 0 us -> 934 us
  blocking collectives: 494 us -> 0 us
  matrix products: 310 us -> 0 us
  local copies, waits for them, and re-layouts: 173 us -> 19 us
  other arithmetic: 174 us -> 35.9 us
    pallas_call x0 -> x31, Pallas kernels: none -> 934 us  [the longest x11 451 us: remote_call(): pl.pallas_call(kernel, out_shape=list(out_shape) + job_out, grid=grid, in...]
    reduce_scatter x10 -> x0, waiting for transfers between devices: 726 us -> none  [the longest x4 281 us: narrow(): lax.psum_scatter(partial_sum.astype(jnp.bfloat16), 'head', scatter_dimens...]
    all_gather x14 -> x2, waiting for transfers between devices: 564 us -> 0.04 us  [gather(): lax.all_gather(shard, ('dp', 'head')).reshape(BLOCKS, GROUPS, LANES, -1)]
    psum x18 -> x0, blocking collectives: 398 us -> none  [the longest x1 153 us: local(): lax.psum((jnp.stack(usage_rows), jnp.sum(row_weight) * stream.shape[1]),...]
    dot_general x80 -> x0, matrix products: 310 us -> none  [the longest x2 55.3 us: local(): hidden = jnp.dot(normed_ffn, up_full, preferred_element_type=jnp.float32)]
    all_gather x10 -> x0, blocking collectives: 96.5 us -> none  [the longest x4 43.1 us: widen(): lax.all_gather(shift_row.astype(jnp.bfloat16), 'head', axis=0, tiled=True)]
    unnamed x36 -> x2, waiting for transfers between devices: 77.1 us -> 0.03 us
    reduce_sum x30 -> x2, other arithmetic: 73.4 us -> 1.04 us  [the longest x1 0.86 us: local(): totals = jnp.sum(summed[28 * layers:31 * layers + 1], axis=1)]
  transfers between devices with their start and end apart: 30 -> 18, of which waited for: 23 -> 6; matrix products, arithmetic and copies ran while one was open for 11% -> 2% of each run, Pallas kernels for 0% -> 55%
where the time goes in v2:
time: 1060 us; the launch traced here: 1040 us
  Pallas kernels  934 us (88%)
  other arithmetic  35.9 us (3%)
  waiting for transfers between devices  27.6 us (3%)
  local copies, waits for them, and re-layouts  19 us (2%)
  between operations  16 us (2%)
  starting transfers between devices  10.7 us (1%)
    pallas_call x11, Pallas kernels, remote_call(): pl.pallas_call(kernel, out_shape=list(out_shape) + job_out, grid=grid, in...  451 us
    pallas_call x1, Pallas kernels, end_call(): pl.pallas_call(kernel, out_shape=[jax.ShapeDtypeStruct((GROUPS, tokens, w...  111 us
    pallas_call x1, Pallas kernels, gather_call(): pl.pallas_call(kernel, out_shape=[jax.ShapeDtypeStruct((BLOCKS, GROUPS) +...  107 us
    pallas_call x8, Pallas kernels, unit_call(): pl.pallas_call(lambda *refs: kernel(n, *refs), out_shape=out_shape, grid_...  81.7 us
    pallas_call x1, Pallas kernels, start_call(): pl.pallas_call(kernel, out_shape=[jax.ShapeDtypeStruct((BLOCKS, GROUPS) +...  65.3 us
    pallas_call x4, Pallas kernels, ffn_grad_call(): pl.pallas_call(lambda *refs: ffn_grad_kernel(count, added, *refs), out_sh...  53.8 us
    pallas_call x1, Pallas kernels, plain_call(): pl.pallas_call(lambda *refs: body(Host(n, []), *refs), out_shape=out_shap...  33.2 us
    pallas_call x3, Pallas kernels, head_grad_call(): pl.pallas_call(lambda *refs: head_grad_kernel(n, count, added, *refs), ou...  28.1 us
  transfers between devices with their start and end apart: 18, of which 6 were waited for; matrix products, arithmetic and copies ran while one was open for 2% of the time, Pallas kernels for 55%

profile of v2, /device:TPU:0, one launch (start us, length us, event | category | flops | bytes accessed | tf_op | source)
XLA Modules:
  0.0 1043.4 jit_solution(7712238309958854226)
XLA Ops:
  10.6 2.7 convert_element_type.175
  13.2 2.7 pack.1
  15.9 65.3 %start.1 = (bf16[8,4,128,1024]{3,2,1,0:T(8,128)(2,1)}, bf16[512,1024]{1,0:T(8,128)(2,1)}, bf16[2,512,256]{2,1,0:T(8,128)(2,1)}, f32[4,56,128]{2,1,0:T(8,128)}, s32[24,128]{1,0:T(8,128)}) custom-call(bf16[128,1024]{1,0:T(8,128)(2,1)} %get-tuple-element.177.refs_0_, bf16[4,512,256]{2,1,0:T(8,128)(2,1)} %bitcast.51, f32[56,128]{1,0:T(8,128)} %reshape.258.refs_2_, ...), custom_call_target="tpu_custom_call" | custom-call | bytes 314572800 | tf_op jit(solution)/shard_map/start/pallas_call | solution.py:1561
  81.3 29.7 %qkv.4 = (bf16[3,512,128]{2,1,0:T(8,128)(2,1)}, bf16[3,512,128]{2,1,0:T(8,128)(2,1)}, bf16[3,512,128]{2,1,0:T(8,128)(2,1)}, bf16[3,512,128]{2,1,0:T(8,128)(2,1)}...) custom-call(bf16[512,1024]{1,0:T(8,128)(2,1)} %get-tuple-element.181, ...), custom_call_target="tpu_custom_call" | custom-call | flops 32212254720 | bytes 10485760 | tf_op jit(solution)/shard_map/qkv/pallas_call | solution.py:431
  118.2 9.2 attention.4
  127.5 11.4 %collective-permute-done.2.refs_6_ = bf16[3,512,128]{2,1,0:T(8,128)(2,1)S(1)} collective-permute-done((bf16[3,512,128]{2,1,0:T(8,128)(2,1)}, bf16[3,512,128]{2,1,0:T(8,128)(2,1)S(1)}, u32[]{:S(2)}, u32[]{:S(2)}) %collective-permute-start.2) | collective-permute-done | bytes 393248 | tf_op jit(solution)/shard_map/ppermute | solution.py:2009
  139.6 9.2 attention.5
  150.7 1.6 convert_element_type.178.refs_1_
  154.3 28.5 %projection.2 = (f32[512,1024]{1,0:T(8,128)}, bf16[512,1024]{1,0:T(8,128)(2,1)}, f32[8,1024]{1,0:T(8,128)}) custom-call(f32[512,1]{1,0:T(8,128)} %copy.26.refs_0_.refs_4_, f32[512,1024]{1,0:T(8,128)} %convert_element_type.178.refs_1_, f32[4,56,128]{2,1,0:T(8,128)} %get-tuple-element.182.refs_1_.refs_2_.refs_5_, ...), custom_call_target="tpu_custom_call" | custom-call | flops 16106127360 | bytes 10485760 | tf_op jit(solution)/shard_map/projection/pallas_call | solution.py:431
  182.9 107.4 %gather.8.refs_2_.refs_3_.refs_4_.refs_5_ = bf16[8,4,128,1024]{3,2,1,0:T(8,128)(2,1)} custom-call(bf16[128,1024]{1,0:T(8,128)(2,1)} %get-tuple-element.199.refs_0_), custom_call_target="tpu_custom_call" | custom-call | bytes 157286400 | tf_op jit(solution)/shard_map/gather/pallas_call | solution.py:1409
  290.3 33.2 %ffn.2 = (bf16[4,512,1024]{2,1,0:T(8,128)(2,1)}, bf16[4,512,1024]{2,1,0:T(8,128)(2,1)}, bf16[4,512,1024]{2,1,0:T(8,128)(2,1)}, bf16[512,1024]{1,0:T(8,128)(2,1)}...) custom-call(f32[512,1]{1,0:T(8,128)} %copy.26.refs_0_.refs_4_, ...), custom_call_target="tpu_custom_call" | custom-call | flops 34359738368 | bytes 10485760 | tf_op jit(solution)/shard_map/ffn/pallas_call | solution.py:383
  323.5 38.7 %qkv.5 = (bf16[3,512,128]{2,1,0:T(8,128)(2,1)}, bf16[3,512,128]{2,1,0:T(8,128)(2,1)}, bf16[3,512,128]{2,1,0:T(8,128)(2,1)}, bf16[3,512,128]{2,1,0:T(8,128)(2,1)}...) custom-call(bf16[512,1024]{1,0:T(8,128)(2,1)} %get-tuple-element.206, ...), custom_call_target="tpu_custom_call" | custom-call | flops 32212254720 | bytes 10485760 | tf_op jit(solution)/shard_map/qkv/pallas_call | solution.py:431
  362.8 1.6 collective-permute-start.5
  364.5 9.3 attention.6
  374.7 5.5 collective-permute-done.5.refs_6_
  381.0 9.1 attention.7
  390.1 33.5 %projection.3 = (f32[512,1024]{1,0:T(8,128)}, bf16[512,1024]{1,0:T(8,128)(2,1)}, f32[8,1024]{1,0:T(8,128)}, bf16[256,1024]{1,0:T(8,128)(2,1)}) custom-call(f32[512,1]{1,0:T(8,128)} %copy.26.refs_0_.refs_4_, f32[512,1024]{1,0:T(8,128)} %get-tuple-element.219.refs_1_, f32[4,56,128]{2,1,0:T(8,128)} %get-tuple-element.182.refs_1_.refs_2_.refs_5_, ...), custom_call_target="tpu_custom_call" | custom-call | flops 16106127360 | bytes 10485760 | tf_op jit(solution)/shard_map/projection/pallas_call | solution.py:431
  423.7 42.8 %ffn.3 = (bf16[4,512,1024]{2,1,0:T(8,128)(2,1)}, bf16[4,512,1024]{2,1,0:T(8,128)(2,1)}, bf16[4,512,1024]{2,1,0:T(8,128)(2,1)}, bf16[512,1024]{1,0:T(8,128)(2,1)}...) custom-call(f32[512,1]{1,0:T(8,128)} %copy.26.refs_0_.refs_4_, ...), custom_call_target="tpu_custom_call" | custom-call | flops 34359738368 | bytes 10485760 | tf_op jit(solution)/shard_map/ffn/pallas_call | solution.py:431
  466.5 2.8 maximum_convert_fusion.refs_0_
  470.5 34.4 %ffn_back.2 = (bf16[4,512,1024]{2,1,0:T(8,128)(2,1)}, bf16[8,128,512]{2,1,0:T(8,128)(2,1)}, bf16[8,128,512]{2,1,0:T(8,128)(2,1)}, f32[512,1024]{1,0:T(8,128)}, f...) custom-call(f32[512,1024]{1,0:T(8,128)} %maximum_convert_fusion.refs_0_, ...), custom_call_target="tpu_custom_call" | custom-call | flops 34359738368 | bytes 10485760 | tf_op jit(solution)/shard_map/ffn_back/pallas_call | solution.py:431
  504.9 12.5 %ffn_grad.4.refs_4_ = bf16[4,4,128,2048]{3,2,1,0:T(8,128)(2,1)} custom-call(s32[6]{0:T(128)} %stack.44.refs_0_, bf16[8,128,512]{2,1,0:T(8,128)(2,1)} %get-tuple-element.242.refs_1_, bf16[8,128,512]{2,1,0:T(8,128)(2,1)} %get-tuple-element.236.refs_2_, bf16[4,512,1024]{2,1,0:T(8,128)(2,1)} %get-tuple-element.234.refs_3_, ...), custom_call_target="tpu_custom_call" | custom-call | flops 17179869184 | bytes 25165824 | tf_op jit(solution)/shard_map/ffn_grad/pallas_call | solution.py:1206
  517.4 28.0 %projection_back.2 = (bf16[4,512,128]{2,1,0:T(8,128)(2,1)}, bf16[4,512,128]{2,1,0:T(8,128)(2,1)}, bf16[8,128,512]{2,1,0:T(8,128)(2,1)}, bf16[512,1024]{1,0:T(8,1...) custom-call(f32[512,1024]{1,0:T(8,128)} %get-tuple-element.252.refs_0_, ...), custom_call_target="tpu_custom_call" | custom-call | flops 16106127360 | bytes 10485760 | tf_op jit(solution)/shard_map/projection_back/pallas_call | solution.py:431
  545.4 14.4 %ffn_grad.5 = (bf16[2,4,128,2048]{3,2,1,0:T(8,128)(2,1)}, bf16[2,4,128,2048]{3,2,1,0:T(8,128)(2,1)}) custom-call(s32[6]{0:T(128)} %stack.49.refs_0_, bf16[8,128,512]{2,1,0:T(8,128)(2,1)} %get-tuple-element.242.refs_1_, bf16[8,128,512]{2,1,0:T(8,128)(2,1)} %get-tuple-element.236.refs_2_, bf16[4,512,1024]{2,1,0:T(8,128)(2,1)} %get-tuple-element.234.refs_3_, ...), custom_call_target="tpu_custom_call" | custom-call | flops 17179869184 | bytes 25165824 | tf_op jit(solution)/shard_map/ffn_grad/pallas_call | solution.py:1206
  559.8 11.3 %attention_back.4 = (bf16[3,512,128]{2,1,0:T(8,128)(2,1)}, bf16[3,512,128]{2,1,0:T(8,128)(2,1)}, bf16[3,512,128]{2,1,0:T(8,128)(2,1)}, bf16[3,512,128]{2,1,0:T(8,128)(2,1)}) custom-call(s32[16]{0:T(128)} %reshape.268.refs_0_, bf16[4,512,128]{2,1,0:T(8,128)(2,1)} %select_convert_fusion.refs_1_, bf16[512,128]{1,0:T(8,128)(2,1)} %broadcast_in_dim.53.refs_2_, ...), custom_call_target="tpu_custom_call" | custom-call | flops 30064771072 | bytes 8388608 | tf_op jit(solution)/shard_map/attention_back/pallas_call | solution.py:571
  571.4 1.4 collective-permute-start.7
  572.9 11.2 %attention_back.5 = (bf16[3,512,128]{2,1,0:T(8,128)(2,1)}, bf16[3,512,128]{2,1,0:T(8,128)(2,1)}, bf16[3,512,128]{2,1,0:T(8,128)(2,1)}, bf16[3,512,128]{2,1,0:T(8,128)(2,1)}) custom-call(s32[16]{0:T(128)} %reshape.268.refs_0_, bf16[4,512,128]{2,1,0:T(8,128)(2,1)} %select_convert_fusion.refs_1_, bf16[512,128]{1,0:T(8,128)(2,1)} %broadcast_in_dim.53.refs_2_, ...), custom_call_target="tpu_custom_call" | custom-call | flops 30064771072 | bytes 8388608 | tf_op jit(solution)/shard_map/attention_back/pallas_call | solution.py:571
  584.1 1.5 bitcast_convert_fusion.1
  585.7 5.8 collective-permute-done.7.refs_8_.refs_6_
  592.3 68.4 %qkv_back.2 = (bf16[3,512,128]{2,1,0:T(8,128)(2,1)}, bf16[3,512,128]{2,1,0:T(8,128)(2,1)}, bf16[3,512,128]{2,1,0:T(8,128)(2,1)}, bf16[3,512,128]{2,1,0:T(8,128)(...) custom-call(f32[512,1024]{1,0:T(8,128)} %get-tuple-element.252.refs_, ...), custom_call_target="tpu_custom_call" | custom-call | flops 26843545600 | bytes 10485760 | tf_op jit(solution)/shard_map/qkv_back/pallas_call | solution.py:431
  660.8 7.8 head_grad.3.refs_7_
  668.6 5.3 fusion.1
  673.9 32.9 %ffn_back.3 = (bf16[4,512,1024]{2,1,0:T(8,128)(2,1)}, bf16[8,128,512]{2,1,0:T(8,128)(2,1)}, bf16[8,128,512]{2,1,0:T(8,128)(2,1)}, f32[512,1024]{1,0:T(8,128)}, f...) custom-call(f32[512,1024]{1,0:T(8,128)} %get-tuple-element.268.refs_, ...), custom_call_target="tpu_custom_call" | custom-call | flops 34359738368 | bytes 10485760 | tf_op jit(solution)/shard_map/ffn_back/pallas_call | solution.py:431
  706.8 9.0 head_grad.4
  715.8 12.5 %ffn_grad.6.refs_4_ = bf16[4,4,128,2048]{3,2,1,0:T(8,128)(2,1)} custom-call(s32[6]{0:T(128)} %stack.44.refs_0_, bf16[8,128,512]{2,1,0:T(8,128)(2,1)} %get-tuple-element.291.refs_1_, bf16[8,128,512]{2,1,0:T(8,128)(2,1)} %get-tuple-element.282.refs_2_, bf16[4,512,1024]{2,1,0:T(8,128)(2,1)} %get-tuple-element.277.refs_3_, ...), custom_call_target="tpu_custom_call" | custom-call | flops 17179869184 | bytes 25165824 | tf_op jit(solution)/shard_map/ffn_grad/pallas_call | solution.py:1206
  728.3 3.8 add_convert_fusion.4
  732.2 39.1 %projection_back.3 = (bf16[4,512,128]{2,1,0:T(8,128)(2,1)}, bf16[4,512,128]{2,1,0:T(8,128)(2,1)}, bf16[8,128,512]{2,1,0:T(8,128)(2,1)}, bf16[512,1024]{1,0:T(8,1...) custom-call(f32[512,1024]{1,0:T(8,128)} %get-tuple-element.302.refs_0_, ...), custom_call_target="tpu_custom_call" | custom-call | flops 16106127360 | bytes 10485760 | tf_op jit(solution)/shard_map/projection_back/pallas_call | solution.py:431
  771.3 3.6 fusion.5
  776.1 14.4 %ffn_grad.7 = (bf16[2,4,128,2048]{3,2,1,0:T(8,128)(2,1)}, bf16[2,4,128,2048]{3,2,1,0:T(8,128)(2,1)}) custom-call(s32[6]{0:T(128)} %stack.49.refs_0_, bf16[8,128,512]{2,1,0:T(8,128)(2,1)} %get-tuple-element.291.refs_1_, bf16[8,128,512]{2,1,0:T(8,128)(2,1)} %get-tuple-element.282.refs_2_, bf16[4,512,1024]{2,1,0:T(8,128)(2,1)} %get-tuple-element.277.refs_3_, ...), custom_call_target="tpu_custom_call" | custom-call | flops 17179869184 | bytes 25165824 | tf_op jit(solution)/shard_map/ffn_grad/pallas_call | solution.py:1206
  790.5 11.1 %attention_back.6 = (bf16[3,512,128]{2,1,0:T(8,128)(2,1)}, bf16[3,512,128]{2,1,0:T(8,128)(2,1)}, bf16[3,512,128]{2,1,0:T(8,128)(2,1)}, bf16[3,512,128]{2,1,0:T(8,128)(2,1)}) custom-call(s32[16]{0:T(128)} %reshape.268.refs_0_, bf16[4,512,128]{2,1,0:T(8,128)(2,1)} %select_convert_fusion.refs_1_, bf16[512,128]{1,0:T(8,128)(2,1)} %broadcast_in_dim.53.refs_2_, ...), custom_call_target="tpu_custom_call" | custom-call | flops 30064771072 | bytes 8388608 | tf_op jit(solution)/shard_map/attention_back/pallas_call | solution.py:571
  802.7 1.8 collective-permute-start.15
  804.5 1.4 add_convert_fusion.5.refs_15_.refs_5_
  805.9 11.3 %attention_back.7 = (bf16[3,512,128]{2,1,0:T(8,128)(2,1)}, bf16[3,512,128]{2,1,0:T(8,128)(2,1)}, bf16[3,512,128]{2,1,0:T(8,128)(2,1)}, bf16[3,512,128]{2,1,0:T(8,128)(2,1)}) custom-call(s32[16]{0:T(128)} %reshape.268.refs_0_, bf16[4,512,128]{2,1,0:T(8,128)(2,1)} %select_convert_fusion.refs_1_, bf16[512,128]{1,0:T(8,128)(2,1)} %broadcast_in_dim.53.refs_2_, ...), custom_call_target="tpu_custom_call" | custom-call | flops 30064771072 | bytes 8388608 | tf_op jit(solution)/shard_map/attention_back/pallas_call | solution.py:571
  817.2 3.1 collective-permute-done.13.refs_8_.refs_6_
  821.8 74.8 %qkv_back.3 = (bf16[3,512,128]{2,1,0:T(8,128)(2,1)}, bf16[3,512,128]{2,1,0:T(8,128)(2,1)}, bf16[3,512,128]{2,1,0:T(8,128)(2,1)}, bf16[3,512,128]{2,1,0:T(8,128)(...) custom-call(f32[512,1024]{1,0:T(8,128)} %get-tuple-element.302.refs_, ...), custom_call_target="tpu_custom_call" | custom-call | flops 26843545600 | bytes 10485760 | tf_op jit(solution)/shard_map/qkv_back/pallas_call | solution.py:431
  896.5 11.3 %head_grad.5.refs_1_ = bf16[8,4,128,1024]{3,2,1,0:T(8,128)(2,1)} custom-call(s32[10]{0:T(128)} %concatenate.22.refs_0_, bf16[8,128,512]{2,1,0:T(8,128)(2,1)} %get-tuple-element.312.refs_1_, bf16[8,128,512]{2,1,0:T(8,128)(2,1)} %get-tuple-element.313.refs_2_, bf16[512,1024]{1,0:T(8,128)(2,1)} %get-tuple-element.314.refs_3_, ...), custom_call_target="tpu_custom_call" | custom-call | flops 34359738368 | bytes 16777216 | tf_op jit(solution)/shard_map/head_grad/pallas_call | solution.py:1250
  907.8 5.6 fusion.3
  913.4 111.1 %end.1 = (bf16[4,512,256]{2,1,0:T(8,128)(2,1)}, f32[2,3,128,256]{3,2,1,0:T(8,128)}, f32[2,256,128]{2,1,0:T(8,128)}, f32[2,128,1024]{2,1,0:T(8,128)}, f32[2,1024,128]{2,1,0:T(8,128)}, /*index=5*/f32[64,128]{1,0:T(8,128)}) custom-call(bf16[512,1024]{1,0:T(8,128)(2,1)} %get-tuple-element.318.refs_0_, bf16[8,4,128,1024]{3,2,1,0:T(8,128)(2,1)} %head_grad.5.refs_1_, ...), custom_call_target="tpu_custom_call" | custom-call | bytes 314572800 | tf_op jit(solution)/shard_map/end/pallas_call | solution.py:1913
  1029.4 2.8 bitcast_convert_fusion
  (129 shorter events, 31.5 us)
Async XLA Ops:
  7.2 283.1 %all-gather.5.cloned.1.call-start = ((), (), s32[]{:S(2)}) async-start(), calls=%async_computation | async-start | bytes 17301504 | tf_op jit(solution)/shard_map/all_gather | solution.py:2016
  81.3 342.4 %all-gather.7.cloned.1.call-start = ((), (), s32[]{:S(2)}) async-start(), calls=%async_computation.1 | async-start | bytes 17301504 | tf_op jit(solution)/shard_map/all_gather | solution.py:2016
  81.3 32.3 %copy-start.11 = (s32[24,128]{1,0:T(8,128)S(1)}, s32[24,128]{1,0:T(8,128)}, u32[]{:S(2)}) copy-start(s32[24,128]{1,0:T(8,128)} %get-tuple-element.178) | copy-start | bytes 36868
  111.0 16.4 %collective-permute-start = (bf16[3,512,128]{2,1,0:T(8,128)(2,1)}, bf16[3,512,128]{2,1,0:T(8,128)(2,1)S(1)}, u32[]{:S(2)}, u32[]{:S(2)}) collective-permute-start(bf16[3,512,128]{2,1,0:T(8,128)(2,1)} %get-tuple-element.191), channel_id=1, source_target_pairs={{0,4},{4,8},{8,12},{12,0},{16,20},{20,24},{24,28},{28,16},{1,5},{5... | collective-permute-start | bytes 1179656 | tf_op jit(solution)/shard_map/ppermute | solution.py:2009
  111.6 15.9 %collective-permute-start.1 = (bf16[3,512,128]{2,1,0:T(8,128)(2,1)}, bf16[3,512,128]{2,1,0:T(8,128)(2,1)S(1)}, u32[]{:S(2)}, u32[]{:S(2)}) collective-permute-start(bf16[3,512,128]{2,1,0:T(8,128)(2,1)} %get-tuple-element.192), channel_id=1, source_target_pairs={{0,8},{4,12},{8,0},{12,4},{16,24},{20,28},{24,16},{28,20},{1,9},{5... | collective-permute-start | bytes 1179656 | tf_op jit(solution)/shard_map/ppermute | solution.py:2009
  112.7 26.2 %collective-permute-start.2 = (bf16[3,512,128]{2,1,0:T(8,128)(2,1)}, bf16[3,512,128]{2,1,0:T(8,128)(2,1)S(1)}, u32[]{:S(2)}, u32[]{:S(2)}) collective-permute-start(bf16[3,512,128]{2,1,0:T(8,128)(2,1)} %get-tuple-element.193), channel_id=1, source_target_pairs={{0,12},{4,0},{8,4},{12,8},{16,28},{20,16},{24,20},{28,24},{1,13},{... | collective-permute-start | bytes 1179656 | tf_op jit(solution)/shard_map/ppermute | solution.py:2009
  127.4 11.4 %copy-start.12 = (bf16[3,512,128]{2,1,0:T(8,128)(2,1)}, bf16[3,512,128]{2,1,0:T(8,128)(2,1)S(1)}, u32[]{:S(2)}) copy-start(bf16[3,512,128]{2,1,0:T(8,128)(2,1)S(1)} %collective-permute-done.refs_4_) | copy-start | bytes 1179652
  127.4 11.4 %copy-start.13 = (bf16[3,512,128]{2,1,0:T(8,128)(2,1)}, bf16[3,512,128]{2,1,0:T(8,128)(2,1)S(1)}, u32[]{:S(2)}) copy-start(bf16[3,512,128]{2,1,0:T(8,128)(2,1)S(1)} %collective-permute-done.1.refs_5_) | copy-start | bytes 1179652
  138.9 0.8 copy-start.14
  139.6 11.1 %copy-start.3 = (bf16[512,1024]{1,0:T(8,128)(2,1)S(1)}, bf16[512,1024]{1,0:T(8,128)(2,1)}, u32[]{:S(2)}) copy-start(bf16[512,1024]{1,0:T(8,128)(2,1)} %get-tuple-element.181.refs_0_.refs_1_) | copy-start | bytes 3145732
  148.8 3.5 copy-start.1
  362.3 11.5 %collective-permute-start.3 = (bf16[3,512,128]{2,1,0:T(8,128)(2,1)}, bf16[3,512,128]{2,1,0:T(8,128)(2,1)S(1)}, u32[]{:S(2)}, u32[]{:S(2)}) collective-permute-start(bf16[3,512,128]{2,1,0:T(8,128)(2,1)} %get-tuple-element.215), channel_id=1, source_target_pairs={{0,4},{4,8},{8,12},{12,0},{16,20},{20,24},{24,28},{28,16},{1,5},{5... | collective-permute-start | bytes 1179656 | tf_op jit(solution)/shard_map/ppermute | solution.py:2009
  362.5 12.2 %collective-permute-start.4 = (bf16[3,512,128]{2,1,0:T(8,128)(2,1)}, bf16[3,512,128]{2,1,0:T(8,128)(2,1)S(1)}, u32[]{:S(2)}, u32[]{:S(2)}) collective-permute-start(bf16[3,512,128]{2,1,0:T(8,128)(2,1)} %get-tuple-element.216), channel_id=1, source_target_pairs={{0,8},{4,12},{8,0},{12,4},{16,24},{20,28},{24,16},{28,20},{1,9},{5... | collective-permute-start | bytes 1179656 | tf_op jit(solution)/shard_map/ppermute | solution.py:2009
  362.8 17.4 %collective-permute-start.5 = (bf16[3,512,128]{2,1,0:T(8,128)(2,1)}, bf16[3,512,128]{2,1,0:T(8,128)(2,1)S(1)}, u32[]{:S(2)}, u32[]{:S(2)}) collective-permute-start(bf16[3,512,128]{2,1,0:T(8,128)(2,1)} %get-tuple-element.217), channel_id=1, source_target_pairs={{0,12},{4,0},{8,4},{12,8},{16,28},{20,16},{24,20},{28,24},{1,13},{... | collective-permute-start | bytes 1179656 | tf_op jit(solution)/shard_map/ppermute | solution.py:2009
  373.8 6.5 copy-start.15
  374.7 5.5 copy-start.16
  380.2 0.8 copy-start.17
  423.7 42.8 %copy-start.9 = (bf16[256,1024]{1,0:T(8,128)(2,1)S(1)}, bf16[256,1024]{1,0:T(8,128)(2,1)}, u32[]{:S(2)}) copy-start(bf16[256,1024]{1,0:T(8,128)(2,1)} %get-tuple-element.224) | copy-start | bytes 1572868
  466.5 2.8 copy-start.2
  559.8 13.1 %copy-start.7 = (bf16[4,256,256]{2,1,0:T(8,128)(2,1)S(1)}, bf16[4,256,256]{2,1,0:T(8,128)(2,1)}, u32[]{:S(2)}) copy-start(bf16[4,256,256]{2,1,0:T(8,128)(2,1)} %get-tuple-element.231) | copy-start | bytes 1572868
  559.8 13.1 %copy-start.8 = (bf16[4,256,256]{2,1,0:T(8,128)(2,1)S(1)}, bf16[4,256,256]{2,1,0:T(8,128)(2,1)}, u32[]{:S(2)}) copy-start(bf16[4,256,256]{2,1,0:T(8,128)(2,1)} %get-tuple-element.240) | copy-start | bytes 1572868
  571.1 14.5 %collective-permute-start.6 = (bf16[3,512,128]{2,1,0:T(8,128)(2,1)}, bf16[3,512,128]{2,1,0:T(8,128)(2,1)S(1)}, u32[]{:S(2)}, u32[]{:S(2)}) collective-permute-start(bf16[3,512,128]{2,1,0:T(8,128)(2,1)} %get-tuple-element.253), channel_id=1, source_target_pairs={{0,12},{4,0},{8,4},{12,8},{16,28},{20,16},{24,20},{28,24},{1,13},{... | collective-permute-start | bytes 1179656 | tf_op jit(solution)/shard_map/ppermute | solution.py:2009
  571.4 20.0 %collective-permute-start.7 = (bf16[3,512,128]{2,1,0:T(8,128)(2,1)}, bf16[3,512,128]{2,1,0:T(8,128)(2,1)S(1)}, u32[]{:S(2)}, u32[]{:S(2)}) collective-permute-start(bf16[3,512,128]{2,1,0:T(8,128)(2,1)} %get-tuple-element.254), channel_id=1, source_target_pairs={{0,8},{4,12},{8,0},{12,4},{16,24},{20,28},{24,16},{28,20},{1,9},{5... | collective-permute-start | bytes 1179656 | tf_op jit(solution)/shard_map/ppermute | solution.py:2009
  572.8 18.6 %collective-permute-start.8 = (bf16[3,512,128]{2,1,0:T(8,128)(2,1)}, bf16[3,512,128]{2,1,0:T(8,128)(2,1)S(1)}, u32[]{:S(2)}, u32[]{:S(2)}) collective-permute-start(bf16[3,512,128]{2,1,0:T(8,128)(2,1)} %get-tuple-element.255), channel_id=1, source_target_pairs={{0,4},{4,8},{8,12},{12,0},{16,20},{20,24},{24,28},{28,16},{1,5},{5... | collective-permute-start | bytes 1179656 | tf_op jit(solution)/shard_map/ppermute | solution.py:2009
  572.8 95.8 %collective-permute-start.9 = (bf16[2,4,128,2048]{3,2,1,0:T(8,128)(2,1)}, bf16[2,4,128,2048]{3,2,1,0:T(8,128)(2,1)}, u32[]{:S(2)}, u32[]{:S(2)}) collective-permute-start(bf16[2,4,128,2048]{3,2,1,0:T(8,128)(2,1)} %get-tuple-element.274), channel_id=1, source_target_pairs={{0,16},{4,12},{8,24},{12,4},{16,0},{20,28},{24,8},{28,20},{1,17},{... | collective-permute-start | bytes 12582920 | tf_op jit(solution)/shard_map/ppermute | solution.py:2243
  585.7 5.8 copy-start.18
  591.4 0.8 copy-start.19
  591.4 0.9 copy-start.20
  715.8 55.5 %collective-permute-start.10 = (bf16[2,4,128,1024]{3,2,1,0:T(8,128)(2,1)}, bf16[2,4,128,1024]{3,2,1,0:T(8,128)(2,1)}, u32[]{:S(2)}, u32[]{:S(2)}) collective-permute-start(bf16[2,4,128,1024]{3,2,1,0:T(8,128)(2,1)} %get-tuple-element.290), channel_id=1, source_target_pairs={{0,16},{4,12},{8,24},{12,4},{16,0},{20,28},{24,8},{28,20},{1,17},{... | collective-permute-start | bytes 6291464 | tf_op jit(solution)/shard_map/ppermute | solution.py:2223
  732.2 39.1 %copy-start = (bf16[2,4,128,1024]{3,2,1,0:T(8,128)(2,1)S(1)}, bf16[2,4,128,1024]{3,2,1,0:T(8,128)(2,1)}, u32[]{:S(2)}) copy-start(bf16[2,4,128,1024]{3,2,1,0:T(8,128)(2,1)} %get-tuple-element.288) | copy-start | bytes 6291460
  774.9 29.6 %collective-permute-start.11 = (bf16[4,128,1024]{2,1,0:T(8,128)(2,1)}, bf16[4,128,1024]{2,1,0:T(8,128)(2,1)S(1)}, u32[]{:S(2)}, u32[]{:S(2)}) collective-permute-start(bf16[4,128,1024]{2,1,0:T(8,128)(2,1)} %get-tuple-element.361), channel_id=1, source_target_pairs={{0,8},{4,20},{8,0},{12,28},{16,24},{20,4},{24,16},{28,12},{1,9},{5... | collective-permute-start | bytes 3145736 | tf_op jit(solution)/shard_map/ppermute | solution.py:2240
  801.6 15.6 %collective-permute-start.12 = (bf16[3,512,128]{2,1,0:T(8,128)(2,1)}, bf16[3,512,128]{2,1,0:T(8,128)(2,1)S(1)}, u32[]{:S(2)}, u32[]{:S(2)}) collective-permute-start(bf16[3,512,128]{2,1,0:T(8,128)(2,1)} %get-tuple-element.303), channel_id=1, source_target_pairs={{0,12},{4,0},{8,4},{12,8},{16,28},{20,16},{24,20},{28,24},{1,13},{... | collective-permute-start | bytes 1179656 | tf_op jit(solution)/shard_map/ppermute | solution.py:2009
  801.6 18.7 %collective-permute-start.13 = (bf16[3,512,128]{2,1,0:T(8,128)(2,1)}, bf16[3,512,128]{2,1,0:T(8,128)(2,1)S(1)}, u32[]{:S(2)}, u32[]{:S(2)}) collective-permute-start(bf16[3,512,128]{2,1,0:T(8,128)(2,1)} %get-tuple-element.304), channel_id=1, source_target_pairs={{0,8},{4,12},{8,0},{12,4},{16,24},{20,28},{24,16},{28,20},{1,9},{5... | collective-permute-start | bytes 1179656 | tf_op jit(solution)/shard_map/ppermute | solution.py:2009
  802.4 18.6 %collective-permute-start.14 = (bf16[3,512,128]{2,1,0:T(8,128)(2,1)}, bf16[3,512,128]{2,1,0:T(8,128)(2,1)S(1)}, u32[]{:S(2)}, u32[]{:S(2)}) collective-permute-start(bf16[3,512,128]{2,1,0:T(8,128)(2,1)} %get-tuple-element.305), channel_id=1, source_target_pairs={{0,4},{4,8},{8,12},{12,0},{16,20},{20,24},{24,28},{28,16},{1,5},{5... | collective-permute-start | bytes 1179656 | tf_op jit(solution)/shard_map/ppermute | solution.py:2009
  802.7 105.1 %collective-permute-start.15 = (bf16[2,4,128,2048]{3,2,1,0:T(8,128)(2,1)}, bf16[2,4,128,2048]{3,2,1,0:T(8,128)(2,1)}, u32[]{:S(2)}, u32[]{:S(2)}) collective-permute-start(bf16[2,4,128,2048]{3,2,1,0:T(8,128)(2,1)} %get-tuple-element.321), channel_id=1, source_target_pairs={{0,16},{4,12},{8,24},{12,4},{16,0},{20,28},{24,8},{28,20},{1,17},{... | collective-permute-start | bytes 12582920 | tf_op jit(solution)/shard_map/ppermute | solution.py:2243
  817.2 3.8 copy-start.21
  820.3 0.8 copy-start.22
  821.0 0.7 copy-start.23
  1024.6 8.2 copy-start.6
  1029.4 4.3 copy-start.10
  1029.4 5.0 copy-start.5
  1032.8 2.6 copy-start.4
Sparse Core Ops, SparseCore 0:
  81.4 164.9 all-gather.4
  249.9 121.4 all-gather.6

commit v3 on v2

--- a/solution.py
+++ b/solution.py
@@ -22,7 +22,8 @@
 BROAD = 2 * WIDE
 EPS = 1e-05
 MASKED = -1000000000.0
-ROWS = 64
+ROWS = 256
+CHUNK = 256
 VMEM_BYTES = 60 * 1024 * 1024
 MESH = pl.DeviceIdType.MESH
 
@@ -175,6 +176,10 @@
     def partner(self, way):
         return {"mate": self.mate, "first": self.first, "second": self.second}[way]
 
+    def group(self, p):
+        one, two = 1 - 2 * lax.rem(self.z, 2), 2 - 4 * (self.z // 2)
+        return self.z + (0, two, one, one + two)[p]
+
     def others(self):
         return [{"head": lax.rem(self.z + k, GROUPS)} for k in range(1, GROUPS)]
 
@@ -191,8 +196,13 @@
         self.outs = [jax.ShapeDtypeStruct(array.shape, array.dtype)]
         self.sems = [DMA((2,))]
 
+    def device(self, at):
+        if self.way == "z":
+            return {"head": at.group(1)}
+        return {"dp": at.partner(self.way)}
+
     def peers(self, at):
-        return [{"dp": at.partner(self.way)}], [], 1
+        return [self.device(at)], [], 1
 
     def copy(self, at, ins, outs, sems):
         return pltpu.make_async_remote_copy(
@@ -200,7 +210,7 @@
             dst_ref=outs[0],
             send_sem=sems[0].at[0],
             recv_sem=sems[0].at[1],
-            device_id={"dp": at.partner(self.way)},
+            device_id=self.device(at),
             device_id_type=MESH,
         )
 
@@ -232,10 +242,10 @@
                 dst_ref=outs[0].at[k - 1],
                 send_sem=sems[0].at[0, k - 1],
                 recv_sem=sems[0].at[1, k - 1],
-                device_id={"head": lax.rem(at.z + k, GROUPS)},
+                device_id={"head": at.group(k)},
                 device_id_type=MESH,
             )
-            for k in (2, 1, 3)
+            for k in (1, 2, 3)
         ]
 
     def start(self, *args):
@@ -251,10 +261,12 @@
 
 
 class Turn:
-    aliases = {}
-
-    def __init__(self, array, back):
+    def __init__(self, array, back, half, into=None):
         self.arrays, self.back = [array], back
+        self.aliases = {}
+        if into is not None:
+            self.arrays.append(into)
+            self.aliases = {1: 0}
         if back:
             tokens, wide = array.shape[0], array.shape[1] // GROUPS
             out = (GROUPS, tokens, wide)
@@ -262,6 +274,7 @@
             tokens, wide = array.shape[1:]
             out = (tokens, GROUPS * wide)
         self.wide = wide
+        self.rows = pl.ds(half * (tokens // 2), tokens // 2)
         self.outs = [jax.ShapeDtypeStruct(out, array.dtype)]
         self.sems = [DMA((2, GROUPS)), DMA]
 
@@ -279,12 +292,12 @@
         targets = self.one(at) if self.back else self.many(at)
         for i, (dp, z) in enumerate(targets):
             if self.back:
-                source = ins[0].at[:, pl.ds(i * self.wide, self.wide)]
-                target, slot = outs[0].at[at.lo], at.lo
+                source = ins[0].at[self.rows, pl.ds(i * self.wide, self.wide)]
+                target, slot = outs[0].at[at.lo, self.rows], at.lo
             else:
-                source = ins[0].at[i]
+                source = ins[0].at[i, self.rows]
                 column = pl.multiple_of(at.z * self.wide, self.wide)
-                target, slot = outs[0].at[:, pl.ds(column, self.wide)], at.z
+                target, slot = outs[0].at[self.rows, pl.ds(column, self.wide)], at.z
 
             def remote(i=i, dp=dp, z=z, source=source, target=target, slot=slot):
                 copy = pltpu.make_async_remote_copy(
@@ -319,9 +332,9 @@
             @pl.when((dp != at.dp) | (z != at.z))
             def _(slot=slot):
                 if self.back:
-                    spot = outs[0].at[slot]
+                    spot = outs[0].at[slot, self.rows]
                 else:
-                    spot = outs[0].at[:, pl.ds(slot * self.wide, self.wide)]
+                    spot = outs[0].at[self.rows, pl.ds(slot * self.wide, self.wide)]
                 pltpu.make_async_remote_copy(
                     src_ref=spot,
                     dst_ref=spot,
@@ -334,7 +347,7 @@
 
 class Host:
     def __init__(self, n, parts):
-        self.n, self.parts = n, parts
+        self.n, self.parts, self.turns = n, parts, 0
         self.at = Place() if parts else None
 
     def barrier(self, group=True):
@@ -371,7 +384,22 @@
         for job, *refs in self.parts:
             job.middle(self.at, *refs)
 
+    def tick(self):
+        for job, *refs in self.parts:
+            if isinstance(job, Everywhere) and self.turns < len(job.chunks) + 3:
+                job.tick(self.turns, self.at, *refs)
+        self.turns += 1
+
+    def tick_at(self, step):
+        for job, *refs in self.parts:
+            if isinstance(job, Everywhere):
+                for t in range(len(job.chunks) + 3):
+                    pl.when(step == t)(lambda t=t, job=job, refs=refs: job.tick(t, self.at, *refs))
+        self.turns = 64
+
     def finish(self):
+        while any(isinstance(v[0], Everywhere) for v in self.parts) and self.turns < 64:
+            self.tick()
         for job, *refs in self.parts:
             job.finish(self.at, *refs)
 
@@ -519,6 +547,54 @@
     return [res[u * n : (u + 1) * n] for u in range(units)], res[n * units :]
 
 
+def masks_kernel(n, sc, flags, aux, one, valid, need):
+    tokens = aux.shape[1]
+    rows = tokens // LANES
+    first = lax.broadcasted_iota(jnp.int32, (LANES, LANES), 1) == 0
+    one[...] = jnp.where(lax.broadcasted_iota(jnp.int32, one.shape, 1) == 0, 1.0, 0.0).astype(bf16)
+    long = jnp.max(flags[LONG // LANES : LONG // LANES + 1, 0:1]) == 1
+    alive, sequence = [], []
+    for k in range(n):
+        place = lax.rem(sc[0] + n - k, n)
+        some = jnp.float32(0)
+        for i in range(rows):
+            row = flags[pl.ds(place * rows + i, 1), :].astype(f32)
+            some = jnp.maximum(some, jnp.max(row))
+            column = jnp.transpose(jnp.broadcast_to(row, (LANES, LANES)), (1, 0))
+            spot = slice(i * LANES, (i + 1) * LANES)
+            aux[k, spot, :] = jnp.where(first & (column == 0), MASKED, 0.0).astype(bf16)
+            if k == 0:
+                valid[spot, :] = column[:, 0:1]
+        alive.append(some > 0)
+        sequence.append(place * tokens // SHORT)
+    for i in range(n):
+        for j in range(n):
+            joined = long | (sequence[i] == sequence[j])
+            need[i * n + j] = jnp.where(joined & alive[j], 1, 0).astype(jnp.int32)
+
+
+def masks_call(n, lo, flags):
+    tokens = LONG // n
+    return pl.pallas_call(
+        lambda *refs: masks_kernel(n, *refs),
+        out_shape=[
+            jax.ShapeDtypeStruct((n, tokens, LANES), bf16),
+            jax.ShapeDtypeStruct((tokens, LANES), bf16),
+            jax.ShapeDtypeStruct((tokens, 1), f32),
+            jax.ShapeDtypeStruct((n * n,), jnp.int32),
+        ],
+        grid_spec=pltpu.PrefetchScalarGridSpec(
+            num_scalar_prefetch=1,
+            grid=(),
+            in_specs=[VM],
+            out_specs=[VM, VM, VM, pl.BlockSpec(memory_space=pltpu.SMEM)],
+        ),
+        compiler_params=params(),
+        cost_estimate=cost(0, 2**20),
+        name="masks",
+    )(lo, flags)
+
+
 def head_lanes(value, head):
     lane = lax.broadcasted_iota(jnp.int32, value.shape, 1)
     keep = (lane < DH) if head == 0 else (lane >= DH)
@@ -536,15 +612,37 @@
         vt[r, 1] = jnp.concatenate([turned[DH:], ones], axis=0)
         qs[r] = (qkv[r][0].astype(f32) * (1.0 / math.sqrt(DH))).astype(bf16)
 
-    def each_query(i, carry):
+    halves = jnp.where(
+        lax.broadcasted_iota(jnp.int32, (LANES, LANES), 0) // DH
+        == lax.broadcasted_iota(jnp.int32, (LANES, LANES), 1),
+        1.0,
+        0.0,
+    ).astype(bf16)
+    reach = jnp.zeros((1, LANES), f32)
+    longest = jnp.zeros((1, LANES), f32)
+    for r in range(n):
+        for which, value in ((0, qs[r]), (1, qkv[r][1])):
+            size = jnp.max(dot(value * value, halves), axis=0, keepdims=True)
+            if which:
+                longest = jnp.maximum(longest, size)
+            else:
+                reach = jnp.maximum(reach, size)
+    bounded = jnp.max(reach * longest) < 70.0 * 70.0
+
+    def each_query(plain, i, carry):
         query = qs[i]
         extended = [jnp.concatenate([head_lanes(query, h), one[...]], axis=1) for h in range(2)]
-        top[...] = jnp.full_like(top, -3e38)
+        top[...] = jnp.zeros_like(top) if plain else jnp.full_like(top, -3e38)
         acc[...] = jnp.zeros_like(acc)
 
         def each_key(j, inner):
             @pl.when(need[i * n + j] == 1)
             def _():
+                if plain:
+                    raised = [jnp.exp(dot_nt(kx[j], extended[h])).astype(bf16) for h in range(2)]
+                    for h in range(2):
+                        acc[h] += dot(vt[j, h], raised[h])
+                    return
                 for h in range(2):
                     scores = dot_nt(kx[j], extended[h])
                     before = top[h : h + 1]
@@ -563,7 +661,13 @@
             lse[i, h : h + 1] = top[h : h + 1] + jnp.log(sums[h])
         return carry
 
-    lax.fori_loop(0, n, each_query, 0)
+    @pl.when(bounded)
+    def _():
+        lax.fori_loop(0, n, functools.partial(each_query, True), 0)
+
+    @pl.when(jnp.logical_not(bounded))
+    def _():
+        lax.fori_loop(0, n, functools.partial(each_query, False), 0)
 
 
 def unit_call(kernel, n, need, aux, one, arrays, out_shape, scratch, work, name):
@@ -620,8 +724,10 @@
     for copy in copies:
         copy.start()
     host.start()
+    host.tick()
     for copy in copies:
         copy.wait()
+    host.tick()
     _, lo = group_place(n)
     for k in range(n):
         first = lax.rem(lo + k, n) * (units * LANES)
@@ -634,17 +740,19 @@
         xs[r, :] = (hat * gain + shift).astype(bf16)
 
     row_loop(tokens, ROWS, body)
+    host.tick()
     branch = None
     for g in range(GROUPS):
         term = dot_nt(xs[:, g * HEADS : (g + 1) * HEADS], weight[:, g].reshape(D, HEADS))
         branch = term if branch is None else branch + term
     mid[...] = branch
+    host.tick()
     use[...] = jnp.zeros_like(use)
 
     def finish(r):
         part = mid[r, :]
         use[...] += fold_rows(valid[r, :] * part * part)
-        mid[r, :] = stream[r, :] + part
+        mid[r, :] = stream[r, :].astype(f32) + part
 
     row_loop(tokens, ROWS, finish)
     host.middle()
@@ -714,7 +822,7 @@
             act[step, r, :] = h * half
             slope[0, r, :] = (half + h * bell).astype(bf16)
 
-        row_loop(tokens, 32, body)
+        row_loop(tokens, CHUNK, body)
 
     @pl.when(step == GROUPS)
     def _():
@@ -725,10 +833,10 @@
             total = sum_lanes(sum(fold_lanes(b) for b in blocks)) / FF
             square = sum(fold_lanes((b - total) * (b - total)) for b in blocks)
             rstd = lax.rsqrt(sum_lanes(square) / FF + EPS)
-            mean[r, :] = jnp.broadcast_to(total, (32, LANES))
-            rstd_out[r, :] = jnp.broadcast_to(rstd, (32, LANES))
-
-        row_loop(tokens, 32, body)
+            mean[r, :] = jnp.broadcast_to(total, (CHUNK, LANES))
+            rstd_out[r, :] = jnp.broadcast_to(rstd, (CHUNK, LANES))
+
+        row_loop(tokens, CHUNK, body)
 
     @pl.when(step >= GROUPS)
     def _():
@@ -740,7 +848,7 @@
             hat[0, r, :] = value.astype(bf16)
             normed[0, r, :] = (value * hgain + hshift).astype(bf16)
 
-        row_loop(tokens, 32, body)
+        row_loop(tokens, CHUNK, body)
         acc[...] += dot_nt(normed[0], weight[...].reshape(D, WIDE))
 
     @pl.when(step == 2 * GROUPS - 1)
@@ -755,6 +863,11 @@
             use[1] += fold_rows(keep * out * out)
 
         row_loop(tokens, ROWS, body)
+
+    host.tick_at(step)
+
+    @pl.when(step == 2 * GROUPS - 1)
+    def _():
         host.middle()
         host.finish()
 
@@ -846,7 +959,7 @@
             cross[r, :] += fold_lanes(dx * value)
             dxs[step, r, :] = dx
 
-        row_loop(tokens, 32, body)
+        row_loop(tokens, CHUNK, body)
 
     @pl.when(step == GROUPS)
     def _():
@@ -866,7 +979,7 @@
             inner = dxs[g, r, :] - first[r, 0:1] - hat[0, r, :].astype(f32) * cross[r, 0:1]
             dhid[0, r, :] = (slope[0, r, :].astype(f32) * (rstd_in[r, 0:1] * inner)).astype(bf16)
 
-        row_loop(tokens, 32, body)
+        row_loop(tokens, CHUNK, body)
         acc[...] += dot_nt(dhid[0], weight[...].reshape(D, WIDE))
 
     @pl.when(step == 2 * GROUPS - 1)
@@ -878,7 +991,7 @@
             dy = acc[r, :]
             grads[0] += fold_rows(dy * value)
             grads[1] += fold_rows(dy)
-            grad_out[r, :] = grad[r, :] + norm_back(dy, value, rstd, gain)
+            grad_out[r, :] = grad[r, :].astype(f32) + norm_back(dy, value, rstd, gain)
             gs[r, :] = (value * gain + shift).astype(bf16)
 
         row_loop(tokens, ROWS, body)
@@ -1109,12 +1222,12 @@
     for i, k in enumerate(steps):
         copies[k].wait()
         group, offset = head_columns(n, k)
-        total = None
+        left, right = [], []
         for c, weight in enumerate((wq, wk, wv)):
-            left = jnp.concatenate([blocks[u][k][c] for u in range(units)], axis=1)
-            right = weight[:, group, :, pl.ds(offset, units * LANES)].reshape(D, units * LANES)
-            term = dot_nt(left, right)
-            total = term if total is None else total + term
+            left += [blocks[u][k][c] for u in range(units)]
+            part = weight[:, group, :, pl.ds(offset, units * LANES)]
+            right.append(part.reshape(D, units * LANES))
+        total = dot_nt(jnp.concatenate(left, axis=1), jnp.concatenate(right, axis=1))
         if i == 0:
             acc[...] = total
         else:
@@ -1166,8 +1279,12 @@
     return [res[:n], *res[n:]]
 
 
-def pick_rows(sc, turned, count):
-    return jnp.concatenate([turned[sc[m]] for m in range(count)], axis=0)
+def slot_group(p):
+    return 2 * (p % 2) + p // 2
+
+
+def pick_rows(sc, first, turned, count):
+    return jnp.concatenate([turned[sc[first + m]] for m in range(count)], axis=0)
 
 
 def put_rows(value, extra, outs, spot):
@@ -1181,22 +1298,22 @@
             outs[0][(m,) + spot] = part.astype(bf16)
 
 
-def ffn_grad_kernel(count, added, sc, up_turned, down_turned, dhid, normed, *refs):
+def ffn_grad_kernel(first, count, added, sc, up_turned, down_turned, dhid, normed, *refs):
     extra, outs = (refs[0], refs[1:]) if added else (None, refs)
 
     @pl.when(pl.program_id(0) == 0)
     def _():
-        put_rows(dot(pick_rows(sc, up_turned, count), dhid[0]), extra, outs, (0,))
+        put_rows(dot(pick_rows(sc, first, up_turned, count), dhid[0]), extra, outs, (0,))
 
     @pl.when(pl.program_id(0) == 1)
     def _():
-        put_rows(dot(pick_rows(sc, down_turned, count), normed[0]), extra, outs, (0,))
-
-
-def ffn_grad_call(count, sc, up_turned, down_turned, dhid, normed, extra=None):
+        put_rows(dot(pick_rows(sc, first, down_turned, count), normed[0]), extra, outs, (0,))
+
+
+def ffn_grad_call(first, count, sc, up_turned, down_turned, dhid, normed, extra=None):
     tokens = up_turned.shape[2]
     added = extra is not None
-    at = lambda g, sc: lax.rem(g + sc[count], GROUPS)
+    at = lambda g, sc: jnp.bitwise_xor(slot_group(g), sc[BLOCKS])
     left = pl.BlockSpec(
         (1, tokens, WIDE), lambda j, g, sc: (at(jnp.where(j == 0, g, GROUPS - 1), sc), 0, 0)
     )
@@ -1204,7 +1321,7 @@
     piece = lambda m: pl.BlockSpec((m, 1, LANES, WIDE), lambda j, g, sc: (0, g, 0, j))
     outs = [2, 2] if added else [count]
     return pl.pallas_call(
-        lambda *refs: ffn_grad_kernel(count, added, *refs),
+        lambda *refs: ffn_grad_kernel(first, count, added, *refs),
         out_shape=[jax.ShapeDtypeStruct((m, GROUPS, LANES, 2 * WIDE), bf16) for m in outs],
         grid_spec=pltpu.PrefetchScalarGridSpec(
             num_scalar_prefetch=1,
@@ -1219,36 +1336,37 @@
     )(sc, up_turned, down_turned, dhid, normed, *([extra] if added else []))
 
 
-def head_grad_kernel(n, count, added, sc, in_turned, out_turned, normed, *refs):
+def head_grad_kernel(n, first, count, added, sc, in_turned, out_turned, normed, *refs):
     units = BLOCKS // n
     dqkv, refs = refs[: n * units], refs[n * units :]
     extra, outs = (refs[0], refs[1:]) if added else (None, refs)
-    left = pick_rows(sc, in_turned, count)
+    left = pick_rows(sc, first, in_turned, count)
     for k in range(n):
         for c in range(3):
             right = jnp.concatenate([dqkv[u * n + k][c] for u in range(units)], axis=1)
             value = dot(left, right)
             if n == GROUPS:
-                slot = lax.rem(lax.rem(sc[count + 1] + k, n) + GROUPS - sc[count], GROUPS)
+                slot = slot_group(jnp.bitwise_xor(lax.rem(sc[BLOCKS + 1] + k, n), sc[BLOCKS]))
                 put_rows(value, extra, outs, (slot, slice(None), slice(c * HEADS, (c + 1) * HEADS)))
             else:
-                unit = lax.rem(sc[count + 1] + k, n) * units
+                unit = lax.rem(sc[BLOCKS + 1] + k, n) * units
                 at = pl.multiple_of(c * HEADS + lax.rem(unit, 2) * LANES, LANES)
-                put_rows(value, extra, outs, (unit // 2, slice(None), pl.ds(at, LANES)))
-    left = pick_rows(sc, out_turned, count)
+                slot = slot_group(unit // 2)
+                put_rows(value, extra, outs, (slot, slice(None), pl.ds(at, LANES)))
+    left = pick_rows(sc, first, out_turned, count)
     for g in range(GROUPS):
-        slot = lax.rem(g + GROUPS - sc[count], GROUPS)
+        slot = slot_group(jnp.bitwise_xor(g, sc[BLOCKS]))
         value = dot(left, normed[:, g * HEADS : (g + 1) * HEADS])
         put_rows(value, extra, outs, (slot, slice(None), slice(3 * HEADS, 4 * HEADS)))
 
 
-def head_grad_call(n, count, sc, in_turned, out_turned, dqkv, normed, extra=None):
+def head_grad_call(n, first, count, sc, in_turned, out_turned, dqkv, normed, extra=None):
     tokens = in_turned.shape[2]
     added = extra is not None
     outs = [2, 2] if added else [count]
     inner = (GROUPS, LANES, 4 * HEADS)
     return pl.pallas_call(
-        lambda *refs: head_grad_kernel(n, count, added, *refs),
+        lambda *refs: head_grad_kernel(n, first, count, added, *refs),
         out_shape=[jax.ShapeDtypeStruct((m,) + inner, bf16) for m in outs],
         grid_spec=pltpu.PrefetchScalarGridSpec(
             num_scalar_prefetch=1,
@@ -1312,13 +1430,22 @@
 
 
 class Weights:
-    def __init__(self, at, chunks, shards, gathered, hsem, ssem, rsem, lsem):
+    def __init__(self, at, chunks, shards, gathered, hsem, ssem, rsem, lsem, only=None):
+        self.only = only
         self.at, self.chunks, self.pairs = at, chunks, list(zip(shards, gathered))
         self.hsem, self.ssem, self.rsem = hsem, ssem, rsem
-        self.owns = [
-            pltpu.make_async_copy(shard, out.at[at.dp, at.z], lsem.at[i])
-            for i, (shard, out) in enumerate(self.pairs)
-        ]
+        self.lsem = lsem
+
+    def owns(self):
+        at = self.at
+        copies = []
+        for i, (shard, out) in enumerate(self.pairs):
+            source, target = shard, out.at[at.dp, at.z]
+            if self.only:
+                source = shard.at[:, pl.ds(*self.only)]
+                target = out.at[at.dp, at.z, :, pl.ds(*self.only)]
+            copies.append(pltpu.make_async_copy(source, target, self.lsem.at[i]))
+        return copies
 
     def near(self, c):
         kind, columns = self.chunks[c][0], pl.ds(*self.chunks[c][1:])
@@ -1359,63 +1486,79 @@
         rows = (at.dp, at.first, at.second, at.both)
         return [self.far(3 + i, row, at.mate, c) for i, row in enumerate(rows)]
 
-    def run(self, aside):
-        parts = len(self.chunks)
-        for c in range(min(2, parts)):
+    def begin(self):
+        for c in range(min(2, len(self.chunks))):
             for copy in self.near(c):
                 copy.start()
-        for t in range(parts + 3):
-            for stage in (1, 2, 3):
-                c = t + 1 - stage
-                if 0 <= c < parts:
-                    if stage == 1 and c == 0:
-                        for copy in self.owns:
-                            copy.wait()
-                    for copy in self.hops(stage - 1, c):
+
+    def turn(self, t):
+        parts = len(self.chunks)
+        for stage in (1, 2, 3):
+            c = t + 1 - stage
+            if 0 <= c < parts:
+                if stage == 1 and c == 0:
+                    for copy in self.owns():
                         copy.wait()
-                    for copy in self.hops(stage, c):
-                        copy.start()
-            if t + 2 < parts:
-                for copy in self.near(t + 2):
+                for copy in self.hops(stage - 1, c):
+                    copy.wait()
+                for copy in self.hops(stage, c):
                     copy.start()
+        if t + 2 < parts:
+            for copy in self.near(t + 2):
+                copy.start()
+        c = t - 3
+        if 0 <= c < parts:
+            for copy in self.hops(3, c):
+                copy.wait()
+
+    def run(self, aside):
+        self.begin()
+        for t in range(len(self.chunks) + 3):
+            self.turn(t)
             aside(t)
-            c = t - 3
-            if 0 <= c < parts:
-                for copy in self.hops(3, c):
-                    copy.wait()
-
-
-def weight_chunks(shards):
-    step = 512
+
+
+def weight_chunks(shards, step=512):
     return [(i, c, step) for i, v in enumerate(shards) for c in range(0, v.shape[1], step)]
 
 
-def weight_sems(shards):
-    parts = len(weight_chunks(shards))
+def weight_sems(shards, step=512):
+    parts = len(weight_chunks(shards, step))
     return [DMA((2, 3, parts)), DMA((7, parts)), DMA((7, parts)), DMA((len(shards),))]
 
 
-def gather_call(shards):
-    count = len(shards)
-
-    def kernel(*refs):
-        at = Place()
-        weights = Weights(at, weight_chunks(shards), refs[:count], refs[count : 2 * count], *refs[2 * count :])
-        for copy in weights.owns:
+class Everywhere:
+    def __init__(self, shard, half, into=None):
+        self.arrays = [shard] if into is None else [shard, into]
+        self.aliases = {} if into is None else {1: 0}
+        self.outs = [jax.ShapeDtypeStruct((BLOCKS, GROUPS) + shard.shape, shard.dtype)]
+        wide = shard.shape[1] // 2
+        self.half = (half * wide, wide)
+        self.chunks = weight_chunks([shard], wide // 2)[2 * half : 2 * half + 2]
+        parts = len(self.chunks)
+        self.sems = [DMA((2, 3, parts)), DMA((7, parts)), DMA((7, parts)), DMA((1,))]
+
+    def peers(self, at):
+        partners = [{"dp": v} for v in (at.first, at.second, at.mate)]
+        return at.others() + partners, [], GROUPS + 2
+
+    def weights(self, at, ins, outs, sems):
+        return Weights(at, self.chunks, ins[:1], outs, *sems, only=self.half)
+
+    def start(self, *args):
+        weights = self.weights(*args)
+        for copy in weights.owns():
             copy.start()
-        greet(pltpu.get_barrier_semaphore(), at, at.z, [], 0)
-        weights.run(lambda t: None)
-
-    return pl.pallas_call(
-        kernel,
-        out_shape=[jax.ShapeDtypeStruct((BLOCKS, GROUPS) + v.shape, bf16) for v in shards],
-        in_specs=[HB] * count,
-        out_specs=[HB] * count,
-        scratch_shapes=weight_sems(shards),
-        compiler_params=params(collective_id=7, has_side_effects=True),
-        cost_estimate=cost(0, 150 * 2**20),
-        name="gather",
-    )(*shards)
+        weights.begin()
+
+    def tick(self, t, *args):
+        self.weights(*args).turn(t)
+
+    def middle(self, *args):
+        pass
+
+    def finish(self, *args):
+        pass
 
 
 def start_kernel(
@@ -1438,7 +1581,7 @@
         return [(dp - core + lax.rem(z, 2), g) for g in range(n)]
 
     turn_dp, turn_z = dp - lo + z, lo
-    for copy in weights.owns:
+    for copy in weights.owns():
         copy.start()
     own_vector = pltpu.make_async_copy(vector, vectors.at[z], lsem.at[2])
     own_vector.start()
@@ -1589,10 +1732,11 @@
 
 
 def end_kernel(
-    layers, rows, grads, fmine, fsent, valid, tops, vecs, uses,
-    rows_out, qkv_out, out_out, up_out, down_out, vectors_out,
-    mine, got, pair, last, near, pieces, fm, flast, fnear, vec, vgot, vsum,
-    gsem, hsem, psem, qsem, nsem, zsem, tsem, xsem, vsem, lsem, fsem, esem,
+    layers, rows, grads, fsum, turned, valid, tops, vecs, uses,
+    stream_out, rows_out, qkv_out, out_out, up_out, down_out,
+    gains_out, shifts_out, hgains_out, hshifts_out, rms_out,
+    mine, got, pair, last, near, pieces, crossed, fm, fnear, vec, vgot, vsum,
+    gsem, hsem, psem, qsem, nsem, tsem, xsem, vsem, lsem, esem,
 ):
     at = Place()
     dp, core, bit_x = at.dp, at.core, at.bit_x
@@ -1600,7 +1744,7 @@
     n = GROUPS
     parts = 4
     width = grads.shape[3] // parts
-    step = fmine.shape[2] // parts
+    step = fsum.shape[2] // parts
     wide = rows.shape[1] // n
     sem = pltpu.get_barrier_semaphore()
 
@@ -1616,7 +1760,7 @@
                 grads.at[pl.ds(0, 4), :, :, columns(c)], mine.at[:, :, :, columns(c)], gsem.at[0, c]
             ),
             pltpu.make_async_copy(
-                fmine.at[:, :, broad(c)], fm.at[:, :, broad(c)], gsem.at[1, c]
+                fsum.at[:, :, broad(c)], fm.at[:, :, broad(c)], gsem.at[1, c]
             ),
         ]
 
@@ -1682,34 +1826,43 @@
             device_id_type=MESH,
         )
 
-    def ffn_hop(c):
+    def way(source, target, sems, i, c):
         return pltpu.make_async_remote_copy(
-            src_ref=fsent.at[:, :, broad(c)],
-            dst_ref=flast.at[:, :, broad(c)],
-            send_sem=fsem.at[0, c],
-            recv_sem=fsem.at[1, c],
-            device_id={"dp": at.first},
+            src_ref=source,
+            dst_ref=target,
+            send_sem=sems.at[0, i, c],
+            recv_sem=sems.at[1, i, c],
+            device_id={"head": at.group(2 - i)},
             device_id_type=MESH,
         )
 
-    def around(source, target, cols, sems, c):
-        return [
-            pltpu.make_async_remote_copy(
-                src_ref=source(k, cols),
-                dst_ref=target.at[k - 1, :, cols],
-                send_sem=sems.at[0, k - 1, c],
-                recv_sem=sems.at[1, k - 1, c],
-                device_id={"head": lax.rem(z + k, n)},
-                device_id_type=MESH,
-            )
-            for k in (2, 1, 3)
-        ]
-
-    def head_around(c):
-        return around(lambda k, cols: mine.at[0, k, :, cols], near, columns(c), nsem, c)
-
-    def ffn_around(c):
-        return around(lambda k, cols: fm.at[k, :, cols], fnear, broad(c), esem, c)
+    def head_way(i, c):
+        if i == 0:
+            source, target = mine.at[0, pl.ds(2, 2), :, columns(c)], near.at[pl.ds(0, 2), :, columns(c)]
+        else:
+            source, target = mine.at[0, 1, :, columns(c)], near.at[2, :, columns(c)]
+        return way(source, target, nsem, i, c)
+
+    def ffn_way(i, c):
+        if i == 0:
+            source, target = fm.at[pl.ds(2, 2), :, broad(c)], fnear.at[pl.ds(0, 2), :, broad(c)]
+        else:
+            source, target = fm.at[1, :, broad(c)], fnear.at[2, :, broad(c)]
+        return way(source, target, esem, i, c)
+
+    def head_between(c):
+        head_way(0, c).wait()
+        for k in range(2):
+            value = mine[0, k, :, columns(c)].astype(f32) + near[k, :, columns(c)].astype(f32)
+            mine[0, k, :, columns(c)] = value.astype(bf16)
+        head_way(1, c).start()
+
+    def ffn_between(c):
+        ffn_way(0, c).wait()
+        for k in range(2):
+            value = fm[k, :, broad(c)].astype(f32) + fnear[k, :, broad(c)].astype(f32)
+            fm[k, :, broad(c)] = value.astype(bf16)
+        ffn_way(1, c).start()
 
     def add(count, other, c):
         def body(i, carry):
@@ -1761,14 +1914,12 @@
 
     cross = pltpu.make_async_remote_copy(
         src_ref=pieces.at[1 - bit_x],
-        dst_ref=rows_out.at[pl.ds(2 * bit_x, 2)],
+        dst_ref=crossed,
         send_sem=xsem.at[0],
         recv_sem=xsem.at[1],
         device_id={"dp": at.by_x},
         device_id_type=MESH,
     )
-    stay = pltpu.make_async_copy(pieces.at[bit_x], rows_out.at[pl.ds(2 * bit_x, 2)], lsem.at[1])
-
     def vector_near(k):
         return pltpu.make_async_remote_copy(
             src_ref=vec.at[lax.rem(z + k, n)],
@@ -1803,7 +1954,6 @@
 
     row_copies("start")
     for c in range(parts):
-        ffn_hop(c).start()
         hop(0, c).start()
     for k in range(1, n):
         vector_near(k).start()
@@ -1816,16 +1966,7 @@
             hop(0, c).wait()
             add(4, lambda m, g, c=c: got[m, g, :, columns(c)], c)
             hop(1, c).start()
-            ffn_hop(c).wait()
-
-            def body(g, carry, c=c):
-                value = fm[g, :, broad(c)].astype(f32) + flast[g, :, broad(c)].astype(f32)
-                fm[g, :, broad(c)] = value.astype(bf16)
-                return carry
-
-            lax.fori_loop(0, GROUPS, body, 0)
-            for copy in ffn_around(c):
-                copy.start()
+            ffn_way(0, c).start()
         c = t - 1
         if 0 <= c < parts:
             hop(1, c).wait()
@@ -1835,8 +1976,7 @@
         if 0 <= c < parts:
             hop(2, c).wait()
             add(1, lambda m, g, c=c: last[g, :, columns(c)], c)
-            for copy in head_around(c):
-                copy.start()
+            head_way(0, c).start()
         if t == 1:
             for k in range(1, n):
                 vector_near(k).wait()
@@ -1852,43 +1992,64 @@
             row_copies("wait")
             row_arrivals()
             cross.start()
-            stay.start()
+        if t == 3:
+            stream_out[...] = turned[...].astype(f32)
         if t == 4:
             for l in range(1, layers):
-                heads, hnear, ups, unear, downs, dnear = tops[6 * l - 6 : 6 * l]
+                heads, heads_other, wide_own, wide_other = tops[4 * l - 4 : 4 * l]
                 for c in range(parts):
                     cols = slice(c * width, (c + 1) * width)
-                    put_head(l, c, total_of(heads[0, :, cols], [hnear[k, :, cols] for k in range(3)]))
-                up_out[l] = total_of(ups[0], [unear[k] for k in range(3)])
-                down_out[l] = jnp.transpose(total_of(downs[0], [dnear[k] for k in range(3)]), (1, 0))
+                    put_head(l, c, total_of(heads[0, :, cols], [heads_other[:, cols]]))
+                up_out[l] = total_of(wide_own[0, :, :WIDE], [wide_other[:, :WIDE]])
+                down = total_of(wide_own[0, :, WIDE:], [wide_other[:, WIDE:]])
+                down_out[l] = jnp.transpose(down, (1, 0))
+        c = t - 1
+        if 0 <= c < parts:
+            ffn_between(c)
+        c = t - 3
+        if 0 <= c < parts:
+            head_between(c)
         c = t - 4
         if 0 <= c < parts:
-            for copy in ffn_around(c):
-                copy.wait()
-            value = total_of(fm[0, :, broad(c)], [fnear[k, :, broad(c)] for k in range(3)])
+            ffn_way(1, c).wait()
+            value = total_of(fm[0, :, broad(c)], [fnear[2, :, broad(c)]])
             if c < parts // 2:
                 up_out[0, :, broad(c)] = value
             else:
                 down_out[0, pl.ds(c * step - WIDE, step), :] = jnp.transpose(value, (1, 0))
     for c in range(parts):
-        for copy in head_around(c):
-            copy.wait()
-        others = [near[k, :, columns(c)] for k in range(3)]
-        put_head(0, c, total_of(mine[0, 0, :, columns(c)], others))
-    vectors_out[...] = vsum[3]
+        head_way(1, c).wait()
+        put_head(0, c, total_of(mine[0, 0, :, columns(c)], [near[2, :, columns(c)]]))
+    for l in range(layers):
+        base = 28 * l
+        for kind, (norm_out, hid_out) in enumerate(
+            ((gains_out, hgains_out), (shifts_out, hshifts_out))
+        ):
+            for i in range(3):
+                at_row = base + (3 * kind + i) * 2
+                parts_of = [vsum[3, at_row + p : at_row + p + 1, :] for p in range(2)]
+                norm_out[l, i : i + 1, :] = jnp.concatenate(parts_of, axis=1)
+            at_row = base + 12 + 8 * kind
+            parts_of = [vsum[3, at_row + p : at_row + p + 1, :] for p in range(BLOCKS)]
+            hid_out[l : l + 1, :] = jnp.concatenate(parts_of, axis=1)
+    totals = sum_lanes(vsum[3, 28 * layers : 31 * layers + 1, :])
+    rms = jnp.sqrt(totals[: 3 * layers] / totals[3 * layers :])
+    rms_out[0 : 3 * layers, :] = jnp.broadcast_to(rms, (3 * layers, LANES))
     cross.wait()
-    stay.wait()
-
-
-def end_call(rows, grads, fmine, fsent, valid, tops, vecs, uses):
+    for c2 in range(2):
+        rows_out[2 * bit_x + c2] = pieces[bit_x, c2].astype(f32)
+        rows_out[2 - 2 * bit_x + c2] = crossed[c2].astype(f32)
+
+
+def end_call(rows, grads, fsum, turned, valid, tops, vecs, uses):
     parts = 4
     layers = len(vecs) // 4
     tokens = rows.shape[0]
     wide = rows.shape[1] // GROUPS
     block = grads.shape[1:]
-    broad = fmine.shape
+    broad = fsum.shape
     vector = (vector_rows(layers), LANES)
-    inputs = [rows, grads, fmine, fsent, valid, *tops, *vecs, *uses]
+    inputs = [rows, grads, fsum, turned, valid, *tops, *vecs, *uses]
 
     def spec(i, v):
         if i % 2 == 0:
@@ -1903,22 +2064,29 @@
             refs = refs[len(values) :]
         end_kernel(layers, *fixed, *lists, *refs)
 
-    outs = [
-        jax.ShapeDtypeStruct((layers, 3, LANES, HEADS), f32),
-        jax.ShapeDtypeStruct((layers, HEADS, LANES), f32),
-        jax.ShapeDtypeStruct((layers, LANES, WIDE), f32),
-        jax.ShapeDtypeStruct((layers, WIDE, LANES), f32),
-        jax.ShapeDtypeStruct(vector, f32),
+    dims = [
+        turned.shape,
+        turned.shape,
+        (layers, 3, LANES, HEADS),
+        (layers, HEADS, LANES),
+        (layers, LANES, WIDE),
+        (layers, WIDE, LANES),
+        (layers, 3, HEADS),
+        (layers, 3, HEADS),
+        (layers, WIDE),
+        (layers, WIDE),
+        (8 * (-(-3 * layers // 8)), LANES),
     ]
+    outs = [jax.ShapeDtypeStruct(d, f32) for d in dims]
     return pl.pallas_call(
         kernel,
-        out_shape=[jax.ShapeDtypeStruct((GROUPS, tokens, wide), bf16)] + outs,
+        out_shape=outs,
         grid=(1,),
-        in_specs=[HB] * 4
-        + [whole(valid.shape)]
+        in_specs=[HB] * 3
+        + [whole(turned.shape), whole(valid.shape)]
         + [spec(i, v) for i, v in enumerate(tops)]
         + [whole(v.shape) for v in (*vecs, *uses)],
-        out_specs=[HB] + [whole(v.shape) for v in outs],
+        out_specs=[whole(v.shape) for v in outs],
         scratch_shapes=[
             pltpu.VMEM((4,) + block, bf16),
             pltpu.VMEM((4,) + block, bf16),
@@ -1926,7 +2094,7 @@
             pltpu.VMEM(block, bf16),
             pltpu.VMEM((3,) + block[1:], bf16),
             pltpu.VMEM((2, 2, tokens, wide), bf16),
-            pltpu.VMEM(broad, bf16),
+            pltpu.VMEM((2, tokens, wide), bf16),
             pltpu.VMEM(broad, bf16),
             pltpu.VMEM((3,) + broad[1:], bf16),
             pltpu.VMEM((GROUPS,) + vector, f32),
@@ -1936,14 +2104,12 @@
             DMA((2, parts)),
             DMA((2, parts)),
             DMA((2, parts)),
-            DMA((2, 3, parts)),
-            DMA((2, 3, parts)),
+            DMA((2, 2, parts)),
             DMA((2, 4)),
             DMA((2,)),
             DMA((2, 6)),
             DMA((2,)),
-            DMA((2, parts)),
-            DMA((2, 3, parts)),
+            DMA((2, 2, parts)),
         ],
         compiler_params=params(collective_id=6, has_side_effects=True),
         cost_estimate=cost(0, 300 * 2**20),
@@ -1990,16 +2156,14 @@
         self.one_way = [(i, i ^ core_zero[i % 2]) for i in range(n_dp)]
         self.other_way = [(i, i ^ core_zero[1 - i % 2]) for i in range(n_dp)]
         self.core = [(i, i ^ 1) for i in range(n_dp)]
-        ends = [jnp.int32(0), self.lo]
-        self.all_rows = jnp.stack([jnp.int32(i) for i in range(BLOCKS)] + ends)
         if self.fast:
             step = jnp.where(self.own % 2 == 0, 2, 4).astype(jnp.int32)
             mine = [jnp.int32(0), step, 6 - step, jnp.int32(6)]
             theirs = [jnp.int32(0), 6 - step, step, jnp.int32(6)]
-            ends = [self.z, self.lo]
-            self.even = jnp.stack([self.own ^ v for v in mine] + ends)
-            self.odd = jnp.stack([self.own ^ v ^ 1 for v in theirs] + ends)
-            self.pieces = jnp.concatenate([self.even[:4], self.odd])
+            rows = [self.own ^ v for v in mine] + [self.own ^ v ^ 1 for v in theirs]
+            self.table = jnp.stack(rows + [self.z, self.lo])
+        else:
+            self.table = jnp.stack([jnp.int32(i) for i in range(BLOCKS)] + [jnp.int32(0), self.lo])
 
     def shift(self, value, k):
         n = self.n
@@ -2007,6 +2171,9 @@
             return value
         pairs = [(i, (i // n) * n + (i + k) % n) for i in range(self.n_dp)]
         return lax.ppermute(value, "dp", pairs)
+
+    def across(self, value, bits):
+        return lax.ppermute(value, "head", [(i, i ^ bits) for i in range(self.n)])
 
     def spin(self, value, k):
         n = self.n
@@ -2034,6 +2201,7 @@
 
     def scatter(self, full, widths):
         columns = full.shape[3]
+        full = jnp.stack([full[:, slot_group(g)] for g in range(GROUPS)], axis=1)
         if self.fast:
             full = full.reshape(BLOCKS * GROUPS, LANES, columns)
         else:
@@ -2118,6 +2286,7 @@
     order = Order()
 
     flags = jnp.concatenate([valid_mask, buckets])
+    flags = jnp.pad(flags, (0, -flags.shape[0] % 1024))
     vectors = [
         v.reshape(layers, -1) for v in (norm_gains, norm_shifts, hidden_gains, hidden_shifts)
     ]
@@ -2126,12 +2295,11 @@
     if net.fast:
         small, large = pack_call(qkv_weight, out_weight, up_weight, down_weight)
         rows = stream_in.astype(bf16).reshape(n, tokens, D // n)
-        flags = jnp.pad(flags, (0, -flags.shape[0] % 1024)).reshape(-1, LANES)
+        flags = flags.reshape(-1, LANES)
         vector = packed.reshape(-1, LANES)
-        started = order(start_call, small[:1], rows, vector, flags, first=1)
-        (narrow[0],), stream, _, packed, flags = started
-        flags = flags.reshape(-1)
-        broad[0] = net.gather(order.hold(large[0]))
+        started = order(start_call, [small[0], large[0]], rows, vector, flags, first=1)
+        (narrow[0], broad[0]), stream, _, packed, flags = started
+        narrow[1:] = [net.gather(order.hold(v)) for v in small[1:]]
     else:
         for l in range(layers):
             narrow[l], broad[l] = net.gather_any(
@@ -2140,22 +2308,9 @@
         stream = net.rows_in_end(net.rows_in(stream_in))
         flags = lax.ppermute(flags, ("dp", "head"), net.turn(0))
         packed = lax.all_gather(packed.reshape(-1, LANES), "head")
-    slab_mask = flags[:LONG].reshape(n, tokens)
-    bucket = flags[LONG]
-    rel_blocks = (net.lo - jnp.arange(n)) % n
-    rel_mask = jnp.take(slab_mask, rel_blocks, axis=0)
-    lane = jnp.arange(LANES)[None, None, :] == 0
-    aux = jnp.where((rel_mask[:, :, None] == 0) & lane, MASKED, 0.0).astype(bf16)
-    one = jnp.broadcast_to((jnp.arange(LANES)[None, :] == 0), (tokens, LANES)).astype(bf16)
-    sequence = jnp.where(bucket == 1, 0, (rel_blocks * tokens) // SHORT)
-    alive = jnp.sum(rel_mask, axis=1) > 0
-    need = ((sequence[:, None] == sequence[None, :]) & alive[None, :]).astype(jnp.int32)
-    need = need.reshape(n * n)
-    valid = lax.dynamic_index_in_dim(slab_mask, net.lo, 0, False).astype(f32)[:, None]
+    aux, one, valid, need = masks_call(n, net.lo[None], flags.reshape(-1, LANES))
 
     low = stream
-    stream = stream.astype(f32)
-    halves = lambda v, axis: jnp.split(v, 2, axis=axis)
     cot = cotangent.astype(bf16).reshape(n, tokens, D // n)
     kept = []
     usage = []
@@ -2163,28 +2318,25 @@
     for l in range(layers):
         ahead = net.fast and l + 1 < layers
         parts, _ = order(qkv_call, n, next(idents), [], l, low, packed, narrow[l], first=4)
+        if ahead:
+            broad[l + 1] = net.gather(order.hold(large[l + 1]))
         parts = [parts[0]] + [[net.shift(v, k) for k, v in enumerate(p)] for p in parts[1:]]
         att, lse = [], []
         for p in parts:
             outs = order(attn_call, n, need, aux, one, p, first=2)
             att.append(outs[0])
             lse.append(outs[1])
-        if ahead:
-            broad[l + 1] = net.gather(order.hold(large[l + 1]))
-        rows_job = []
-        if net.fast and l + 1 == layers:
-            rows_job = [Turn(half, False) for half in halves(cot, 1)]
-        mid, rows, use_branch, *late = order(
-            proj_call, n, next(idents), rows_job[1:], l, valid, stream, packed, narrow[l], att,
-            first=5,
+        last = net.fast and l + 1 == layers
+        jobs = [Turn(cot, False, 0)] if last else []
+        mid, rows, use_branch, *extra = order(
+            proj_call, n, next(idents), jobs, l, valid, stream, packed, narrow[l], att, first=5
         )
-        if ahead:
-            (narrow[l + 1],) = order(gather_call, [order.hold(small[l + 1])], first=0)
-        slope, hat, normed, low_mid, rstd, stream, next_low, use_rest, *early = order(
-            ffn_call, n, next(idents), rows_job[:1], l, valid, mid, packed, broad[l], first=5
+        jobs = [Turn(cot, False, 1, extra[0])] if last else []
+        slope, hat, normed, low_mid, rstd, stream, next_low, use_rest, *extra = order(
+            ffn_call, n, next(idents), jobs, l, valid, mid, packed, broad[l], first=5
         )
-        if rows_job:
-            grad = jnp.concatenate(early + late, axis=0).astype(f32)
+        if last:
+            grad = extra[0]
         usage += [use_branch, use_rest]
         kept.append((low, parts, att, lse, rows, slope, hat, normed, low_mid, rstd))
         low = next_low
@@ -2193,6 +2345,7 @@
         grad = net.rows_in_end(net.rows_in(cotangent)).astype(f32)
     if not net.fast:
         grad = net.rows_in_end(net.rows_in(cotangent)).astype(f32)
+    low_out = low
     units = BLOCKS // n
     ffn_grads, head_grads = [None] * layers, [None] * layers
     vectors, tops = [None] * layers, []
@@ -2203,28 +2356,30 @@
         last = net.fast and l + 1 == layers
         jobs = []
         if last:
-            jobs = [Turn(half, True) for half in halves(stream.astype(bf16), 0)]
+            jobs = [Turn(low_out, True, 0)]
         if more:
-            ffn_mine, sent = net.add_pair(order.hold(ffn_keep), ffn_pair)
-            jobs = [Hop(head_odd, "mate"), Hop(sent, "first")]
+            jobs = [Hop(head_odd, "mate")]
         dhid, grad_turned, ffn_turned, grad, hgrads, grads2, *extra = order(
-            ffn_back_call, n, next(idents), jobs[:1] if last else jobs, l, grad, hat, slope, rstd,
+            ffn_back_call, n, next(idents), jobs, l, grad, hat, slope, rstd,
             low_mid, packed, broad[l], first=4,
         )
         ffn_args = (ffn_turned, grad_turned, dhid, normed)
         if net.fast:
             moved = extra
             if more:
-                ups = net.add_last(ffn_mine[..., :WIDE], extra[1][..., :WIDE])
-                downs = net.add_last(ffn_mine[..., WIDE:], extra[1][..., WIDE:])
                 head_keep, send = order(
-                    head_grad_call, n, 4, net.even, *head_args, extra[0], first=3
+                    head_grad_call, n, 0, 4, net.table, *head_args, extra[0], first=4
                 )
                 head_pair = lax.ppermute(order.hold(send), "dp", net.other_way)
-            (odd,) = order(ffn_grad_call, 4, net.odd, *ffn_args, first=2)
-            jobs = [Hop(odd, "mate")] + ([Near(ups)] if more else jobs[1:])
+            (odd,) = order(ffn_grad_call, 4, 4, net.table, *ffn_args, first=3)
+            jobs = [Hop(odd, "mate")]
+            if more:
+                ffn_mine, sent = net.add_pair(order.hold(ffn_keep), ffn_pair)
+                ffn_last = lax.ppermute(order.want(sent), "dp", net.one_way)
+            if last:
+                jobs.append(Turn(low_out, True, 1, moved[0]))
         else:
-            (full,) = order(ffn_grad_call, BLOCKS, net.all_rows, *ffn_args, first=2)
+            (full,) = order(ffn_grad_call, 0, BLOCKS, net.table, *ffn_args, first=3)
             ffn_grads[l] = net.scatter(full, (WIDE, WIDE))
         res = order(
             proj_back_call, n, next(idents), jobs, l, grad, packed, narrow[l], rows, first=4
@@ -2232,15 +2387,18 @@
         datt, (out_turned, normed_mid, grads1, *extra) = res[:units], res[units:]
         if net.fast:
             if last:
-                stream_out = jnp.concatenate([moved[0], extra[1]], axis=1)
-                stream_out = stream_out.reshape(LONG, D // n).astype(f32)
+                turned = extra[1]
             if more:
-                unear = extra[1]
                 head_mine, sent = net.add_pair(order.hold(head_keep), head_pair)
                 head_last = lax.ppermute(sent, "dp", net.one_way)
                 order.want(sent)
-            ffn_keep, send = order(ffn_grad_call, 4, net.even, *ffn_args, extra[0], first=2)
-            ffn_pair = lax.ppermute(order.hold(send), "dp", net.other_way)
+            ffn_keep, send = order(ffn_grad_call, 0, 4, net.table, *ffn_args, extra[0], first=3)
+            ffn_send = send
+            if more:
+                ffn_sum = order.want(net.add_last(order.hold(ffn_mine), ffn_last))
+                ffn_near = net.across(ffn_sum[2:], 1)
+            if l == 0:
+                ffn_pair = lax.ppermute(order.hold(send), "dp", net.other_way)
         dparts, ready = [], []
         for u in range(units):
             ready += [net.shift(v, -k) for k, v in enumerate(dparts)]
@@ -2249,7 +2407,14 @@
             )
             if more and u == 0:
                 head_sum = order.want(net.add_last(order.hold(head_mine), head_last))
-        jobs = [Near(downs), Near(head_sum)] if more else []
+                ffn_own = order.want(net.add_last(order.hold(ffn_sum[:2]), ffn_near))
+        jobs = []
+        if net.fast and l == 0:
+            ffn_mine, sent = net.add_pair(order.hold(ffn_keep), ffn_pair)
+            ffn_last = lax.ppermute(order.want(sent), "dp", net.one_way)
+        if more:
+            ffn_other = net.across(order.hold(ffn_own[1]), 2)
+            head_near = net.across(order.hold(head_sum)[2:], 1)
         dlast, grad, in_turned, grads0, grad_low, *extra = order(
             qkv_back_call, n, next(idents), jobs, l, grad, low, packed, narrow[l], ready, dparts,
             first=4,
@@ -2258,27 +2423,29 @@
         vectors[l] = [grads0, grads1, grads2, hgrads]
         if net.fast:
             if more:
-                tops = [head_sum, extra[1], ups, unear, downs, extra[0]] + tops
+                head_own = order.want(net.add_last(order.hold(head_sum[:2]), head_near))
+                tops = [head_own, net.across(head_own[1], 2), ffn_own, ffn_other] + tops
             if l:
-                (head_odd,) = order(head_grad_call, n, 4, net.odd, *head_args, first=3)
+                ffn_pair = lax.ppermute(order.hold(ffn_send), "dp", net.other_way)
+                (head_odd,) = order(head_grad_call, n, 4, 4, net.table, *head_args, first=4)
             else:
-                (full,) = order(head_grad_call, n, BLOCKS, net.pieces, *head_args, first=3)
+                (full,) = order(head_grad_call, n, 0, BLOCKS, net.table, *head_args, first=4)
         else:
-            (full,) = order(head_grad_call, n, BLOCKS, net.all_rows, *head_args, first=3)
+            (full,) = order(head_grad_call, n, 0, BLOCKS, net.table, *head_args, first=4)
             head_grads[l] = net.scatter(full, (HEADS,) * 4)
     vectors = [v for part in vectors for v in part]
     if net.fast:
-        ffn_mine, sent = net.add_pair(order.hold(ffn_keep), ffn_pair)
-        moved, qkv_grad, out_grad, up_grad, down_grad, summed = order(
-            end_call, grad_low, full, ffn_mine, sent, valid, tops, vectors, usage
+        ffn_sum = net.add_last(order.hold(ffn_mine), ffn_last)
+        (
+            stream_out, stream_grad, qkv_grad, out_grad, up_grad, down_grad,
+            gains_grad, shifts_grad, hidden_gains_grad, hidden_shifts_grad, usage_rms,
+        ) = order(
+            end_call, grad_low, full, ffn_sum, turned, valid, tops, vectors, usage
         )
-        stream_grad = moved.reshape(LONG, D // n).astype(f32)
+        stream_out = stream_out.reshape(LONG, D // n)
+        stream_grad = stream_grad.reshape(LONG, D // n)
         stacked = [qkv_grad, out_grad, up_grad, down_grad]
-        norms = summed[: 28 * layers].reshape(layers, 28, LANES)
-        hids = norms[:, 12:].reshape(layers, 2, FF // n)
-        norms = norms[:, :12].reshape(layers, 2, 3, D // n)
-        totals = jnp.sum(summed[28 * layers : 31 * layers + 1], axis=1)
-        usage_rms = jnp.sqrt(totals[:-1] / totals[-1]).reshape(layers, 3)
+        usage_rms = usage_rms[: 3 * layers, 0].reshape(layers, 3)
     else:
         stream_out = net.rows_out_end(net.rows_out(stream))
         stream_grad = net.rows_out_end(net.rows_out(grad))
@@ -2306,8 +2473,8 @@
                 (qkv, heads[:, 3 * width :].T, ffn_grads[l][:, :half], ffn_grads[l][:, half:].T)
             )
         stacked = [jnp.stack([weight_grads[l][k] for l in range(layers)]) for k in range(4)]
-    gains_grad, shifts_grad = norms[:, 0], norms[:, 1]
-    hidden_gains_grad, hidden_shifts_grad = hids[:, 0], hids[:, 1]
+        gains_grad, shifts_grad = norms[:, 0], norms[:, 1]
+        hidden_gains_grad, hidden_shifts_grad = hids[:, 0], hids[:, 1]
     return (
         stream_out,
         stream_grad,

time: 1060 us -> 997 us (0.941)
  Pallas kernels: 934 us -> 833 us
  starting transfers between devices: 10.7 us -> 52.4 us
    pallas_call x9, Pallas kernels: 300 us -> 181 us  [the longest x1 95.3 us: end_call(): pl.pallas_call(kernel, out_shape=outs, grid=(1,), in_specs=[HB] * 3 + [wh...]
    pallas_call x11, Pallas kernels: 451 us -> 371 us  [remote_call(): pl.pallas_call(kernel, out_shape=list(out_shape) + job_out, grid=grid, in...]
    pallas_call x1, Pallas kernels: 65.3 us -> 144 us  [start_call(): pl.pallas_call(kernel, out_shape=[jax.ShapeDtypeStruct((BLOCKS, GROUPS) +...]
    ppermute x0 -> x7, starting transfers between devices: none -> 29.3 us  [the longest x4 26.3 us: across(): return lax.ppermute(value, 'head', [(i, i ^ bits) for i in range(self.n)])]
    pallas_call x8, Pallas kernels: 81.7 us -> 108 us  [unit_call(): pl.pallas_call(lambda *refs: kernel(n, *refs), out_shape=out_shape, grid_...]
    ppermute x12, waiting for transfers between devices: 27.5 us -> 11 us  [shift(): return lax.ppermute(value, 'dp', pairs)]
    all_gather x2, waiting for transfers between devices: 0.04 us -> 16 us  [gather(): lax.all_gather(shard, ('dp', 'head')).reshape(BLOCKS, GROUPS, LANES, -1)]
    ppermute x12, starting transfers between devices: 7.58 us -> 19.9 us  [shift(): return lax.ppermute(value, 'dp', pairs)]
  transfers between devices with their start and end apart: 18 -> 24, of which waited for: 6 -> 6; matrix products, arithmetic and copies ran while one was open for 2% -> 3% of each run, Pallas kernels for 55% -> 43%
where the time goes in v3:
time: 997 us; the launch traced here: 984 us
  Pallas kernels  833 us (84%)
  starting transfers between devices  52.4 us (5%)
  other arithmetic  30.7 us (3%)
  waiting for transfers between devices  30.4 us (3%)
  local copies, waits for them, and re-layouts  21.9 us (2%)
  between operations  15.5 us (2%)
    pallas_call x11, Pallas kernels, remote_call(): pl.pallas_call(kernel, out_shape=list(out_shape) + job_out, grid=grid, in...  371 us
    pallas_call x1, Pallas kernels, start_call(): pl.pallas_call(kernel, out_shape=[jax.ShapeDtypeStruct((BLOCKS, GROUPS) +...  144 us
    pallas_call x8, Pallas kernels, unit_call(): pl.pallas_call(lambda *refs: kernel(n, *refs), out_shape=out_shape, grid_...  108 us
    pallas_call x1, Pallas kernels, end_call(): pl.pallas_call(kernel, out_shape=outs, grid=(1,), in_specs=[HB] * 3 + [wh...  95.3 us
    pallas_call x4, Pallas kernels, ffn_grad_call(): pl.pallas_call(lambda *refs: ffn_grad_kernel(first, count, added, *refs),...  54.2 us
    pallas_call x3, Pallas kernels, head_grad_call(): pl.pallas_call(lambda *refs: head_grad_kernel(n, first, count, added, *re...  29.5 us
    ppermute x4, starting transfers between devices, across(): return lax.ppermute(value, 'head', [(i, i ^ bits) for i in range(self.n)])  26.3 us
    pallas_call x1, Pallas kernels, plain_call(): pl.pallas_call(lambda *refs: body(Host(n, []), *refs), out_shape=out_shap...  25.8 us
  transfers between devices with their start and end apart: 24, of which 6 were waited for; matrix products, arithmetic and copies ran while one was open for 3% of the time, Pallas kernels for 43%

profile of v3, /device:TPU:0, one launch (start us, length us, event | category | flops | bytes accessed | tf_op | source)
XLA Modules:
  0.0 983.9 jit_solution(4693070869626681094)
XLA Ops:
  10.6 2.7 convert_element_type.135
  13.2 2.8 pack.1
  16.0 144.3 %start.1 = (bf16[8,4,128,1024]{3,2,1,0:T(8,128)(2,1)}, bf16[8,4,128,2048]{3,2,1,0:T(8,128)(2,1)}, bf16[512,1024]{1,0:T(8,128)(2,1)}, bf16[2,512,256]{2,1,0:T(8,1...) custom-call(bf16[128,1024]{1,0:T(8,128)(2,1)} %get-tuple-element.186.refs_0_, ...), custom_call_target="tpu_custom_call" | custom-call | bytes 314572800 | tf_op jit(solution)/shard_map/start/pallas_call | solution.py:1704
  160.4 26.8 %qkv.4 = (bf16[3,512,128]{2,1,0:T(8,128)(2,1)}, bf16[3,512,128]{2,1,0:T(8,128)(2,1)}, bf16[3,512,128]{2,1,0:T(8,128)(2,1)}, bf16[3,512,128]{2,1,0:T(8,128)(2,1)}...) custom-call(bf16[512,1024]{1,0:T(8,128)(2,1)} %get-tuple-element.209, ...), custom_call_target="tpu_custom_call" | custom-call | flops 32212254720 | bytes 10485760 | tf_op jit(solution)/shard_map/qkv/pallas_call | solution.py:459
  189.9 2.0 masks.1
  191.8 9.9 %attention.4 = (bf16[4,512,128]{2,1,0:T(8,128)(2,1)}, f32[4,8,512]{2,1,0:T(8,128)}) custom-call(s32[16]{0:T(128)} %get-tuple-element.191.refs_0_, bf16[4,512,128]{2,1,0:T(8,128)(2,1)} %get-tuple-element.309.refs_1_, bf16[512,128]{1,0:T(8,128)(2,1)} %get-tuple-element.198.refs_2_, bf16[3,512,128]{2,1,0:T(8,128)(2,1)} %get-tuple-element.196.refs_3_, ...), custom_call_target="tpu_custom_call" | custom-call | flops 25769803776 | bytes 8388608 | tf_op jit(solution)/shard_map/attention/pallas_call | solution.py:675
  204.8 2.5 collective-permute-done.1.refs_5_
  207.3 6.2 collective-permute-done.2.refs_6_
  214.3 10.1 %attention.5 = (bf16[4,512,128]{2,1,0:T(8,128)(2,1)}, f32[4,8,512]{2,1,0:T(8,128)}) custom-call(s32[16]{0:T(128)} %get-tuple-element.191.refs_0_, bf16[4,512,128]{2,1,0:T(8,128)(2,1)} %get-tuple-element.309.refs_1_, bf16[512,128]{1,0:T(8,128)(2,1)} %get-tuple-element.198.refs_2_, bf16[3,512,128]{2,1,0:T(8,128)(2,1)} %get-tuple-element.204.refs_3_, ...), custom_call_target="tpu_custom_call" | custom-call | flops 25769803776 | bytes 8388608 | tf_op jit(solution)/shard_map/attention/pallas_call | solution.py:675
  224.4 26.1 %projection.2 = (f32[512,1024]{1,0:T(8,128)}, bf16[512,1024]{1,0:T(8,128)(2,1)}, f32[8,1024]{1,0:T(8,128)}) custom-call(f32[512,1]{1,0:T(8,128)} %get-tuple-element.189.refs_0_.refs_4_, bf16[512,1024]{1,0:T(8,128)(2,1)} %get-tuple-element.209.refs_0_.refs_1_, f32[4,56,128]{2,1,0:T(8,128)} %get-tuple-element.195.refs_1_.refs_2_.refs_5_, ...), custom_call_target="tpu_custom_call" | custom-call | flops 16106127360 | bytes 10485760 | tf_op jit(solution)/shard_map/projection/pallas_call | solution.py:459
  250.5 25.8 %ffn.2 = (bf16[4,512,1024]{2,1,0:T(8,128)(2,1)}, bf16[4,512,1024]{2,1,0:T(8,128)(2,1)}, bf16[4,512,1024]{2,1,0:T(8,128)(2,1)}, bf16[512,1024]{1,0:T(8,128)(2,1)}...) custom-call(f32[512,1]{1,0:T(8,128)} %get-tuple-element.189.refs_0_.refs_4_, ...), custom_call_target="tpu_custom_call" | custom-call | flops 34359738368 | bytes 10485760 | tf_op jit(solution)/shard_map/ffn/pallas_call | solution.py:411
  276.4 36.9 %qkv.5 = (bf16[3,512,128]{2,1,0:T(8,128)(2,1)}, bf16[3,512,128]{2,1,0:T(8,128)(2,1)}, bf16[3,512,128]{2,1,0:T(8,128)(2,1)}, bf16[3,512,128]{2,1,0:T(8,128)(2,1)}...) custom-call(bf16[512,1024]{1,0:T(8,128)(2,1)} %get-tuple-element.215, ...), custom_call_target="tpu_custom_call" | custom-call | flops 32212254720 | bytes 10485760 | tf_op jit(solution)/shard_map/qkv/pallas_call | solution.py:459
  315.5 11.7 %collective-permute-start.5 = (bf16[3,512,128]{2,1,0:T(8,128)(2,1)}, bf16[3,512,128]{2,1,0:T(8,128)(2,1)S(1)}, u32[]{:S(2)}, u32[]{:S(2)}) collective-permute-start(bf16[3,512,128]{2,1,0:T(8,128)(2,1)} %get-tuple-element.228), channel_id=1, source_target_pairs={{0,12},{4,0},{8,4},{12,8},{16,28},{20,16},{24,20},{28,24},{1,13},{... | collective-permute-start | bytes 1179656 | tf_op jit(solution)/shard_map/ppermute | solution.py:2173
  327.2 9.8 attention.6
  338.0 9.8 attention.7
  347.9 38.7 %projection.3 = (f32[512,1024]{1,0:T(8,128)}, bf16[512,1024]{1,0:T(8,128)(2,1)}, f32[8,1024]{1,0:T(8,128)}, bf16[512,1024]{1,0:T(8,128)(2,1)}) custom-call(f32[512,1]{1,0:T(8,128)} %get-tuple-element.189.refs_0_.refs_4_, f32[512,1024]{1,0:T(8,128)} %get-tuple-element.230.refs_1_, f32[4,56,128]{2,1,0:T(8,128)} %get-tuple-element.195.refs_1_.refs_2_.refs_5_, ...), custom_call_target="tpu_custom_call" | custom-call | flops 16106127360 | bytes 10485760 | tf_op jit(solution)/shard_map/projection/pallas_call | solution.py:459
  386.6 16.0 %all-gather.7.cloned.1.call-done = bf16[4096,2048]{1,0:T(8,128)(2,1)} async-done(((bf16[128,2048]{1,0:T(8,128)(2,1)}), bf16[4096,2048]{1,0:T(8,128)(2,1)}) %all-gather.7.cloned.1.call-update) | async-done | bytes 16777232 | tf_op jit(solution)/shard_map/all_gather | solution.py:2183
  402.6 26.2 %ffn.3 = (bf16[4,512,1024]{2,1,0:T(8,128)(2,1)}, bf16[4,512,1024]{2,1,0:T(8,128)(2,1)}, bf16[4,512,1024]{2,1,0:T(8,128)(2,1)}, bf16[512,1024]{1,0:T(8,128)(2,1)}...) custom-call(f32[512,1]{1,0:T(8,128)} %get-tuple-element.189.refs_0_., ...), custom_call_target="tpu_custom_call", output_to_operand_aliasing={{8}: (5, {})} | custom-call | flops 34359738368 | bytes 10485760 | tf_op jit(solution)/shard_map/ffn/pallas_call | solution.py:459
  428.8 34.3 %ffn_back.2 = (bf16[4,512,1024]{2,1,0:T(8,128)(2,1)}, bf16[8,128,512]{2,1,0:T(8,128)(2,1)}, bf16[8,128,512]{2,1,0:T(8,128)(2,1)}, f32[512,1024]{1,0:T(8,128)}, f...) custom-call(bf16[512,1024]{1,0:T(8,128)(2,1)} %get-tuple-element.237.refs_0_, ...), custom_call_target="tpu_custom_call" | custom-call | flops 34359738368 | bytes 10485760 | tf_op jit(solution)/shard_map/ffn_back/pallas_call | solution.py:459
  463.1 12.8 %ffn_grad.4.refs_4_ = bf16[4,4,128,2048]{3,2,1,0:T(8,128)(2,1)} custom-call(s32[10]{0:T(128)} %stack.40.refs_0_, bf16[8,128,512]{2,1,0:T(8,128)(2,1)} %get-tuple-element.252.refs_1_, bf16[8,128,512]{2,1,0:T(8,128)(2,1)} %get-tuple-element.246.refs_2_, bf16[4,512,1024]{2,1,0:T(8,128)(2,1)} %get-tuple-element.244.refs_3_, ...), custom_call_target="tpu_custom_call" | custom-call | flops 17179869184 | bytes 25165824 | tf_op jit(solution)/shard_map/ffn_grad/pallas_call | solution.py:1323
  475.8 28.3 %projection_back.2 = (bf16[4,512,128]{2,1,0:T(8,128)(2,1)}, bf16[4,512,128]{2,1,0:T(8,128)(2,1)}, bf16[8,128,512]{2,1,0:T(8,128)(2,1)}, bf16[512,1024]{1,0:T(8,1...) custom-call(f32[512,1024]{1,0:T(8,128)} %get-tuple-element.262.refs_, ...), custom_call_target="tpu_custom_call", output_to_operand_aliasing={{6}: (6, {})} | custom-call | flops 16106127360 | bytes 10485760 | tf_op jit(solution)/shard_map/projection_back/pallas_call | solution.py:459
  504.1 14.4 %ffn_grad.5 = (bf16[2,4,128,2048]{3,2,1,0:T(8,128)(2,1)}, bf16[2,4,128,2048]{3,2,1,0:T(8,128)(2,1)}) custom-call(s32[10]{0:T(128)} %stack.40.refs_0_, bf16[8,128,512]{2,1,0:T(8,128)(2,1)} %get-tuple-element.252.refs_1_, bf16[8,128,512]{2,1,0:T(8,128)(2,1)} %get-tuple-element.246.refs_2_, bf16[4,512,1024]{2,1,0:T(8,128)(2,1)} %get-tuple-element.244.refs_3_, ...), custom_call_target="tpu_custom_call" | custom-call | flops 17179869184 | bytes 25165824 | tf_op jit(solution)/shard_map/ffn_grad/pallas_call | solution.py:1323
  518.6 17.0 %attention_back.4 = (bf16[3,512,128]{2,1,0:T(8,128)(2,1)}, bf16[3,512,128]{2,1,0:T(8,128)(2,1)}, bf16[3,512,128]{2,1,0:T(8,128)(2,1)}, bf16[3,512,128]{2,1,0:T(8,128)(2,1)}) custom-call(s32[16]{0:T(128)} %get-tuple-element.191.refs_0_, bf16[4,512,128]{2,1,0:T(8,128)(2,1)} %get-tuple-element.309.refs_1_, bf16[512,128]{1,0:T(8,128)(2,1)} %get-tuple-element.198.refs_2_, ...), custom_call_target="tpu_custom_call" | custom-call | flops 30064771072 | bytes 8388608 | tf_op jit(solution)/shard_map/attention_back/pallas_call | solution.py:675
  537.4 17.4 %attention_back.5 = (bf16[3,512,128]{2,1,0:T(8,128)(2,1)}, bf16[3,512,128]{2,1,0:T(8,128)(2,1)}, bf16[3,512,128]{2,1,0:T(8,128)(2,1)}, bf16[3,512,128]{2,1,0:T(8,128)(2,1)}) custom-call(s32[16]{0:T(128)} %get-tuple-element.191.refs_0_, bf16[4,512,128]{2,1,0:T(8,128)(2,1)} %get-tuple-element.309.refs_1_, bf16[512,128]{1,0:T(8,128)(2,1)} %get-tuple-element.198.refs_2_, ...), custom_call_target="tpu_custom_call" | custom-call | flops 30064771072 | bytes 8388608 | tf_op jit(solution)/shard_map/attention_back/pallas_call | solution.py:675
  556.6 30.1 %qkv_back.2 = (bf16[3,512,128]{2,1,0:T(8,128)(2,1)}, bf16[3,512,128]{2,1,0:T(8,128)(2,1)}, bf16[3,512,128]{2,1,0:T(8,128)(2,1)}, bf16[3,512,128]{2,1,0:T(8,128)(...) custom-call(f32[512,1024]{1,0:T(8,128)} %get-tuple-element.262.refs_, ...), custom_call_target="tpu_custom_call" | custom-call | flops 26843545600 | bytes 10485760 | tf_op jit(solution)/shard_map/qkv_back/pallas_call | solution.py:459
  586.8 8.1 head_grad.3.refs_7_
  594.9 26.9 %ffn_back.3 = (bf16[4,512,1024]{2,1,0:T(8,128)(2,1)}, bf16[8,128,512]{2,1,0:T(8,128)(2,1)}, bf16[8,128,512]{2,1,0:T(8,128)(2,1)}, f32[512,1024]{1,0:T(8,128)}, f...) custom-call(f32[512,1024]{1,0:T(8,128)} %get-tuple-element.278.refs_0_, ...), custom_call_target="tpu_custom_call" | custom-call | flops 34359738368 | bytes 10485760 | tf_op jit(solution)/shard_map/ffn_back/pallas_call | solution.py:459
  621.8 9.4 head_grad.4
  631.2 2.0 collective-permute-start.10
  633.2 12.6 %ffn_grad.6.refs_4_ = bf16[4,4,128,2048]{3,2,1,0:T(8,128)(2,1)} custom-call(s32[10]{0:T(128)} %stack.40.refs_0_, bf16[8,128,512]{2,1,0:T(8,128)(2,1)} %get-tuple-element.300.refs_1_, bf16[8,128,512]{2,1,0:T(8,128)(2,1)} %get-tuple-element.289.refs_2_, bf16[4,512,1024]{2,1,0:T(8,128)(2,1)} %get-tuple-element.284.refs_3_, ...), custom_call_target="tpu_custom_call" | custom-call | flops 17179869184 | bytes 25165824 | tf_op jit(solution)/shard_map/ffn_grad/pallas_call | solution.py:1323
  645.8 5.3 fusion.1
  652.0 46.2 %projection_back.3 = (bf16[4,512,128]{2,1,0:T(8,128)(2,1)}, bf16[4,512,128]{2,1,0:T(8,128)(2,1)}, bf16[8,128,512]{2,1,0:T(8,128)(2,1)}, bf16[512,1024]{1,0:T(8,1...) custom-call(f32[512,1024]{1,0:T(8,128)} %get-tuple-element.316.refs_0_, ...), custom_call_target="tpu_custom_call" | custom-call | flops 16106127360 | bytes 10485760 | tf_op jit(solution)/shard_map/projection_back/pallas_call | solution.py:459
  698.2 4.2 fusion.5
  703.5 14.4 %ffn_grad.7 = (bf16[2,4,128,2048]{3,2,1,0:T(8,128)(2,1)}, bf16[2,4,128,2048]{3,2,1,0:T(8,128)(2,1)}) custom-call(s32[10]{0:T(128)} %stack.40.refs_0_, bf16[8,128,512]{2,1,0:T(8,128)(2,1)} %get-tuple-element.300.refs_1_, bf16[8,128,512]{2,1,0:T(8,128)(2,1)} %get-tuple-element.289.refs_2_, bf16[4,512,1024]{2,1,0:T(8,128)(2,1)} %get-tuple-element.284.refs_3_, ...), custom_call_target="tpu_custom_call" | custom-call | flops 17179869184 | bytes 25165824 | tf_op jit(solution)/shard_map/ffn_grad/pallas_call | solution.py:1323
  718.0 2.4 add_convert_fusion.3
  721.5 13.9 %collective-permute-start.13 = (bf16[2,128,2048]{2,1,0:T(8,128)(2,1)}, bf16[2,128,2048]{2,1,0:T(8,128)(2,1)}, u32[]{:S(2)}, u32[]{:S(2)}) collective-permute-start(bf16[2,128,2048]{2,1,0:T(8,128)(2,1)} %get-tuple-element.390), channel_id=1, source_target_pairs={{0,1},{1,0},{2,3},{3,2},{4,5},{5,4},{6,7},{7,6},{8,9},{9,8},{10,11... | collective-permute-start | bytes 3145736 | tf_op jit(solution)/shard_map/ppermute | solution.py:2176
  735.4 17.0 %attention_back.6 = (bf16[3,512,128]{2,1,0:T(8,128)(2,1)}, bf16[3,512,128]{2,1,0:T(8,128)(2,1)}, bf16[3,512,128]{2,1,0:T(8,128)(2,1)}, bf16[3,512,128]{2,1,0:T(8,128)(2,1)}) custom-call(s32[16]{0:T(128)} %get-tuple-element.191.refs_0_, bf16[4,512,128]{2,1,0:T(8,128)(2,1)} %get-tuple-element.309.refs_1_, bf16[512,128]{1,0:T(8,128)(2,1)} %get-tuple-element.198.refs_2_, ...), custom_call_target="tpu_custom_call" | custom-call | flops 30064771072 | bytes 8388608 | tf_op jit(solution)/shard_map/attention_back/pallas_call | solution.py:675
  754.1 1.6 add_convert_fusion.7
  755.7 3.4 collective-permute-done.13
  760.7 17.1 %attention_back.7 = (bf16[3,512,128]{2,1,0:T(8,128)(2,1)}, bf16[3,512,128]{2,1,0:T(8,128)(2,1)}, bf16[3,512,128]{2,1,0:T(8,128)(2,1)}, bf16[3,512,128]{2,1,0:T(8,128)(2,1)}) custom-call(s32[16]{0:T(128)} %get-tuple-element.191.refs_0_, bf16[4,512,128]{2,1,0:T(8,128)(2,1)} %get-tuple-element.309.refs_1_, bf16[512,128]{1,0:T(8,128)(2,1)} %get-tuple-element.198.refs_2_, ...), custom_call_target="tpu_custom_call" | custom-call | flops 30064771072 | bytes 8388608 | tf_op jit(solution)/shard_map/attention_back/pallas_call | solution.py:675
  779.5 12.0 %collective-permute-start.21 = (bf16[128,2048]{1,0:T(8,128)(2,1)}, bf16[128,2048]{1,0:T(8,128)(2,1)S(1)}, u32[]{:S(2)}, u32[]{:S(2)}) collective-permute-start(bf16[128,2048]{1,0:T(8,128)(2,1)} %slice_bitcast_fusion), channel_id=1, source_target_pairs={{0,2},{1,3},{2,0},{3,1},{4,6},{5,7},{6,4},{7,5},{8,10},{9,11},{10,... | collective-permute-start | bytes 1572872 | tf_op jit(solution)/shard_map/ppermute | solution.py:2176
  791.5 5.3 fusion.3
  796.8 2.1 collective-permute-start.19
  798.9 50.3 %qkv_back.3 = (bf16[3,512,128]{2,1,0:T(8,128)(2,1)}, bf16[3,512,128]{2,1,0:T(8,128)(2,1)}, bf16[3,512,128]{2,1,0:T(8,128)(2,1)}, bf16[3,512,128]{2,1,0:T(8,128)(...) custom-call(f32[512,1024]{1,0:T(8,128)} %get-tuple-element.316.refs_, ...), custom_call_target="tpu_custom_call" | custom-call | flops 26843545600 | bytes 10485760 | tf_op jit(solution)/shard_map/qkv_back/pallas_call | solution.py:459
  850.9 12.0 %head_grad.5.refs_1_ = bf16[8,4,128,1024]{3,2,1,0:T(8,128)(2,1)} custom-call(s32[10]{0:T(128)} %stack.40.refs_0_, bf16[8,128,512]{2,1,0:T(8,128)(2,1)} %get-tuple-element.328.refs_1_, bf16[8,128,512]{2,1,0:T(8,128)(2,1)} %get-tuple-element.329.refs_2_, bf16[512,1024]{1,0:T(8,128)(2,1)} %get-tuple-element.330.refs_3_, ...), custom_call_target="tpu_custom_call" | custom-call | flops 34359738368 | bytes 16777216 | tf_op jit(solution)/shard_map/head_grad/pallas_call | solution.py:1368
  862.9 3.8 add_convert_fusion.refs_2_
  867.6 95.3 %end.1 = (f32[4,512,256]{2,1,0:T(8,128)}, f32[4,512,256]{2,1,0:T(8,128)}, f32[2,3,128,256]{3,2,1,0:T(8,128)}, f32[2,256,128]{2,1,0:T(8,128)}, f32[2,128,1024]{2,...) custom-call(bf16[512,1024]{1,0:T(8,128)(2,1)} %get-tuple-element.334, ...), custom_call_target="tpu_custom_call" | custom-call | bytes 314572800 | tf_op jit(solution)/shard_map/end/pallas_call | solution.py:2081
  967.0 3.2 copy.40
  (112 shorter events, 37.0 us)
Async XLA Ops:
  7.2 269.2 %all-gather.5.cloned.1.call-start = ((), (), s32[]{:S(2)}) async-start(), calls=%async_computation | async-start | bytes 8650752 | tf_op jit(solution)/shard_map/all_gather | solution.py:2183
  160.3 242.2 %all-gather.7.cloned.1.call-start = ((), (), s32[]{:S(2)}) async-start(), calls=%async_computation.1 | async-start | bytes 17301504 | tf_op jit(solution)/shard_map/all_gather | solution.py:2183
  187.3 17.5 %collective-permute-start = (bf16[3,512,128]{2,1,0:T(8,128)(2,1)}, bf16[3,512,128]{2,1,0:T(8,128)(2,1)S(1)}, u32[]{:S(2)}, u32[]{:S(2)}) collective-permute-start(bf16[3,512,128]{2,1,0:T(8,128)(2,1)} %get-tuple-element.205), channel_id=1, source_target_pairs={{0,4},{4,8},{8,12},{12,0},{16,20},{20,24},{24,28},{28,16},{1,5},{5... | collective-permute-start | bytes 1179656 | tf_op jit(solution)/shard_map/ppermute | solution.py:2173
  187.6 19.6 %collective-permute-start.1 = (bf16[3,512,128]{2,1,0:T(8,128)(2,1)}, bf16[3,512,128]{2,1,0:T(8,128)(2,1)S(1)}, u32[]{:S(2)}, u32[]{:S(2)}) collective-permute-start(bf16[3,512,128]{2,1,0:T(8,128)(2,1)} %get-tuple-element.206), channel_id=1, source_target_pairs={{0,8},{4,12},{8,0},{12,4},{16,24},{20,28},{24,16},{28,20},{1,9},{5... | collective-permute-start | bytes 1179656 | tf_op jit(solution)/shard_map/ppermute | solution.py:2173
  188.7 24.8 %collective-permute-start.2 = (bf16[3,512,128]{2,1,0:T(8,128)(2,1)}, bf16[3,512,128]{2,1,0:T(8,128)(2,1)S(1)}, u32[]{:S(2)}, u32[]{:S(2)}) collective-permute-start(bf16[3,512,128]{2,1,0:T(8,128)(2,1)} %get-tuple-element.207), channel_id=1, source_target_pairs={{0,12},{4,0},{8,4},{12,8},{16,28},{20,16},{24,20},{28,24},{1,13},{... | collective-permute-start | bytes 1179656 | tf_op jit(solution)/shard_map/ppermute | solution.py:2173
  191.8 10.0 %copy-start.3 = (f32[2048,256]{1,0:T(8,128)S(1)}, f32[2048,256]{1,0:T(8,128)}, u32[]{:S(2)}) copy-start(f32[2048,256]{1,0:T(8,128)} %param.23) | copy-start | bytes 6291460
  204.7 8.8 copy-start.13
  207.3 6.3 copy-start.14
  213.5 0.8 copy-start.15
  313.3 23.7 %collective-permute-start.3 = (bf16[3,512,128]{2,1,0:T(8,128)(2,1)}, bf16[3,512,128]{2,1,0:T(8,128)(2,1)S(1)}, u32[]{:S(2)}, u32[]{:S(2)}) collective-permute-start(bf16[3,512,128]{2,1,0:T(8,128)(2,1)} %get-tuple-element.226), channel_id=1, source_target_pairs={{0,4},{4,8},{8,12},{12,0},{16,20},{20,24},{24,28},{28,16},{1,5},{5... | collective-permute-start | bytes 1179656 | tf_op jit(solution)/shard_map/ppermute | solution.py:2173
  315.0 22.1 %collective-permute-start.4 = (bf16[3,512,128]{2,1,0:T(8,128)(2,1)}, bf16[3,512,128]{2,1,0:T(8,128)(2,1)S(1)}, u32[]{:S(2)}, u32[]{:S(2)}) collective-permute-start(bf16[3,512,128]{2,1,0:T(8,128)(2,1)} %get-tuple-element.227), channel_id=1, source_target_pairs={{0,8},{4,12},{8,0},{12,4},{16,24},{20,28},{24,16},{28,20},{1,9},{5... | collective-permute-start | bytes 1179656 | tf_op jit(solution)/shard_map/ppermute | solution.py:2173
  315.5 21.6 %collective-permute-start.5 = (bf16[3,512,128]{2,1,0:T(8,128)(2,1)}, bf16[3,512,128]{2,1,0:T(8,128)(2,1)S(1)}, u32[]{:S(2)}, u32[]{:S(2)}) collective-permute-start(bf16[3,512,128]{2,1,0:T(8,128)(2,1)} %get-tuple-element.228), channel_id=1, source_target_pairs={{0,12},{4,0},{8,4},{12,8},{16,28},{20,16},{24,20},{28,24},{1,13},{... | collective-permute-start | bytes 1179656 | tf_op jit(solution)/shard_map/ppermute | solution.py:2173
  337.0 0.7 copy-start.16
  337.0 0.9 copy-start.17
  337.1 1.0 copy-start.18
  535.6 19.2 %collective-permute-start.6 = (bf16[3,512,128]{2,1,0:T(8,128)(2,1)}, bf16[3,512,128]{2,1,0:T(8,128)(2,1)S(1)}, u32[]{:S(2)}, u32[]{:S(2)}) collective-permute-start(bf16[3,512,128]{2,1,0:T(8,128)(2,1)} %get-tuple-element.263), channel_id=1, source_target_pairs={{0,12},{4,0},{8,4},{12,8},{16,28},{20,16},{24,20},{28,24},{1,13},{... | collective-permute-start | bytes 1179656 | tf_op jit(solution)/shard_map/ppermute | solution.py:2173
  536.0 19.8 %collective-permute-start.7 = (bf16[3,512,128]{2,1,0:T(8,128)(2,1)}, bf16[3,512,128]{2,1,0:T(8,128)(2,1)S(1)}, u32[]{:S(2)}, u32[]{:S(2)}) collective-permute-start(bf16[3,512,128]{2,1,0:T(8,128)(2,1)} %get-tuple-element.264), channel_id=1, source_target_pairs={{0,8},{4,12},{8,0},{12,4},{16,24},{20,28},{24,16},{28,20},{1,9},{5... | collective-permute-start | bytes 1179656 | tf_op jit(solution)/shard_map/ppermute | solution.py:2173
  537.4 18.4 %collective-permute-start.8 = (bf16[3,512,128]{2,1,0:T(8,128)(2,1)}, bf16[3,512,128]{2,1,0:T(8,128)(2,1)S(1)}, u32[]{:S(2)}, u32[]{:S(2)}) collective-permute-start(bf16[3,512,128]{2,1,0:T(8,128)(2,1)} %get-tuple-element.265), channel_id=1, source_target_pairs={{0,4},{4,8},{8,12},{12,0},{16,20},{20,24},{24,28},{28,16},{1,5},{5... | collective-permute-start | bytes 1179656 | tf_op jit(solution)/shard_map/ppermute | solution.py:2173
  554.8 1.0 copy-start.20
  555.8 0.7 copy-start.21
  555.8 0.9 copy-start.22
  594.9 50.9 %collective-permute-start.9 = (bf16[2,4,128,2048]{3,2,1,0:T(8,128)(2,1)}, bf16[2,4,128,2048]{3,2,1,0:T(8,128)(2,1)}, u32[]{:S(2)}, u32[]{:S(2)}) collective-permute-start(bf16[2,4,128,2048]{3,2,1,0:T(8,128)(2,1)} %get-tuple-element.293), channel_id=1, source_target_pairs={{0,16},{4,12},{8,24},{12,4},{16,0},{20,28},{24,8},{28,20},{1,17},{... | collective-permute-start | bytes 12582920 | tf_op jit(solution)/shard_map/ppermute | solution.py:2429
  631.2 67.0 %collective-permute-start.10 = (bf16[2,4,128,1024]{3,2,1,0:T(8,128)(2,1)}, bf16[2,4,128,1024]{3,2,1,0:T(8,128)(2,1)}, u32[]{:S(2)}, u32[]{:S(2)}) collective-permute-start(bf16[2,4,128,1024]{3,2,1,0:T(8,128)(2,1)} %get-tuple-element.299), channel_id=1, source_target_pairs={{0,16},{4,12},{8,24},{12,4},{16,0},{20,28},{24,8},{28,20},{1,17},{... | collective-permute-start | bytes 6291464 | tf_op jit(solution)/shard_map/ppermute | solution.py:2373
  651.1 66.9 %collective-permute-start.11 = (bf16[4,128,2048]{2,1,0:T(8,128)(2,1)}, bf16[4,128,2048]{2,1,0:T(8,128)(2,1)}, u32[]{:S(2)}, u32[]{:S(2)}) collective-permute-start(bf16[4,128,2048]{2,1,0:T(8,128)(2,1)} %get-tuple-element.386), channel_id=1, source_target_pairs={{0,8},{4,20},{8,0},{12,28},{16,24},{20,4},{24,16},{28,12},{1,9},{5... | collective-permute-start | bytes 6291464 | tf_op jit(solution)/shard_map/ppermute | solution.py:2378
  702.4 51.4 %collective-permute-start.12 = (bf16[4,128,1024]{2,1,0:T(8,128)(2,1)}, bf16[4,128,1024]{2,1,0:T(8,128)(2,1)}, u32[]{:S(2)}, u32[]{:S(2)}) collective-permute-start(bf16[4,128,1024]{2,1,0:T(8,128)(2,1)} %get-tuple-element.388), channel_id=1, source_target_pairs={{0,8},{4,20},{8,0},{12,28},{16,24},{20,4},{24,16},{28,12},{1,9},{5... | collective-permute-start | bytes 3145736 | tf_op jit(solution)/shard_map/ppermute | solution.py:2393
  718.0 73.5 %collective-permute-start.14 = (bf16[2,4,128,2048]{3,2,1,0:T(8,128)(2,1)}, bf16[2,4,128,2048]{3,2,1,0:T(8,128)(2,1)}, u32[]{:S(2)}, u32[]{:S(2)}) collective-permute-start(bf16[2,4,128,2048]{3,2,1,0:T(8,128)(2,1)} %get-tuple-element.315), channel_id=1, source_target_pairs={{0,16},{4,12},{8,24},{12,4},{16,0},{20,28},{24,8},{28,20},{1,17},{... | collective-permute-start | bytes 12582920 | tf_op jit(solution)/shard_map/ppermute | solution.py:2401
  721.5 37.6 %collective-permute-start.13 = (bf16[2,128,2048]{2,1,0:T(8,128)(2,1)}, bf16[2,128,2048]{2,1,0:T(8,128)(2,1)}, u32[]{:S(2)}, u32[]{:S(2)}) collective-permute-start(bf16[2,128,2048]{2,1,0:T(8,128)(2,1)} %get-tuple-element.390), channel_id=1, source_target_pairs={{0,1},{1,0},{2,3},{3,2},{4,5},{5,4},{6,7},{7,6},{8,9},{9,8},{10,11... | collective-permute-start | bytes 3145736 | tf_op jit(solution)/shard_map/ppermute | solution.py:2176
  752.4 44.5 %collective-permute-start.15 = (bf16[3,512,128]{2,1,0:T(8,128)(2,1)}, bf16[3,512,128]{2,1,0:T(8,128)(2,1)S(1)}, u32[]{:S(2)}, u32[]{:S(2)}) collective-permute-start(bf16[3,512,128]{2,1,0:T(8,128)(2,1)} %get-tuple-element.317), channel_id=1, source_target_pairs={{0,12},{4,0},{8,4},{12,8},{16,28},{20,16},{24,20},{28,24},{1,13},{... | collective-permute-start | bytes 1179656 | tf_op jit(solution)/shard_map/ppermute | solution.py:2173
  753.5 45.4 %collective-permute-start.16 = (bf16[3,512,128]{2,1,0:T(8,128)(2,1)}, bf16[3,512,128]{2,1,0:T(8,128)(2,1)}, u32[]{:S(2)}, u32[]{:S(2)}) collective-permute-start(bf16[3,512,128]{2,1,0:T(8,128)(2,1)} %get-tuple-element.318), channel_id=1, source_target_pairs={{0,8},{4,12},{8,0},{12,4},{16,24},{20,28},{24,16},{28,20},{1,9},{5... | collective-permute-start | bytes 1179656 | tf_op jit(solution)/shard_map/ppermute | solution.py:2173
  753.9 45.1 %collective-permute-start.17 = (bf16[3,512,128]{2,1,0:T(8,128)(2,1)}, bf16[3,512,128]{2,1,0:T(8,128)(2,1)}, u32[]{:S(2)}, u32[]{:S(2)}) collective-permute-start(bf16[3,512,128]{2,1,0:T(8,128)(2,1)} %get-tuple-element.319), channel_id=1, source_target_pairs={{0,4},{4,8},{8,12},{12,0},{16,20},{20,24},{24,28},{28,16},{1,5},{5... | collective-permute-start | bytes 1179656 | tf_op jit(solution)/shard_map/ppermute | solution.py:2173
  755.7 22.1 %copy-start.1 = (bf16[4,128,1024]{2,1,0:T(8,128)(2,1)}, bf16[4,128,1024]{2,1,0:T(8,128)(2,1)S(1)}, u32[]{:S(2)}) copy-start(bf16[4,128,1024]{2,1,0:T(8,128)(2,1)S(1)} %add_convert_fusion.7) | copy-start | bytes 3145732
  760.7 17.9 %copy-start = (bf16[2,128,2048]{2,1,0:T(8,128)(2,1)}, bf16[2,128,2048]{2,1,0:T(8,128)(2,1)S(1)}, u32[]{:S(2)}) copy-start(bf16[2,128,2048]{2,1,0:T(8,128)(2,1)S(1)} %add_convert_fusion.6.refs_7_) | copy-start | bytes 3145732
  779.5 87.2 %collective-permute-start.21 = (bf16[128,2048]{1,0:T(8,128)(2,1)}, bf16[128,2048]{1,0:T(8,128)(2,1)S(1)}, u32[]{:S(2)}, u32[]{:S(2)}) collective-permute-start(bf16[128,2048]{1,0:T(8,128)(2,1)} %slice_bitcast_fusion), channel_id=1, source_target_pairs={{0,2},{1,3},{2,0},{3,1},{4,6},{5,7},{6,4},{7,5},{8,10},{9,11},{10,... | collective-permute-start | bytes 1572872 | tf_op jit(solution)/shard_map/ppermute | solution.py:2176
  791.5 57.7 %collective-permute-start.18 = (bf16[2,128,1024]{2,1,0:T(8,128)(2,1)}, bf16[2,128,1024]{2,1,0:T(8,128)(2,1)}, u32[]{:S(2)}, u32[]{:S(2)}) collective-permute-start(bf16[2,128,1024]{2,1,0:T(8,128)(2,1)} %slice.70), channel_id=1, source_target_pairs={{0,1},{1,0},{2,3},{3,2},{4,5},{5,4},{6,7},{7,6},{8,9},{9,8},{10,11... | collective-permute-start | bytes 1572872 | tf_op jit(solution)/shard_map/ppermute | solution.py:2176
  796.8 2.1 copy-start.19
  796.8 66.1 %collective-permute-start.19 = (bf16[4,128,2048]{2,1,0:T(8,128)(2,1)}, bf16[4,128,2048]{2,1,0:T(8,128)(2,1)}, u32[]{:S(2)}, u32[]{:S(2)}) collective-permute-start(bf16[4,128,2048]{2,1,0:T(8,128)(2,1)} %get-tuple-element.384), channel_id=1, source_target_pairs={{0,8},{4,20},{8,0},{12,28},{16,24},{20,4},{24,16},{28,12},{1,9},{5... | collective-permute-start | bytes 6291464 | tf_op jit(solution)/shard_map/ppermute | solution.py:2414
  798.9 50.3 %slice-start = ((bf16[4,128,1024]{2,1,0:T(8,128)(2,1)}), bf16[2,128,1024]{2,1,0:T(8,128)(2,1)S(1)}, s32[]{:S(2)}) async-start(bf16[4,128,1024]{2,1,0:T(8,128)(2,1)} %copy-done.1), calls=%async_computation.2 | async-start | bytes 1048576 | tf_op jit(solution)/shard_map/slice | solution.py:2426
  850.5 12.4 %copy-start.2 = (bf16[2,128,1024]{2,1,0:T(8,128)(2,1)}, bf16[2,128,1024]{2,1,0:T(8,128)(2,1)S(1)}, u32[]{:S(2)}) copy-start(bf16[2,128,1024]{2,1,0:T(8,128)(2,1)S(1)} %add_convert_fusion.10.refs_5_) | copy-start | bytes 1572868
  850.5 16.2 %collective-permute-start.20 = (bf16[128,1024]{1,0:T(8,128)(2,1)S(1)}, bf16[128,1024]{1,0:T(8,128)(2,1)S(1)}, u32[]{:S(2)}, u32[]{:S(2)}) collective-permute-start(bf16[128,1024]{1,0:T(8,128)(2,1)S(1)} %slice_bitcast_fusion.1), channel_id=1, source_target_pairs={{0,2},{1,3},{2,0},{3,1},{4,6},{5,7},{6,4},{7,5},{8,10},{9,11},{10,... | collective-permute-start | bytes 786440 | tf_op jit(solution)/shard_map/ppermute | solution.py:2176
  866.7 0.8 copy-start.8
  866.7 0.9 copy-start.9
  967.0 3.2 copy-start.4
  970.2 1.7 copy-start.7
  970.2 2.6 copy-start.10
  971.8 1.6 copy-start.6
  971.8 2.6 copy-start.5
  973.4 1.9 copy-start.12
  973.4 2.5 copy-start.11
Sparse Core Ops, SparseCore 0:
  160.5 90.6 all-gather.4
  254.1 148.3 all-gather.6

commit v4 on v3

--- a/solution.py
+++ b/solution.py
@@ -197,8 +197,6 @@
         self.sems = [DMA((2,))]
 
     def device(self, at):
-        if self.way == "z":
-            return {"head": at.group(1)}
         return {"dp": at.partner(self.way)}
 
     def peers(self, at):
@@ -217,51 +215,12 @@
     def start(self, *args):
         self.copy(*args).start()
 
-    def middle(self, *args):
-        pass
-
     def finish(self, *args):
         self.copy(*args).wait()
 
 
-class Near:
-    aliases = {}
-
-    def __init__(self, array):
-        self.arrays = [array]
-        self.outs = [jax.ShapeDtypeStruct((GROUPS - 1,) + array.shape[1:], array.dtype)]
-        self.sems = [DMA((2, GROUPS - 1))]
-
-    def peers(self, at):
-        return at.others(), [], GROUPS - 1
-
-    def copies(self, at, ins, outs, sems):
-        return [
-            pltpu.make_async_remote_copy(
-                src_ref=ins[0].at[k],
-                dst_ref=outs[0].at[k - 1],
-                send_sem=sems[0].at[0, k - 1],
-                recv_sem=sems[0].at[1, k - 1],
-                device_id={"head": at.group(k)},
-                device_id_type=MESH,
-            )
-            for k in (1, 2, 3)
-        ]
-
-    def start(self, *args):
-        for copy in self.copies(*args):
-            copy.start()
-
-    def middle(self, *args):
-        pass
-
-    def finish(self, *args):
-        for copy in self.copies(*args):
-            copy.wait()
-
-
 class Turn:
-    def __init__(self, array, back, half, into=None):
+    def __init__(self, array, back, half=None, into=None):
         self.arrays, self.back = [array], back
         self.aliases = {}
         if into is not None:
@@ -274,7 +233,7 @@
             tokens, wide = array.shape[1:]
             out = (tokens, GROUPS * wide)
         self.wide = wide
-        self.rows = pl.ds(half * (tokens // 2), tokens // 2)
+        self.rows = pl.ds(0, tokens) if half is None else pl.ds(half * (tokens // 2), tokens // 2)
         self.outs = [jax.ShapeDtypeStruct(out, array.dtype)]
         self.sems = [DMA((2, GROUPS)), DMA]
 
@@ -320,9 +279,6 @@
 
     def start(self, *args):
         self.each("start", *args)
-
-    def middle(self, *args):
-        pass
 
     def finish(self, at, ins, outs, sems):
         self.each("wait", at, ins, outs, sems)
@@ -347,7 +303,7 @@
 
 class Host:
     def __init__(self, n, parts):
-        self.n, self.parts, self.turns = n, parts, 0
+        self.n, self.parts = n, parts
         self.at = Place() if parts else None
 
     def barrier(self, group=True):
@@ -380,26 +336,7 @@
         for job, *refs in self.parts:
             job.start(self.at, *refs)
 
-    def middle(self):
-        for job, *refs in self.parts:
-            job.middle(self.at, *refs)
-
-    def tick(self):
-        for job, *refs in self.parts:
-            if isinstance(job, Everywhere) and self.turns < len(job.chunks) + 3:
-                job.tick(self.turns, self.at, *refs)
-        self.turns += 1
-
-    def tick_at(self, step):
-        for job, *refs in self.parts:
-            if isinstance(job, Everywhere):
-                for t in range(len(job.chunks) + 3):
-                    pl.when(step == t)(lambda t=t, job=job, refs=refs: job.tick(t, self.at, *refs))
-        self.turns = 64
-
     def finish(self):
-        while any(isinstance(v[0], Everywhere) for v in self.parts) and self.turns < 64:
-            self.tick()
         for job, *refs in self.parts:
             job.finish(self.at, *refs)
 
@@ -471,77 +408,98 @@
     return list(res)
 
 
-def qkv_kernel(layer, host, low, packed, weight, *refs):
-    n = host.n
-    vectors = Vectors(n, layer, packed)
-    gain, shift = vectors.norm(0, 0), vectors.norm(1, 0)
-    outs, (xs, wide, send, wsem, ssem, rsem, lsem) = refs[:-7], refs[-7:]
-    tokens = low.shape[0]
-    units = BLOCKS // n
-    width = units * LANES
-    steps = order_of(n) + [0]
-
-    def fetch(i):
-        group, offset = head_columns(n, steps[i])
+class Queries:
+    def __init__(self, n, weight, outs, xs, wide, send, wsem, ssem, rsem, lsem):
+        self.n, self.weight, self.outs, self.xs, self.wide, self.send = n, weight, outs, xs, wide, send
+        self.wsem, self.ssem, self.rsem, self.lsem = wsem, ssem, rsem, lsem
+        self.units = BLOCKS // n
+        self.steps = order_of(n) + [0]
+
+    def fetch(self, i):
+        group, offset = head_columns(self.n, self.steps[i])
+        width = self.units * LANES
         return [
             pltpu.make_async_copy(
-                weight.at[:, group, :, pl.ds(c * HEADS + offset, width)],
-                wide.at[i % 2, c],
-                wsem.at[i % 2, c],
+                self.weight.at[:, group, :, pl.ds(c * HEADS + offset, width)],
+                self.wide.at[i % 2, c],
+                self.wsem.at[i % 2, c],
             )
             for c in range(3)
         ]
 
-    for copy in fetch(0):
-        copy.start()
-
-    def body(r):
-        hat, _ = row_stats(low[r, :].astype(f32))
-        xs[r, :] = (hat * gain + shift).astype(bf16)
-
-    row_loop(tokens, ROWS, body)
+    def begin(self):
+        for copy in self.fetch(0):
+            copy.start()
+
+    def norm(self, low, gain, shift):
+        def body(r):
+            hat, _ = row_stats(low[r, :].astype(f32))
+            self.xs[r, :] = (hat * gain + shift).astype(bf16)
+
+        row_loop(low.shape[0], ROWS, body)
+
+    def copy(self, k):
+        if k:
+            return group_send(
+                self.n, k, self.send.at[k], self.outs[k], self.ssem.at[k], self.rsem.at[k]
+            )
+        return pltpu.make_async_copy(self.send.at[0], self.outs[0], self.lsem)
+
+    def step(self, i):
+        k = self.steps[i]
+        if i + 1 < self.n:
+            for copy in self.fetch(i + 1):
+                copy.start()
+        for c, copy in enumerate(self.fetch(i)):
+            copy.wait()
+            value = dot(self.xs[...], self.wide[i % 2, c].reshape(D, -1)).astype(bf16)
+            self.send[k, c] = value[:, :LANES]
+            for u in range(1, self.units):
+                self.outs[u * self.n + k][c] = value[:, u * LANES : (u + 1) * LANES]
+        self.copy(k).start()
+
+    def finish(self):
+        for k in self.steps:
+            self.copy(k).wait()
+
+
+def queries_scratch(n, tokens):
+    return [
+        pltpu.VMEM((tokens, D), bf16),
+        pltpu.VMEM((2, 3, BLOCKS, LANES, BLOCKS // n * LANES), bf16),
+        pltpu.VMEM((n, 3, tokens, LANES), bf16),
+        DMA((2, 3)),
+        DMA((n,)),
+        DMA((n,)),
+        DMA,
+    ]
+
+
+def queries_outs(n, tokens):
+    count = BLOCKS // n * n
+    return [jax.ShapeDtypeStruct((3, tokens, LANES), bf16)] * count, [HB] * n + [VM] * (count - n)
+
+
+def qkv_kernel(layer, host, low, packed, weight, *refs):
+    vectors = Vectors(host.n, layer, packed)
+    queries = Queries(host.n, weight, refs[:-7], *refs[-7:])
+    queries.begin()
+    queries.norm(low, vectors.norm(0, 0), vectors.norm(1, 0))
     host.barrier()
     host.start()
-    copies = []
-    for i, k in enumerate(steps):
-        if i + 1 < n:
-            for copy in fetch(i + 1):
-                copy.start()
-        for c, copy in enumerate(fetch(i)):
-            copy.wait()
-            value = dot(xs[...], wide[i % 2, c].reshape(D, width)).astype(bf16)
-            send[k, c] = value[:, :LANES]
-            for u in range(1, units):
-                outs[u * n + k][c] = value[:, u * LANES : (u + 1) * LANES]
-        if k:
-            copy = group_send(n, k, send.at[k], outs[k], ssem.at[k], rsem.at[k])
-        else:
-            copy = pltpu.make_async_copy(send.at[0], outs[0], lsem)
-        copy.start()
-        copies.append(copy)
-    host.middle()
-    for copy in copies:
-        copy.wait()
+    for i in range(host.n):
+        queries.step(i)
+    queries.finish()
     host.finish()
 
 
 def qkv_call(n, ident, jobs, layer, low, packed, weight):
     tokens = low.shape[0]
     units = BLOCKS // n
-    block = (3, tokens, LANES)
+    out_shape, out_specs = queries_outs(n, tokens)
     res = remote_call(
         functools.partial(qkv_kernel, layer), n, "qkv", ident,
-        [low, packed, weight], [VM, VM, HB],
-        [jax.ShapeDtypeStruct(block, bf16)] * (n * units), [HB] * n + [VM] * (n * (units - 1)),
-        [
-            pltpu.VMEM((tokens, D), bf16),
-            pltpu.VMEM((2, 3, BLOCKS, LANES, units * LANES), bf16),
-            pltpu.VMEM((n,) + block, bf16),
-            DMA((2, 3)),
-            DMA((n,)),
-            DMA((n,)),
-            DMA,
-        ],
+        [low, packed, weight], [VM, VM, HB], out_shape, out_specs, queries_scratch(n, tokens),
         60 * tokens * D * D, jobs,
     )
     return [res[u * n : (u + 1) * n] for u in range(units)], res[n * units :]
@@ -724,10 +682,8 @@
     for copy in copies:
         copy.start()
     host.start()
-    host.tick()
     for copy in copies:
         copy.wait()
-    host.tick()
     _, lo = group_place(n)
     for k in range(n):
         first = lax.rem(lo + k, n) * (units * LANES)
@@ -740,13 +696,11 @@
         xs[r, :] = (hat * gain + shift).astype(bf16)
 
     row_loop(tokens, ROWS, body)
-    host.tick()
     branch = None
     for g in range(GROUPS):
         term = dot_nt(xs[:, g * HEADS : (g + 1) * HEADS], weight[:, g].reshape(D, HEADS))
         branch = term if branch is None else branch + term
     mid[...] = branch
-    host.tick()
     use[...] = jnp.zeros_like(use)
 
     def finish(r):
@@ -755,7 +709,6 @@
         mid[r, :] = stream[r, :].astype(f32) + part
 
     row_loop(tokens, ROWS, finish)
-    host.middle()
     host.finish()
 
 
@@ -864,11 +817,6 @@
 
         row_loop(tokens, ROWS, body)
 
-    host.tick_at(step)
-
-    @pl.when(step == 2 * GROUPS - 1)
-    def _():
-        host.middle()
         host.finish()
 
 
@@ -997,7 +945,6 @@
         row_loop(tokens, ROWS, body)
         for b in range(BLOCKS):
             normed_turned[b] = flip(gs[:, b * LANES : (b + 1) * LANES])
-        host.middle()
         host.finish()
 
 
@@ -1085,7 +1032,6 @@
             copies.append(copy)
     for b in range(BLOCKS):
         grad_turned[b] = flip(gs[:, b * LANES : (b + 1) * LANES])
-    host.middle()
     for copy in copies:
         copy.wait()
     host.finish()
@@ -1243,7 +1189,6 @@
         grad_low[r, :] = total.astype(bf16)
 
     row_loop(tokens, ROWS, body)
-    host.middle()
     host.finish()
 
 
@@ -1298,42 +1243,61 @@
             outs[0][(m,) + spot] = part.astype(bf16)
 
 
-def ffn_grad_kernel(first, count, added, sc, up_turned, down_turned, dhid, normed, *refs):
+def ffn_grad_kernel(ups, first, count, added, sc, up_turned, down_turned, *refs):
+    split = added and ups
+    dhid, normed, refs = [v.at[0] for v in refs[:2]], [v.at[0] for v in refs[2:4]], refs[4:]
     extra, outs = (refs[0], refs[1:]) if added else (None, refs)
 
     @pl.when(pl.program_id(0) == 0)
     def _():
-        put_rows(dot(pick_rows(sc, first, up_turned, count), dhid[0]), extra, outs, (0,))
+        left = pick_rows(sc, first + ups, up_turned, count)
+        for i in range(2):
+            put_rows(dot(left, dhid[i][...]), extra, outs[:2] if split else outs, (i,))
 
     @pl.when(pl.program_id(0) == 1)
     def _():
-        put_rows(dot(pick_rows(sc, first, down_turned, count), normed[0]), extra, outs, (0,))
-
-
-def ffn_grad_call(first, count, sc, up_turned, down_turned, dhid, normed, extra=None):
+        left = pick_rows(sc, first, down_turned, count)
+        for i in range(2):
+            put_rows(dot(left, normed[i][...]), extra, outs[2:] if split else outs, (i,))
+
+
+def ffn_grad_call(ups, first, count, sc, up_turned, down_turned, dhid, normed, extra=None):
     tokens = up_turned.shape[2]
     added = extra is not None
-    at = lambda g, sc: jnp.bitwise_xor(slot_group(g), sc[BLOCKS])
-    left = pl.BlockSpec(
-        (1, tokens, WIDE), lambda j, g, sc: (at(jnp.where(j == 0, g, GROUPS - 1), sc), 0, 0)
-    )
-    right = pl.BlockSpec((1, tokens, WIDE), lambda j, g, sc: (at(jnp.where(j == 1, g, 0), sc), 0, 0))
-    piece = lambda m: pl.BlockSpec((m, 1, LANES, WIDE), lambda j, g, sc: (0, g, 0, j))
+    def block(i, kind, idle):
+        def at(j, p, sc):
+            p = jnp.where(j == kind, p, idle)
+            return (jnp.bitwise_xor(p + 2 * i, sc[BLOCKS]), 0, 0)
+
+        return pl.BlockSpec((1, tokens, WIDE), at)
+
+    lefts = [block(i, 0, 1) for i in range(2)]
+    rights = [block(i, 1, 0) for i in range(2)]
+    piece = lambda m: pl.BlockSpec((m, 2, LANES, WIDE), lambda j, p, sc: (0, p, 0, j))
     outs = [2, 2] if added else [count]
+    specs = [piece(m) for m in outs]
+    wide = 2 * WIDE
+    if added and ups:
+
+        def half(kind, idle):
+            at = lambda j, p, sc: (0, jnp.where(j == kind, p, idle), 0, 0)
+            return pl.BlockSpec((2, 2, LANES, WIDE), at)
+
+        outs, specs, wide = [2] * 4, [half(0, 1)] * 2 + [half(1, 0)] * 2, WIDE
     return pl.pallas_call(
-        lambda *refs: ffn_grad_kernel(first, count, added, *refs),
-        out_shape=[jax.ShapeDtypeStruct((m, GROUPS, LANES, 2 * WIDE), bf16) for m in outs],
+        lambda *refs: ffn_grad_kernel(ups, first, count, added, *refs),
+        out_shape=[jax.ShapeDtypeStruct((m, GROUPS, LANES, wide), bf16) for m in outs],
         grid_spec=pltpu.PrefetchScalarGridSpec(
             num_scalar_prefetch=1,
-            grid=(2, GROUPS),
-            in_specs=[whole(up_turned.shape), whole(down_turned.shape), left, right]
+            grid=(2, GROUPS // 2),
+            in_specs=[whole(up_turned.shape), whole(down_turned.shape), *lefts, *rights]
             + ([piece(count)] if added else []),
-            out_specs=[piece(m) for m in outs],
+            out_specs=specs,
         ),
         compiler_params=params(),
         cost_estimate=cost(16 * tokens * count * LANES * FF, 24 * 2**20),
         name="ffn_grad",
-    )(sc, up_turned, down_turned, dhid, normed, *([extra] if added else []))
+    )(sc, up_turned, down_turned, dhid, dhid, normed, normed, *([extra] if added else []))
 
 
 def head_grad_kernel(n, first, count, added, sc, in_turned, out_turned, normed, *refs):
@@ -1430,22 +1394,17 @@
 
 
 class Weights:
-    def __init__(self, at, chunks, shards, gathered, hsem, ssem, rsem, lsem, only=None):
-        self.only = only
+    def __init__(self, at, chunks, shards, gathered, hsem, ssem, rsem, lsem):
         self.at, self.chunks, self.pairs = at, chunks, list(zip(shards, gathered))
         self.hsem, self.ssem, self.rsem = hsem, ssem, rsem
         self.lsem = lsem
 
     def owns(self):
         at = self.at
-        copies = []
-        for i, (shard, out) in enumerate(self.pairs):
-            source, target = shard, out.at[at.dp, at.z]
-            if self.only:
-                source = shard.at[:, pl.ds(*self.only)]
-                target = out.at[at.dp, at.z, :, pl.ds(*self.only)]
-            copies.append(pltpu.make_async_copy(source, target, self.lsem.at[i]))
-        return copies
+        return [
+            pltpu.make_async_copy(shard, out.at[at.dp, at.z], self.lsem.at[i])
+            for i, (shard, out) in enumerate(self.pairs)
+        ]
 
     def near(self, c):
         kind, columns = self.chunks[c][0], pl.ds(*self.chunks[c][1:])
@@ -1527,44 +1486,11 @@
     return [DMA((2, 3, parts)), DMA((7, parts)), DMA((7, parts)), DMA((len(shards),))]
 
 
-class Everywhere:
-    def __init__(self, shard, half, into=None):
-        self.arrays = [shard] if into is None else [shard, into]
-        self.aliases = {} if into is None else {1: 0}
-        self.outs = [jax.ShapeDtypeStruct((BLOCKS, GROUPS) + shard.shape, shard.dtype)]
-        wide = shard.shape[1] // 2
-        self.half = (half * wide, wide)
-        self.chunks = weight_chunks([shard], wide // 2)[2 * half : 2 * half + 2]
-        parts = len(self.chunks)
-        self.sems = [DMA((2, 3, parts)), DMA((7, parts)), DMA((7, parts)), DMA((1,))]
-
-    def peers(self, at):
-        partners = [{"dp": v} for v in (at.first, at.second, at.mate)]
-        return at.others() + partners, [], GROUPS + 2
-
-    def weights(self, at, ins, outs, sems):
-        return Weights(at, self.chunks, ins[:1], outs, *sems, only=self.half)
-
-    def start(self, *args):
-        weights = self.weights(*args)
-        for copy in weights.owns():
-            copy.start()
-        weights.begin()
-
-    def tick(self, t, *args):
-        self.weights(*args).turn(t)
-
-    def middle(self, *args):
-        pass
-
-    def finish(self, *args):
-        pass
-
-
 def start_kernel(
-    chunks, shards, rows, vector, flags, gathered, low, side, vectors, flags_out,
-    hsem, ssem, rsem, wsem, xsem, tsem, vsem, fsem, lsem,
+    chunks, shards, rows, vector, flags, gathered, low, side, vectors, flags_out, blocks,
+    hsem, ssem, rsem, wsem, xsem, tsem, vsem, fsem, lsem, low_here, vectors_here, *scratch,
 ):
+    queries = Queries(GROUPS, gathered[0], blocks, *scratch)
     at = Place()
     weights = Weights(at, chunks, shards, gathered, hsem, ssem, rsem, wsem)
     dp, core, bit_x, by_x = at.dp, at.core, at.bit_x, at.by_x
@@ -1586,7 +1512,11 @@
     own_vector = pltpu.make_async_copy(vector, vectors.at[z], lsem.at[2])
     own_vector.start()
     turned = [(turn_dp, turn_z)]
-    greet(sem, at, z, sources() + turned, n - 1 + unlike(lax.rem(z, 2), core) + unlike(z, lo))
+    across = at.by_x + 1 - 2 * core
+    greet(
+        sem, at, z, sources() + turned + [(across, z)],
+        n + unlike(lax.rem(z, 2), core) + unlike(z, lo),
+    )
     small = [
         pltpu.make_async_remote_copy(
             src_ref=vector,
@@ -1666,30 +1596,50 @@
 
     cross.start()
 
+    def arrivals():
+        spread("wait")
+        for from_dp, g in sources():
+
+            @pl.when((from_dp != dp) | (g != z))
+            def _(g=g):
+                spot = low.at[:, pl.ds(g * wide, wide)]
+                pltpu.make_async_remote_copy(
+                    src_ref=spot,
+                    dst_ref=spot,
+                    send_sem=tsem.at[0, 0],
+                    recv_sem=tsem.at[1, g],
+                    device_id={"dp": by_x},
+                    device_id_type=MESH,
+                ).wait_recv()
+
+    ready = sum(kind == 0 for kind, *_ in chunks) + 2
+    loads = [
+        pltpu.make_async_copy(low, low_here, lsem.at[0]),
+        pltpu.make_async_copy(vectors, vectors_here, lsem.at[2]),
+    ]
+
     def aside(t):
         if t == 1:
             cross.wait()
             spread("start")
+        if t == ready:
+            queries.begin()
+            own_vector.wait()
+            for copy in small:
+                copy.wait()
+            arrivals()
+            for copy in loads:
+                copy.start()
+            for copy in loads:
+                copy.wait()
+            norms = Vectors(n, 0, vectors_here)
+            queries.norm(low_here, norms.norm(0, 0), norms.norm(1, 0))
+        if ready < t <= ready + n:
+            queries.step(t - ready - 1)
 
     weights.run(aside)
-    own_vector.wait()
     flag_copy("wait")
-    for copy in small:
-        copy.wait()
-    spread("wait")
-    for from_dp, g in sources():
-
-        @pl.when((from_dp != dp) | (g != z))
-        def _(g=g):
-            spot = low.at[:, pl.ds(g * wide, wide)]
-            pltpu.make_async_remote_copy(
-                src_ref=spot,
-                dst_ref=spot,
-                send_sem=tsem.at[0, 0],
-                recv_sem=tsem.at[1, g],
-                device_id={"dp": by_x},
-                device_id_type=MESH,
-            ).wait_recv()
+    queries.finish()
 
 
 def start_call(shards, rows, vector, flags):
@@ -1697,9 +1647,15 @@
     chunks = weight_chunks(shards)
     tokens, wide = rows.shape[1:]
 
+    out_shape, out_specs = queries_outs(GROUPS, tokens)
+
     def kernel(*refs):
         taken, refs = refs[:count], refs[count:]
-        start_kernel(chunks, taken, *refs[:3], refs[3 : 3 + count], *refs[3 + count :])
+        given, refs = refs[:3], refs[3:]
+        gathered, refs = refs[:count], refs[count:]
+        others, refs = refs[:4], refs[4:]
+        blocks, refs = refs[: len(out_shape)], refs[len(out_shape) :]
+        start_kernel(chunks, taken, *given, gathered, *others, blocks, *refs)
 
     res = pl.pallas_call(
         kernel,
@@ -1709,9 +1665,10 @@
             jax.ShapeDtypeStruct((2, tokens, wide), bf16),
             jax.ShapeDtypeStruct((GROUPS,) + vector.shape, f32),
             jax.ShapeDtypeStruct(flags.shape, jnp.int32),
-        ],
+        ]
+        + out_shape,
         in_specs=[HB] * (count + 3),
-        out_specs=[HB] * (count + 4),
+        out_specs=[HB] * (count + 4) + out_specs,
         scratch_shapes=[
             *weight_sems(shards),
             DMA((2,)),
@@ -1719,12 +1676,17 @@
             DMA((2, 3)),
             DMA((2,)),
             DMA((4,)),
+            pltpu.VMEM((tokens, GROUPS * wide), bf16),
+            pltpu.VMEM((GROUPS,) + vector.shape, f32),
+            *queries_scratch(GROUPS, tokens),
         ],
         compiler_params=params(collective_id=5, has_side_effects=True),
         cost_estimate=cost(0, 300 * 2**20),
         name="start",
     )(*shards, rows, vector, flags)
-    return [res[:count], *res[count:]]
+    blocks = res[count + 4 :]
+    parts = [blocks[u * GROUPS : (u + 1) * GROUPS] for u in range(len(blocks) // GROUPS)]
+    return [res[:count], *res[count : count + 4], parts]
 
 
 def vector_rows(layers):
@@ -1996,13 +1958,12 @@
             stream_out[...] = turned[...].astype(f32)
         if t == 4:
             for l in range(1, layers):
-                heads, heads_other, wide_own, wide_other = tops[4 * l - 4 : 4 * l]
+                heads, heads_other, ups, ups_other, downs, downs_other = tops[6 * l - 6 : 6 * l]
                 for c in range(parts):
                     cols = slice(c * width, (c + 1) * width)
                     put_head(l, c, total_of(heads[0, :, cols], [heads_other[:, cols]]))
-                up_out[l] = total_of(wide_own[0, :, :WIDE], [wide_other[:, :WIDE]])
-                down = total_of(wide_own[0, :, WIDE:], [wide_other[:, WIDE:]])
-                down_out[l] = jnp.transpose(down, (1, 0))
+                up_out[l] = total_of(ups[0], [ups_other[...]])
+                down_out[l] = jnp.transpose(total_of(downs[0], [downs_other[...]]), (1, 0))
         c = t - 1
         if 0 <= c < parts:
             ffn_between(c)
@@ -2155,13 +2116,16 @@
         core_zero = [2, 4]
         self.one_way = [(i, i ^ core_zero[i % 2]) for i in range(n_dp)]
         self.other_way = [(i, i ^ core_zero[1 - i % 2]) for i in range(n_dp)]
+        self.by_x = [(i, i ^ 2) for i in range(n_dp)]
+        self.by_y = [(i, i ^ 4) for i in range(n_dp)]
         self.core = [(i, i ^ 1) for i in range(n_dp)]
         if self.fast:
             step = jnp.where(self.own % 2 == 0, 2, 4).astype(jnp.int32)
             mine = [jnp.int32(0), step, 6 - step, jnp.int32(6)]
             theirs = [jnp.int32(0), 6 - step, step, jnp.int32(6)]
             rows = [self.own ^ v for v in mine] + [self.own ^ v ^ 1 for v in theirs]
-            self.table = jnp.stack(rows + [self.z, self.lo])
+            straight = [self.own ^ v for v in (0, 2, 4, 6, 1, 3, 5, 7)]
+            self.table = jnp.stack(rows + [self.z, self.lo] + straight)
         else:
             self.table = jnp.stack([jnp.int32(i) for i in range(BLOCKS)] + [jnp.int32(0), self.lo])
 
@@ -2298,7 +2262,7 @@
         flags = flags.reshape(-1, LANES)
         vector = packed.reshape(-1, LANES)
         started = order(start_call, [small[0], large[0]], rows, vector, flags, first=1)
-        (narrow[0], broad[0]), stream, _, packed, flags = started
+        (narrow[0], broad[0]), stream, _, packed, flags, first_parts = started
         narrow[1:] = [net.gather(order.hold(v)) for v in small[1:]]
     else:
         for l in range(layers):
@@ -2317,7 +2281,10 @@
     idents = iter(range(10, 64))
     for l in range(layers):
         ahead = net.fast and l + 1 < layers
-        parts, _ = order(qkv_call, n, next(idents), [], l, low, packed, narrow[l], first=4)
+        if net.fast and l == 0:
+            parts = first_parts
+        else:
+            parts, _ = order(qkv_call, n, next(idents), [], l, low, packed, narrow[l], first=4)
         if ahead:
             broad[l + 1] = net.gather(order.hold(large[l + 1]))
         parts = [parts[0]] + [[net.shift(v, k) for k, v in enumerate(p)] for p in parts[1:]]
@@ -2371,15 +2338,19 @@
                     head_grad_call, n, 0, 4, net.table, *head_args, extra[0], first=4
                 )
                 head_pair = lax.ppermute(order.hold(send), "dp", net.other_way)
-            (odd,) = order(ffn_grad_call, 4, 4, net.table, *ffn_args, first=3)
+            ups = BLOCKS + 2 if l else 0
+            (odd,) = order(ffn_grad_call, ups, 4, 4, net.table, *ffn_args, first=4)
             jobs = [Hop(odd, "mate")]
             if more:
-                ffn_mine, sent = net.add_pair(order.hold(ffn_keep), ffn_pair)
-                ffn_last = lax.ppermute(order.want(sent), "dp", net.one_way)
+                wide_sums = [
+                    net.add_last(order.hold(ups_mine), ups_last),
+                    net.add_last(order.hold(downs_mine), downs_last),
+                ]
+                wide_near = [net.across(order.want(v)[2:], 1) for v in wide_sums]
             if last:
                 jobs.append(Turn(low_out, True, 1, moved[0]))
         else:
-            (full,) = order(ffn_grad_call, 0, BLOCKS, net.table, *ffn_args, first=3)
+            (full,) = order(ffn_grad_call, 0, 0, BLOCKS, net.table, *ffn_args, first=4)
             ffn_grads[l] = net.scatter(full, (WIDE, WIDE))
         res = order(
             proj_back_call, n, next(idents), jobs, l, grad, packed, narrow[l], rows, first=4
@@ -2392,13 +2363,17 @@
                 head_mine, sent = net.add_pair(order.hold(head_keep), head_pair)
                 head_last = lax.ppermute(sent, "dp", net.one_way)
                 order.want(sent)
-            ffn_keep, send = order(ffn_grad_call, 0, 4, net.table, *ffn_args, extra[0], first=3)
-            ffn_send = send
+            sums = order(ffn_grad_call, ups, 0, 4, net.table, *ffn_args, extra[0], first=4)
+            if l:
+                up_pair = lax.ppermute(order.hold(sums[1]), "dp", net.by_y)
+                down_pair = lax.ppermute(order.hold(sums[3]), "dp", net.other_way)
             if more:
-                ffn_sum = order.want(net.add_last(order.hold(ffn_mine), ffn_last))
-                ffn_near = net.across(ffn_sum[2:], 1)
+                wide_own = [
+                    order.want(net.add_last(order.hold(v[:2]), other))
+                    for v, other in zip(wide_sums, wide_near)
+                ]
             if l == 0:
-                ffn_pair = lax.ppermute(order.hold(send), "dp", net.other_way)
+                ffn_pair = lax.ppermute(order.hold(sums[1]), "dp", net.other_way)
         dparts, ready = [], []
         for u in range(units):
             ready += [net.shift(v, -k) for k, v in enumerate(dparts)]
@@ -2407,13 +2382,14 @@
             )
             if more and u == 0:
                 head_sum = order.want(net.add_last(order.hold(head_mine), head_last))
-                ffn_own = order.want(net.add_last(order.hold(ffn_sum[:2]), ffn_near))
+                wide_other = [net.across(order.hold(v[1]), 2) for v in wide_own]
+            if net.fast and l and u == 0:
+                order.want(down_pair)
         jobs = []
         if net.fast and l == 0:
-            ffn_mine, sent = net.add_pair(order.hold(ffn_keep), ffn_pair)
+            ffn_mine, sent = net.add_pair(order.hold(sums[0]), ffn_pair)
             ffn_last = lax.ppermute(order.want(sent), "dp", net.one_way)
         if more:
-            ffn_other = net.across(order.hold(ffn_own[1]), 2)
             head_near = net.across(order.hold(head_sum)[2:], 1)
         dlast, grad, in_turned, grads0, grad_low, *extra = order(
             qkv_back_call, n, next(idents), jobs, l, grad, low, packed, narrow[l], ready, dparts,
@@ -2424,10 +2400,16 @@
         if net.fast:
             if more:
                 head_own = order.want(net.add_last(order.hold(head_sum[:2]), head_near))
-                tops = [head_own, net.across(head_own[1], 2), ffn_own, ffn_other] + tops
+                pairs = [v for pair in zip(wide_own, wide_other) for v in pair]
+                tops = [head_own, net.across(head_own[1], 2), *pairs] + tops
             if l:
-                ffn_pair = lax.ppermute(order.hold(ffn_send), "dp", net.other_way)
                 (head_odd,) = order(head_grad_call, n, 4, 4, net.table, *head_args, first=4)
+                ups_mine, ups_sent = net.add_pair(order.hold(sums[0]), up_pair)
+                downs_mine, downs_sent = net.add_pair(order.hold(sums[2]), down_pair)
+                order.want(ups_sent)
+                order.want(downs_sent)
+                ups_last = lax.ppermute(ups_sent, "dp", net.by_x)
+                downs_last = lax.ppermute(downs_sent, "dp", net.one_way)
             else:
                 (full,) = order(head_grad_call, n, 0, BLOCKS, net.table, *head_args, first=4)
         else:

time: 997 us -> 982 us (0.985)
  Pallas kernels: 833 us -> 748 us
  waiting for transfers between devices: 30.4 us -> 68.8 us
  starting transfers between devices: 52.4 us -> 82.3 us
    pallas_call x11 -> x10, Pallas kernels: 371 us -> 314 us  [remote_call(): pl.pallas_call(kernel, out_shape=list(out_shape) + job_out, grid=grid, in...]
    pallas_call x8, Pallas kernels: 108 us -> 74.5 us  [unit_call(): pl.pallas_call(lambda *refs: kernel(n, *refs), out_shape=out_shape, grid_...]
    all_gather x2, waiting for transfers between devices: 16 us -> 41.5 us  [gather(): lax.all_gather(shard, ('dp', 'head')).reshape(BLOCKS, GROUPS, LANES, -1)]
    ppermute x2 -> x5, starting transfers between devices: 0.01 us -> 20.8 us  [the longest x1 13 us: local(): up_pair = lax.ppermute(order.hold(sums[1]), 'dp', net.by_y)]
    pallas_call x1, Pallas kernels: 144 us -> 160 us  [start_call(): pl.pallas_call(kernel, out_shape=[jax.ShapeDtypeStruct((BLOCKS, GROUPS) +...]
    ppermute x4 -> x6, starting transfers between devices: 26.3 us -> 31.3 us  [across(): return lax.ppermute(value, 'head', [(i, i ^ bits) for i in range(self.n)])]
  transfers between devices with their start and end apart: 24 -> 28, of which waited for: 6 -> 7; matrix products, arithmetic and copies ran while one was open for 3% -> 3% of each run, Pallas kernels for 43% -> 39%
where the time goes in v4:
time: 982 us; the launch traced here: 969 us
  Pallas kernels  748 us (76%)
  starting transfers between devices  82.3 us (8%)
  waiting for transfers between devices  68.8 us (7%)
  other arithmetic  30.3 us (3%)
  local copies, waits for them, and re-layouts  24.6 us (3%)
  between operations  15.6 us (2%)
    pallas_call x10, Pallas kernels, remote_call(): pl.pallas_call(kernel, out_shape=list(out_shape) + job_out, grid=grid, in...  314 us
    pallas_call x1, Pallas kernels, start_call(): pl.pallas_call(kernel, out_shape=[jax.ShapeDtypeStruct((BLOCKS, GROUPS) +...  160 us
    pallas_call x1, Pallas kernels, end_call(): pl.pallas_call(kernel, out_shape=outs, grid=(1,), in_specs=[HB] * 3 + [wh...  90.3 us
    pallas_call x8, Pallas kernels, unit_call(): pl.pallas_call(lambda *refs: kernel(n, *refs), out_shape=out_shape, grid_...  74.5 us
    pallas_call x4, Pallas kernels, ffn_grad_call(): pl.pallas_call(lambda *refs: ffn_grad_kernel(ups, first, count, added, *r...  48.6 us
    all_gather x2, waiting for transfers between devices, gather(): lax.all_gather(shard, ('dp', 'head')).reshape(BLOCKS, GROUPS, LANES, -1)  41.5 us
    ppermute x6, starting transfers between devices, across(): return lax.ppermute(value, 'head', [(i, i ^ bits) for i in range(self.n)])  31.3 us
    pallas_call x3, Pallas kernels, head_grad_call(): pl.pallas_call(lambda *refs: head_grad_kernel(n, first, count, added, *re...  29.7 us
  transfers between devices with their start and end apart: 28, of which 7 were waited for; matrix products, arithmetic and copies ran while one was open for 3% of the time, Pallas kernels for 39%

profile of v4, /device:TPU:0, one launch (start us, length us, event | category | flops | bytes accessed | tf_op | source)
XLA Modules:
  0.0 969.2 jit_solution(341153436836211987)
XLA Ops:
  10.6 2.7 convert_element_type.181
  13.2 2.7 pack.1
  15.9 159.6 %start.1 = (bf16[8,4,128,1024]{3,2,1,0:T(8,128)(2,1)}, bf16[8,4,128,2048]{3,2,1,0:T(8,128)(2,1)}, bf16[512,1024]{1,0:T(8,128)(2,1)}, bf16[2,512,256]{2,1,0:T(8,1...) custom-call(bf16[128,1024]{1,0:T(8,128)(2,1)} %get-tuple-element.192, ...), custom_call_target="tpu_custom_call" | custom-call | bytes 314572800 | tf_op jit(solution)/shard_map/start/pallas_call | solution.py:1660
  180.9 7.4 attention.4
  190.1 6.9 collective-permute-done.2.refs_6_
  197.7 7.5 attention.5
  205.2 26.0 %projection.2 = (f32[512,1024]{1,0:T(8,128)}, bf16[512,1024]{1,0:T(8,128)(2,1)}, f32[8,1024]{1,0:T(8,128)}) custom-call(f32[512,1]{1,0:T(8,128)} %get-tuple-element.195.refs_0_.refs_4_, bf16[512,1024]{1,0:T(8,128)(2,1)} %get-tuple-element.213.refs_1_, f32[4,56,128]{2,1,0:T(8,128)} %get-tuple-element.214.refs_2_.refs_1_.refs_5_, ...), custom_call_target="tpu_custom_call" | custom-call | flops 16106127360 | bytes 10485760 | tf_op jit(solution)/shard_map/projection/pallas_call | solution.py:396
  231.2 25.8 %ffn.2 = (bf16[4,512,1024]{2,1,0:T(8,128)(2,1)}, bf16[4,512,1024]{2,1,0:T(8,128)(2,1)}, bf16[4,512,1024]{2,1,0:T(8,128)(2,1)}, bf16[512,1024]{1,0:T(8,128)(2,1)}...) custom-call(f32[512,1]{1,0:T(8,128)} %get-tuple-element.195.refs_0_.refs_4_, ...), custom_call_target="tpu_custom_call" | custom-call | flops 34359738368 | bytes 10485760 | tf_op jit(solution)/shard_map/ffn/pallas_call | solution.py:348
  258.8 28.6 %qkv.3 = (bf16[3,512,128]{2,1,0:T(8,128)(2,1)}, bf16[3,512,128]{2,1,0:T(8,128)(2,1)}, bf16[3,512,128]{2,1,0:T(8,128)(2,1)}, bf16[3,512,128]{2,1,0:T(8,128)(2,1)}...) custom-call(bf16[512,1024]{1,0:T(8,128)(2,1)} %get-tuple-element.220, ...), custom_call_target="tpu_custom_call" | custom-call | flops 32212254720 | bytes 10485760 | tf_op jit(solution)/shard_map/qkv/pallas_call | solution.py:396
  289.2 12.0 %collective-permute-start.5 = (bf16[3,512,128]{2,1,0:T(8,128)(2,1)}, bf16[3,512,128]{2,1,0:T(8,128)(2,1)S(1)}, u32[]{:S(2)}, u32[]{:S(2)}) collective-permute-start(bf16[3,512,128]{2,1,0:T(8,128)(2,1)} %get-tuple-element.233), channel_id=1, source_target_pairs={{0,12},{4,0},{8,4},{12,8},{16,28},{20,16},{24,20},{28,24},{1,13},{... | collective-permute-start | bytes 1179656 | tf_op jit(solution)/shard_map/ppermute | solution.py:2137
  301.2 7.3 attention.6
  308.5 12.2 %collective-permute-done.5.refs_6_ = bf16[3,512,128]{2,1,0:T(8,128)(2,1)S(1)} collective-permute-done((bf16[3,512,128]{2,1,0:T(8,128)(2,1)}, bf16[3,512,128]{2,1,0:T(8,128)(2,1)S(1)}, u32[]{:S(2)}, u32[]{:S(2)}) %collective-permute-start.5) | collective-permute-done | bytes 393248 | tf_op jit(solution)/shard_map/ppermute | solution.py:2137
  321.5 7.2 attention.7
  328.8 38.4 %projection.3 = (f32[512,1024]{1,0:T(8,128)}, bf16[512,1024]{1,0:T(8,128)(2,1)}, f32[8,1024]{1,0:T(8,128)}, bf16[512,1024]{1,0:T(8,128)(2,1)}) custom-call(f32[512,1]{1,0:T(8,128)} %get-tuple-element.195.refs_0_.refs_4_, f32[512,1024]{1,0:T(8,128)} %get-tuple-element.235.refs_1_, f32[4,56,128]{2,1,0:T(8,128)} %get-tuple-element.214.refs_2_.refs_1_.refs_5_, ...), custom_call_target="tpu_custom_call" | custom-call | flops 16106127360 | bytes 10485760 | tf_op jit(solution)/shard_map/projection/pallas_call | solution.py:396
  367.2 39.8 %all-gather.7.cloned.1.call-done = bf16[4096,2048]{1,0:T(8,128)(2,1)} async-done(((bf16[128,2048]{1,0:T(8,128)(2,1)}), bf16[4096,2048]{1,0:T(8,128)(2,1)}) %all-gather.7.cloned.1.call-update) | async-done | bytes 16777232 | tf_op jit(solution)/shard_map/all_gather | solution.py:2147
  407.0 26.2 %ffn.3 = (bf16[4,512,1024]{2,1,0:T(8,128)(2,1)}, bf16[4,512,1024]{2,1,0:T(8,128)(2,1)}, bf16[4,512,1024]{2,1,0:T(8,128)(2,1)}, bf16[512,1024]{1,0:T(8,128)(2,1)}...) custom-call(f32[512,1]{1,0:T(8,128)} %get-tuple-element.195.refs_0_., ...), custom_call_target="tpu_custom_call", output_to_operand_aliasing={{8}: (5, {})} | custom-call | flops 34359738368 | bytes 10485760 | tf_op jit(solution)/shard_map/ffn/pallas_call | solution.py:396
  433.1 34.3 %ffn_back.2 = (bf16[4,512,1024]{2,1,0:T(8,128)(2,1)}, bf16[8,128,512]{2,1,0:T(8,128)(2,1)}, bf16[8,128,512]{2,1,0:T(8,128)(2,1)}, f32[512,1024]{1,0:T(8,128)}, f...) custom-call(bf16[512,1024]{1,0:T(8,128)(2,1)} %get-tuple-element.242.refs_0_, ...), custom_call_target="tpu_custom_call" | custom-call | flops 34359738368 | bytes 10485760 | tf_op jit(solution)/shard_map/ffn_back/pallas_call | solution.py:396
  467.4 11.7 %ffn_grad.4.refs_4_ = bf16[4,4,128,2048]{3,2,1,0:T(8,128)(2,1)} custom-call(s32[18]{0:T(128)} %stack.63.refs_0_, bf16[8,128,512]{2,1,0:T(8,128)(2,1)} %get-tuple-element.257.refs_1_, bf16[8,128,512]{2,1,0:T(8,128)(2,1)} %get-tuple-element.251.refs_2_, bf16[4,512,1024]{2,1,0:T(8,128)(2,1)} %get-tuple-element.249.refs_3_.refs_4_, ...), custom_call_target="tpu_custom_call" | custom-call | flops 17179869184 | bytes 25165824 | tf_op jit(solution)/shard_map/ffn_grad/pallas_call | solution.py:1287
  479.1 28.2 %projection_back.2 = (bf16[4,512,128]{2,1,0:T(8,128)(2,1)}, bf16[4,512,128]{2,1,0:T(8,128)(2,1)}, bf16[8,128,512]{2,1,0:T(8,128)(2,1)}, bf16[512,1024]{1,0:T(8,1...) custom-call(f32[512,1024]{1,0:T(8,128)} %get-tuple-element.269.refs_, ...), custom_call_target="tpu_custom_call", output_to_operand_aliasing={{6}: (6, {})} | custom-call | flops 16106127360 | bytes 10485760 | tf_op jit(solution)/shard_map/projection_back/pallas_call | solution.py:396
  507.3 12.7 %ffn_grad.5 = (bf16[2,4,128,1024]{3,2,1,0:T(8,128)(2,1)}, bf16[2,4,128,1024]{3,2,1,0:T(8,128)(2,1)}, bf16[2,4,128,1024]{3,2,1,0:T(8,128)(2,1)}, bf16[2,4,128,1024]{3,2,1,0:T(8,128)(2,1)}) custom-call(s32[18]{0:T(128)} %stack.63.refs_0_, bf16[8,128,512]{2,1,0:T(8,128)(2,1)} %get-tuple-element.257.refs_1_, bf16[8,128,512]{2,1,0:T(8,128)(2,1)} %get-tuple-element.251.refs_2_, ...), custom_call_target="tpu_custom_call" | custom-call | flops 17179869184 | bytes 25165824 | tf_op jit(solution)/shard_map/ffn_grad/pallas_call | solution.py:1287
  520.0 5.1 collective-permute-start.6
  525.1 11.2 %attention_back.4 = (bf16[3,512,128]{2,1,0:T(8,128)(2,1)}, bf16[3,512,128]{2,1,0:T(8,128)(2,1)}, bf16[3,512,128]{2,1,0:T(8,128)(2,1)}, bf16[3,512,128]{2,1,0:T(8,128)(2,1)}) custom-call(s32[16]{0:T(128)} %get-tuple-element.197.refs_0_, bf16[4,512,128]{2,1,0:T(8,128)(2,1)} %get-tuple-element.320.refs_1_, bf16[512,128]{1,0:T(8,128)(2,1)} %get-tuple-element.201.refs_2_, ...), custom_call_target="tpu_custom_call" | custom-call | flops 30064771072 | bytes 8388608 | tf_op jit(solution)/shard_map/attention_back/pallas_call | solution.py:633
  537.2 13.0 %collective-permute-start.10 = (bf16[2,4,128,1024]{3,2,1,0:T(8,128)(2,1)}, bf16[2,4,128,1024]{3,2,1,0:T(8,128)(2,1)}, u32[]{:S(2)}, u32[]{:S(2)}) collective-permute-start(bf16[2,4,128,1024]{3,2,1,0:T(8,128)(2,1)} %get-tuple-element.287), channel_id=1, source_target_pairs={{0,16},{4,20},{8,24},{12,28},{16,0},{20,4},{24,8},{28,12},{1,17},{... | collective-permute-start | bytes 6291464 | tf_op jit(solution)/shard_map/ppermute | solution.py:2368
  550.2 11.6 %attention_back.5 = (bf16[3,512,128]{2,1,0:T(8,128)(2,1)}, bf16[3,512,128]{2,1,0:T(8,128)(2,1)}, bf16[3,512,128]{2,1,0:T(8,128)(2,1)}, bf16[3,512,128]{2,1,0:T(8,128)(2,1)}) custom-call(s32[16]{0:T(128)} %get-tuple-element.197.refs_0_, bf16[4,512,128]{2,1,0:T(8,128)(2,1)} %get-tuple-element.320.refs_1_, bf16[512,128]{1,0:T(8,128)(2,1)} %get-tuple-element.201.refs_2_, ...), custom_call_target="tpu_custom_call" | custom-call | flops 30064771072 | bytes 8388608 | tf_op jit(solution)/shard_map/attention_back/pallas_call | solution.py:633
  563.0 31.7 %qkv_back.2 = (bf16[3,512,128]{2,1,0:T(8,128)(2,1)}, bf16[3,512,128]{2,1,0:T(8,128)(2,1)}, bf16[3,512,128]{2,1,0:T(8,128)(2,1)}, bf16[3,512,128]{2,1,0:T(8,128)(...) custom-call(f32[512,1024]{1,0:T(8,128)} %get-tuple-element.269.refs_, ...), custom_call_target="tpu_custom_call" | custom-call | flops 26843545600 | bytes 10485760 | tf_op jit(solution)/shard_map/qkv_back/pallas_call | solution.py:396
  594.7 8.3 head_grad.3.refs_7_
  603.1 3.7 fusion.4
  606.9 2.0 fusion.5
  610.9 35.5 %ffn_back.3 = (bf16[4,512,1024]{2,1,0:T(8,128)(2,1)}, bf16[8,128,512]{2,1,0:T(8,128)(2,1)}, bf16[8,128,512]{2,1,0:T(8,128)(2,1)}, f32[512,1024]{1,0:T(8,128)}, f...) custom-call(f32[512,1024]{1,0:T(8,128)} %get-tuple-element.290.refs_0_, ...), custom_call_target="tpu_custom_call" | custom-call | flops 34359738368 | bytes 10485760 | tf_op jit(solution)/shard_map/ffn_back/pallas_call | solution.py:396
  646.4 9.4 head_grad.4
  655.8 2.5 collective-permute-start.13
  658.3 11.5 %ffn_grad.6.refs_4_ = bf16[4,4,128,2048]{3,2,1,0:T(8,128)(2,1)} custom-call(s32[18]{0:T(128)} %stack.63.refs_0_, bf16[8,128,512]{2,1,0:T(8,128)(2,1)} %get-tuple-element.311.refs_1_, bf16[8,128,512]{2,1,0:T(8,128)(2,1)} %get-tuple-element.301.refs_2_, bf16[4,512,1024]{2,1,0:T(8,128)(2,1)} %get-tuple-element.296.refs_3_.refs_4_, ...), custom_call_target="tpu_custom_call" | custom-call | flops 17179869184 | bytes 25165824 | tf_op jit(solution)/shard_map/ffn_grad/pallas_call | solution.py:1287
  673.8 2.0 collective-permute-start.15
  675.8 21.3 %projection_back.3 = (bf16[4,512,128]{2,1,0:T(8,128)(2,1)}, bf16[4,512,128]{2,1,0:T(8,128)(2,1)}, bf16[8,128,512]{2,1,0:T(8,128)(2,1)}, bf16[512,1024]{1,0:T(8,1...) custom-call(f32[512,1024]{1,0:T(8,128)} %get-tuple-element.327.refs_0_, ...), custom_call_target="tpu_custom_call" | custom-call | flops 16106127360 | bytes 10485760 | tf_op jit(solution)/shard_map/projection_back/pallas_call | solution.py:396
  697.2 3.6 fusion.7
  701.4 12.7 %ffn_grad.7 = (bf16[2,4,128,2048]{3,2,1,0:T(8,128)(2,1)}, bf16[2,4,128,2048]{3,2,1,0:T(8,128)(2,1)}) custom-call(s32[18]{0:T(128)} %stack.63.refs_0_, bf16[8,128,512]{2,1,0:T(8,128)(2,1)} %get-tuple-element.311.refs_1_, bf16[8,128,512]{2,1,0:T(8,128)(2,1)} %get-tuple-element.301.refs_2_, bf16[4,512,1024]{2,1,0:T(8,128)(2,1)} %get-tuple-element.296.refs_3_.refs_4_, ...), custom_call_target="tpu_custom_call" | custom-call | flops 17179869184 | bytes 25165824 | tf_op jit(solution)/shard_map/ffn_grad/pallas_call | solution.py:1287
  717.6 11.1 %attention_back.6 = (bf16[3,512,128]{2,1,0:T(8,128)(2,1)}, bf16[3,512,128]{2,1,0:T(8,128)(2,1)}, bf16[3,512,128]{2,1,0:T(8,128)(2,1)}, bf16[3,512,128]{2,1,0:T(8,128)(2,1)}) custom-call(s32[16]{0:T(128)} %get-tuple-element.197.refs_0_, bf16[4,512,128]{2,1,0:T(8,128)(2,1)} %get-tuple-element.320.refs_1_, bf16[512,128]{1,0:T(8,128)(2,1)} %get-tuple-element.201.refs_2_, ...), custom_call_target="tpu_custom_call" | custom-call | flops 30064771072 | bytes 8388608 | tf_op jit(solution)/shard_map/attention_back/pallas_call | solution.py:633
  730.1 13.7 %collective-permute-start.25 = (bf16[128,1024]{1,0:T(8,128)(2,1)}, bf16[128,1024]{1,0:T(8,128)(2,1)S(1)}, u32[]{:S(2)}, u32[]{:S(2)}) collective-permute-start(bf16[128,1024]{1,0:T(8,128)(2,1)} %slice_bitcast_fusion), channel_id=1, source_target_pairs={{0,2},{1,3},{2,0},{3,1},{4,6},{5,7},{6,4},{7,5},{8,10},{9,11},{10,... | collective-permute-start | bytes 786440 | tf_op jit(solution)/shard_map/ppermute | solution.py:2140
  747.9 11.3 %attention_back.7 = (bf16[3,512,128]{2,1,0:T(8,128)(2,1)}, bf16[3,512,128]{2,1,0:T(8,128)(2,1)}, bf16[3,512,128]{2,1,0:T(8,128)(2,1)}, bf16[3,512,128]{2,1,0:T(8,128)(2,1)}) custom-call(s32[16]{0:T(128)} %get-tuple-element.197.refs_0_, bf16[4,512,128]{2,1,0:T(8,128)(2,1)} %get-tuple-element.320.refs_1_, bf16[512,128]{1,0:T(8,128)(2,1)} %get-tuple-element.201.refs_2_, ...), custom_call_target="tpu_custom_call" | custom-call | flops 30064771072 | bytes 8388608 | tf_op jit(solution)/shard_map/attention_back/pallas_call | solution.py:633
  760.0 5.7 collective-permute-done.17
  765.7 7.2 collective-permute-start.20
  773.0 5.5 fusion.1
  782.2 44.1 %qkv_back.3 = (bf16[3,512,128]{2,1,0:T(8,128)(2,1)}, bf16[3,512,128]{2,1,0:T(8,128)(2,1)}, bf16[3,512,128]{2,1,0:T(8,128)(2,1)}, bf16[3,512,128]{2,1,0:T(8,128)(...) custom-call(f32[512,1024]{1,0:T(8,128)} %get-tuple-element.327.refs_, ...), custom_call_target="tpu_custom_call" | custom-call | flops 26843545600 | bytes 10485760 | tf_op jit(solution)/shard_map/qkv_back/pallas_call | solution.py:396
  826.6 14.7 %collective-permute-start.23 = (bf16[128,1024]{1,0:T(8,128)(2,1)S(1)}, bf16[128,1024]{1,0:T(8,128)(2,1)S(1)}, u32[]{:S(2)}, u32[]{:S(2)}) collective-permute-start(bf16[128,1024]{1,0:T(8,128)(2,1)S(1)} %slice_bitcast_fusion.2), channel_id=1, source_target_pairs={{0,2},{1,3},{2,0},{3,1},{4,6},{5,7},{6,4},{7,5},{8,10},{9,11},{10,... | collective-permute-start | bytes 786440 | tf_op jit(solution)/shard_map/ppermute | solution.py:2140
  841.2 12.0 %head_grad.5.refs_1_ = bf16[8,4,128,1024]{3,2,1,0:T(8,128)(2,1)} custom-call(s32[18]{0:T(128)} %stack.63.refs_0_, bf16[8,128,512]{2,1,0:T(8,128)(2,1)} %get-tuple-element.339.refs_1_, bf16[8,128,512]{2,1,0:T(8,128)(2,1)} %get-tuple-element.340.refs_2_, bf16[512,1024]{1,0:T(8,128)(2,1)} %get-tuple-element.341.refs_3_, ...), custom_call_target="tpu_custom_call" | custom-call | flops 34359738368 | bytes 16777216 | tf_op jit(solution)/shard_map/head_grad/pallas_call | solution.py:1332
  853.3 3.8 add_convert_fusion.refs_2_
  857.9 90.3 %end.1 = (f32[4,512,256]{2,1,0:T(8,128)}, f32[4,512,256]{2,1,0:T(8,128)}, f32[2,3,128,256]{3,2,1,0:T(8,128)}, f32[2,256,128]{2,1,0:T(8,128)}, f32[2,128,1024]{2,...) custom-call(bf16[512,1024]{1,0:T(8,128)(2,1)} %get-tuple-element.345, ...), custom_call_target="tpu_custom_call" | custom-call | bytes 314572800 | tf_op jit(solution)/shard_map/end/pallas_call | solution.py:2042
  952.2 3.2 copy.40
  (144 shorter events, 48.4 us)
Async XLA Ops:
  7.2 251.6 %all-gather.5.cloned.1.call-start = ((), (), s32[]{:S(2)}) async-start(), calls=%async_computation | async-start | bytes 8650752 | tf_op jit(solution)/shard_map/all_gather | solution.py:2147
  175.6 231.4 %all-gather.7.cloned.1.call-start = ((), (), s32[]{:S(2)}) async-start(), calls=%async_computation.1 | async-start | bytes 17301504 | tf_op jit(solution)/shard_map/all_gather | solution.py:2147
  176.3 13.7 %collective-permute-start = (bf16[3,512,128]{2,1,0:T(8,128)(2,1)}, bf16[3,512,128]{2,1,0:T(8,128)(2,1)S(1)}, u32[]{:S(2)}, u32[]{:S(2)}) collective-permute-start(bf16[3,512,128]{2,1,0:T(8,128)(2,1)} %get-tuple-element.209), channel_id=1, source_target_pairs={{0,4},{4,8},{8,12},{12,0},{16,20},{20,24},{24,28},{28,16},{1,5},{5... | collective-permute-start | bytes 1179656 | tf_op jit(solution)/shard_map/ppermute | solution.py:2137
  176.5 13.5 %collective-permute-start.1 = (bf16[3,512,128]{2,1,0:T(8,128)(2,1)}, bf16[3,512,128]{2,1,0:T(8,128)(2,1)S(1)}, u32[]{:S(2)}, u32[]{:S(2)}) collective-permute-start(bf16[3,512,128]{2,1,0:T(8,128)(2,1)} %get-tuple-element.210), channel_id=1, source_target_pairs={{0,8},{4,12},{8,0},{12,4},{16,24},{20,28},{24,16},{28,20},{1,9},{5... | collective-permute-start | bytes 1179656 | tf_op jit(solution)/shard_map/ppermute | solution.py:2137
  177.5 19.4 %collective-permute-start.2 = (bf16[3,512,128]{2,1,0:T(8,128)(2,1)}, bf16[3,512,128]{2,1,0:T(8,128)(2,1)S(1)}, u32[]{:S(2)}, u32[]{:S(2)}) collective-permute-start(bf16[3,512,128]{2,1,0:T(8,128)(2,1)} %get-tuple-element.211), channel_id=1, source_target_pairs={{0,12},{4,0},{8,4},{12,8},{16,28},{20,16},{24,20},{28,24},{1,13},{... | collective-permute-start | bytes 1179656 | tf_op jit(solution)/shard_map/ppermute | solution.py:2137
  180.8 7.4 copy-start.9
  190.0 6.9 copy-start.22
  190.0 6.9 copy-start.23
  287.5 21.0 %collective-permute-start.3 = (bf16[3,512,128]{2,1,0:T(8,128)(2,1)}, bf16[3,512,128]{2,1,0:T(8,128)(2,1)S(1)}, u32[]{:S(2)}, u32[]{:S(2)}) collective-permute-start(bf16[3,512,128]{2,1,0:T(8,128)(2,1)} %get-tuple-element.231), channel_id=1, source_target_pairs={{0,4},{4,8},{8,12},{12,0},{16,20},{20,24},{24,28},{28,16},{1,5},{5... | collective-permute-start | bytes 1179656 | tf_op jit(solution)/shard_map/ppermute | solution.py:2137
  288.1 20.4 %collective-permute-start.4 = (bf16[3,512,128]{2,1,0:T(8,128)(2,1)}, bf16[3,512,128]{2,1,0:T(8,128)(2,1)S(1)}, u32[]{:S(2)}, u32[]{:S(2)}) collective-permute-start(bf16[3,512,128]{2,1,0:T(8,128)(2,1)} %get-tuple-element.232), channel_id=1, source_target_pairs={{0,8},{4,12},{8,0},{12,4},{16,24},{20,28},{24,16},{28,20},{1,9},{5... | collective-permute-start | bytes 1179656 | tf_op jit(solution)/shard_map/ppermute | solution.py:2137
  289.2 31.5 %collective-permute-start.5 = (bf16[3,512,128]{2,1,0:T(8,128)(2,1)}, bf16[3,512,128]{2,1,0:T(8,128)(2,1)S(1)}, u32[]{:S(2)}, u32[]{:S(2)}) collective-permute-start(bf16[3,512,128]{2,1,0:T(8,128)(2,1)} %get-tuple-element.233), channel_id=1, source_target_pairs={{0,12},{4,0},{8,4},{12,8},{16,28},{20,16},{24,20},{28,24},{1,13},{... | collective-permute-start | bytes 1179656 | tf_op jit(solution)/shard_map/ppermute | solution.py:2137
  308.5 12.3 %copy-start.25 = (bf16[3,512,128]{2,1,0:T(8,128)(2,1)}, bf16[3,512,128]{2,1,0:T(8,128)(2,1)S(1)}, u32[]{:S(2)}) copy-start(bf16[3,512,128]{2,1,0:T(8,128)(2,1)S(1)} %collective-permute-done.3.refs_4_) | copy-start | bytes 1179652
  308.5 12.3 %copy-start.26 = (bf16[3,512,128]{2,1,0:T(8,128)(2,1)}, bf16[3,512,128]{2,1,0:T(8,128)(2,1)S(1)}, u32[]{:S(2)}) copy-start(bf16[3,512,128]{2,1,0:T(8,128)(2,1)S(1)} %collective-permute-done.4.refs_5_) | copy-start | bytes 1179652
  520.0 30.2 %collective-permute-start.6 = (bf16[2,4,128,1024]{3,2,1,0:T(8,128)(2,1)}, bf16[2,4,128,1024]{3,2,1,0:T(8,128)(2,1)S(1)}, u32[]{:S(2)}, u32[]{:S(2)}) collective-permute-start(bf16[2,4,128,1024]{3,2,1,0:T(8,128)(2,1)} %get-tuple-element.264), channel_id=1, source_target_pairs={{0,16},{4,12},{8,24},{12,4},{16,0},{20,28},{24,8},{28,20},{1,17},{... | collective-permute-start | bytes 6291464 | tf_op jit(solution)/shard_map/ppermute | solution.py:2369
  536.3 25.5 %collective-permute-start.7 = (bf16[3,512,128]{2,1,0:T(8,128)(2,1)}, bf16[3,512,128]{2,1,0:T(8,128)(2,1)S(1)}, u32[]{:S(2)}, u32[]{:S(2)}) collective-permute-start(bf16[3,512,128]{2,1,0:T(8,128)(2,1)} %get-tuple-element.270), channel_id=1, source_target_pairs={{0,12},{4,0},{8,4},{12,8},{16,28},{20,16},{24,20},{28,24},{1,13},{... | collective-permute-start | bytes 1179656 | tf_op jit(solution)/shard_map/ppermute | solution.py:2137
  536.3 25.5 %collective-permute-start.8 = (bf16[3,512,128]{2,1,0:T(8,128)(2,1)}, bf16[3,512,128]{2,1,0:T(8,128)(2,1)S(1)}, u32[]{:S(2)}, u32[]{:S(2)}) collective-permute-start(bf16[3,512,128]{2,1,0:T(8,128)(2,1)} %get-tuple-element.271), channel_id=1, source_target_pairs={{0,8},{4,12},{8,0},{12,4},{16,24},{20,28},{24,16},{28,20},{1,9},{5... | collective-permute-start | bytes 1179656 | tf_op jit(solution)/shard_map/ppermute | solution.py:2137
  536.9 25.3 %collective-permute-start.9 = (bf16[3,512,128]{2,1,0:T(8,128)(2,1)}, bf16[3,512,128]{2,1,0:T(8,128)(2,1)S(1)}, u32[]{:S(2)}, u32[]{:S(2)}) collective-permute-start(bf16[3,512,128]{2,1,0:T(8,128)(2,1)} %get-tuple-element.272), channel_id=1, source_target_pairs={{0,4},{4,8},{8,12},{12,0},{16,20},{20,24},{24,28},{28,16},{1,5},{5... | collective-permute-start | bytes 1179656 | tf_op jit(solution)/shard_map/ppermute | solution.py:2137
  537.2 65.9 %collective-permute-start.10 = (bf16[2,4,128,1024]{3,2,1,0:T(8,128)(2,1)}, bf16[2,4,128,1024]{3,2,1,0:T(8,128)(2,1)}, u32[]{:S(2)}, u32[]{:S(2)}) collective-permute-start(bf16[2,4,128,1024]{3,2,1,0:T(8,128)(2,1)} %get-tuple-element.287), channel_id=1, source_target_pairs={{0,16},{4,20},{8,24},{12,28},{16,0},{20,4},{24,8},{28,12},{1,17},{... | collective-permute-start | bytes 6291464 | tf_op jit(solution)/shard_map/ppermute | solution.py:2368
  550.2 11.6 %copy-start.6 = (bf16[2,4,128,1024]{3,2,1,0:T(8,128)(2,1)}, bf16[2,4,128,1024]{3,2,1,0:T(8,128)(2,1)S(1)}, u32[]{:S(2)}) copy-start(bf16[2,4,128,1024]{3,2,1,0:T(8,128)(2,1)S(1)} %collective-permute-done.6) | copy-start | bytes 6291460
  594.7 8.4 copy-start.5
  603.1 3.8 copy-start.4
  603.1 3.8 copy-start.7
  606.8 64.6 %collective-permute-start.11 = (bf16[4,128,1024]{2,1,0:T(8,128)(2,1)}, bf16[4,128,1024]{2,1,0:T(8,128)(2,1)S(1)}, u32[]{:S(2)}, u32[]{:S(2)}) collective-permute-start(bf16[4,128,1024]{2,1,0:T(8,128)(2,1)} %get-tuple-element.402), channel_id=1, source_target_pairs={{0,8},{4,12},{8,0},{12,4},{16,24},{20,28},{24,16},{28,20},{1,9},{5... | collective-permute-start | bytes 3145736 | tf_op jit(solution)/shard_map/ppermute | solution.py:2411
  608.9 60.9 %collective-permute-start.12 = (bf16[4,128,1024]{2,1,0:T(8,128)(2,1)}, bf16[4,128,1024]{2,1,0:T(8,128)(2,1)}, u32[]{:S(2)}, u32[]{:S(2)}) collective-permute-start(bf16[4,128,1024]{2,1,0:T(8,128)(2,1)} %get-tuple-element.400), channel_id=1, source_target_pairs={{0,8},{4,20},{8,0},{12,28},{16,24},{20,4},{24,16},{28,12},{1,9},{5... | collective-permute-start | bytes 3145736 | tf_op jit(solution)/shard_map/ppermute | solution.py:2412
  655.8 41.3 %collective-permute-start.13 = (bf16[2,4,128,1024]{3,2,1,0:T(8,128)(2,1)}, bf16[2,4,128,1024]{3,2,1,0:T(8,128)(2,1)}, u32[]{:S(2)}, u32[]{:S(2)}) collective-permute-start(bf16[2,4,128,1024]{3,2,1,0:T(8,128)(2,1)} %get-tuple-element.310), channel_id=1, source_target_pairs={{0,16},{4,12},{8,24},{12,4},{16,0},{20,28},{24,8},{28,20},{1,17},{... | collective-permute-start | bytes 6291464 | tf_op jit(solution)/shard_map/ppermute | solution.py:2340
  672.9 42.5 %collective-permute-start.14 = (bf16[2,128,1024]{2,1,0:T(8,128)(2,1)}, bf16[2,128,1024]{2,1,0:T(8,128)(2,1)}, u32[]{:S(2)}, u32[]{:S(2)}) collective-permute-start(bf16[2,128,1024]{2,1,0:T(8,128)(2,1)} %get-tuple-element.406), channel_id=1, source_target_pairs={{0,1},{1,0},{2,3},{3,2},{4,5},{5,4},{6,7},{7,6},{8,9},{9,8},{10,11... | collective-permute-start | bytes 1572872 | tf_op jit(solution)/shard_map/ppermute | solution.py:2140
  673.8 40.3 %collective-permute-start.15 = (bf16[2,128,1024]{2,1,0:T(8,128)(2,1)S(1)}, bf16[2,128,1024]{2,1,0:T(8,128)(2,1)}, u32[]{:S(2)}, u32[]{:S(2)}) collective-permute-start(bf16[2,128,1024]{2,1,0:T(8,128)(2,1)S(1)} %get-tuple-element.404), channel_id=1, source_target_pairs={{0,1},{1,0},{2,3},{3,2},{4,5},{5,4},{6,7},{7,6},{8,9},{9,8},{10,11... | collective-permute-start | bytes 1572872 | tf_op jit(solution)/shard_map/ppermute | solution.py:2140
  675.8 21.3 %copy-start.8 = (bf16[2,4,128,1024]{3,2,1,0:T(8,128)(2,1)S(1)}, bf16[2,4,128,1024]{3,2,1,0:T(8,128)(2,1)}, u32[]{:S(2)}) copy-start(bf16[2,4,128,1024]{3,2,1,0:T(8,128)(2,1)} %get-tuple-element.308) | copy-start | bytes 6291460
  700.7 43.3 %collective-permute-start.16 = (bf16[4,128,1024]{2,1,0:T(8,128)(2,1)}, bf16[4,128,1024]{2,1,0:T(8,128)(2,1)S(1)}, u32[]{:S(2)}, u32[]{:S(2)}) collective-permute-start(bf16[4,128,1024]{2,1,0:T(8,128)(2,1)} %get-tuple-element.398), channel_id=1, source_target_pairs={{0,8},{4,20},{8,0},{12,28},{16,24},{20,4},{24,16},{28,12},{1,9},{5... | collective-permute-start | bytes 3145736 | tf_op jit(solution)/shard_map/ppermute | solution.py:2364
  701.4 12.7 %copy-start.12 = (bf16[2,128,1024]{2,1,0:T(8,128)(2,1)S(1)}, bf16[2,128,1024]{2,1,0:T(8,128)(2,1)}, u32[]{:S(2)}) copy-start(bf16[2,128,1024]{2,1,0:T(8,128)(2,1)} %get-tuple-element.315) | copy-start | bytes 1572868
  701.4 14.0 %copy-start.11 = (bf16[2,128,1024]{2,1,0:T(8,128)(2,1)S(1)}, bf16[2,128,1024]{2,1,0:T(8,128)(2,1)}, u32[]{:S(2)}) copy-start(bf16[2,128,1024]{2,1,0:T(8,128)(2,1)} %get-tuple-element.314) | copy-start | bytes 1572868
  715.4 14.0 %copy-start.1 = (bf16[2,128,1024]{2,1,0:T(8,128)(2,1)}, bf16[2,128,1024]{2,1,0:T(8,128)(2,1)S(1)}, u32[]{:S(2)}) copy-start(bf16[2,128,1024]{2,1,0:T(8,128)(2,1)S(1)} %add_convert_fusion.13.refs_9_) | copy-start | bytes 1572868
  716.8 11.9 %copy-start.2 = (bf16[2,128,1024]{2,1,0:T(8,128)(2,1)}, bf16[2,128,1024]{2,1,0:T(8,128)(2,1)S(1)}, u32[]{:S(2)}) copy-start(bf16[2,128,1024]{2,1,0:T(8,128)(2,1)S(1)} %add_convert_fusion.14.refs_7_) | copy-start | bytes 1572868
  716.8 48.9 %collective-permute-start.17 = (bf16[2,4,128,2048]{3,2,1,0:T(8,128)(2,1)}, bf16[2,4,128,2048]{3,2,1,0:T(8,128)(2,1)}, u32[]{:S(2)}, u32[]{:S(2)}) collective-permute-start(bf16[2,4,128,2048]{3,2,1,0:T(8,128)(2,1)} %get-tuple-element.326), channel_id=1, source_target_pairs={{0,16},{4,12},{8,24},{12,4},{16,0},{20,28},{24,8},{28,20},{1,17},{... | collective-permute-start | bytes 12582920 | tf_op jit(solution)/shard_map/ppermute | solution.py:2376
  730.1 127.0 %collective-permute-start.25 = (bf16[128,1024]{1,0:T(8,128)(2,1)}, bf16[128,1024]{1,0:T(8,128)(2,1)S(1)}, u32[]{:S(2)}, u32[]{:S(2)}) collective-permute-start(bf16[128,1024]{1,0:T(8,128)(2,1)} %slice_bitcast_fusion), channel_id=1, source_target_pairs={{0,2},{1,3},{2,0},{3,1},{4,6},{5,7},{6,4},{7,5},{8,10},{9,11},{10,... | collective-permute-start | bytes 786440 | tf_op jit(solution)/shard_map/ppermute | solution.py:2140
  743.9 113.2 %collective-permute-start.24 = (bf16[128,1024]{1,0:T(8,128)(2,1)}, bf16[128,1024]{1,0:T(8,128)(2,1)}, u32[]{:S(2)}, u32[]{:S(2)}) collective-permute-start(bf16[128,1024]{1,0:T(8,128)(2,1)} %slice_bitcast_fusion.1), channel_id=1, source_target_pairs={{0,2},{1,3},{2,0},{3,1},{4,6},{5,7},{6,4},{7,5},{8,10},{9,11},{10,... | collective-permute-start | bytes 786440 | tf_op jit(solution)/shard_map/ppermute | solution.py:2140
  743.9 34.6 %collective-permute-start.18 = (bf16[3,512,128]{2,1,0:T(8,128)(2,1)}, bf16[3,512,128]{2,1,0:T(8,128)(2,1)}, u32[]{:S(2)}, u32[]{:S(2)}) collective-permute-start(bf16[3,512,128]{2,1,0:T(8,128)(2,1)} %get-tuple-element.328), channel_id=1, source_target_pairs={{0,12},{4,0},{8,4},{12,8},{16,28},{20,16},{24,20},{28,24},{1,13},{... | collective-permute-start | bytes 1179656 | tf_op jit(solution)/shard_map/ppermute | solution.py:2137
  745.0 34.4 %collective-permute-start.19 = (bf16[3,512,128]{2,1,0:T(8,128)(2,1)}, bf16[3,512,128]{2,1,0:T(8,128)(2,1)}, u32[]{:S(2)}, u32[]{:S(2)}) collective-permute-start(bf16[3,512,128]{2,1,0:T(8,128)(2,1)} %get-tuple-element.329), channel_id=1, source_target_pairs={{0,8},{4,12},{8,0},{12,4},{16,24},{20,28},{24,16},{28,20},{1,9},{5... | collective-permute-start | bytes 1179656 | tf_op jit(solution)/shard_map/ppermute | solution.py:2137
  747.9 11.3 %copy-start = (bf16[4,128,1024]{2,1,0:T(8,128)(2,1)}, bf16[4,128,1024]{2,1,0:T(8,128)(2,1)S(1)}, u32[]{:S(2)}) copy-start(bf16[4,128,1024]{2,1,0:T(8,128)(2,1)S(1)} %add_convert_fusion.3) | copy-start | bytes 3145732
  759.1 6.6 copy-start.31
  765.7 15.7 %collective-permute-start.20 = (bf16[3,512,128]{2,1,0:T(8,128)(2,1)S(1)}, bf16[3,512,128]{2,1,0:T(8,128)(2,1)S(1)}, u32[]{:S(2)}, u32[]{:S(2)}) collective-permute-start(bf16[3,512,128]{2,1,0:T(8,128)(2,1)S(1)} %copy-done.31), channel_id=1, source_target_pairs={{0,4},{4,8},{8,12},{12,0},{16,20},{20,24},{24,28},{28,16},{1,5},{5... | collective-permute-start | bytes 1179656 | tf_op jit(solution)/shard_map/ppermute | solution.py:2137
  778.5 47.8 %collective-permute-start.21 = (bf16[2,128,1024]{2,1,0:T(8,128)(2,1)}, bf16[2,128,1024]{2,1,0:T(8,128)(2,1)S(1)}, u32[]{:S(2)}, u32[]{:S(2)}) collective-permute-start(bf16[2,128,1024]{2,1,0:T(8,128)(2,1)} %slice.97), channel_id=1, source_target_pairs={{0,1},{1,0},{2,3},{3,2},{4,5},{5,4},{6,7},{7,6},{8,9},{9,8},{10,11... | collective-permute-start | bytes 1572872 | tf_op jit(solution)/shard_map/ppermute | solution.py:2140
  779.3 73.9 %collective-permute-start.22 = (bf16[4,128,2048]{2,1,0:T(8,128)(2,1)}, bf16[4,128,2048]{2,1,0:T(8,128)(2,1)}, u32[]{:S(2)}, u32[]{:S(2)}) collective-permute-start(bf16[4,128,2048]{2,1,0:T(8,128)(2,1)} %get-tuple-element.396), channel_id=1, source_target_pairs={{0,8},{4,20},{8,0},{12,28},{16,24},{20,4},{24,16},{28,12},{1,9},{5... | collective-permute-start | bytes 6291464 | tf_op jit(solution)/shard_map/ppermute | solution.py:2391
  782.2 44.1 %slice-start = ((bf16[4,128,1024]{2,1,0:T(8,128)(2,1)}), bf16[2,128,1024]{2,1,0:T(8,128)(2,1)S(1)}, s32[]{:S(2)}) async-start(bf16[4,128,1024]{2,1,0:T(8,128)(2,1)} %copy-done), calls=%async_computation.2 | async-start | bytes 1048576 | tf_op jit(solution)/shard_map/slice | solution.py:2402
  826.5 26.7 %copy-start.3 = (bf16[2,128,1024]{2,1,0:T(8,128)(2,1)}, bf16[2,128,1024]{2,1,0:T(8,128)(2,1)S(1)}, u32[]{:S(2)}) copy-start(bf16[2,128,1024]{2,1,0:T(8,128)(2,1)S(1)} %add_convert_fusion.12.refs_5_) | copy-start | bytes 1572868
  826.6 30.5 %collective-permute-start.23 = (bf16[128,1024]{1,0:T(8,128)(2,1)S(1)}, bf16[128,1024]{1,0:T(8,128)(2,1)S(1)}, u32[]{:S(2)}, u32[]{:S(2)}) collective-permute-start(bf16[128,1024]{1,0:T(8,128)(2,1)S(1)} %slice_bitcast_fusion.2), channel_id=1, source_target_pairs={{0,2},{1,3},{2,0},{3,1},{4,6},{5,7},{6,4},{7,5},{8,10},{9,11},{10,... | collective-permute-start | bytes 786440 | tf_op jit(solution)/shard_map/ppermute | solution.py:2140
  952.2 3.2 copy-start.10
  957.1 2.6 copy-start.14
  (14 other events, 17.5 us)
Sparse Core Ops, SparseCore 0:
  175.7 83.0 all-gather.4
  261.8 145.1 all-gather.6

commit v5 on v4

--- a/solution.py
+++ b/solution.py
@@ -22,7 +22,7 @@
 BROAD = 2 * WIDE
 EPS = 1e-05
 MASKED = -1000000000.0
-ROWS = 256
+ROWS = 512
 CHUNK = 256
 VMEM_BYTES = 60 * 1024 * 1024
 MESH = pl.DeviceIdType.MESH
@@ -44,6 +44,8 @@
 
 
 def row_loop(total, step, body):
+    step = min(step, total)
+
     def advance(i, carry):
         body(pl.ds(pl.multiple_of(i * step, step), step))
         return carry
@@ -914,8 +916,8 @@
         acc[...] = jnp.zeros_like(acc)
 
         def body(r):
-            first[r, :] = jnp.broadcast_to(sum_lanes(first[r, :]) / FF, (ROWS, LANES))
-            cross[r, :] = jnp.broadcast_to(sum_lanes(cross[r, :]) / FF, (ROWS, LANES))
+            for ref in (first, cross):
+                ref[r, :] = jnp.broadcast_to(sum_lanes(ref[r, :]) / FF, ref[r, :].shape)
 
         row_loop(tokens, ROWS, body)
 
@@ -1145,7 +1147,7 @@
     ready, refs = refs[:early_count], refs[early_count:]
     dparts, refs = refs[:n], refs[n:]
     dlast, refs = refs[:n], refs[n:]
-    grad_out, normed_turned, grads, grad_low, acc, ns, ssem, rsem, lsem = refs
+    grad_out, normed_turned, grads, grad_low, acc, ns, hats, scales, ssem, rsem, lsem = refs
     blocks = [ready[u * n : (u + 1) * n] for u in range(units - 1)] + [dlast]
     host.barrier()
     steps = [0] + order_of(n)[::-1]
@@ -1159,7 +1161,9 @@
     grads[...] = jnp.zeros_like(grads)
 
     def early(r):
-        value, _ = row_stats(low[r, :].astype(f32))
+        value, rstd = row_stats(low[r, :].astype(f32))
+        hats[r, :] = value
+        scales[r, :] = jnp.broadcast_to(rstd, scales[r, :].shape)
         ns[r, :] = (value * gain + shift).astype(bf16)
 
     row_loop(tokens, ROWS, early)
@@ -1180,7 +1184,7 @@
             acc[...] += total
 
     def body(r):
-        value, rstd = row_stats(low[r, :].astype(f32))
+        value, rstd = hats[r, :], scales[r, 0:1]
         dy = acc[r, :]
         grads[0] += fold_rows(dy * value)
         grads[1] += fold_rows(dy)
@@ -1215,6 +1219,8 @@
         [
             pltpu.VMEM(flat, f32),
             pltpu.VMEM(flat, bf16),
+            pltpu.VMEM(flat, f32),
+            pltpu.VMEM((tokens, LANES), f32),
             DMA((n,)),
             DMA((n,)),
             DMA,

time: 982 us -> 981 us (level)
  waiting for transfers between devices: 68.8 us -> 81.8 us
  starting transfers between devices: 82.3 us -> 69.4 us
    ppermute x12, starting transfers between devices: 25.8 us -> 15.4 us  [shift(): return lax.ppermute(value, 'dp', pairs)]
  transfers between devices with their start and end apart: 28 -> 28, of which waited for: 7 -> 8; matrix products, arithmetic and copies ran while one was open for 3% -> 3% of each run, Pallas kernels for 39% -> 39%
where the time goes in v5:
time: 981 us; the launch traced here: 968 us
  Pallas kernels  747 us (76%)
  waiting for transfers between devices  81.8 us (8%)
  starting transfers between devices  69.4 us (7%)
  other arithmetic  30.1 us (3%)
  local copies, waits for them, and re-layouts  24.6 us (3%)
  between operations  15.4 us (2%)
    pallas_call x10, Pallas kernels, remote_call(): pl.pallas_call(kernel, out_shape=list(out_shape) + job_out, grid=grid, in...  311 us
    pallas_call x1, Pallas kernels, start_call(): pl.pallas_call(kernel, out_shape=[jax.ShapeDtypeStruct((BLOCKS, GROUPS) +...  160 us
    pallas_call x1, Pallas kernels, end_call(): pl.pallas_call(kernel, out_shape=outs, grid=(1,), in_specs=[HB] * 3 + [wh...  92.4 us
    pallas_call x8, Pallas kernels, unit_call(): pl.pallas_call(lambda *refs: kernel(n, *refs), out_shape=out_shape, grid_...  74.1 us
    pallas_call x4, Pallas kernels, ffn_grad_call(): pl.pallas_call(lambda *refs: ffn_grad_kernel(ups, first, count, added, *r...  48.9 us
    all_gather x2, waiting for transfers between devices, gather(): lax.all_gather(shard, ('dp', 'head')).reshape(BLOCKS, GROUPS, LANES, -1)  44.3 us
    ppermute x12, waiting for transfers between devices, shift(): return lax.ppermute(value, 'dp', pairs)  30.4 us
    pallas_call x3, Pallas kernels, head_grad_call(): pl.pallas_call(lambda *refs: head_grad_kernel(n, first, count, added, *re...  29.7 us
  transfers between devices with their start and end apart: 28, of which 8 were waited for; matrix products, arithmetic and copies ran while one was open for 3% of the time, Pallas kernels for 39%

profile of v5, /device:TPU:0, one launch (start us, length us, event | category | flops | bytes accessed | tf_op | source)
XLA Modules:
  0.0 968.3 jit_solution(2092943523389481726)
XLA Ops:
  10.6 2.7 convert_element_type.181
  13.2 2.7 pack.1
  15.9 159.6 %start.1 = (bf16[8,4,128,1024]{3,2,1,0:T(8,128)(2,1)}, bf16[8,4,128,2048]{3,2,1,0:T(8,128)(2,1)}, bf16[512,1024]{1,0:T(8,128)(2,1)}, bf16[2,512,256]{2,1,0:T(8,1...) custom-call(bf16[128,1024]{1,0:T(8,128)(2,1)} %get-tuple-element.192, ...), custom_call_target="tpu_custom_call" | custom-call | bytes 314572800 | tf_op jit(solution)/shard_map/start/pallas_call | solution.py:1666
  180.9 7.4 attention.4
  190.1 6.9 collective-permute-done.2.refs_6_
  197.7 7.2 attention.5
  204.9 25.5 %projection.2 = (f32[512,1024]{1,0:T(8,128)}, bf16[512,1024]{1,0:T(8,128)(2,1)}, f32[8,1024]{1,0:T(8,128)}) custom-call(f32[512,1]{1,0:T(8,128)} %get-tuple-element.195.refs_0_.refs_4_, bf16[512,1024]{1,0:T(8,128)(2,1)} %get-tuple-element.213.refs_1_, f32[4,56,128]{2,1,0:T(8,128)} %get-tuple-element.214.refs_2_.refs_1_.refs_5_, ...), custom_call_target="tpu_custom_call" | custom-call | flops 16106127360 | bytes 10485760 | tf_op jit(solution)/shard_map/projection/pallas_call | solution.py:398
  230.4 26.6 %ffn.2 = (bf16[4,512,1024]{2,1,0:T(8,128)(2,1)}, bf16[4,512,1024]{2,1,0:T(8,128)(2,1)}, bf16[4,512,1024]{2,1,0:T(8,128)(2,1)}, bf16[512,1024]{1,0:T(8,128)(2,1)}...) custom-call(f32[512,1]{1,0:T(8,128)} %get-tuple-element.195.refs_0_.refs_4_, ...), custom_call_target="tpu_custom_call" | custom-call | flops 34359738368 | bytes 10485760 | tf_op jit(solution)/shard_map/ffn/pallas_call | solution.py:350
  257.1 3.8 all-gather.5.cloned.1.call-done
  260.8 28.6 %qkv.3 = (bf16[3,512,128]{2,1,0:T(8,128)(2,1)}, bf16[3,512,128]{2,1,0:T(8,128)(2,1)}, bf16[3,512,128]{2,1,0:T(8,128)(2,1)}, bf16[3,512,128]{2,1,0:T(8,128)(2,1)}...) custom-call(bf16[512,1024]{1,0:T(8,128)(2,1)} %get-tuple-element.220, ...), custom_call_target="tpu_custom_call" | custom-call | flops 32212254720 | bytes 10485760 | tf_op jit(solution)/shard_map/qkv/pallas_call | solution.py:398
  292.6 7.3 attention.6
  299.9 2.8 collective-permute-done.3.refs_4_
  302.7 4.7 collective-permute-done.4.refs_5_
  307.4 15.6 %collective-permute-done.5.refs_6_ = bf16[3,512,128]{2,1,0:T(8,128)(2,1)S(1)} collective-permute-done((bf16[3,512,128]{2,1,0:T(8,128)(2,1)}, bf16[3,512,128]{2,1,0:T(8,128)(2,1)S(1)}, u32[]{:S(2)}, u32[]{:S(2)}) %collective-permute-start.5) | collective-permute-done | bytes 393248 | tf_op jit(solution)/shard_map/ppermute | solution.py:2143
  323.8 7.2 attention.7
  331.0 37.6 %projection.3 = (f32[512,1024]{1,0:T(8,128)}, bf16[512,1024]{1,0:T(8,128)(2,1)}, f32[8,1024]{1,0:T(8,128)}, bf16[512,1024]{1,0:T(8,128)(2,1)}) custom-call(f32[512,1]{1,0:T(8,128)} %get-tuple-element.195.refs_0_.refs_4_, f32[512,1024]{1,0:T(8,128)} %get-tuple-element.235.refs_1_, f32[4,56,128]{2,1,0:T(8,128)} %get-tuple-element.214.refs_2_.refs_1_.refs_5_, ...), custom_call_target="tpu_custom_call" | custom-call | flops 16106127360 | bytes 10485760 | tf_op jit(solution)/shard_map/projection/pallas_call | solution.py:398
  368.6 40.5 %all-gather.7.cloned.1.call-done = bf16[4096,2048]{1,0:T(8,128)(2,1)} async-done(((bf16[128,2048]{1,0:T(8,128)(2,1)}), bf16[4096,2048]{1,0:T(8,128)(2,1)}) %all-gather.7.cloned.1.call-update) | async-done | bytes 16777232 | tf_op jit(solution)/shard_map/all_gather | solution.py:2153
  409.2 26.1 %ffn.3 = (bf16[4,512,1024]{2,1,0:T(8,128)(2,1)}, bf16[4,512,1024]{2,1,0:T(8,128)(2,1)}, bf16[4,512,1024]{2,1,0:T(8,128)(2,1)}, bf16[512,1024]{1,0:T(8,128)(2,1)}...) custom-call(f32[512,1]{1,0:T(8,128)} %get-tuple-element.195.refs_0_., ...), custom_call_target="tpu_custom_call", output_to_operand_aliasing={{8}: (5, {})} | custom-call | flops 34359738368 | bytes 10485760 | tf_op jit(solution)/shard_map/ffn/pallas_call | solution.py:398
  435.2 34.6 %ffn_back.2 = (bf16[4,512,1024]{2,1,0:T(8,128)(2,1)}, bf16[8,128,512]{2,1,0:T(8,128)(2,1)}, bf16[8,128,512]{2,1,0:T(8,128)(2,1)}, f32[512,1024]{1,0:T(8,128)}, f...) custom-call(bf16[512,1024]{1,0:T(8,128)(2,1)} %get-tuple-element.242.refs_0_, ...), custom_call_target="tpu_custom_call" | custom-call | flops 34359738368 | bytes 10485760 | tf_op jit(solution)/shard_map/ffn_back/pallas_call | solution.py:398
  469.8 11.5 %ffn_grad.4.refs_4_ = bf16[4,4,128,2048]{3,2,1,0:T(8,128)(2,1)} custom-call(s32[18]{0:T(128)} %stack.63.refs_0_, bf16[8,128,512]{2,1,0:T(8,128)(2,1)} %get-tuple-element.257.refs_1_, bf16[8,128,512]{2,1,0:T(8,128)(2,1)} %get-tuple-element.251.refs_2_, bf16[4,512,1024]{2,1,0:T(8,128)(2,1)} %get-tuple-element.249.refs_3_.refs_4_, ...), custom_call_target="tpu_custom_call" | custom-call | flops 17179869184 | bytes 25165824 | tf_op jit(solution)/shard_map/ffn_grad/pallas_call | solution.py:1293
  481.3 28.0 %projection_back.2 = (bf16[4,512,128]{2,1,0:T(8,128)(2,1)}, bf16[4,512,128]{2,1,0:T(8,128)(2,1)}, bf16[8,128,512]{2,1,0:T(8,128)(2,1)}, bf16[512,1024]{1,0:T(8,1...) custom-call(f32[512,1024]{1,0:T(8,128)} %get-tuple-element.269.refs_, ...), custom_call_target="tpu_custom_call", output_to_operand_aliasing={{6}: (6, {})} | custom-call | flops 16106127360 | bytes 10485760 | tf_op jit(solution)/shard_map/projection_back/pallas_call | solution.py:398
  509.3 12.9 %ffn_grad.5 = (bf16[2,4,128,1024]{3,2,1,0:T(8,128)(2,1)}, bf16[2,4,128,1024]{3,2,1,0:T(8,128)(2,1)}, bf16[2,4,128,1024]{3,2,1,0:T(8,128)(2,1)}, bf16[2,4,128,1024]{3,2,1,0:T(8,128)(2,1)}) custom-call(s32[18]{0:T(128)} %stack.63.refs_0_, bf16[8,128,512]{2,1,0:T(8,128)(2,1)} %get-tuple-element.257.refs_1_, bf16[8,128,512]{2,1,0:T(8,128)(2,1)} %get-tuple-element.251.refs_2_, ...), custom_call_target="tpu_custom_call" | custom-call | flops 17179869184 | bytes 25165824 | tf_op jit(solution)/shard_map/ffn_grad/pallas_call | solution.py:1293
  522.2 5.4 collective-permute-start.6
  527.6 11.2 %attention_back.4 = (bf16[3,512,128]{2,1,0:T(8,128)(2,1)}, bf16[3,512,128]{2,1,0:T(8,128)(2,1)}, bf16[3,512,128]{2,1,0:T(8,128)(2,1)}, bf16[3,512,128]{2,1,0:T(8,128)(2,1)}) custom-call(s32[16]{0:T(128)} %get-tuple-element.197.refs_0_, bf16[4,512,128]{2,1,0:T(8,128)(2,1)} %get-tuple-element.320.refs_1_, bf16[512,128]{1,0:T(8,128)(2,1)} %get-tuple-element.201.refs_2_, ...), custom_call_target="tpu_custom_call" | custom-call | flops 30064771072 | bytes 8388608 | tf_op jit(solution)/shard_map/attention_back/pallas_call | solution.py:635
  540.0 13.0 %collective-permute-start.10 = (bf16[2,4,128,1024]{3,2,1,0:T(8,128)(2,1)}, bf16[2,4,128,1024]{3,2,1,0:T(8,128)(2,1)}, u32[]{:S(2)}, u32[]{:S(2)}) collective-permute-start(bf16[2,4,128,1024]{3,2,1,0:T(8,128)(2,1)} %get-tuple-element.287), channel_id=1, source_target_pairs={{0,16},{4,20},{8,24},{12,28},{16,0},{20,4},{24,8},{28,12},{1,17},{... | collective-permute-start | bytes 6291464 | tf_op jit(solution)/shard_map/ppermute | solution.py:2374
  553.0 11.2 %attention_back.5 = (bf16[3,512,128]{2,1,0:T(8,128)(2,1)}, bf16[3,512,128]{2,1,0:T(8,128)(2,1)}, bf16[3,512,128]{2,1,0:T(8,128)(2,1)}, bf16[3,512,128]{2,1,0:T(8,128)(2,1)}) custom-call(s32[16]{0:T(128)} %get-tuple-element.197.refs_0_, bf16[4,512,128]{2,1,0:T(8,128)(2,1)} %get-tuple-element.320.refs_1_, bf16[512,128]{1,0:T(8,128)(2,1)} %get-tuple-element.201.refs_2_, ...), custom_call_target="tpu_custom_call" | custom-call | flops 30064771072 | bytes 8388608 | tf_op jit(solution)/shard_map/attention_back/pallas_call | solution.py:635
  565.3 29.7 %qkv_back.2 = (bf16[3,512,128]{2,1,0:T(8,128)(2,1)}, bf16[3,512,128]{2,1,0:T(8,128)(2,1)}, bf16[3,512,128]{2,1,0:T(8,128)(2,1)}, bf16[3,512,128]{2,1,0:T(8,128)(...) custom-call(f32[512,1024]{1,0:T(8,128)} %get-tuple-element.269.refs_, ...), custom_call_target="tpu_custom_call" | custom-call | flops 26843545600 | bytes 10485760 | tf_op jit(solution)/shard_map/qkv_back/pallas_call | solution.py:398
  595.0 8.3 head_grad.3.refs_7_
  603.4 3.7 fusion.4
  611.2 36.5 %ffn_back.3 = (bf16[4,512,1024]{2,1,0:T(8,128)(2,1)}, bf16[8,128,512]{2,1,0:T(8,128)(2,1)}, bf16[8,128,512]{2,1,0:T(8,128)(2,1)}, f32[512,1024]{1,0:T(8,128)}, f...) custom-call(f32[512,1024]{1,0:T(8,128)} %get-tuple-element.290.refs_0_, ...), custom_call_target="tpu_custom_call" | custom-call | flops 34359738368 | bytes 10485760 | tf_op jit(solution)/shard_map/ffn_back/pallas_call | solution.py:398
  647.7 9.4 head_grad.4
  659.3 11.8 %ffn_grad.6.refs_4_ = bf16[4,4,128,2048]{3,2,1,0:T(8,128)(2,1)} custom-call(s32[18]{0:T(128)} %stack.63.refs_0_, bf16[8,128,512]{2,1,0:T(8,128)(2,1)} %get-tuple-element.311.refs_1_, bf16[8,128,512]{2,1,0:T(8,128)(2,1)} %get-tuple-element.301.refs_2_, bf16[4,512,1024]{2,1,0:T(8,128)(2,1)} %get-tuple-element.296.refs_3_.refs_4_, ...), custom_call_target="tpu_custom_call" | custom-call | flops 17179869184 | bytes 25165824 | tf_op jit(solution)/shard_map/ffn_grad/pallas_call | solution.py:1293
  677.2 20.3 %projection_back.3 = (bf16[4,512,128]{2,1,0:T(8,128)(2,1)}, bf16[4,512,128]{2,1,0:T(8,128)(2,1)}, bf16[8,128,512]{2,1,0:T(8,128)(2,1)}, bf16[512,1024]{1,0:T(8,1...) custom-call(f32[512,1024]{1,0:T(8,128)} %get-tuple-element.327.refs_0_, ...), custom_call_target="tpu_custom_call" | custom-call | flops 16106127360 | bytes 10485760 | tf_op jit(solution)/shard_map/projection_back/pallas_call | solution.py:398
  697.6 3.6 fusion.7
  702.1 12.7 %ffn_grad.7 = (bf16[2,4,128,2048]{3,2,1,0:T(8,128)(2,1)}, bf16[2,4,128,2048]{3,2,1,0:T(8,128)(2,1)}) custom-call(s32[18]{0:T(128)} %stack.63.refs_0_, bf16[8,128,512]{2,1,0:T(8,128)(2,1)} %get-tuple-element.311.refs_1_, bf16[8,128,512]{2,1,0:T(8,128)(2,1)} %get-tuple-element.301.refs_2_, bf16[4,512,1024]{2,1,0:T(8,128)(2,1)} %get-tuple-element.296.refs_3_.refs_4_, ...), custom_call_target="tpu_custom_call" | custom-call | flops 17179869184 | bytes 25165824 | tf_op jit(solution)/shard_map/ffn_grad/pallas_call | solution.py:1293
  717.9 11.1 %attention_back.6 = (bf16[3,512,128]{2,1,0:T(8,128)(2,1)}, bf16[3,512,128]{2,1,0:T(8,128)(2,1)}, bf16[3,512,128]{2,1,0:T(8,128)(2,1)}, bf16[3,512,128]{2,1,0:T(8,128)(2,1)}) custom-call(s32[16]{0:T(128)} %get-tuple-element.197.refs_0_, bf16[4,512,128]{2,1,0:T(8,128)(2,1)} %get-tuple-element.320.refs_1_, bf16[512,128]{1,0:T(8,128)(2,1)} %get-tuple-element.201.refs_2_, ...), custom_call_target="tpu_custom_call" | custom-call | flops 30064771072 | bytes 8388608 | tf_op jit(solution)/shard_map/attention_back/pallas_call | solution.py:635
  730.5 13.3 %collective-permute-start.25 = (bf16[128,1024]{1,0:T(8,128)(2,1)}, bf16[128,1024]{1,0:T(8,128)(2,1)S(1)}, u32[]{:S(2)}, u32[]{:S(2)}) collective-permute-start(bf16[128,1024]{1,0:T(8,128)(2,1)} %slice_bitcast_fusion), channel_id=1, source_target_pairs={{0,2},{1,3},{2,0},{3,1},{4,6},{5,7},{6,4},{7,5},{8,10},{9,11},{10,... | collective-permute-start | bytes 786440 | tf_op jit(solution)/shard_map/ppermute | solution.py:2146
  747.8 11.4 %attention_back.7 = (bf16[3,512,128]{2,1,0:T(8,128)(2,1)}, bf16[3,512,128]{2,1,0:T(8,128)(2,1)}, bf16[3,512,128]{2,1,0:T(8,128)(2,1)}, bf16[3,512,128]{2,1,0:T(8,128)(2,1)}) custom-call(s32[16]{0:T(128)} %get-tuple-element.197.refs_0_, bf16[4,512,128]{2,1,0:T(8,128)(2,1)} %get-tuple-element.320.refs_1_, bf16[512,128]{1,0:T(8,128)(2,1)} %get-tuple-element.201.refs_2_, ...), custom_call_target="tpu_custom_call" | custom-call | flops 30064771072 | bytes 8388608 | tf_op jit(solution)/shard_map/attention_back/pallas_call | solution.py:635
  760.0 6.4 collective-permute-done.17
  766.4 7.0 collective-permute-start.20
  773.4 5.3 fusion.1
  778.7 4.9 collective-permute-start.21
  785.3 44.2 %qkv_back.3 = (bf16[3,512,128]{2,1,0:T(8,128)(2,1)}, bf16[3,512,128]{2,1,0:T(8,128)(2,1)}, bf16[3,512,128]{2,1,0:T(8,128)(2,1)}, bf16[3,512,128]{2,1,0:T(8,128)(...) custom-call(f32[512,1024]{1,0:T(8,128)} %get-tuple-element.327.refs_, ...), custom_call_target="tpu_custom_call" | custom-call | flops 26843545600 | bytes 10485760 | tf_op jit(solution)/shard_map/qkv_back/pallas_call | solution.py:398
  829.7 8.8 collective-permute-start.23
  838.5 12.0 %head_grad.5.refs_1_ = bf16[8,4,128,1024]{3,2,1,0:T(8,128)(2,1)} custom-call(s32[18]{0:T(128)} %stack.63.refs_0_, bf16[8,128,512]{2,1,0:T(8,128)(2,1)} %get-tuple-element.339.refs_1_, bf16[8,128,512]{2,1,0:T(8,128)(2,1)} %get-tuple-element.340.refs_2_, bf16[512,1024]{1,0:T(8,128)(2,1)} %get-tuple-element.341.refs_3_, ...), custom_call_target="tpu_custom_call" | custom-call | flops 34359738368 | bytes 16777216 | tf_op jit(solution)/shard_map/head_grad/pallas_call | solution.py:1338
  850.5 3.8 add_convert_fusion.refs_2_
  855.1 92.4 %end.1 = (f32[4,512,256]{2,1,0:T(8,128)}, f32[4,512,256]{2,1,0:T(8,128)}, f32[2,3,128,256]{3,2,1,0:T(8,128)}, f32[2,256,128]{2,1,0:T(8,128)}, f32[2,128,1024]{2,...) custom-call(bf16[512,1024]{1,0:T(8,128)(2,1)} %get-tuple-element.345, ...), custom_call_target="tpu_custom_call" | custom-call | bytes 314572800 | tf_op jit(solution)/shard_map/end/pallas_call | solution.py:2048
  951.6 3.2 copy.40
  (144 shorter events, 52.5 us)
Async XLA Ops:
  7.2 253.7 %all-gather.5.cloned.1.call-start = ((), (), s32[]{:S(2)}) async-start(), calls=%async_computation | async-start | bytes 8650752 | tf_op jit(solution)/shard_map/all_gather | solution.py:2153
  175.6 233.6 %all-gather.7.cloned.1.call-start = ((), (), s32[]{:S(2)}) async-start(), calls=%async_computation.1 | async-start | bytes 17301504 | tf_op jit(solution)/shard_map/all_gather | solution.py:2153
  176.3 13.7 %collective-permute-start = (bf16[3,512,128]{2,1,0:T(8,128)(2,1)}, bf16[3,512,128]{2,1,0:T(8,128)(2,1)S(1)}, u32[]{:S(2)}, u32[]{:S(2)}) collective-permute-start(bf16[3,512,128]{2,1,0:T(8,128)(2,1)} %get-tuple-element.209), channel_id=1, source_target_pairs={{0,4},{4,8},{8,12},{12,0},{16,20},{20,24},{24,28},{28,16},{1,5},{5... | collective-permute-start | bytes 1179656 | tf_op jit(solution)/shard_map/ppermute | solution.py:2143
  176.5 13.5 %collective-permute-start.1 = (bf16[3,512,128]{2,1,0:T(8,128)(2,1)}, bf16[3,512,128]{2,1,0:T(8,128)(2,1)S(1)}, u32[]{:S(2)}, u32[]{:S(2)}) collective-permute-start(bf16[3,512,128]{2,1,0:T(8,128)(2,1)} %get-tuple-element.210), channel_id=1, source_target_pairs={{0,8},{4,12},{8,0},{12,4},{16,24},{20,28},{24,16},{28,20},{1,9},{5... | collective-permute-start | bytes 1179656 | tf_op jit(solution)/shard_map/ppermute | solution.py:2143
  177.5 19.4 %collective-permute-start.2 = (bf16[3,512,128]{2,1,0:T(8,128)(2,1)}, bf16[3,512,128]{2,1,0:T(8,128)(2,1)S(1)}, u32[]{:S(2)}, u32[]{:S(2)}) collective-permute-start(bf16[3,512,128]{2,1,0:T(8,128)(2,1)} %get-tuple-element.211), channel_id=1, source_target_pairs={{0,12},{4,0},{8,4},{12,8},{16,28},{20,16},{24,20},{28,24},{1,13},{... | collective-permute-start | bytes 1179656 | tf_op jit(solution)/shard_map/ppermute | solution.py:2143
  180.8 7.4 copy-start.9
  190.0 6.9 copy-start.22
  190.0 6.9 copy-start.23
  289.4 13.2 %collective-permute-start.3 = (bf16[3,512,128]{2,1,0:T(8,128)(2,1)}, bf16[3,512,128]{2,1,0:T(8,128)(2,1)S(1)}, u32[]{:S(2)}, u32[]{:S(2)}) collective-permute-start(bf16[3,512,128]{2,1,0:T(8,128)(2,1)} %get-tuple-element.231), channel_id=1, source_target_pairs={{0,4},{4,8},{8,12},{12,0},{16,20},{20,24},{24,28},{28,16},{1,5},{5... | collective-permute-start | bytes 1179656 | tf_op jit(solution)/shard_map/ppermute | solution.py:2143
  290.3 17.1 %collective-permute-start.4 = (bf16[3,512,128]{2,1,0:T(8,128)(2,1)}, bf16[3,512,128]{2,1,0:T(8,128)(2,1)S(1)}, u32[]{:S(2)}, u32[]{:S(2)}) collective-permute-start(bf16[3,512,128]{2,1,0:T(8,128)(2,1)} %get-tuple-element.232), channel_id=1, source_target_pairs={{0,8},{4,12},{8,0},{12,4},{16,24},{20,28},{24,16},{28,20},{1,9},{5... | collective-permute-start | bytes 1179656 | tf_op jit(solution)/shard_map/ppermute | solution.py:2143
  291.5 31.5 %collective-permute-start.5 = (bf16[3,512,128]{2,1,0:T(8,128)(2,1)}, bf16[3,512,128]{2,1,0:T(8,128)(2,1)S(1)}, u32[]{:S(2)}, u32[]{:S(2)}) collective-permute-start(bf16[3,512,128]{2,1,0:T(8,128)(2,1)} %get-tuple-element.233), channel_id=1, source_target_pairs={{0,12},{4,0},{8,4},{12,8},{16,28},{20,16},{24,20},{28,24},{1,13},{... | collective-permute-start | bytes 1179656 | tf_op jit(solution)/shard_map/ppermute | solution.py:2143
  302.7 20.4 %copy-start.25 = (bf16[3,512,128]{2,1,0:T(8,128)(2,1)}, bf16[3,512,128]{2,1,0:T(8,128)(2,1)S(1)}, u32[]{:S(2)}) copy-start(bf16[3,512,128]{2,1,0:T(8,128)(2,1)S(1)} %collective-permute-done.3.refs_4_) | copy-start | bytes 1179652
  307.4 15.6 %copy-start.26 = (bf16[3,512,128]{2,1,0:T(8,128)(2,1)}, bf16[3,512,128]{2,1,0:T(8,128)(2,1)S(1)}, u32[]{:S(2)}) copy-start(bf16[3,512,128]{2,1,0:T(8,128)(2,1)S(1)} %collective-permute-done.4.refs_5_) | copy-start | bytes 1179652
  522.2 30.9 %collective-permute-start.6 = (bf16[2,4,128,1024]{3,2,1,0:T(8,128)(2,1)}, bf16[2,4,128,1024]{3,2,1,0:T(8,128)(2,1)S(1)}, u32[]{:S(2)}, u32[]{:S(2)}) collective-permute-start(bf16[2,4,128,1024]{3,2,1,0:T(8,128)(2,1)} %get-tuple-element.264), channel_id=1, source_target_pairs={{0,16},{4,12},{8,24},{12,4},{16,0},{20,28},{24,8},{28,20},{1,17},{... | collective-permute-start | bytes 6291464 | tf_op jit(solution)/shard_map/ppermute | solution.py:2375
  538.7 25.5 %collective-permute-start.7 = (bf16[3,512,128]{2,1,0:T(8,128)(2,1)}, bf16[3,512,128]{2,1,0:T(8,128)(2,1)S(1)}, u32[]{:S(2)}, u32[]{:S(2)}) collective-permute-start(bf16[3,512,128]{2,1,0:T(8,128)(2,1)} %get-tuple-element.270), channel_id=1, source_target_pairs={{0,12},{4,0},{8,4},{12,8},{16,28},{20,16},{24,20},{28,24},{1,13},{... | collective-permute-start | bytes 1179656 | tf_op jit(solution)/shard_map/ppermute | solution.py:2143
  538.7 25.5 %collective-permute-start.8 = (bf16[3,512,128]{2,1,0:T(8,128)(2,1)}, bf16[3,512,128]{2,1,0:T(8,128)(2,1)S(1)}, u32[]{:S(2)}, u32[]{:S(2)}) collective-permute-start(bf16[3,512,128]{2,1,0:T(8,128)(2,1)} %get-tuple-element.271), channel_id=1, source_target_pairs={{0,8},{4,12},{8,0},{12,4},{16,24},{20,28},{24,16},{28,20},{1,9},{5... | collective-permute-start | bytes 1179656 | tf_op jit(solution)/shard_map/ppermute | solution.py:2143
  539.8 24.7 %collective-permute-start.9 = (bf16[3,512,128]{2,1,0:T(8,128)(2,1)}, bf16[3,512,128]{2,1,0:T(8,128)(2,1)S(1)}, u32[]{:S(2)}, u32[]{:S(2)}) collective-permute-start(bf16[3,512,128]{2,1,0:T(8,128)(2,1)} %get-tuple-element.272), channel_id=1, source_target_pairs={{0,4},{4,8},{8,12},{12,0},{16,20},{20,24},{24,28},{28,16},{1,5},{5... | collective-permute-start | bytes 1179656 | tf_op jit(solution)/shard_map/ppermute | solution.py:2143
  540.0 63.4 %collective-permute-start.10 = (bf16[2,4,128,1024]{3,2,1,0:T(8,128)(2,1)}, bf16[2,4,128,1024]{3,2,1,0:T(8,128)(2,1)}, u32[]{:S(2)}, u32[]{:S(2)}) collective-permute-start(bf16[2,4,128,1024]{3,2,1,0:T(8,128)(2,1)} %get-tuple-element.287), channel_id=1, source_target_pairs={{0,16},{4,20},{8,24},{12,28},{16,0},{20,4},{24,8},{28,12},{1,17},{... | collective-permute-start | bytes 6291464 | tf_op jit(solution)/shard_map/ppermute | solution.py:2374
  553.0 11.2 %copy-start.6 = (bf16[2,4,128,1024]{3,2,1,0:T(8,128)(2,1)}, bf16[2,4,128,1024]{3,2,1,0:T(8,128)(2,1)S(1)}, u32[]{:S(2)}) copy-start(bf16[2,4,128,1024]{3,2,1,0:T(8,128)(2,1)S(1)} %collective-permute-done.6) | copy-start | bytes 6291460
  595.0 8.4 copy-start.5
  603.4 4.7 copy-start.4
  603.4 4.7 copy-start.7
  607.1 65.7 %collective-permute-start.11 = (bf16[4,128,1024]{2,1,0:T(8,128)(2,1)}, bf16[4,128,1024]{2,1,0:T(8,128)(2,1)S(1)}, u32[]{:S(2)}, u32[]{:S(2)}) collective-permute-start(bf16[4,128,1024]{2,1,0:T(8,128)(2,1)} %get-tuple-element.402), channel_id=1, source_target_pairs={{0,8},{4,12},{8,0},{12,4},{16,24},{20,28},{24,16},{28,20},{1,9},{5... | collective-permute-start | bytes 3145736 | tf_op jit(solution)/shard_map/ppermute | solution.py:2417
  610.1 61.1 %collective-permute-start.12 = (bf16[4,128,1024]{2,1,0:T(8,128)(2,1)}, bf16[4,128,1024]{2,1,0:T(8,128)(2,1)}, u32[]{:S(2)}, u32[]{:S(2)}) collective-permute-start(bf16[4,128,1024]{2,1,0:T(8,128)(2,1)} %get-tuple-element.400), channel_id=1, source_target_pairs={{0,8},{4,20},{8,0},{12,28},{16,24},{20,4},{24,16},{28,12},{1,9},{5... | collective-permute-start | bytes 3145736 | tf_op jit(solution)/shard_map/ppermute | solution.py:2418
  657.1 40.4 %collective-permute-start.13 = (bf16[2,4,128,1024]{3,2,1,0:T(8,128)(2,1)}, bf16[2,4,128,1024]{3,2,1,0:T(8,128)(2,1)}, u32[]{:S(2)}, u32[]{:S(2)}) collective-permute-start(bf16[2,4,128,1024]{3,2,1,0:T(8,128)(2,1)} %get-tuple-element.310), channel_id=1, source_target_pairs={{0,16},{4,12},{8,24},{12,4},{16,0},{20,28},{24,8},{28,20},{1,17},{... | collective-permute-start | bytes 6291464 | tf_op jit(solution)/shard_map/ppermute | solution.py:2346
  674.3 41.8 %collective-permute-start.14 = (bf16[2,128,1024]{2,1,0:T(8,128)(2,1)}, bf16[2,128,1024]{2,1,0:T(8,128)(2,1)}, u32[]{:S(2)}, u32[]{:S(2)}) collective-permute-start(bf16[2,128,1024]{2,1,0:T(8,128)(2,1)} %get-tuple-element.406), channel_id=1, source_target_pairs={{0,1},{1,0},{2,3},{3,2},{4,5},{5,4},{6,7},{7,6},{8,9},{9,8},{10,11... | collective-permute-start | bytes 1572872 | tf_op jit(solution)/shard_map/ppermute | solution.py:2146
  676.2 38.6 %collective-permute-start.15 = (bf16[2,128,1024]{2,1,0:T(8,128)(2,1)S(1)}, bf16[2,128,1024]{2,1,0:T(8,128)(2,1)}, u32[]{:S(2)}, u32[]{:S(2)}) collective-permute-start(bf16[2,128,1024]{2,1,0:T(8,128)(2,1)S(1)} %get-tuple-element.404), channel_id=1, source_target_pairs={{0,1},{1,0},{2,3},{3,2},{4,5},{5,4},{6,7},{7,6},{8,9},{9,8},{10,11... | collective-permute-start | bytes 1572872 | tf_op jit(solution)/shard_map/ppermute | solution.py:2146
  677.2 20.4 %copy-start.8 = (bf16[2,4,128,1024]{3,2,1,0:T(8,128)(2,1)S(1)}, bf16[2,4,128,1024]{3,2,1,0:T(8,128)(2,1)}, u32[]{:S(2)}) copy-start(bf16[2,4,128,1024]{3,2,1,0:T(8,128)(2,1)} %get-tuple-element.308) | copy-start | bytes 6291460
  701.1 43.1 %collective-permute-start.16 = (bf16[4,128,1024]{2,1,0:T(8,128)(2,1)}, bf16[4,128,1024]{2,1,0:T(8,128)(2,1)S(1)}, u32[]{:S(2)}, u32[]{:S(2)}) collective-permute-start(bf16[4,128,1024]{2,1,0:T(8,128)(2,1)} %get-tuple-element.398), channel_id=1, source_target_pairs={{0,8},{4,20},{8,0},{12,28},{16,24},{20,4},{24,16},{28,12},{1,9},{5... | collective-permute-start | bytes 3145736 | tf_op jit(solution)/shard_map/ppermute | solution.py:2370
  702.1 12.7 %copy-start.12 = (bf16[2,128,1024]{2,1,0:T(8,128)(2,1)S(1)}, bf16[2,128,1024]{2,1,0:T(8,128)(2,1)}, u32[]{:S(2)}) copy-start(bf16[2,128,1024]{2,1,0:T(8,128)(2,1)} %get-tuple-element.315) | copy-start | bytes 1572868
  702.1 14.0 %copy-start.11 = (bf16[2,128,1024]{2,1,0:T(8,128)(2,1)S(1)}, bf16[2,128,1024]{2,1,0:T(8,128)(2,1)}, u32[]{:S(2)}) copy-start(bf16[2,128,1024]{2,1,0:T(8,128)(2,1)} %get-tuple-element.314) | copy-start | bytes 1572868
  716.1 13.7 %copy-start.1 = (bf16[2,128,1024]{2,1,0:T(8,128)(2,1)}, bf16[2,128,1024]{2,1,0:T(8,128)(2,1)S(1)}, u32[]{:S(2)}) copy-start(bf16[2,128,1024]{2,1,0:T(8,128)(2,1)S(1)} %add_convert_fusion.13.refs_9_) | copy-start | bytes 1572868
  717.5 11.5 %copy-start.2 = (bf16[2,128,1024]{2,1,0:T(8,128)(2,1)}, bf16[2,128,1024]{2,1,0:T(8,128)(2,1)S(1)}, u32[]{:S(2)}) copy-start(bf16[2,128,1024]{2,1,0:T(8,128)(2,1)S(1)} %add_convert_fusion.14.refs_7_) | copy-start | bytes 1572868
  717.6 48.9 %collective-permute-start.17 = (bf16[2,4,128,2048]{3,2,1,0:T(8,128)(2,1)}, bf16[2,4,128,2048]{3,2,1,0:T(8,128)(2,1)}, u32[]{:S(2)}, u32[]{:S(2)}) collective-permute-start(bf16[2,4,128,2048]{3,2,1,0:T(8,128)(2,1)} %get-tuple-element.326), channel_id=1, source_target_pairs={{0,16},{4,12},{8,24},{12,4},{16,0},{20,28},{24,8},{28,20},{1,17},{... | collective-permute-start | bytes 12582920 | tf_op jit(solution)/shard_map/ppermute | solution.py:2382
  730.5 123.8 %collective-permute-start.25 = (bf16[128,1024]{1,0:T(8,128)(2,1)}, bf16[128,1024]{1,0:T(8,128)(2,1)S(1)}, u32[]{:S(2)}, u32[]{:S(2)}) collective-permute-start(bf16[128,1024]{1,0:T(8,128)(2,1)} %slice_bitcast_fusion), channel_id=1, source_target_pairs={{0,2},{1,3},{2,0},{3,1},{4,6},{5,7},{6,4},{7,5},{8,10},{9,11},{10,... | collective-permute-start | bytes 786440 | tf_op jit(solution)/shard_map/ppermute | solution.py:2146
  743.8 110.6 %collective-permute-start.24 = (bf16[128,1024]{1,0:T(8,128)(2,1)}, bf16[128,1024]{1,0:T(8,128)(2,1)}, u32[]{:S(2)}, u32[]{:S(2)}) collective-permute-start(bf16[128,1024]{1,0:T(8,128)(2,1)} %slice_bitcast_fusion.1), channel_id=1, source_target_pairs={{0,2},{1,3},{2,0},{3,1},{4,6},{5,7},{6,4},{7,5},{8,10},{9,11},{10,... | collective-permute-start | bytes 786440 | tf_op jit(solution)/shard_map/ppermute | solution.py:2146
  743.8 34.9 %collective-permute-start.18 = (bf16[3,512,128]{2,1,0:T(8,128)(2,1)}, bf16[3,512,128]{2,1,0:T(8,128)(2,1)}, u32[]{:S(2)}, u32[]{:S(2)}) collective-permute-start(bf16[3,512,128]{2,1,0:T(8,128)(2,1)} %get-tuple-element.328), channel_id=1, source_target_pairs={{0,12},{4,0},{8,4},{12,8},{16,28},{20,16},{24,20},{28,24},{1,13},{... | collective-permute-start | bytes 1179656 | tf_op jit(solution)/shard_map/ppermute | solution.py:2143
  745.2 38.4 %collective-permute-start.19 = (bf16[3,512,128]{2,1,0:T(8,128)(2,1)}, bf16[3,512,128]{2,1,0:T(8,128)(2,1)}, u32[]{:S(2)}, u32[]{:S(2)}) collective-permute-start(bf16[3,512,128]{2,1,0:T(8,128)(2,1)} %get-tuple-element.329), channel_id=1, source_target_pairs={{0,8},{4,12},{8,0},{12,4},{16,24},{20,28},{24,16},{28,20},{1,9},{5... | collective-permute-start | bytes 1179656 | tf_op jit(solution)/shard_map/ppermute | solution.py:2143
  747.8 11.4 %copy-start = (bf16[4,128,1024]{2,1,0:T(8,128)(2,1)}, bf16[4,128,1024]{2,1,0:T(8,128)(2,1)S(1)}, u32[]{:S(2)}) copy-start(bf16[4,128,1024]{2,1,0:T(8,128)(2,1)S(1)} %add_convert_fusion.3) | copy-start | bytes 3145732
  759.2 7.2 copy-start.31
  766.4 18.1 %collective-permute-start.20 = (bf16[3,512,128]{2,1,0:T(8,128)(2,1)S(1)}, bf16[3,512,128]{2,1,0:T(8,128)(2,1)S(1)}, u32[]{:S(2)}, u32[]{:S(2)}) collective-permute-start(bf16[3,512,128]{2,1,0:T(8,128)(2,1)S(1)} %copy-done.31), channel_id=1, source_target_pairs={{0,4},{4,8},{8,12},{12,0},{16,20},{20,24},{24,28},{28,16},{1,5},{5... | collective-permute-start | bytes 1179656 | tf_op jit(solution)/shard_map/ppermute | solution.py:2143
  778.7 50.7 %collective-permute-start.21 = (bf16[2,128,1024]{2,1,0:T(8,128)(2,1)}, bf16[2,128,1024]{2,1,0:T(8,128)(2,1)S(1)}, u32[]{:S(2)}, u32[]{:S(2)}) collective-permute-start(bf16[2,128,1024]{2,1,0:T(8,128)(2,1)} %slice.97), channel_id=1, source_target_pairs={{0,1},{1,0},{2,3},{3,2},{4,5},{5,4},{6,7},{7,6},{8,9},{9,8},{10,11... | collective-permute-start | bytes 1572872 | tf_op jit(solution)/shard_map/ppermute | solution.py:2146
  783.6 67.0 %collective-permute-start.22 = (bf16[4,128,2048]{2,1,0:T(8,128)(2,1)}, bf16[4,128,2048]{2,1,0:T(8,128)(2,1)}, u32[]{:S(2)}, u32[]{:S(2)}) collective-permute-start(bf16[4,128,2048]{2,1,0:T(8,128)(2,1)} %get-tuple-element.396), channel_id=1, source_target_pairs={{0,8},{4,20},{8,0},{12,28},{16,24},{20,4},{24,16},{28,12},{1,9},{5... | collective-permute-start | bytes 6291464 | tf_op jit(solution)/shard_map/ppermute | solution.py:2397
  785.3 44.2 %slice-start = ((bf16[4,128,1024]{2,1,0:T(8,128)(2,1)}), bf16[2,128,1024]{2,1,0:T(8,128)(2,1)S(1)}, s32[]{:S(2)}) async-start(bf16[4,128,1024]{2,1,0:T(8,128)(2,1)} %copy-done), calls=%async_computation.2 | async-start | bytes 1048576 | tf_op jit(solution)/shard_map/slice | solution.py:2408
  829.6 20.9 %copy-start.3 = (bf16[2,128,1024]{2,1,0:T(8,128)(2,1)}, bf16[2,128,1024]{2,1,0:T(8,128)(2,1)S(1)}, u32[]{:S(2)}) copy-start(bf16[2,128,1024]{2,1,0:T(8,128)(2,1)S(1)} %add_convert_fusion.12.refs_5_) | copy-start | bytes 1572868
  829.7 24.7 %collective-permute-start.23 = (bf16[128,1024]{1,0:T(8,128)(2,1)S(1)}, bf16[128,1024]{1,0:T(8,128)(2,1)S(1)}, u32[]{:S(2)}, u32[]{:S(2)}) collective-permute-start(bf16[128,1024]{1,0:T(8,128)(2,1)S(1)} %slice_bitcast_fusion.2), channel_id=1, source_target_pairs={{0,2},{1,3},{2,0},{3,1},{4,6},{5,7},{6,4},{7,5},{8,10},{9,11},{10,... | collective-permute-start | bytes 786440 | tf_op jit(solution)/shard_map/ppermute | solution.py:2146
  951.6 3.2 copy-start.10
  956.5 2.6 copy-start.14
  (14 other events, 17.5 us)
Sparse Core Ops, SparseCore 0:
  175.7 85.1 all-gather.4
  263.8 145.2 all-gather.6

commit v6 on v5

--- a/solution.py
+++ b/solution.py
@@ -1700,8 +1700,8 @@
 
 
 def end_kernel(
-    layers, rows, grads, fsum, turned, valid, tops, vecs, uses,
-    stream_out, rows_out, qkv_out, out_out, up_out, down_out,
+    layers, rows, grads, fsum, valid, tops, vecs, uses,
+    rows_out, qkv_out, out_out, up_out, down_out,
     gains_out, shifts_out, hgains_out, hshifts_out, rms_out,
     mine, got, pair, last, near, pieces, crossed, fm, fnear, vec, vgot, vsum,
     gsem, hsem, psem, qsem, nsem, tsem, xsem, vsem, lsem, esem,
@@ -1960,8 +1960,6 @@
             row_copies("wait")
             row_arrivals()
             cross.start()
-        if t == 3:
-            stream_out[...] = turned[...].astype(f32)
         if t == 4:
             for l in range(1, layers):
                 heads, heads_other, ups, ups_other, downs, downs_other = tops[6 * l - 6 : 6 * l]
@@ -2004,11 +2002,11 @@
     rms_out[0 : 3 * layers, :] = jnp.broadcast_to(rms, (3 * layers, LANES))
     cross.wait()
     for c2 in range(2):
-        rows_out[2 * bit_x + c2] = pieces[bit_x, c2].astype(f32)
-        rows_out[2 - 2 * bit_x + c2] = crossed[c2].astype(f32)
-
-
-def end_call(rows, grads, fsum, turned, valid, tops, vecs, uses):
+        rows_out[2 * bit_x + c2] = pieces[bit_x, c2]
+        rows_out[2 - 2 * bit_x + c2] = crossed[c2]
+
+
+def end_call(rows, grads, fsum, valid, tops, vecs, uses):
     parts = 4
     layers = len(vecs) // 4
     tokens = rows.shape[0]
@@ -2016,7 +2014,7 @@
     block = grads.shape[1:]
     broad = fsum.shape
     vector = (vector_rows(layers), LANES)
-    inputs = [rows, grads, fsum, turned, valid, *tops, *vecs, *uses]
+    inputs = [rows, grads, fsum, valid, *tops, *vecs, *uses]
 
     def spec(i, v):
         if i % 2 == 0:
@@ -2024,7 +2022,7 @@
         return whole(v.shape)
 
     def kernel(*refs):
-        fixed, refs = refs[:5], refs[5:]
+        fixed, refs = refs[:4], refs[4:]
         lists = []
         for values in (tops, vecs, uses):
             lists.append(refs[: len(values)])
@@ -2032,8 +2030,7 @@
         end_kernel(layers, *fixed, *lists, *refs)
 
     dims = [
-        turned.shape,
-        turned.shape,
+        (GROUPS, tokens, wide),
         (layers, 3, LANES, HEADS),
         (layers, HEADS, LANES),
         (layers, LANES, WIDE),
@@ -2044,13 +2041,13 @@
         (layers, WIDE),
         (8 * (-(-3 * layers // 8)), LANES),
     ]
-    outs = [jax.ShapeDtypeStruct(d, f32) for d in dims]
+    outs = [jax.ShapeDtypeStruct(d, f32 if i else bf16) for i, d in enumerate(dims)]
     return pl.pallas_call(
         kernel,
         out_shape=outs,
         grid=(1,),
         in_specs=[HB] * 3
-        + [whole(turned.shape), whole(valid.shape)]
+        + [whole(valid.shape)]
         + [spec(i, v) for i, v in enumerate(tops)]
         + [whole(v.shape) for v in (*vecs, *uses)],
         out_specs=[whole(v.shape) for v in outs],
@@ -2425,13 +2422,13 @@
     if net.fast:
         ffn_sum = net.add_last(order.hold(ffn_mine), ffn_last)
         (
-            stream_out, stream_grad, qkv_grad, out_grad, up_grad, down_grad,
+            moved, qkv_grad, out_grad, up_grad, down_grad,
             gains_grad, shifts_grad, hidden_gains_grad, hidden_shifts_grad, usage_rms,
         ) = order(
-            end_call, grad_low, full, ffn_sum, turned, valid, tops, vectors, usage
+            end_call, grad_low, full, ffn_sum, valid, tops, vectors, usage
         )
-        stream_out = stream_out.reshape(LONG, D // n)
-        stream_grad = stream_grad.reshape(LONG, D // n)
+        stream_out = turned.reshape(LONG, D // n).astype(f32)
+        stream_grad = moved.reshape(LONG, D // n).astype(f32)
         stacked = [qkv_grad, out_grad, up_grad, down_grad]
         usage_rms = usage_rms[: 3 * layers, 0].reshape(layers, 3)
     else:

time: 981 us -> 979 us (level)
  Pallas kernels: 747 us -> 767 us
  waiting for transfers between devices: 81.8 us -> 69.9 us
  starting transfers between devices: 69.4 us -> 59.2 us
    pallas_call x8, Pallas kernels: 74.1 us -> 108 us  [unit_call(): pl.pallas_call(lambda *refs: kernel(n, *refs), out_shape=out_shape, grid_...]
    ppermute x1, starting transfers between devices: 13 us -> 0.01 us  [local(): up_pair = lax.ppermute(order.hold(sums[1]), 'dp', net.by_y)]
  transfers between devices with their start and end apart: 28 -> 28, of which waited for: 8 -> 7; matrix products, arithmetic and copies ran while one was open for 3% -> 3% of each run, Pallas kernels for 39% -> 42%
where the time goes in v6:
time: 979 us; the launch traced here: 965 us
  Pallas kernels  767 us (78%)
  waiting for transfers between devices  69.9 us (7%)
  starting transfers between devices  59.2 us (6%)
  other arithmetic  34.5 us (4%)
  local copies, waits for them, and re-layouts  19.4 us (2%)
  between operations  15.3 us (2%)
    pallas_call x10, Pallas kernels, remote_call(): pl.pallas_call(kernel, out_shape=list(out_shape) + job_out, grid=grid, in...  302 us
    pallas_call x1, Pallas kernels, start_call(): pl.pallas_call(kernel, out_shape=[jax.ShapeDtypeStruct((BLOCKS, GROUPS) +...  160 us
    pallas_call x8, Pallas kernels, unit_call(): pl.pallas_call(lambda *refs: kernel(n, *refs), out_shape=out_shape, grid_...  108 us
    pallas_call x1, Pallas kernels, end_call(): pl.pallas_call(kernel, out_shape=outs, grid=(1,), in_specs=[HB] * 3 + [wh...  88.3 us
    pallas_call x4, Pallas kernels, ffn_grad_call(): pl.pallas_call(lambda *refs: ffn_grad_kernel(ups, first, count, added, *r...  48.7 us
    all_gather x2, waiting for transfers between devices, gather(): lax.all_gather(shard, ('dp', 'head')).reshape(BLOCKS, GROUPS, LANES, -1)  36.8 us
    ppermute x6, starting transfers between devices, across(): return lax.ppermute(value, 'head', [(i, i ^ bits) for i in range(self.n)])  33.8 us
    pallas_call x3, Pallas kernels, head_grad_call(): pl.pallas_call(lambda *refs: head_grad_kernel(n, first, count, added, *re...  29.7 us
  transfers between devices with their start and end apart: 28, of which 7 were waited for; matrix products, arithmetic and copies ran while one was open for 3% of the time, Pallas kernels for 42%

profile of v6, /device:TPU:0, one launch (start us, length us, event | category | flops | bytes accessed | tf_op | source)
XLA Modules:
  0.0 965.1 jit_solution(11740244174664958671)
XLA Ops:
  10.6 2.7 convert_element_type.193
  13.2 2.7 pack.1
  15.9 159.6 %start.1 = (bf16[8,4,128,1024]{3,2,1,0:T(8,128)(2,1)}, bf16[8,4,128,2048]{3,2,1,0:T(8,128)(2,1)}, bf16[512,1024]{1,0:T(8,128)(2,1)}, bf16[2,512,256]{2,1,0:T(8,1...) custom-call(bf16[128,1024]{1,0:T(8,128)(2,1)} %get-tuple-element.191, ...), custom_call_target="tpu_custom_call" | custom-call | bytes 314572800 | tf_op jit(solution)/shard_map/start/pallas_call | solution.py:1666
  180.9 10.0 %attention.4 = (bf16[4,512,128]{2,1,0:T(8,128)(2,1)}, f32[4,8,512]{2,1,0:T(8,128)}) custom-call(s32[16]{0:T(128)} %get-tuple-element.196.refs_0_, bf16[4,512,128]{2,1,0:T(8,128)(2,1)} %get-tuple-element.320.refs_1_, bf16[512,128]{1,0:T(8,128)(2,1)} %get-tuple-element.200.refs_2_, bf16[3,512,128]{2,1,0:T(8,128)(2,1)} %get-tuple-element.201.refs_3_, ...), custom_call_target="tpu_custom_call" | custom-call | flops 25769803776 | bytes 8388608 | tf_op jit(solution)/shard_map/attention/pallas_call | solution.py:635
  192.6 4.4 collective-permute-done.2.refs_6_
  197.7 9.8 %attention.5 = (bf16[4,512,128]{2,1,0:T(8,128)(2,1)}, f32[4,8,512]{2,1,0:T(8,128)}) custom-call(s32[16]{0:T(128)} %get-tuple-element.196.refs_0_, bf16[4,512,128]{2,1,0:T(8,128)(2,1)} %get-tuple-element.320.refs_1_, bf16[512,128]{1,0:T(8,128)(2,1)} %get-tuple-element.200.refs_2_, bf16[3,512,128]{2,1,0:T(8,128)(2,1)} %get-tuple-element.207.refs_3_, ...), custom_call_target="tpu_custom_call" | custom-call | flops 25769803776 | bytes 8388608 | tf_op jit(solution)/shard_map/attention/pallas_call | solution.py:635
  207.6 22.8 %projection.2 = (f32[512,1024]{1,0:T(8,128)}, bf16[512,1024]{1,0:T(8,128)(2,1)}, f32[8,1024]{1,0:T(8,128)}) custom-call(f32[512,1]{1,0:T(8,128)} %get-tuple-element.194.refs_0_.refs_3_, bf16[512,1024]{1,0:T(8,128)(2,1)} %get-tuple-element.212.refs_1_, f32[4,56,128]{2,1,0:T(8,128)} %get-tuple-element.213.refs_2_.refs_1_.refs_5_, ...), custom_call_target="tpu_custom_call" | custom-call | flops 16106127360 | bytes 10485760 | tf_op jit(solution)/shard_map/projection/pallas_call | solution.py:398
  230.4 25.7 %ffn.2 = (bf16[4,512,1024]{2,1,0:T(8,128)(2,1)}, bf16[4,512,1024]{2,1,0:T(8,128)(2,1)}, bf16[4,512,1024]{2,1,0:T(8,128)(2,1)}, bf16[512,1024]{1,0:T(8,128)(2,1)}...) custom-call(f32[512,1]{1,0:T(8,128)} %get-tuple-element.194.refs_0_.refs_3_, ...), custom_call_target="tpu_custom_call" | custom-call | flops 34359738368 | bytes 10485760 | tf_op jit(solution)/shard_map/ffn/pallas_call | solution.py:350
  256.2 2.3 all-gather.5.cloned.1.call-done
  258.4 28.6 %qkv.3 = (bf16[3,512,128]{2,1,0:T(8,128)(2,1)}, bf16[3,512,128]{2,1,0:T(8,128)(2,1)}, bf16[3,512,128]{2,1,0:T(8,128)(2,1)}, bf16[3,512,128]{2,1,0:T(8,128)(2,1)}...) custom-call(bf16[512,1024]{1,0:T(8,128)(2,1)} %get-tuple-element.219, ...), custom_call_target="tpu_custom_call" | custom-call | flops 32212254720 | bytes 10485760 | tf_op jit(solution)/shard_map/qkv/pallas_call | solution.py:398
  290.1 9.8 %attention.6 = (bf16[4,512,128]{2,1,0:T(8,128)(2,1)}, f32[4,8,512]{2,1,0:T(8,128)}) custom-call(s32[16]{0:T(128)} %get-tuple-element.196.refs_0_, bf16[4,512,128]{2,1,0:T(8,128)(2,1)} %get-tuple-element.320.refs_1_, bf16[512,128]{1,0:T(8,128)(2,1)} %get-tuple-element.200.refs_2_, bf16[3,512,128]{2,1,0:T(8,128)(2,1)} %get-tuple-element.222.refs_3_, ...), custom_call_target="tpu_custom_call" | custom-call | flops 25769803776 | bytes 8388608 | tf_op jit(solution)/shard_map/attention/pallas_call | solution.py:635
  300.1 4.7 collective-permute-done.4.refs_5_
  304.9 15.6 %collective-permute-done.5.refs_6_ = bf16[3,512,128]{2,1,0:T(8,128)(2,1)S(1)} collective-permute-done((bf16[3,512,128]{2,1,0:T(8,128)(2,1)}, bf16[3,512,128]{2,1,0:T(8,128)(2,1)S(1)}, u32[]{:S(2)}, u32[]{:S(2)}) %collective-permute-start.5) | collective-permute-done | bytes 393248 | tf_op jit(solution)/shard_map/ppermute | solution.py:2140
  321.3 9.8 %attention.7 = (bf16[4,512,128]{2,1,0:T(8,128)(2,1)}, f32[4,8,512]{2,1,0:T(8,128)}) custom-call(s32[16]{0:T(128)} %get-tuple-element.196.refs_0_, bf16[4,512,128]{2,1,0:T(8,128)(2,1)} %get-tuple-element.320.refs_1_, bf16[512,128]{1,0:T(8,128)(2,1)} %get-tuple-element.200.refs_2_, bf16[3,512,128]{2,1,0:T(8,128)(2,1)} %get-tuple-element.229.refs_3_, ...), custom_call_target="tpu_custom_call" | custom-call | flops 25769803776 | bytes 8388608 | tf_op jit(solution)/shard_map/attention/pallas_call | solution.py:635
  331.1 41.1 %projection.3 = (f32[512,1024]{1,0:T(8,128)}, bf16[512,1024]{1,0:T(8,128)(2,1)}, f32[8,1024]{1,0:T(8,128)}, bf16[512,1024]{1,0:T(8,128)(2,1)}) custom-call(f32[512,1]{1,0:T(8,128)} %get-tuple-element.194.refs_0_.refs_3_, f32[512,1024]{1,0:T(8,128)} %get-tuple-element.234.refs_1_, f32[4,56,128]{2,1,0:T(8,128)} %get-tuple-element.213.refs_2_.refs_1_.refs_5_, ...), custom_call_target="tpu_custom_call" | custom-call | flops 16106127360 | bytes 10485760 | tf_op jit(solution)/shard_map/projection/pallas_call | solution.py:398
  372.2 34.5 %all-gather.7.cloned.1.call-done = bf16[4096,2048]{1,0:T(8,128)(2,1)} async-done(((bf16[128,2048]{1,0:T(8,128)(2,1)}), bf16[4096,2048]{1,0:T(8,128)(2,1)}) %all-gather.7.cloned.1.call-update) | async-done | bytes 16777232 | tf_op jit(solution)/shard_map/all_gather | solution.py:2150
  406.7 26.9 %ffn.3 = (bf16[4,512,1024]{2,1,0:T(8,128)(2,1)}, bf16[4,512,1024]{2,1,0:T(8,128)(2,1)}, bf16[4,512,1024]{2,1,0:T(8,128)(2,1)}, bf16[512,1024]{1,0:T(8,128)(2,1)}...) custom-call(f32[512,1]{1,0:T(8,128)} %get-tuple-element.194.refs_0_., ...), custom_call_target="tpu_custom_call", output_to_operand_aliasing={{8}: (5, {})} | custom-call | flops 34359738368 | bytes 10485760 | tf_op jit(solution)/shard_map/ffn/pallas_call | solution.py:398
  433.6 34.2 %ffn_back.2 = (bf16[4,512,1024]{2,1,0:T(8,128)(2,1)}, bf16[8,128,512]{2,1,0:T(8,128)(2,1)}, bf16[8,128,512]{2,1,0:T(8,128)(2,1)}, f32[512,1024]{1,0:T(8,128)}, f...) custom-call(bf16[512,1024]{1,0:T(8,128)(2,1)} %get-tuple-element.241.refs_0_, ...), custom_call_target="tpu_custom_call" | custom-call | flops 34359738368 | bytes 10485760 | tf_op jit(solution)/shard_map/ffn_back/pallas_call | solution.py:398
  467.9 11.5 %ffn_grad.4.refs_4_ = bf16[4,4,128,2048]{3,2,1,0:T(8,128)(2,1)} custom-call(s32[18]{0:T(128)} %stack.63.refs_0_, bf16[8,128,512]{2,1,0:T(8,128)(2,1)} %get-tuple-element.257.refs_1_, bf16[8,128,512]{2,1,0:T(8,128)(2,1)} %get-tuple-element.250.refs_2_, bf16[4,512,1024]{2,1,0:T(8,128)(2,1)} %get-tuple-element.248.refs_3_.refs_4_, ...), custom_call_target="tpu_custom_call" | custom-call | flops 17179869184 | bytes 25165824 | tf_op jit(solution)/shard_map/ffn_grad/pallas_call | solution.py:1293
  479.3 28.0 %projection_back.2 = (bf16[4,512,128]{2,1,0:T(8,128)(2,1)}, bf16[4,512,128]{2,1,0:T(8,128)(2,1)}, bf16[8,128,512]{2,1,0:T(8,128)(2,1)}, bf16[512,1024]{1,0:T(8,1...) custom-call(f32[512,1024]{1,0:T(8,128)} %get-tuple-element.269.refs_, ...), custom_call_target="tpu_custom_call", output_to_operand_aliasing={{6}: (6, {})} | custom-call | flops 16106127360 | bytes 10485760 | tf_op jit(solution)/shard_map/projection_back/pallas_call | solution.py:398
  507.3 12.7 %ffn_grad.5 = (bf16[2,4,128,1024]{3,2,1,0:T(8,128)(2,1)}, bf16[2,4,128,1024]{3,2,1,0:T(8,128)(2,1)}, bf16[2,4,128,1024]{3,2,1,0:T(8,128)(2,1)}, bf16[2,4,128,1024]{3,2,1,0:T(8,128)(2,1)}) custom-call(s32[18]{0:T(128)} %stack.63.refs_0_, bf16[8,128,512]{2,1,0:T(8,128)(2,1)} %get-tuple-element.257.refs_1_, bf16[8,128,512]{2,1,0:T(8,128)(2,1)} %get-tuple-element.250.refs_2_, ...), custom_call_target="tpu_custom_call" | custom-call | flops 17179869184 | bytes 25165824 | tf_op jit(solution)/shard_map/ffn_grad/pallas_call | solution.py:1293
  520.0 7.5 collective-permute-start.6
  527.5 17.3 %attention_back.4 = (bf16[3,512,128]{2,1,0:T(8,128)(2,1)}, bf16[3,512,128]{2,1,0:T(8,128)(2,1)}, bf16[3,512,128]{2,1,0:T(8,128)(2,1)}, bf16[3,512,128]{2,1,0:T(8,128)(2,1)}) custom-call(s32[16]{0:T(128)} %get-tuple-element.196.refs_0_, bf16[4,512,128]{2,1,0:T(8,128)(2,1)} %get-tuple-element.320.refs_1_, bf16[512,128]{1,0:T(8,128)(2,1)} %get-tuple-element.200.refs_2_, ...), custom_call_target="tpu_custom_call" | custom-call | flops 30064771072 | bytes 8388608 | tf_op jit(solution)/shard_map/attention_back/pallas_call | solution.py:635
  547.6 7.4 collective-permute-done.6
  555.0 17.2 %attention_back.5 = (bf16[3,512,128]{2,1,0:T(8,128)(2,1)}, bf16[3,512,128]{2,1,0:T(8,128)(2,1)}, bf16[3,512,128]{2,1,0:T(8,128)(2,1)}, bf16[3,512,128]{2,1,0:T(8,128)(2,1)}) custom-call(s32[16]{0:T(128)} %get-tuple-element.196.refs_0_, bf16[4,512,128]{2,1,0:T(8,128)(2,1)} %get-tuple-element.320.refs_1_, bf16[512,128]{1,0:T(8,128)(2,1)} %get-tuple-element.200.refs_2_, ...), custom_call_target="tpu_custom_call" | custom-call | flops 30064771072 | bytes 8388608 | tf_op jit(solution)/shard_map/attention_back/pallas_call | solution.py:635
  573.2 29.2 %qkv_back.2 = (bf16[3,512,128]{2,1,0:T(8,128)(2,1)}, bf16[3,512,128]{2,1,0:T(8,128)(2,1)}, bf16[3,512,128]{2,1,0:T(8,128)(2,1)}, bf16[3,512,128]{2,1,0:T(8,128)(...) custom-call(f32[512,1024]{1,0:T(8,128)} %get-tuple-element.269.refs_, ...), custom_call_target="tpu_custom_call" | custom-call | flops 26843545600 | bytes 10485760 | tf_op jit(solution)/shard_map/qkv_back/pallas_call | solution.py:398
  602.3 8.3 head_grad.3.refs_7_
  610.7 3.7 fusion.4
  615.5 2.1 fusion.5
  618.5 26.7 %ffn_back.3 = (bf16[4,512,1024]{2,1,0:T(8,128)(2,1)}, bf16[8,128,512]{2,1,0:T(8,128)(2,1)}, bf16[8,128,512]{2,1,0:T(8,128)(2,1)}, f32[512,1024]{1,0:T(8,128)}, f...) custom-call(f32[512,1024]{1,0:T(8,128)} %get-tuple-element.290.refs_0_, ...), custom_call_target="tpu_custom_call" | custom-call | flops 34359738368 | bytes 10485760 | tf_op jit(solution)/shard_map/ffn_back/pallas_call | solution.py:398
  645.3 9.4 head_grad.4
  655.0 11.8 %ffn_grad.6.refs_4_ = bf16[4,4,128,2048]{3,2,1,0:T(8,128)(2,1)} custom-call(s32[18]{0:T(128)} %stack.63.refs_0_, bf16[8,128,512]{2,1,0:T(8,128)(2,1)} %get-tuple-element.311.refs_1_, bf16[8,128,512]{2,1,0:T(8,128)(2,1)} %get-tuple-element.301.refs_2_, bf16[4,512,1024]{2,1,0:T(8,128)(2,1)} %get-tuple-element.296.refs_3_.refs_4_, ...), custom_call_target="tpu_custom_call" | custom-call | flops 17179869184 | bytes 25165824 | tf_op jit(solution)/shard_map/ffn_grad/pallas_call | solution.py:1293
  669.9 2.1 collective-permute-start.14
  672.9 20.4 %projection_back.3 = (bf16[4,512,128]{2,1,0:T(8,128)(2,1)}, bf16[4,512,128]{2,1,0:T(8,128)(2,1)}, bf16[8,128,512]{2,1,0:T(8,128)(2,1)}, bf16[512,1024]{1,0:T(8,1...) custom-call(f32[512,1024]{1,0:T(8,128)} %get-tuple-element.327.refs_0_, ...), custom_call_target="tpu_custom_call" | custom-call | flops 16106127360 | bytes 10485760 | tf_op jit(solution)/shard_map/projection_back/pallas_call | solution.py:398
  693.4 3.6 fusion.7
  698.3 12.7 %ffn_grad.7 = (bf16[2,4,128,2048]{3,2,1,0:T(8,128)(2,1)}, bf16[2,4,128,2048]{3,2,1,0:T(8,128)(2,1)}) custom-call(s32[18]{0:T(128)} %stack.63.refs_0_, bf16[8,128,512]{2,1,0:T(8,128)(2,1)} %get-tuple-element.311.refs_1_, bf16[8,128,512]{2,1,0:T(8,128)(2,1)} %get-tuple-element.301.refs_2_, bf16[4,512,1024]{2,1,0:T(8,128)(2,1)} %get-tuple-element.296.refs_3_.refs_4_, ...), custom_call_target="tpu_custom_call" | custom-call | flops 17179869184 | bytes 25165824 | tf_op jit(solution)/shard_map/ffn_grad/pallas_call | solution.py:1293
  715.1 17.0 %attention_back.6 = (bf16[3,512,128]{2,1,0:T(8,128)(2,1)}, bf16[3,512,128]{2,1,0:T(8,128)(2,1)}, bf16[3,512,128]{2,1,0:T(8,128)(2,1)}, bf16[3,512,128]{2,1,0:T(8,128)(2,1)}) custom-call(s32[16]{0:T(128)} %get-tuple-element.196.refs_0_, bf16[4,512,128]{2,1,0:T(8,128)(2,1)} %get-tuple-element.320.refs_1_, bf16[512,128]{1,0:T(8,128)(2,1)} %get-tuple-element.200.refs_2_, ...), custom_call_target="tpu_custom_call" | custom-call | flops 30064771072 | bytes 8388608 | tf_op jit(solution)/shard_map/attention_back/pallas_call | solution.py:635
  732.8 12.0 %collective-permute-start.25 = (bf16[128,1024]{1,0:T(8,128)(2,1)}, bf16[128,1024]{1,0:T(8,128)(2,1)}, u32[]{:S(2)}, u32[]{:S(2)}) collective-permute-start(bf16[128,1024]{1,0:T(8,128)(2,1)} %slice_bitcast_fusion), channel_id=1, source_target_pairs={{0,2},{1,3},{2,0},{3,1},{4,6},{5,7},{6,4},{7,5},{8,10},{9,11},{10,... | collective-permute-start | bytes 786440 | tf_op jit(solution)/shard_map/ppermute | solution.py:2143
  748.9 17.2 %attention_back.7 = (bf16[3,512,128]{2,1,0:T(8,128)(2,1)}, bf16[3,512,128]{2,1,0:T(8,128)(2,1)}, bf16[3,512,128]{2,1,0:T(8,128)(2,1)}, bf16[3,512,128]{2,1,0:T(8,128)(2,1)}) custom-call(s32[16]{0:T(128)} %get-tuple-element.196.refs_0_, bf16[4,512,128]{2,1,0:T(8,128)(2,1)} %get-tuple-element.320.refs_1_, bf16[512,128]{1,0:T(8,128)(2,1)} %get-tuple-element.200.refs_2_, ...), custom_call_target="tpu_custom_call" | custom-call | flops 30064771072 | bytes 8388608 | tf_op jit(solution)/shard_map/attention_back/pallas_call | solution.py:635
  767.2 3.3 collective-permute-start.20
  770.4 5.3 fusion.1
  775.7 4.4 collective-permute-start.21
  781.9 44.1 %qkv_back.3 = (bf16[3,512,128]{2,1,0:T(8,128)(2,1)}, bf16[3,512,128]{2,1,0:T(8,128)(2,1)}, bf16[3,512,128]{2,1,0:T(8,128)(2,1)}, bf16[3,512,128]{2,1,0:T(8,128)(...) custom-call(f32[512,1024]{1,0:T(8,128)} %get-tuple-element.327.refs_, ...), custom_call_target="tpu_custom_call" | custom-call | flops 26843545600 | bytes 10485760 | tf_op jit(solution)/shard_map/qkv_back/pallas_call | solution.py:398
  826.3 15.2 %collective-permute-start.23 = (bf16[128,1024]{1,0:T(8,128)(2,1)S(1)}, bf16[128,1024]{1,0:T(8,128)(2,1)S(1)}, u32[]{:S(2)}, u32[]{:S(2)}) collective-permute-start(bf16[128,1024]{1,0:T(8,128)(2,1)S(1)} %slice_bitcast_fusion.2), channel_id=1, source_target_pairs={{0,2},{1,3},{2,0},{3,1},{4,6},{5,7},{6,4},{7,5},{8,10},{9,11},{10,... | collective-permute-start | bytes 786440 | tf_op jit(solution)/shard_map/ppermute | solution.py:2143
  841.6 12.0 %head_grad.5.refs_1_ = bf16[8,4,128,1024]{3,2,1,0:T(8,128)(2,1)} custom-call(s32[18]{0:T(128)} %stack.63.refs_0_, bf16[8,128,512]{2,1,0:T(8,128)(2,1)} %get-tuple-element.339.refs_1_, bf16[8,128,512]{2,1,0:T(8,128)(2,1)} %get-tuple-element.340.refs_2_, bf16[512,1024]{1,0:T(8,128)(2,1)} %get-tuple-element.341.refs_3_, ...), custom_call_target="tpu_custom_call" | custom-call | flops 34359738368 | bytes 16777216 | tf_op jit(solution)/shard_map/head_grad/pallas_call | solution.py:1338
  853.6 3.8 add_convert_fusion.refs_2_
  858.1 88.3 %end.1 = (bf16[4,512,256]{2,1,0:T(8,128)(2,1)}, f32[2,3,128,256]{3,2,1,0:T(8,128)}, f32[2,256,128]{2,1,0:T(8,128)}, f32[2,128,1024]{2,1,0:T(8,128)}, f32[2,1024,...) custom-call(bf16[512,1024]{1,0:T(8,128)(2,1)} %get-tuple-element.345, ...), custom_call_target="tpu_custom_call" | custom-call | bytes 314572800 | tf_op jit(solution)/shard_map/end/pallas_call | solution.py:2045
  950.6 2.8 bitcast_convert_fusion
  (140 shorter events, 47.5 us)
Async XLA Ops:
  7.2 251.2 %all-gather.5.cloned.1.call-start = ((), (), s32[]{:S(2)}) async-start(), calls=%async_computation | async-start | bytes 8650752 | tf_op jit(solution)/shard_map/all_gather | solution.py:2150
  175.6 231.1 %all-gather.7.cloned.1.call-start = ((), (), s32[]{:S(2)}) async-start(), calls=%async_computation.1 | async-start | bytes 17301504 | tf_op jit(solution)/shard_map/all_gather | solution.py:2150
  176.3 16.3 %collective-permute-start = (bf16[3,512,128]{2,1,0:T(8,128)(2,1)}, bf16[3,512,128]{2,1,0:T(8,128)(2,1)S(1)}, u32[]{:S(2)}, u32[]{:S(2)}) collective-permute-start(bf16[3,512,128]{2,1,0:T(8,128)(2,1)} %get-tuple-element.208), channel_id=1, source_target_pairs={{0,4},{4,8},{8,12},{12,0},{16,20},{20,24},{24,28},{28,16},{1,5},{5... | collective-permute-start | bytes 1179656 | tf_op jit(solution)/shard_map/ppermute | solution.py:2140
  176.5 16.1 %collective-permute-start.1 = (bf16[3,512,128]{2,1,0:T(8,128)(2,1)}, bf16[3,512,128]{2,1,0:T(8,128)(2,1)S(1)}, u32[]{:S(2)}, u32[]{:S(2)}) collective-permute-start(bf16[3,512,128]{2,1,0:T(8,128)(2,1)} %get-tuple-element.209), channel_id=1, source_target_pairs={{0,8},{4,12},{8,0},{12,4},{16,24},{20,28},{24,16},{28,20},{1,9},{5... | collective-permute-start | bytes 1179656 | tf_op jit(solution)/shard_map/ppermute | solution.py:2140
  177.6 19.4 %collective-permute-start.2 = (bf16[3,512,128]{2,1,0:T(8,128)(2,1)}, bf16[3,512,128]{2,1,0:T(8,128)(2,1)S(1)}, u32[]{:S(2)}, u32[]{:S(2)}) collective-permute-start(bf16[3,512,128]{2,1,0:T(8,128)(2,1)} %get-tuple-element.210), channel_id=1, source_target_pairs={{0,12},{4,0},{8,4},{12,8},{16,28},{20,16},{24,20},{28,24},{1,13},{... | collective-permute-start | bytes 1179656 | tf_op jit(solution)/shard_map/ppermute | solution.py:2140
  180.9 10.0 %copy-start.9 = (f32[2048,256]{1,0:T(8,128)S(1)}, f32[2048,256]{1,0:T(8,128)}, u32[]{:S(2)}) copy-start(f32[2048,256]{1,0:T(8,128)} %param.23) | copy-start | bytes 6291460
  192.6 4.4 copy-start.21
  192.6 4.4 copy-start.22
  287.0 13.1 %collective-permute-start.3 = (bf16[3,512,128]{2,1,0:T(8,128)(2,1)}, bf16[3,512,128]{2,1,0:T(8,128)(2,1)S(1)}, u32[]{:S(2)}, u32[]{:S(2)}) collective-permute-start(bf16[3,512,128]{2,1,0:T(8,128)(2,1)} %get-tuple-element.230), channel_id=1, source_target_pairs={{0,4},{4,8},{8,12},{12,0},{16,20},{20,24},{24,28},{28,16},{1,5},{5... | collective-permute-start | bytes 1179656 | tf_op jit(solution)/shard_map/ppermute | solution.py:2140
  287.8 17.1 %collective-permute-start.4 = (bf16[3,512,128]{2,1,0:T(8,128)(2,1)}, bf16[3,512,128]{2,1,0:T(8,128)(2,1)S(1)}, u32[]{:S(2)}, u32[]{:S(2)}) collective-permute-start(bf16[3,512,128]{2,1,0:T(8,128)(2,1)} %get-tuple-element.231), channel_id=1, source_target_pairs={{0,8},{4,12},{8,0},{12,4},{16,24},{20,28},{24,16},{28,20},{1,9},{5... | collective-permute-start | bytes 1179656 | tf_op jit(solution)/shard_map/ppermute | solution.py:2140
  289.0 31.5 %collective-permute-start.5 = (bf16[3,512,128]{2,1,0:T(8,128)(2,1)}, bf16[3,512,128]{2,1,0:T(8,128)(2,1)S(1)}, u32[]{:S(2)}, u32[]{:S(2)}) collective-permute-start(bf16[3,512,128]{2,1,0:T(8,128)(2,1)} %get-tuple-element.232), channel_id=1, source_target_pairs={{0,12},{4,0},{8,4},{12,8},{16,28},{20,16},{24,20},{28,24},{1,13},{... | collective-permute-start | bytes 1179656 | tf_op jit(solution)/shard_map/ppermute | solution.py:2140
  300.1 20.4 %copy-start.24 = (bf16[3,512,128]{2,1,0:T(8,128)(2,1)}, bf16[3,512,128]{2,1,0:T(8,128)(2,1)S(1)}, u32[]{:S(2)}) copy-start(bf16[3,512,128]{2,1,0:T(8,128)(2,1)S(1)} %collective-permute-done.3.refs_4_) | copy-start | bytes 1179652
  304.9 15.6 %copy-start.25 = (bf16[3,512,128]{2,1,0:T(8,128)(2,1)}, bf16[3,512,128]{2,1,0:T(8,128)(2,1)S(1)}, u32[]{:S(2)}) copy-start(bf16[3,512,128]{2,1,0:T(8,128)(2,1)S(1)} %collective-permute-done.4.refs_5_) | copy-start | bytes 1179652
  520.0 35.1 %collective-permute-start.6 = (bf16[2,4,128,1024]{3,2,1,0:T(8,128)(2,1)}, bf16[2,4,128,1024]{3,2,1,0:T(8,128)(2,1)S(1)}, u32[]{:S(2)}, u32[]{:S(2)}) collective-permute-start(bf16[2,4,128,1024]{3,2,1,0:T(8,128)(2,1)} %get-tuple-element.264), channel_id=1, source_target_pairs={{0,16},{4,12},{8,24},{12,4},{16,0},{20,28},{24,8},{28,20},{1,17},{... | collective-permute-start | bytes 6291464 | tf_op jit(solution)/shard_map/ppermute | solution.py:2372
  527.5 18.6 %copy-start.13 = (bf16[4,512,256]{2,1,0:T(8,128)(2,1)S(1)}, bf16[4,512,256]{2,1,0:T(8,128)(2,1)}, u32[]{:S(2)}) copy-start(bf16[4,512,256]{2,1,0:T(8,128)(2,1)} %get-tuple-element.255) | copy-start | bytes 3145732
  544.8 27.5 %collective-permute-start.7 = (bf16[3,512,128]{2,1,0:T(8,128)(2,1)}, bf16[3,512,128]{2,1,0:T(8,128)(2,1)S(1)}, u32[]{:S(2)}, u32[]{:S(2)}) collective-permute-start(bf16[3,512,128]{2,1,0:T(8,128)(2,1)} %get-tuple-element.270), channel_id=1, source_target_pairs={{0,12},{4,0},{8,4},{12,8},{16,28},{20,16},{24,20},{28,24},{1,13},{... | collective-permute-start | bytes 1179656 | tf_op jit(solution)/shard_map/ppermute | solution.py:2140
  544.8 27.5 %collective-permute-start.8 = (bf16[3,512,128]{2,1,0:T(8,128)(2,1)}, bf16[3,512,128]{2,1,0:T(8,128)(2,1)S(1)}, u32[]{:S(2)}, u32[]{:S(2)}) collective-permute-start(bf16[3,512,128]{2,1,0:T(8,128)(2,1)} %get-tuple-element.271), channel_id=1, source_target_pairs={{0,8},{4,12},{8,0},{12,4},{16,24},{20,28},{24,16},{28,20},{1,9},{5... | collective-permute-start | bytes 1179656 | tf_op jit(solution)/shard_map/ppermute | solution.py:2140
  545.8 26.4 %collective-permute-start.9 = (bf16[3,512,128]{2,1,0:T(8,128)(2,1)}, bf16[3,512,128]{2,1,0:T(8,128)(2,1)}, u32[]{:S(2)}, u32[]{:S(2)}) collective-permute-start(bf16[3,512,128]{2,1,0:T(8,128)(2,1)} %get-tuple-element.272), channel_id=1, source_target_pairs={{0,4},{4,8},{8,12},{12,0},{16,20},{20,24},{24,28},{28,16},{1,5},{5... | collective-permute-start | bytes 1179656 | tf_op jit(solution)/shard_map/ppermute | solution.py:2140
  546.1 64.6 %collective-permute-start.10 = (bf16[2,4,128,1024]{3,2,1,0:T(8,128)(2,1)}, bf16[2,4,128,1024]{3,2,1,0:T(8,128)(2,1)}, u32[]{:S(2)}, u32[]{:S(2)}) collective-permute-start(bf16[2,4,128,1024]{3,2,1,0:T(8,128)(2,1)} %get-tuple-element.287), channel_id=1, source_target_pairs={{0,16},{4,20},{8,24},{12,28},{16,0},{20,4},{24,8},{28,12},{1,17},{... | collective-permute-start | bytes 6291464 | tf_op jit(solution)/shard_map/ppermute | solution.py:2371
  555.0 17.2 %copy-start.6 = (bf16[2,4,128,1024]{3,2,1,0:T(8,128)(2,1)}, bf16[2,4,128,1024]{3,2,1,0:T(8,128)(2,1)S(1)}, u32[]{:S(2)}) copy-start(bf16[2,4,128,1024]{3,2,1,0:T(8,128)(2,1)S(1)} %collective-permute-done.6) | copy-start | bytes 6291460
  602.3 8.4 copy-start.5
  610.7 4.8 copy-start.4
  610.7 4.8 copy-start.7
  614.4 54.0 %collective-permute-start.11 = (bf16[4,128,1024]{2,1,0:T(8,128)(2,1)}, bf16[4,128,1024]{2,1,0:T(8,128)(2,1)S(1)}, u32[]{:S(2)}, u32[]{:S(2)}) collective-permute-start(bf16[4,128,1024]{2,1,0:T(8,128)(2,1)} %get-tuple-element.400), channel_id=1, source_target_pairs={{0,8},{4,12},{8,0},{12,4},{16,24},{20,28},{24,16},{28,20},{1,9},{5... | collective-permute-start | bytes 3145736 | tf_op jit(solution)/shard_map/ppermute | solution.py:2414
  617.6 49.2 %collective-permute-start.12 = (bf16[4,128,1024]{2,1,0:T(8,128)(2,1)}, bf16[4,128,1024]{2,1,0:T(8,128)(2,1)}, u32[]{:S(2)}, u32[]{:S(2)}) collective-permute-start(bf16[4,128,1024]{2,1,0:T(8,128)(2,1)} %get-tuple-element.398), channel_id=1, source_target_pairs={{0,8},{4,20},{8,0},{12,28},{16,24},{20,4},{24,16},{28,12},{1,9},{5... | collective-permute-start | bytes 3145736 | tf_op jit(solution)/shard_map/ppermute | solution.py:2415
  654.6 38.7 %collective-permute-start.13 = (bf16[2,4,128,1024]{3,2,1,0:T(8,128)(2,1)}, bf16[2,4,128,1024]{3,2,1,0:T(8,128)(2,1)}, u32[]{:S(2)}, u32[]{:S(2)}) collective-permute-start(bf16[2,4,128,1024]{3,2,1,0:T(8,128)(2,1)} %get-tuple-element.310), channel_id=1, source_target_pairs={{0,16},{4,12},{8,24},{12,4},{16,0},{20,28},{24,8},{28,20},{1,17},{... | collective-permute-start | bytes 6291464 | tf_op jit(solution)/shard_map/ppermute | solution.py:2343
  669.9 42.4 %collective-permute-start.14 = (bf16[2,128,1024]{2,1,0:T(8,128)(2,1)}, bf16[2,128,1024]{2,1,0:T(8,128)(2,1)}, u32[]{:S(2)}, u32[]{:S(2)}) collective-permute-start(bf16[2,128,1024]{2,1,0:T(8,128)(2,1)} %get-tuple-element.404), channel_id=1, source_target_pairs={{0,1},{1,0},{2,3},{3,2},{4,5},{5,4},{6,7},{7,6},{8,9},{9,8},{10,11... | collective-permute-start | bytes 1572872 | tf_op jit(solution)/shard_map/ppermute | solution.py:2143
  672.9 38.1 %collective-permute-start.15 = (bf16[2,128,1024]{2,1,0:T(8,128)(2,1)S(1)}, bf16[2,128,1024]{2,1,0:T(8,128)(2,1)}, u32[]{:S(2)}, u32[]{:S(2)}) collective-permute-start(bf16[2,128,1024]{2,1,0:T(8,128)(2,1)S(1)} %get-tuple-element.402), channel_id=1, source_target_pairs={{0,1},{1,0},{2,3},{3,2},{4,5},{5,4},{6,7},{7,6},{8,9},{9,8},{10,11... | collective-permute-start | bytes 1572872 | tf_op jit(solution)/shard_map/ppermute | solution.py:2143
  672.9 20.4 %copy-start.8 = (bf16[2,4,128,1024]{3,2,1,0:T(8,128)(2,1)S(1)}, bf16[2,4,128,1024]{3,2,1,0:T(8,128)(2,1)}, u32[]{:S(2)}) copy-start(bf16[2,4,128,1024]{3,2,1,0:T(8,128)(2,1)} %get-tuple-element.308) | copy-start | bytes 6291460
  696.9 48.0 %collective-permute-start.16 = (bf16[4,128,1024]{2,1,0:T(8,128)(2,1)}, bf16[4,128,1024]{2,1,0:T(8,128)(2,1)S(1)}, u32[]{:S(2)}, u32[]{:S(2)}) collective-permute-start(bf16[4,128,1024]{2,1,0:T(8,128)(2,1)} %get-tuple-element.396), channel_id=1, source_target_pairs={{0,8},{4,20},{8,0},{12,28},{16,24},{20,4},{24,16},{28,12},{1,9},{5... | collective-permute-start | bytes 3145736 | tf_op jit(solution)/shard_map/ppermute | solution.py:2367
  698.3 12.8 %copy-start.11 = (bf16[2,128,1024]{2,1,0:T(8,128)(2,1)S(1)}, bf16[2,128,1024]{2,1,0:T(8,128)(2,1)}, u32[]{:S(2)}) copy-start(bf16[2,128,1024]{2,1,0:T(8,128)(2,1)} %get-tuple-element.315) | copy-start | bytes 1572868
  698.3 14.0 %copy-start.10 = (bf16[2,128,1024]{2,1,0:T(8,128)(2,1)S(1)}, bf16[2,128,1024]{2,1,0:T(8,128)(2,1)}, u32[]{:S(2)}) copy-start(bf16[2,128,1024]{2,1,0:T(8,128)(2,1)} %get-tuple-element.314) | copy-start | bytes 1572868
  712.3 19.8 %copy-start.1 = (bf16[2,128,1024]{2,1,0:T(8,128)(2,1)}, bf16[2,128,1024]{2,1,0:T(8,128)(2,1)S(1)}, u32[]{:S(2)}) copy-start(bf16[2,128,1024]{2,1,0:T(8,128)(2,1)S(1)} %add_convert_fusion.13.refs_8_) | copy-start | bytes 1572868
  713.8 18.3 %copy-start.2 = (bf16[2,128,1024]{2,1,0:T(8,128)(2,1)}, bf16[2,128,1024]{2,1,0:T(8,128)(2,1)S(1)}, u32[]{:S(2)}) copy-start(bf16[2,128,1024]{2,1,0:T(8,128)(2,1)S(1)} %add_convert_fusion.14.refs_6_) | copy-start | bytes 1572868
  713.8 53.1 %collective-permute-start.17 = (bf16[2,4,128,2048]{3,2,1,0:T(8,128)(2,1)}, bf16[2,4,128,2048]{3,2,1,0:T(8,128)(2,1)}, u32[]{:S(2)}, u32[]{:S(2)}) collective-permute-start(bf16[2,4,128,2048]{3,2,1,0:T(8,128)(2,1)} %get-tuple-element.326), channel_id=1, source_target_pairs={{0,16},{4,12},{8,24},{12,4},{16,0},{20,28},{24,8},{28,20},{1,17},{... | collective-permute-start | bytes 12582920 | tf_op jit(solution)/shard_map/ppermute | solution.py:2379
  732.8 124.6 %collective-permute-start.25 = (bf16[128,1024]{1,0:T(8,128)(2,1)}, bf16[128,1024]{1,0:T(8,128)(2,1)}, u32[]{:S(2)}, u32[]{:S(2)}) collective-permute-start(bf16[128,1024]{1,0:T(8,128)(2,1)} %slice_bitcast_fusion), channel_id=1, source_target_pairs={{0,2},{1,3},{2,0},{3,1},{4,6},{5,7},{6,4},{7,5},{8,10},{9,11},{10,... | collective-permute-start | bytes 786440 | tf_op jit(solution)/shard_map/ppermute | solution.py:2143
  744.8 112.6 %collective-permute-start.24 = (bf16[128,1024]{1,0:T(8,128)(2,1)S(1)}, bf16[128,1024]{1,0:T(8,128)(2,1)}, u32[]{:S(2)}, u32[]{:S(2)}) collective-permute-start(bf16[128,1024]{1,0:T(8,128)(2,1)S(1)} %slice_bitcast_fusion.1), channel_id=1, source_target_pairs={{0,2},{1,3},{2,0},{3,1},{4,6},{5,7},{6,4},{7,5},{8,10},{9,11},{10,... | collective-permute-start | bytes 786440 | tf_op jit(solution)/shard_map/ppermute | solution.py:2143
  744.9 30.9 %collective-permute-start.18 = (bf16[3,512,128]{2,1,0:T(8,128)(2,1)}, bf16[3,512,128]{2,1,0:T(8,128)(2,1)}, u32[]{:S(2)}, u32[]{:S(2)}) collective-permute-start(bf16[3,512,128]{2,1,0:T(8,128)(2,1)} %get-tuple-element.328), channel_id=1, source_target_pairs={{0,12},{4,0},{8,4},{12,8},{16,28},{20,16},{24,20},{28,24},{1,13},{... | collective-permute-start | bytes 1179656 | tf_op jit(solution)/shard_map/ppermute | solution.py:2140
  745.9 34.2 %collective-permute-start.19 = (bf16[3,512,128]{2,1,0:T(8,128)(2,1)}, bf16[3,512,128]{2,1,0:T(8,128)(2,1)}, u32[]{:S(2)}, u32[]{:S(2)}) collective-permute-start(bf16[3,512,128]{2,1,0:T(8,128)(2,1)} %get-tuple-element.329), channel_id=1, source_target_pairs={{0,8},{4,12},{8,0},{12,4},{16,24},{20,28},{24,16},{28,20},{1,9},{5... | collective-permute-start | bytes 1179656 | tf_op jit(solution)/shard_map/ppermute | solution.py:2140
  748.9 17.2 %copy-start = (bf16[4,128,1024]{2,1,0:T(8,128)(2,1)}, bf16[4,128,1024]{2,1,0:T(8,128)(2,1)S(1)}, u32[]{:S(2)}) copy-start(bf16[4,128,1024]{2,1,0:T(8,128)(2,1)S(1)} %add_convert_fusion.3) | copy-start | bytes 3145732
  767.2 14.0 %collective-permute-start.20 = (bf16[3,512,128]{2,1,0:T(8,128)(2,1)S(1)}, bf16[3,512,128]{2,1,0:T(8,128)(2,1)S(1)}, u32[]{:S(2)}, u32[]{:S(2)}) collective-permute-start(bf16[3,512,128]{2,1,0:T(8,128)(2,1)S(1)} %copy-done.29), channel_id=1, source_target_pairs={{0,4},{4,8},{8,12},{12,0},{16,20},{20,24},{24,28},{28,16},{1,5},{5... | collective-permute-start | bytes 1179656 | tf_op jit(solution)/shard_map/ppermute | solution.py:2140
  775.7 50.4 %collective-permute-start.21 = (bf16[2,128,1024]{2,1,0:T(8,128)(2,1)}, bf16[2,128,1024]{2,1,0:T(8,128)(2,1)S(1)}, u32[]{:S(2)}, u32[]{:S(2)}) collective-permute-start(bf16[2,128,1024]{2,1,0:T(8,128)(2,1)} %slice.97), channel_id=1, source_target_pairs={{0,1},{1,0},{2,3},{3,2},{4,5},{5,4},{6,7},{7,6},{8,9},{9,8},{10,11... | collective-permute-start | bytes 1572872 | tf_op jit(solution)/shard_map/ppermute | solution.py:2143
  780.1 73.5 %collective-permute-start.22 = (bf16[4,128,2048]{2,1,0:T(8,128)(2,1)}, bf16[4,128,2048]{2,1,0:T(8,128)(2,1)}, u32[]{:S(2)}, u32[]{:S(2)}) collective-permute-start(bf16[4,128,2048]{2,1,0:T(8,128)(2,1)} %get-tuple-element.394), channel_id=1, source_target_pairs={{0,8},{4,20},{8,0},{12,28},{16,24},{20,4},{24,16},{28,12},{1,9},{5... | collective-permute-start | bytes 6291464 | tf_op jit(solution)/shard_map/ppermute | solution.py:2394
  781.9 44.2 %slice-start = ((bf16[4,128,1024]{2,1,0:T(8,128)(2,1)}), bf16[2,128,1024]{2,1,0:T(8,128)(2,1)S(1)}, s32[]{:S(2)}) async-start(bf16[4,128,1024]{2,1,0:T(8,128)(2,1)} %copy-done), calls=%async_computation.2 | async-start | bytes 1048576 | tf_op jit(solution)/shard_map/slice | solution.py:2405
  826.3 27.3 %copy-start.3 = (bf16[2,128,1024]{2,1,0:T(8,128)(2,1)}, bf16[2,128,1024]{2,1,0:T(8,128)(2,1)S(1)}, u32[]{:S(2)}) copy-start(bf16[2,128,1024]{2,1,0:T(8,128)(2,1)S(1)} %add_convert_fusion.12.refs_4_) | copy-start | bytes 1572868
  826.3 31.1 %collective-permute-start.23 = (bf16[128,1024]{1,0:T(8,128)(2,1)S(1)}, bf16[128,1024]{1,0:T(8,128)(2,1)S(1)}, u32[]{:S(2)}, u32[]{:S(2)}) collective-permute-start(bf16[128,1024]{1,0:T(8,128)(2,1)S(1)} %slice_bitcast_fusion.2), channel_id=1, source_target_pairs={{0,2},{1,3},{2,0},{3,1},{4,6},{5,7},{6,4},{7,5},{8,10},{9,11},{10,... | collective-permute-start | bytes 786440 | tf_op jit(solution)/shard_map/ppermute | solution.py:2143
  946.4 6.9 copy-start.16
  950.6 4.4 copy-start.15
  (12 other events, 17.5 us)
Sparse Core Ops, SparseCore 0:
  175.7 82.6 all-gather.4
  261.4 145.2 all-gather.6
